TPU v7x, 32 devices: a whole 2x2x4 slice. The times are simulated.
32 devices in a mesh: dp: 8 (over y, x, core), tensor: 4 (over z).
Axes of the slice: x: 2, y: 2, z: 4, core: 2. Of those that a mesh axis runs over, the one named last changes fastest.
Arguments:
- hidden_in: bfloat16 [16, 448, 768], P('dp', 'tensor'), may hold values from -6 to 6
- frames: bfloat16 [16, 1500, 768], P('dp'), may hold values from -6 to 6
- cotangent: bfloat16 [16, 448, 768], P('dp', 'tensor'), may hold values from -6 to 6
- segments: int32 [16, 448], P('dp'), may hold values from 0 to 3, never falling along the last dimension, each value on 1 to 224 neighbouring positions
- stamps: int32 [16, 448], P('dp'), may hold values 0 or 1
- owner_list: int32 [64], replicated, may hold values from 0 to 63, as said below
- master_tiles: float32 [4, 64, 192, 192], P('tensor', 'dp')
- tile_first: float32 [4, 64, 192, 192], P('tensor', 'dp')
- tile_second: float32 [4, 64, 192, 192], P('tensor', 'dp'), as said below
- tile_stats: float32 [4, 64, 2, 192, 192], P('tensor', 'dp'), as said below
- tile_bases: float32 [4, 64, 2, 192, 192], P('tensor', 'dp'), as said below
- master_vectors: float32 [14592], P('dp')
- vector_first: float32 [14592], P('dp')
- vector_second: float32 [14592], P('dp'), as said below
Outputs:
- block_out: float32 [16, 448, 768], P('dp', 'tensor')
- input_grad: float32 [16, 448, 768], P('dp', 'tensor')
- frames_grad: float32 [16, 1500, 768], P('dp', 'tensor')
- new_tiles: float32 [4, 64, 192, 192], P('tensor', 'dp')
- new_tile_first: float32 [4, 64, 192, 192], P('tensor', 'dp')
- new_tile_second: float32 [4, 64, 192, 192], P('tensor', 'dp')
- new_tile_stats: float32 [4, 64, 2, 192, 192], P('tensor', 'dp')
- new_tile_bases: float32 [4, 64, 2, 192, 192], P('tensor', 'dp')
- new_vectors: float32 [14592], P('dp')
- new_vector_first: float32 [14592], P('dp')
- new_vector_second: float32 [14592], P('dp')
Inputs may be any that keep to these rules, and one draw needn't show every extreme that they name: `owner_list`: a permutation of 0 to 63. `tile_stats`: every statistics matrix is symmetric positive definite. `tile_bases`: every basis is orthogonal. `tile_second`: positive. `vector_second`: positive.
All inputs are finite; a program needn't handle non-finite values. No bound on the sum of `stamps` on one device may be relied on, other than what follows from the above.
Results may differ from a plain program's by a relative error of at most 0.015.
The roundings to bfloat16 on the way count: a program that leaves them out, or rounds other values in their place, can miss the bound.
Values may be sent and summed in bfloat16 or wider, within the bound.
No kernel may reach another device: no remote copies, remote signals or barrier semaphores. Data moves between devices by JAX's collectives and lax.ppermute only.
A program may use at most 192 MiB of HBM per device.

v0:
```python
import jax
import jax.numpy as jnp
from jax import lax
from jax.sharding import PartitionSpec as P

HEAD = 64
FF = 3072
STEP = 5


highest = lax.Precision.HIGHEST
norm_eps = 1e-05
beta_one = 0.9
beta_two = 0.95
adam_eps = 1e-08
rate_tiles = 0.05
rate_vectors = 0.3
score_scale = 0.125


def product(left_part, right_part):
    return jnp.dot(left_part, right_part, preferred_element_type=jnp.float32)


def times_transpose(left_part, right_part):
    return jnp.einsum("rn,kn->rk", left_part, right_part, preferred_element_type=jnp.float32)


def weight_grad(inputs, grads):
    return jnp.einsum("rk,rn->kn", inputs, grads, preferred_element_type=jnp.float32)


def flatten_rows(values):
    return values.reshape(-1, values.shape[-1])


def normalize(values, gain, shift):
    centre = jnp.mean(values, axis=-1, keepdims=True)
    centred = values - centre
    inverse = lax.rsqrt(jnp.mean(centred * centred, axis=-1, keepdims=True) + norm_eps)
    return centred * inverse * gain + shift


def normalize_back(values, gain, grads):
    centre = jnp.mean(values, axis=-1, keepdims=True)
    centred = values - centre
    inverse = lax.rsqrt(jnp.mean(centred * centred, axis=-1, keepdims=True) + norm_eps)
    unit_rows = centred * inverse
    scaled = grads * gain
    result = inverse * (
        scaled
        - jnp.mean(scaled, axis=-1, keepdims=True)
        - unit_rows * jnp.mean(scaled * unit_rows, axis=-1, keepdims=True)
    )
    return (result, jnp.sum(grads * unit_rows, axis=(0, 1)), jnp.sum(grads, axis=(0, 1)))


def tile_shapes(tile_side, model_width, hidden_units):
    return (
        [(model_width, tile_side)] * 6
        + [(tile_side, model_width)] * 2
        + [(model_width, hidden_units), (hidden_units, model_width)]
    )


def from_tiles(tiles, row_count, col_count):
    tile_side = tiles.shape[-1]
    return (
        tiles.reshape(row_count // tile_side, col_count // tile_side, tile_side, tile_side)
        .transpose(0, 2, 1, 3)
        .reshape(row_count, col_count)
    )


def to_tiles(matrix, tile_side):
    row_count, col_count = matrix.shape
    return (
        matrix.reshape(row_count // tile_side, tile_side, col_count // tile_side, tile_side)
        .transpose(0, 2, 1, 3)
        .reshape(-1, tile_side, tile_side)
    )


def local_matrices(tiles, model_width, hidden_units):
    tile_side = tiles.shape[-1]
    result = []
    offset = 0
    for row_count, col_count in tile_shapes(tile_side, model_width, hidden_units):
        number = row_count // tile_side * (col_count // tile_side)
        result.append(from_tiles(tiles[offset : offset + number], row_count, col_count))
        offset += number
    return result


def block_scores(query_block, key_heads, mask_rule, sequence, offset, block_rows):
    scores = (
        jnp.einsum("qhd,khd->hqk", query_block, key_heads, preferred_element_type=jnp.float32)
        * score_scale
    )
    if mask_rule is None:
        return scores
    return jnp.where(mask_rule(sequence, offset, block_rows)[None], scores, -1e30)


def attend_forward(queries, key_rows, value_rows, mask_rule):
    seq_count, length, span_width = queries.shape
    head_count = span_width // HEAD
    block_rows = min(512, length)
    per_sequence = length // block_rows

    def one_block(position):
        sequence = position // per_sequence
        offset = position % per_sequence * block_rows
        query_block = queries[sequence].reshape(block_rows, head_count, HEAD)
        key_heads = key_rows[sequence].reshape(-1, head_count, HEAD)
        value_heads = value_rows[sequence].reshape(-1, head_count, HEAD)
        scores = block_scores(query_block, key_heads, mask_rule, sequence, offset, block_rows)
        row_max = jnp.max(scores, axis=-1, keepdims=True)
        weights = jnp.exp(scores - row_max)
        row_total = jnp.sum(weights, axis=-1, keepdims=True)
        attention = (weights / row_total).astype(jnp.bfloat16)
        combined = jnp.einsum(
            "hqk,khd->qhd", attention, value_heads, preferred_element_type=jnp.float32
        )
        return (
            combined.reshape(block_rows, span_width).astype(jnp.bfloat16),
            (row_max + jnp.log(row_total))[..., 0],
        )

    combined, log_totals = lax.map(one_block, jnp.arange(seq_count * per_sequence, dtype=jnp.int32))
    return (combined, log_totals)


def attend_backward(queries, key_rows, value_rows, grad_out, log_totals, mask_rule):
    seq_count, length, span_width = queries.shape
    head_count = span_width // HEAD
    block_rows = min(512, length)
    per_sequence = length // block_rows
    key_count = key_rows.shape[1]

    def one_block(position):
        sequence = position // per_sequence
        offset = position % per_sequence * block_rows
        query_block = queries[sequence].reshape(block_rows, head_count, HEAD)
        grad_block = grad_out[sequence].reshape(block_rows, head_count, HEAD)
        key_heads = key_rows[sequence].reshape(-1, head_count, HEAD)
        value_heads = value_rows[sequence].reshape(-1, head_count, HEAD)
        scores = block_scores(query_block, key_heads, mask_rule, sequence, offset, block_rows)
        attention = jnp.exp(scores - log_totals[position][..., None])
        grad_attention = jnp.einsum(
            "qhd,khd->hqk", grad_block, value_heads, preferred_element_type=jnp.float32
        )
        row_dot = jnp.sum(attention * grad_attention, axis=-1, keepdims=True)
        grad_scores = (attention * (grad_attention - row_dot)).astype(jnp.bfloat16)
        grad_query = (
            jnp.einsum("hqk,khd->qhd", grad_scores, key_heads, preferred_element_type=jnp.float32)
            * score_scale
        )
        grad_key = (
            jnp.einsum("hqk,qhd->khd", grad_scores, query_block, preferred_element_type=jnp.float32)
            * score_scale
        )
        grad_value = jnp.einsum(
            "hqk,qhd->khd",
            attention.astype(jnp.bfloat16),
            grad_block,
            preferred_element_type=jnp.float32,
        )
        return (
            grad_query.reshape(block_rows, span_width).astype(jnp.bfloat16),
            grad_key.reshape(-1, span_width),
            grad_value.reshape(-1, span_width),
        )

    grad_query, grad_key, grad_value = lax.map(
        one_block, jnp.arange(seq_count * per_sequence, dtype=jnp.int32)
    )
    grad_key = (
        grad_key.reshape(seq_count, per_sequence, key_count, span_width)
        .sum(axis=1)
        .astype(jnp.bfloat16)
    )
    grad_value = (
        grad_value.reshape(seq_count, per_sequence, key_count, span_width)
        .sum(axis=1)
        .astype(jnp.bfloat16)
    )
    return (grad_query, grad_key, grad_value)


def rotate(basis_left, middle, basis_right):
    inner = jnp.einsum("nji,njk->nik", basis_left, middle, precision=highest)
    return jnp.einsum("nij,njk->nik", inner, basis_right, precision=highest)


def orthonormal(matrix):
    gram_matrix = jnp.einsum("nki,nkj->nij", matrix, matrix, precision=highest)
    factor = jnp.linalg.cholesky(gram_matrix)
    solved = jax.scipy.linalg.solve_triangular(factor, jnp.swapaxes(matrix, -1, -2), lower=True)
    return jnp.swapaxes(solved, -1, -2)


def soap_update(gradient, master, first, second, statistics, bases):
    basis_left = bases[:, 0]
    basis_right = bases[:, 1]
    new_first = beta_one * first + (1.0 - beta_one) * gradient
    rotated = rotate(basis_left, gradient, basis_right)
    new_second = beta_two * second + (1.0 - beta_two) * rotated * rotated
    moment_rot = rotate(basis_left, new_first, basis_right) / (1.0 - beta_one**STEP)
    normal_step = moment_rot / (jnp.sqrt(new_second / (1.0 - beta_two**STEP)) + adam_eps)
    back_left = jnp.einsum("nij,njk->nik", basis_left, normal_step, precision=highest)
    update = jnp.einsum("nij,nkj->nik", back_left, basis_right, precision=highest)
    new_master = master - rate_tiles * update
    stats_left = beta_two * statistics[:, 0] + (1.0 - beta_two) * jnp.einsum(
        "nij,nkj->nik", gradient, gradient, precision=highest
    )
    stats_right = beta_two * statistics[:, 1] + (1.0 - beta_two) * jnp.einsum(
        "nji,njk->nik", gradient, gradient, precision=highest
    )
    new_left = orthonormal(jnp.einsum("nij,njk->nik", stats_left, basis_left, precision=highest))
    new_right = orthonormal(jnp.einsum("nij,njk->nik", stats_right, basis_right, precision=highest))
    return (
        new_first,
        new_second,
        new_master,
        jnp.stack([stats_left, stats_right], axis=1),
        jnp.stack([new_left, new_right], axis=1),
    )


def shards(
    hidden_in,
    frames,
    cotangent,
    segments,
    stamps,
    owner_list,
    master_tiles,
    tile_first,
    tile_second,
    tile_stats,
    tile_bases,
    master_vectors,
    vector_first,
    vector_second,
):
    tensor_count = lax.axis_size("tensor")
    tensor_rank = lax.axis_index("tensor")
    seq_count, local_rows, model_width = hidden_in.shape
    full_rows = local_rows * tensor_count
    tile_side = master_tiles.shape[-1]
    hidden_units = FF // tensor_count
    tile_count = owner_list.shape[0]
    inverse = (
        jnp.zeros((tile_count,), jnp.int32)
        .at[owner_list]
        .set(jnp.arange(tile_count, dtype=jnp.int32))
    )
    gathered = lax.all_gather(master_tiles[0].astype(jnp.bfloat16), "dp", axis=0, tiled=True)
    by_ident = jnp.take(gathered, inverse, axis=0)
    (
        query_weight,
        key_weight,
        value_weight,
        cross_query_weight,
        cross_key_weight,
        cross_value_weight,
        output_weight,
        cross_output_weight,
        inner_weight,
        outer_weight,
    ) = local_matrices(by_ident, model_width, hidden_units)
    vectors = (
        lax.all_gather(master_vectors.astype(jnp.bfloat16), "dp", axis=0, tiled=True)
        .astype(jnp.float32)
        .reshape(19, model_width)
    )
    head_bias = lax.dynamic_slice_in_dim(vectors[11:15], tensor_rank * tile_side, tile_side, 1)
    inner_bias = lax.dynamic_index_in_dim(vectors[15:19], tensor_rank, 0, keepdims=False)

    def causal_mask(sequence, offset, block_rows):
        segment = segments[sequence]
        stamp_flags = stamps[sequence]
        query_pos = offset + jnp.arange(block_rows, dtype=jnp.int32)
        key_pos = jnp.arange(segment.shape[0], dtype=jnp.int32)
        return (
            (key_pos[None, :] <= query_pos[:, None])
            & (segment[None, :] == segment[:, None])
            & ((stamp_flags[None, :] == 0) | (key_pos[None, :] == query_pos[:, None]))
        )

    def spread(values):
        return lax.all_gather(values, "tensor", axis=1, tiled=True)

    def enter_branch(values):
        return spread(values)

    def leave_branch(partial_sum):
        return lax.psum_scatter(partial_sum, "tensor", scatter_dimension=1, tiled=True)

    def frame_projection():
        frame_flat = flatten_rows(frames)
        key_part = (
            product(frame_flat, cross_key_weight)
            .astype(jnp.bfloat16)
            .reshape(seq_count, -1, tile_side)
        )
        value_part = (
            (product(frame_flat, cross_value_weight) + head_bias[3])
            .astype(jnp.bfloat16)
            .reshape(seq_count, -1, tile_side)
        )
        return (key_part, value_part)

    residual = hidden_in.astype(jnp.float32)
    top_grad = cotangent.astype(jnp.float32)
    shared_share = jnp.float32(1.0)
    wide_shape = (seq_count, full_rows, model_width)
    normed_one = enter_branch(normalize(residual, vectors[0], vectors[1]).astype(jnp.bfloat16))
    normed_flat = flatten_rows(normed_one)
    queries = (
        (product(normed_flat, query_weight) + head_bias[0])
        .astype(jnp.bfloat16)
        .reshape(seq_count, full_rows, tile_side)
    )
    key_rows = (
        product(normed_flat, key_weight)
        .astype(jnp.bfloat16)
        .reshape(seq_count, full_rows, tile_side)
    )
    value_rows = (
        (product(normed_flat, value_weight) + head_bias[1])
        .astype(jnp.bfloat16)
        .reshape(seq_count, full_rows, tile_side)
    )
    attended, log_self = attend_forward(queries, key_rows, value_rows, causal_mask)
    first_sum = (
        residual
        + leave_branch(product(flatten_rows(attended), output_weight).reshape(wide_shape))
        + vectors[8]
    )
    normed_two = enter_branch(normalize(first_sum, vectors[2], vectors[3]).astype(jnp.bfloat16))
    cross_queries = (
        (product(flatten_rows(normed_two), cross_query_weight) + head_bias[2])
        .astype(jnp.bfloat16)
        .reshape(seq_count, full_rows, tile_side)
    )
    cross_keys, cross_values = frame_projection()
    cross_mixed, log_cross = attend_forward(cross_queries, cross_keys, cross_values, None)
    second_sum = (
        first_sum
        + leave_branch(product(flatten_rows(cross_mixed), cross_output_weight).reshape(wide_shape))
        + vectors[9]
    )
    normed_three = enter_branch(normalize(second_sum, vectors[4], vectors[5]).astype(jnp.bfloat16))
    upward = product(flatten_rows(normed_three), inner_weight) + inner_bias
    active = jax.nn.gelu(upward, approximate=False).astype(jnp.bfloat16)
    third_sum = (
        second_sum + leave_branch(product(active, outer_weight).reshape(wide_shape)) + vectors[10]
    )
    block_out = normalize(third_sum, vectors[6], vectors[7])
    grad_third, final_gain_grad, final_shift_grad = normalize_back(third_sum, vectors[6], top_grad)
    branch_three = grad_third.astype(jnp.bfloat16)
    full_three = flatten_rows(enter_branch(branch_three))
    outer_bias_grad = jnp.sum(branch_three.astype(jnp.float32), axis=(0, 1))
    outer_weight_grad = weight_grad(active, full_three)
    grad_active = times_transpose(full_three, outer_weight)
    _, gelu_back = jax.vjp(lambda inner_value: jax.nn.gelu(inner_value, approximate=False), upward)
    grad_up = gelu_back(grad_active)[0].astype(jnp.bfloat16)
    inner_bias_grad = jnp.sum(grad_up.astype(jnp.float32), axis=0)
    inner_weight_grad = weight_grad(flatten_rows(normed_three), grad_up)
    grad_normed_three = leave_branch(times_transpose(grad_up, inner_weight).reshape(wide_shape))
    back_three, inner_gain_grad, inner_shift_grad = normalize_back(
        second_sum, vectors[4], grad_normed_three
    )
    grad_second = grad_third + back_three
    branch_two = grad_second.astype(jnp.bfloat16)
    full_two = flatten_rows(enter_branch(branch_two))
    cross_out_bias_grad = jnp.sum(branch_two.astype(jnp.float32), axis=(0, 1))
    cross_output_grad = weight_grad(flatten_rows(cross_mixed), full_two)
    grad_cross_mixed = (
        times_transpose(full_two, cross_output_weight)
        .astype(jnp.bfloat16)
        .reshape(seq_count, full_rows, tile_side)
    )
    keys_back, values_back = frame_projection()
    grad_cross_query, grad_cross_key, grad_cross_value = attend_backward(
        cross_queries, keys_back, values_back, grad_cross_mixed, log_cross, None
    )
    cross_query_bias_grad = jnp.sum(grad_cross_query.astype(jnp.float32), axis=(0, 1))
    cross_value_bias_grad = jnp.sum(grad_cross_value.astype(jnp.float32), axis=(0, 1))
    frame_flat = flatten_rows(frames)
    cross_query_grad = weight_grad(flatten_rows(normed_two), flatten_rows(grad_cross_query))
    cross_key_grad = weight_grad(frame_flat, flatten_rows(grad_cross_key))
    cross_value_grad = weight_grad(frame_flat, flatten_rows(grad_cross_value))
    part_normed_two = times_transpose(flatten_rows(grad_cross_query), cross_query_weight).reshape(
        wide_shape
    )
    part_frames = (
        times_transpose(flatten_rows(grad_cross_key), cross_key_weight)
        + times_transpose(flatten_rows(grad_cross_value), cross_value_weight)
    ).reshape(seq_count, -1, model_width)
    grad_normed_two, frames_grad = (
        lax.psum_scatter(part_normed_two, "tensor", scatter_dimension=1, tiled=True),
        lax.psum_scatter(part_frames, "tensor", scatter_dimension=1, tiled=True),
    )
    back_two, cross_gain_grad, cross_shift_grad = normalize_back(
        first_sum, vectors[2], grad_normed_two
    )
    grad_first = grad_second + back_two
    branch_one = grad_first.astype(jnp.bfloat16)
    full_one = flatten_rows(enter_branch(branch_one))
    self_out_bias_grad = jnp.sum(branch_one.astype(jnp.float32), axis=(0, 1))
    output_weight_grad = weight_grad(flatten_rows(attended), full_one)
    grad_attended = (
        times_transpose(full_one, output_weight)
        .astype(jnp.bfloat16)
        .reshape(seq_count, full_rows, tile_side)
    )
    grad_query, grad_key, grad_value = attend_backward(
        queries, key_rows, value_rows, grad_attended, log_self, causal_mask
    )
    query_bias_grad = jnp.sum(grad_query.astype(jnp.float32), axis=(0, 1))
    value_bias_grad = jnp.sum(grad_value.astype(jnp.float32), axis=(0, 1))
    query_weight_grad = weight_grad(normed_flat, flatten_rows(grad_query))
    key_weight_grad = weight_grad(normed_flat, flatten_rows(grad_key))
    value_weight_grad = weight_grad(normed_flat, flatten_rows(grad_value))
    part_normed_one = (
        times_transpose(flatten_rows(grad_query), query_weight)
        + times_transpose(flatten_rows(grad_key), key_weight)
        + times_transpose(flatten_rows(grad_value), value_weight)
    ).reshape(wide_shape)
    grad_normed_one = leave_branch(part_normed_one)
    back_one, self_gain_grad, self_shift_grad = normalize_back(
        residual, vectors[0], grad_normed_one
    )
    input_grad = grad_first + back_one
    weight_grads = [
        query_weight_grad,
        key_weight_grad,
        value_weight_grad,
        cross_query_grad,
        cross_key_grad,
        cross_value_grad,
        output_weight_grad,
        cross_output_grad,
        inner_weight_grad,
        outer_weight_grad,
    ]
    tile_terms = jnp.concatenate(
        [to_tiles(grad_item, tile_side) for grad_item in weight_grads], axis=0
    )
    tile_terms = jnp.take(tile_terms, owner_list, axis=0)
    owned_grads = lax.psum_scatter(tile_terms, "dp", scatter_dimension=0, tiled=True)
    shared_rows = (
        jnp.stack(
            [
                self_gain_grad,
                self_shift_grad,
                cross_gain_grad,
                cross_shift_grad,
                inner_gain_grad,
                inner_shift_grad,
                final_gain_grad,
                final_shift_grad,
                self_out_bias_grad,
                cross_out_bias_grad,
                outer_bias_grad,
            ]
        )
        * shared_share
    )
    head_rows = lax.dynamic_update_slice(
        jnp.zeros((4, model_width), jnp.float32),
        jnp.stack([query_bias_grad, value_bias_grad, cross_query_bias_grad, cross_value_bias_grad]),
        (0, tensor_rank * tile_side),
    )
    inner_rows = lax.dynamic_update_slice(
        jnp.zeros((4, model_width), jnp.float32), inner_bias_grad[None], (tensor_rank, 0)
    )
    vector_terms = jnp.concatenate([shared_rows, head_rows, inner_rows], axis=0).reshape(-1)
    owned_vector_terms = lax.psum_scatter(vector_terms, "dp", scatter_dimension=0, tiled=True)
    vector_grad = lax.psum(owned_vector_terms, "tensor")
    new_first, new_second, new_master, new_stats, new_bases = soap_update(
        owned_grads, master_tiles[0], tile_first[0], tile_second[0], tile_stats[0], tile_bases[0]
    )
    new_vector_first = beta_one * vector_first + (1.0 - beta_one) * vector_grad
    new_vector_second = beta_two * vector_second + (1.0 - beta_two) * vector_grad * vector_grad
    new_vectors = master_vectors - rate_vectors * (new_vector_first / (1.0 - beta_one**STEP)) / (
        jnp.sqrt(new_vector_second / (1.0 - beta_two**STEP)) + adam_eps
    )
    return (
        block_out,
        input_grad,
        frames_grad,
        new_master[None],
        new_first[None],
        new_second[None],
        new_stats[None],
        new_bases[None],
        new_vectors,
        new_vector_first,
        new_vector_second,
    )


def solution(mesh):
    in_specs = (
        P("dp", "tensor", None),
        P("dp", None, None),
        P("dp", "tensor", None),
        P("dp", None),
        P("dp", None),
        P(),
        P("tensor", "dp", None, None),
        P("tensor", "dp", None, None),
        P("tensor", "dp", None, None),
        P("tensor", "dp", None, None, None),
        P("tensor", "dp", None, None, None),
        P("dp"),
        P("dp"),
        P("dp"),
    )
    out_specs = (
        P("dp", "tensor", None),
        P("dp", "tensor", None),
        P("dp", "tensor", None),
        P("tensor", "dp", None, None),
        P("tensor", "dp", None, None),
        P("tensor", "dp", None, None),
        P("tensor", "dp", None, None, None),
        P("tensor", "dp", None, None, None),
        P("dp"),
        P("dp"),
        P("dp"),
    )
    return jax.shard_map(shards, mesh=mesh, in_specs=in_specs, out_specs=out_specs, check_vma=False)
```

profile of v0, /device:TPU:0, one launch (start us, length us, event | category | flops | bytes accessed | tf_op | source)
XLA Modules:
  0.0 2037.3 jit_solution(9634107925817089882)
XLA Ops:
  11.5 25.9 %all-reduce.3 = bf16[14592]{0:T(1024)(128)(2,1)S(1)} all-reduce(bf16[14592]{0:T(1024)(128)(2,1)S(1)} %dynamic-update-slice.7), channel_id=1, replica_groups=mesh['dp'=8,'tensor'=4] {'dp'}, use_global_device_ids=true, to_apply=%add.3 | all-reduce | flops 14592 | bytes 58368
  40.5 18.4 all-gather.10.cloned.1.call-done
  58.9 6.4 gather_fusion
  65.3 3.5 broadcast_select_fusion.1
  72.7 22.2 %all-gather.8.cloned.1.call-done = bf16[2,448,768]{2,1,0:T(8,128)(2,1)} async-done(((bf16[2,112,768]{2,1,0:T(8,128)(2,1)}), bf16[2,448,768]{2,1,0:T(8,128)(2,1)}) %all-gather.8.cloned.1.call-update) | async-done | bytes 1376272 | tf_op jit(solution)/shard_map/all_gather | solution.py:293
  102.9 10.7 while.65
  116.6 53.1 %reduce-scatter.8.cloned.1.call-done = f32[2,112,768]{2,1,0:T(8,128)} async-done(((f32[2,448,768]{2,1,0:T(8,128)}), f32[2,112,768]{2,1,0:T(8,128)}) %reduce-scatter.8.cloned.1.call-update) | async-done | bytes 688144 | tf_op jit(solution)/shard_map/reduce_scatter | solution.py:299
  172.4 5.1 copy.304
  177.6 5.6 reshape.727
  183.2 4.8 fusion.28
  188.0 3.9 reshape.728
  192.0 3.8 fusion.27
  212.5 17.4 while.66
  233.2 53.2 %reduce-scatter.10.cloned.1.call-done = f32[2,112,768]{2,1,0:T(8,128)} async-done(((f32[2,448,768]{2,1,0:T(8,128)}), f32[2,112,768]{2,1,0:T(8,128)}) %reduce-scatter.10.cloned.1.call-update) | async-done | bytes 688144 | tf_op jit(solution)/shard_map/reduce_scatter | solution.py:299
  289.5 3.4 fusion.143
  295.2 4.4 reshape.736
  299.6 3.8 copy.408
  303.4 4.0 reshape.833
  307.4 15.7 all-gather.14.cloned.1.call-done
  323.2 9.8 multiply_convert_fusion.2
  335.8 53.2 %reduce-scatter.12.cloned.1.call-done = f32[2,112,768]{2,1,0:T(8,128)} async-done(((f32[2,448,768]{2,1,0:T(8,128)}), f32[2,112,768]{2,1,0:T(8,128)}) %reduce-scatter.12.cloned.1.call-update) | async-done | bytes 688144 | tf_op jit(solution)/shard_map/reduce_scatter | solution.py:299
  393.4 4.2 reshape.738
  397.6 4.0 reshape.834
  401.6 25.5 %all-gather.16.cloned.1.call-done = bf16[2,448,768]{2,1,0:T(8,128)(2,1)} async-done(((bf16[2,112,768]{2,1,0:T(8,128)(2,1)}), bf16[2,448,768]{2,1,0:T(8,128)(2,1)}) %all-gather.16.cloned.1.call-update) | async-done | bytes 1376272 | tf_op jit(solution)/shard_map/all_gather | solution.py:293
  427.1 7.4 convert_reduce_fusion
  437.4 53.2 %reduce-scatter.14.cloned.1.call-done = f32[2,112,768]{2,1,0:T(8,128)} async-done(((f32[2,448,768]{2,1,0:T(8,128)}), f32[2,112,768]{2,1,0:T(8,128)}) %reduce-scatter.14.cloned.1.call-update) | async-done | bytes 688144 | tf_op jit(solution)/shard_map/reduce_scatter | solution.py:299
  492.9 3.9 convert_reduce_fusion.8
  498.9 31.6 %all-gather.18.cloned.1.call-done = bf16[2,448,768]{2,1,0:T(8,128)(2,1)} async-done(((bf16[2,112,768]{2,1,0:T(8,128)(2,1)}), bf16[2,448,768]{2,1,0:T(8,128)(2,1)}) %all-gather.18.cloned.1.call-update) | async-done | bytes 1376272 | tf_op jit(solution)/shard_map/all_gather | solution.py:293
  537.9 27.0 %while.67 = (s32[]{:T(128)}, bf16[2,448,192]{1,2,0:T(8,128)(2,1)}, bf16[2,1500,192]{1,2,0:T(8,128)(2,1)}, bf16[2,1500,192]{1,2,0:T(8,128)(2,1)}, s32[2]{0:T(128)...) while((s32[]{:T(128)}, bf16[2,448,192]{1,2,0:T(8,128)(2,1)}, ...), condition=%wide.region_27.28_spmd, body=%wide.region_25.27_spmd.sunk | while | flops 1315178752 | bytes 89786952 | solution.py:175
  565.0 3.2 fusion.154
  568.3 53.2 %reduce-scatter.16.cloned.1.call-done = f32[2,112,768]{2,1,0:T(8,128)} async-done(((f32[2,448,768]{2,1,0:T(8,128)}), f32[2,112,768]{2,1,0:T(8,128)}) %reduce-scatter.16.cloned.1.call-update) | async-done | bytes 688144 | tf_op jit(solution)/shard_map/reduce_scatter | solution.py:404
  637.8 3.6 copy.323
  641.4 4.3 convert_element_type.280
  648.0 4.1 convert_element_type.282
  654.9 5.1 convolution_add_fusion
  660.0 8.1 reshape.746
  668.1 27.4 %copy.325 = f32[2,1500,768]{2,0,1:T(2,128)} copy(f32[2,1500,768]{2,1,0:T(8,128)} %reshape.746) | data formatting | bytes 18432000 | tf_op jit(solution)/shard_map/reshape | solution.py:402
  695.6 8.5 fusion.39
  709.2 14.9 while.68
  735.2 4.6 fusion.37
  744.3 5.0 fusion.158
  749.3 3.5 fusion.159
  755.2 3.8 convolution_bitcast_fusion.3
  760.1 5.0 convolution_bitcast_fusion.2
  791.3 10.6 gather_fusion.1
  801.9 11.8 broadcast_select_fusion
  838.1 175.1 %all-reduce.8.cloned.1.call-done = f32[2,1500,768]{2,0,1:T(2,128)} async-done(((f32[2,1500,768]{2,0,1:T(2,128)}), f32[2,1500,768]{2,0,1:T(2,128)}) %all-reduce.8.cloned.1.call-update) | async-done | bytes 9216016
  1013.2 3.8 constant_dynamic-slice_fusion.18
  1017.1 51.6 %reduce-scatter.18.cloned.1.call-done = f32[2,112,768]{2,1,0:T(8,128)} async-done(((f32[2,448,768]{2,1,0:T(8,128)}), f32[2,112,768]{2,1,0:T(8,128)}) %reduce-scatter.18.cloned.1.call-update) | async-done | bytes 688144 | tf_op jit(solution)/shard_map/reduce_scatter | solution.py:299
  1072.0 4.2 concatenate.13
  1077.6 25.4 %all-reduce.5 = f32[14592]{0:T(1024)} all-reduce(f32[14592]{0:T(1024)} %reshape.754), channel_id=10, replica_groups=mesh['dp'=8,'tensor'=4] {'dp'}, use_global_device_ids=true, to_apply=%region_59.62.clone | all-reduce | flops 14592 | bytes 116736
  1104.5 11.6 psum.7
  1121.2 43.4 %reduce-scatter.20.cloned.1.call-done = f32[8,192,192]{2,1,0:T(8,128)} async-done(((f32[64,192,192]{2,1,0:T(8,128)}), f32[8,192,192]{2,1,0:T(8,128)}) %reduce-scatter.20.cloned.1.call-update) | async-done | bytes 1179664 | tf_op jit(solution)/shard_map/reduce_scatter | solution.py:454
  1164.7 5.5 fusion.59
  1181.0 94.7 %custom-call.21 = f32[8,128,128]{2,1,0:T(8,128)} custom-call(f32[8,128,128]{2,1,0:T(8,128)S(1)} %cholesky.218), custom_call_target="Cholesky" | custom-call | tf_op jit(solution)/shard_map/jit(cholesky)/cholesky | solution.py:198
  1275.6 3.4 fusion.61
  1289.6 94.2 %custom-call.17 = f32[8,128,128]{2,1,0:T(8,128)S(1)} custom-call(f32[8,128,128]{2,1,0:T(8,128)S(1)} %cholesky.215), custom_call_target="Cholesky" | custom-call | tf_op jit(solution)/shard_map/jit(cholesky)/cholesky | solution.py:198
  1386.2 79.4 %custom-call.22 = f32[8,1,128,128]{2,3,1,0:T(8,128)S(1)} custom-call(f32[8,1,128,128]{3,2,1,0:T(8,128)} %get-tuple-element.995), custom_call_target="InvertDiagBlocksLowerTriangular" | custom-call | tf_op jit(solution)/shard_map/jit(cholesky)/cholesky | solution.py:198
  1470.7 46.9 %custom-call.23 = f32[8,64,64]{2,1,0:T(8,128)S(1)} custom-call(f32[8,64,64]{2,1,0:T(8,128)S(1)} %convolution_subtract_fusion.2), custom_call_target="Cholesky" | custom-call | tf_op jit(solution)/shard_map/jit(cholesky)/cholesky | solution.py:198
  1517.6 80.0 %custom-call.18 = f32[8,1,128,128]{2,3,1,0:T(8,128)} custom-call(f32[8,1,128,128]{3,2,1,0:T(8,128)} %get-tuple-element.994), custom_call_target="InvertDiagBlocksLowerTriangular" | custom-call | tf_op jit(solution)/shard_map/jit(cholesky)/cholesky | solution.py:198
  1602.8 48.4 %custom-call.19 = f32[8,64,64]{2,1,0:T(8,128)} custom-call(f32[8,64,64]{2,1,0:T(8,128)} %convolution_subtract_fusion.3), custom_call_target="Cholesky" | custom-call | tf_op jit(solution)/shard_map/jit(cholesky)/cholesky | solution.py:198
  1670.2 158.7 %custom-call.20 = f32[8,2,128,128]{2,3,1,0:T(8,128)} custom-call(f32[8,2,128,128]{3,2,1,0:T(8,128)} %pad_maximum_fusion), custom_call_target="InvertDiagBlocksLowerTriangular" | custom-call | tf_op jit(solution)/shard_map/jit(_solve_triangular)/vmap()/triangular_solve | solution.py:199
  1839.1 158.8 %custom-call.24 = f32[8,2,128,128]{2,3,1,0:T(8,128)} custom-call(f32[8,2,128,128]{3,2,1,0:T(8,128)} %pad_maximum_fusion.1), custom_call_target="InvertDiagBlocksLowerTriangular" | custom-call | tf_op jit(solution)/shard_map/jit(_solve_triangular)/vmap()/triangular_solve | solution.py:199
  2017.9 3.4 fusion.74
  (632 shorter events, 322.2 us)
Async XLA Ops:
  7.2 30.2 %copy-start.22 = (bf16[2,112,768]{2,1,0:T(8,128)(2,1)S(1)}, bf16[2,112,768]{2,1,0:T(8,128)(2,1)}, u32[]{:S(2)}) copy-start(bf16[2,112,768]{2,1,0:T(8,128)(2,1)} %param.25) | copy-start | bytes 1032196
  7.2 32.3 %copy-start.126 = (s32[64]{0:T(128)S(1)}, s32[64]{0:T(128)}, u32[]{:S(2)}) copy-start(s32[64]{0:T(128)} %param.30) | copy-start | bytes 772
  7.2 51.7 %all-gather.10.cloned.1.call-start = ((), (), s32[]{:S(2)}) async-start(), calls=%async_computation.8 | async-start | bytes 7077888 | tf_op jit(solution)/shard_map/all_gather | solution.py:259
  9.7 85.2 %all-gather.8.cloned.1.call-start = ((), (), s32[]{:S(2)}) async-start(), calls=%async_computation.7 | async-start | bytes 1720320 | tf_op jit(solution)/shard_map/all_gather | solution.py:293
  38.4 26.9 %copy-start.99 = (f32[768]{0:T(1024)}, f32[768]{0:T(1024)S(1)}, u32[]{:S(2)}) copy-start(f32[768]{0:T(1024)S(1)} %get-tuple-element.1009) | copy-start | bytes 9220
  38.4 132.8 %copy-start.100 = (f32[768]{0:T(1024)}, f32[768]{0:T(1024)S(1)}, u32[]{:S(2)}) copy-start(f32[768]{0:T(1024)S(1)} %get-tuple-element.1006) | copy-start | bytes 9220
  39.4 130.3 %reduce-scatter.8.cloned.1.call-start = ((), (), s32[]{:S(2)}) async-start(), calls=%async_computation.9 | async-start | bytes 3440640 | tf_op jit(solution)/shard_map/reduce_scatter | solution.py:299
  72.7 25.0 %copy-start.42 = (bf16[4,192,192]{2,1,0:T(8,128)(2,1)}, bf16[4,192,192]{2,1,0:T(8,128)(2,1)S(1)}, u32[]{:S(2)}) copy-start(bf16[4,192,192]{2,1,0:T(8,128)(2,1)S(1)} %get-tuple-element.990) | copy-start | bytes 884740
  72.7 27.7 %copy-start.52 = (bf16[4,192,192]{2,1,0:T(8,128)(2,1)}, bf16[4,192,192]{2,1,0:T(8,128)(2,1)S(1)}, u32[]{:S(2)}) copy-start(bf16[4,192,192]{2,1,0:T(8,128)(2,1)S(1)} %get-tuple-element.989) | copy-start | bytes 884740
  72.7 29.1 %copy-start.44 = (bf16[4,192,192]{2,1,0:T(8,128)(2,1)}, bf16[4,192,192]{2,1,0:T(8,128)(2,1)S(1)}, u32[]{:S(2)}) copy-start(bf16[4,192,192]{2,1,0:T(8,128)(2,1)S(1)} %get-tuple-element.988) | copy-start | bytes 884740
  102.9 10.7 copy-start.69
  116.5 89.4 %all-gather.12.cloned.1.call-start = ((), (), s32[]{:S(2)}) async-start(), calls=%async_computation.10 | async-start | bytes 1720320 | tf_op jit(solution)/shard_map/all_gather | solution.py:293
  171.0 6.6 copy-start.109
  171.2 6.3 copy-start.118
  172.2 114.2 %reduce-scatter.10.cloned.1.call-start = ((), (), s32[]{:S(2)}) async-start(), calls=%async_computation.11 | async-start | bytes 3440640 | tf_op jit(solution)/shard_map/reduce_scatter | solution.py:299
  177.6 5.6 copy-start.67
  195.8 10.2 copy-start.46
  233.1 90.0 %all-gather.14.cloned.1.call-start = ((), (), s32[]{:S(2)}) async-start(), calls=%async_computation.12 | async-start | bytes 1720320 | tf_op jit(solution)/shard_map/all_gather | solution.py:293
  289.4 99.6 %reduce-scatter.12.cloned.1.call-start = ((), (), s32[]{:S(2)}) async-start(), calls=%async_computation.13 | async-start | bytes 3440640 | tf_op jit(solution)/shard_map/reduce_scatter | solution.py:299
  323.2 9.8 copy-start.88
  335.8 53.3 %copy-start.111 = (f32[768]{0:T(1024)S(1)}, f32[768]{0:T(1024)}, u32[]{:S(2)}) copy-start(f32[768]{0:T(1024)} %get-tuple-element.1002) | copy-start | bytes 9220
  335.8 55.0 %copy-start.104 = (f32[768]{0:T(1024)S(1)}, f32[768]{0:T(1024)}, u32[]{:S(2)}) copy-start(f32[768]{0:T(1024)} %get-tuple-element.1000) | copy-start | bytes 9220
  335.8 91.3 %all-gather.16.cloned.1.call-start = ((), (), s32[]{:S(2)}) async-start(), calls=%async_computation.14 | async-start | bytes 1720320 | tf_op jit(solution)/shard_map/all_gather | solution.py:293
  393.3 97.3 %reduce-scatter.14.cloned.1.call-start = ((), (), s32[]{:S(2)}) async-start(), calls=%async_computation.15 | async-start | bytes 3440640 | tf_op jit(solution)/shard_map/reduce_scatter | solution.py:299
  427.1 7.4 copy-start.87
  437.3 55.5 %copy-start.120 = (f32[768]{0:T(1024)S(1)}, f32[768]{0:T(1024)}, u32[]{:S(2)}) copy-start(f32[768]{0:T(1024)} %get-tuple-element.1001) | copy-start | bytes 9220
  437.3 93.2 %all-gather.18.cloned.1.call-start = ((), (), s32[]{:S(2)}) async-start(), calls=%async_computation.16 | async-start | bytes 1720320 | tf_op jit(solution)/shard_map/all_gather | solution.py:293
  496.8 124.7 %reduce-scatter.16.cloned.1.call-start = ((), (), s32[]{:S(2)}) async-start(), calls=%async_computation.17 | async-start | bytes 3440640 | tf_op jit(solution)/shard_map/reduce_scatter | solution.py:404
  565.0 56.5 %copy-start.101 = (f32[768]{0:T(1024)S(1)}, f32[768]{0:T(1024)}, u32[]{:S(2)}) copy-start(f32[768]{0:T(1024)} %copy-done.100) | copy-start | bytes 9220
  565.0 56.5 %copy-start.110 = (f32[2,112]{1,0:T(2,128)S(1)}, f32[2,112]{1,0:T(2,128)}, u32[]{:S(2)}) copy-start(f32[2,112]{1,0:T(2,128)} %copy-done.109) | copy-start | bytes 2692
  565.0 56.5 %copy-start.119 = (f32[2,112]{1,0:T(2,128)S(1)}, f32[2,112]{1,0:T(2,128)}, u32[]{:S(2)}) copy-start(f32[2,112]{1,0:T(2,128)} %copy-done.118) | copy-start | bytes 2692
  568.2 55.3 %copy-start.61 = (f32[2,112,768]{2,1,0:T(8,128)S(1)}, f32[2,112,768]{2,1,0:T(8,128)}, u32[]{:S(2)}) copy-start(f32[2,112,768]{2,1,0:T(8,128)} %get-tuple-element.951) | copy-start | bytes 2064388
  568.2 58.4 %copy-start.125 = (s32[64]{0:T(128)S(1)}, s32[64]{0:T(128)}, u32[]{:S(2)}) copy-start(s32[64]{0:T(128)} %copy-done.124) | copy-start | bytes 772
  568.2 58.4 %copy-start.127 = (s32[64]{0:T(128)S(1)}, s32[64]{0:T(128)}, u32[]{:S(2)}) copy-start(s32[64]{0:T(128)} %param.30) | copy-start | bytes 772
  568.3 58.4 %copy-start.10 = (bf16[2,448,768]{2,1,0:T(8,128)(2,1)S(1)}, bf16[2,448,768]{2,1,0:T(8,128)(2,1)}, u32[]{:S(2)}) copy-start(bf16[2,448,768]{2,1,0:T(8,128)(2,1)} %all-gather.8.cloned.1.call-done) | copy-start | bytes 4128772
  568.3 138.5 %all-gather.20.cloned.1.call-start = ((), (), s32[]{:S(2)}) async-start(), calls=%async_computation.18 | async-start | bytes 1720320 | tf_op jit(solution)/shard_map/all_gather | solution.py:293
  626.5 386.7 %all-reduce.8.cloned.1.call-start = ((), (), s32[]{:S(2)}) async-start(), calls=%async_computation.21 | async-start | bytes 18432000
  637.8 7.9 copy-start.38
  645.7 6.4 copy-start.75
  695.6 373.2 %reduce-scatter.18.cloned.1.call-start = ((), (), s32[]{:S(2)}) async-start(), calls=%async_computation.19 | async-start | bytes 3440640 | tf_op jit(solution)/shard_map/reduce_scatter | solution.py:299
  704.1 5.1 copy-start.17
  724.2 6.5 copy-start.45
  727.2 5.2 copy-start.47
  727.2 5.2 copy-start.53
  735.2 429.5 %reduce-scatter.20.cloned.1.call-start = ((), (), s32[]{:S(2)}) async-start(), calls=%async_computation.20 | async-start | bytes 14155776 | tf_op jit(solution)/shard_map/reduce_scatter | solution.py:454
  760.1 7.2 copy-start.30
  818.6 5.2 copy-start.113
  818.6 5.8 copy-start.112
  818.6 6.4 copy-start.122
  818.6 6.4 copy-start.121
  818.6 7.0 copy-start.116
  818.6 7.6 copy-start.115
  819.2 351.0 %copy-start.1 = (f32[1,8,2,192,192]{4,3,1,2,0:T(8,128)}, f32[1,8,2,192,192]{4,3,1,2,0:T(8,128)S(1)}, u32[]{:S(2)}) copy-start(f32[1,8,2,192,192]{4,3,1,2,0:T(8,128)S(1)} %copy.407) | copy-start | bytes 7077892
  829.5 239.2 %copy-start.23 = (bf16[2,112,768]{2,1,0:T(8,128)(2,1)S(1)}, bf16[2,112,768]{2,1,0:T(8,128)(2,1)}, u32[]{:S(2)}) copy-start(bf16[2,112,768]{2,1,0:T(8,128)(2,1)} %param.25) | copy-start | bytes 1032196
  1178.0 97.7 %copy-start = (f32[8,192,192]{2,1,0:T(8,128)S(1)}, f32[8,192,192]{2,1,0:T(8,128)}, u32[]{:S(2)}) copy-start(f32[8,192,192]{2,1,0:T(8,128)} %reduce-scatter.20.cloned.1.call-done) | copy-start | bytes 3538948
  1286.8 97.0 %copy-start.102 = (pred[128,128]{1,0:T(8,128)(4,1)S(1)}, pred[128,128]{1,0:T(8,128)(4,1)}, u32[]{:S(2)}) copy-start(pred[128,128]{1,0:T(8,128)(4,1)} %get-tuple-element.1027) | copy-start | bytes 49156
  1286.8 97.0 %copy-start.103 = (pred[128,128]{1,0:T(8,128)(4,1)S(1)}, pred[128,128]{1,0:T(8,128)(4,1)}, u32[]{:S(2)}) copy-start(pred[128,128]{1,0:T(8,128)(4,1)} %get-tuple-element.1028) | copy-start | bytes 49156
  1289.6 176.0 %copy-start.63 = (f32[8,128,128]{2,1,0:T(8,128)S(1)}, f32[8,128,128]{2,1,0:T(8,128)}, u32[]{:S(2)}) copy-start(f32[8,128,128]{2,1,0:T(8,128)} %custom-call.21) | copy-start | bytes 1572868
  1383.8 85.3 %copy-start.62 = (f32[8,128,128]{2,1,0:T(8,128)}, f32[8,128,128]{2,1,0:T(8,128)S(1)}, u32[]{:S(2)}) copy-start(f32[8,128,128]{2,1,0:T(8,128)S(1)} %custom-call.17) | copy-start | bytes 1572868
  1469.2 182.1 %copy-start.106 = (pred[64,64]{1,0:T(8,128)(4,1)S(1)}, pred[64,64]{1,0:T(8,128)(4,1)}, u32[]{:S(2)}) copy-start(pred[64,64]{1,0:T(8,128)(4,1)} %iota_compare_fusion.9) | copy-start | bytes 12292
  1597.6 55.8 %copy-start.94 = (pred[192,192]{1,0:T(8,128)(4,1)S(1)}, pred[192,192]{1,0:T(8,128)(4,1)}, u32[]{:S(2)}) copy-start(pred[192,192]{1,0:T(8,128)(4,1)} %iota_compare_fusion.5) | copy-start | bytes 110596
  1657.7 7.6 copy-start.6
  1667.0 161.9 %copy-start.26 = (f32[8,192,192]{1,2,0:T(8,128)S(1)}, f32[8,192,192]{1,2,0:T(8,128)}, u32[]{:S(2)}) copy-start(f32[8,192,192]{1,2,0:T(8,128)} %copy.354) | copy-start | bytes 3538948
  1836.8 161.1 %copy-start.25 = (f32[8,192,192]{1,2,0:T(8,128)S(1)}, f32[8,192,192]{1,2,0:T(8,128)}, u32[]{:S(2)}) copy-start(f32[8,192,192]{1,2,0:T(8,128)} %copy.363) | copy-start | bytes 3538948
  (89 other events, 230.3 us)
Sparse Core Ops, SparseCore 0:
  10.5 48.3 all-gather.9
  61.0 33.8 all-gather.7
  116.6 53.0 reduce-scatter.7
  172.3 33.5 all-gather.11
  233.2 53.0 reduce-scatter.9
  289.5 33.5 all-gather.13
  335.9 53.0 reduce-scatter.11
  393.4 33.5 all-gather.15
  437.5 53.0 reduce-scatter.13
  496.9 33.5 all-gather.17
  568.4 53.0 reduce-scatter.15
  626.7 33.5 all-gather.19
  695.7 317.5 all-reduce.7
  1015.5 53.1 reduce-scatter.17
  1072.5 92.1 reduce-scatter.19
where the time goes:
time: 2050 us; the launch traced here: 2040 us
  other arithmetic  858 us (42%)
  waiting for transfers between devices  652 us (32%)
  local copies, waits for them, and re-layouts  247 us (12%)
  matrix products  182 us (9%)
  blocking collectives  63 us (3%)
    another operation x16, other arithmetic, orthonormal(): factor = jnp.linalg.cholesky(gram_matrix)  449 us
    another operation x9, other arithmetic, orthonormal(): jax.scipy.linalg.solve_triangular(factor, jnp.swapaxes(matrix, -1, -2), l...  325 us
    reduce_scatter x5, waiting for transfers between devices, leave_branch(): lax.psum_scatter(partial_sum, 'tensor', scatter_dimension=1, tiled=True)  264 us
    unnamed x16, waiting for transfers between devices  175 us
    all_gather x6, waiting for transfers between devices, spread(): return lax.all_gather(values, 'tensor', axis=1, tiled=True)  97.6 us
    reduce_scatter x1, waiting for transfers between devices, shards(): lax.psum_scatter(part_normed_two, 'tensor', scatter_dimension=1, tiled=True)  53.2 us
    unnamed x2, blocking collectives  51.4 us
    reduce_scatter x1, waiting for transfers between devices, shards(): lax.psum_scatter(tile_terms, 'dp', scatter_dimension=0, tiled=True)  43.4 us
  transfers between devices with their start and end apart: 15, of which 14 were waited for; matrix products, arithmetic and copies ran while one was open for 14% of the time, Pallas kernels for 0%

commit v1 on v0

--- a/solution.py
+++ b/solution.py
@@ -1,6 +1,10 @@
+import functools
+
 import jax
 import jax.numpy as jnp
 from jax import lax
+from jax.experimental import pallas as pl
+from jax.experimental.pallas import tpu as pltpu
 from jax.sharding import PartitionSpec as P
 
 HEAD = 64
@@ -188,44 +192,150 @@
     return (grad_query, grad_key, grad_value)
 
 
-def rotate(basis_left, middle, basis_right):
-    inner = jnp.einsum("nji,njk->nik", basis_left, middle, precision=highest)
-    return jnp.einsum("nij,njk->nik", inner, basis_right, precision=highest)
-
-
-def orthonormal(matrix):
-    gram_matrix = jnp.einsum("nki,nkj->nij", matrix, matrix, precision=highest)
-    factor = jnp.linalg.cholesky(gram_matrix)
-    solved = jax.scipy.linalg.solve_triangular(factor, jnp.swapaxes(matrix, -1, -2), lower=True)
-    return jnp.swapaxes(solved, -1, -2)
-
-
-def soap_update(gradient, master, first, second, statistics, bases):
-    basis_left = bases[:, 0]
-    basis_right = bases[:, 1]
-    new_first = beta_one * first + (1.0 - beta_one) * gradient
-    rotated = rotate(basis_left, gradient, basis_right)
-    new_second = beta_two * second + (1.0 - beta_two) * rotated * rotated
-    moment_rot = rotate(basis_left, new_first, basis_right) / (1.0 - beta_one**STEP)
-    normal_step = moment_rot / (jnp.sqrt(new_second / (1.0 - beta_two**STEP)) + adam_eps)
-    back_left = jnp.einsum("nij,njk->nik", basis_left, normal_step, precision=highest)
-    update = jnp.einsum("nij,nkj->nik", back_left, basis_right, precision=highest)
-    new_master = master - rate_tiles * update
-    stats_left = beta_two * statistics[:, 0] + (1.0 - beta_two) * jnp.einsum(
-        "nij,nkj->nik", gradient, gradient, precision=highest
-    )
-    stats_right = beta_two * statistics[:, 1] + (1.0 - beta_two) * jnp.einsum(
-        "nji,njk->nik", gradient, gradient, precision=highest
-    )
-    new_left = orthonormal(jnp.einsum("nij,njk->nik", stats_left, basis_left, precision=highest))
-    new_right = orthonormal(jnp.einsum("nij,njk->nik", stats_right, basis_right, precision=highest))
-    return (
-        new_first,
-        new_second,
-        new_master,
-        jnp.stack([stats_left, stats_right], axis=1),
-        jnp.stack([new_left, new_right], axis=1),
-    )
+HI = lax.Precision.HIGHEST
+
+def split2(a):
+    hi = a.astype(jnp.bfloat16)
+    lo = (a - hi.astype(jnp.float32)).astype(jnp.bfloat16)
+    return hi, lo
+
+def bdot(a, b, dims):
+    return lax.dot_general(a, b, (dims, ((), ())), preferred_element_type=jnp.float32)
+
+NN = ((1,), (0,)); TN = ((0,), (0,)); NT = ((1,), (1,))
+
+def dot3(a, b, dims):
+    (ah, al), (bh, bl) = a, b
+    return bdot(ah, bh, dims) + (bdot(ah, bl, dims) + bdot(al, bh, dims))
+
+def dothi(a, b, dims):
+    return lax.dot_general(a, b, (dims, ((), ())), precision=HI, preferred_element_type=jnp.float32)
+
+def soap_pre_kernel(first, stats, bases, rot_first, stats_rot):
+    ql, qr = split2(bases[0, 0]), split2(bases[0, 1])
+    inner = split2(dot3(ql, split2(first[0]), TN))
+    rot_first[0] = dot3(inner, qr, NN)
+    stats_rot[0, 0] = dot3(split2(stats[0, 0]), ql, NN)
+    stats_rot[0, 1] = dot3(split2(stats[0, 1]), qr, NN)
+
+def soap_main_kernel(grad, master, first, second, stats, bases, rot_first, stats_rot,
+                     new_master, new_first, new_second, new_stats, turned, grams):
+    g32 = grad[0].astype(jnp.float32)
+    g, ql, qr = split2(g32), split2(bases[0, 0]), split2(bases[0, 1])
+    new_first[0] = beta_one * first[0] + (1.0 - beta_one) * g32
+    part_left = split2(dot3(ql, g, TN))
+    rotated = dot3(part_left, qr, NN)
+    fresh = beta_two * second[0] + (1.0 - beta_two) * rotated * rotated
+    new_second[0] = fresh
+    moment = (beta_one * rot_first[0] + (1.0 - beta_one) * rotated) / (1.0 - beta_one**STEP)
+    step = moment / (jnp.sqrt(fresh / (1.0 - beta_two**STEP)) + adam_eps)
+    back = split2(dot3(ql, split2(step), NN))
+    new_master[0] = master[0] - rate_tiles * dot3(back, qr, NT)
+    new_stats[0, 0] = beta_two * stats[0, 0] + (1.0 - beta_two) * dot3(g, g, NT)
+    new_stats[0, 1] = beta_two * stats[0, 1] + (1.0 - beta_two) * dot3(g, g, TN)
+    part_right = split2(dot3(g, qr, NN))
+    for side, term in ((0, dot3(g, part_left, NT)), (1, dot3(g, part_right, TN))):
+        side_turned = beta_two * stats_rot[0, side] + (1.0 - beta_two) * term
+        turned[0, side] = side_turned
+        halves = split2(side_turned)
+        grams[0, side] = dot3(halves, halves, TN)
+
+def chol_kernel(turned, grams, out, work, inv, fac, *, block):
+    count, side = work.shape[0], work.shape[1]
+    row = lax.broadcasted_iota(jnp.int32, (side, side), 0)
+    col = lax.broadcasted_iota(jnp.int32, (side, side), 1)
+    eye = (row == col).astype(jnp.float32)
+    for m in range(count):
+        work[m] = grams[m]
+        inv[m] = eye
+    brow = lax.broadcasted_iota(jnp.int32, (count, block, 2 * block), 1)
+    bcol = lax.broadcasted_iota(jnp.int32, (count, block, 2 * block), 2)
+    aug_eye = ((bcol - block) == brow).astype(jnp.float32)
+    for k in range(side // block):
+        lo = k * block
+        diag = work[:, lo : lo + block, lo : lo + block]
+        w = jnp.concatenate([diag, jnp.zeros_like(diag)], axis=2) + aug_eye
+        for j in range(block - 1):
+            piv = w[:, j : j + 1, :]
+            ratio = w[:, :, j : j + 1] / w[:, j : j + 1, j : j + 1]
+            w = w - jnp.where(brow > j, ratio * piv, 0.0)
+        d = jnp.sum(jnp.where(brow == bcol, w, 0.0), axis=2, keepdims=True)
+        fac[...] = w[:, :, block:] * lax.rsqrt(d)
+
+        def one(m, _):
+            x = fac[m]
+            y = dothi(x, work[m, lo : lo + block, :], NN)
+            z = dothi(x, inv[m, lo : lo + block, :], NN)
+            inv[m, lo : lo + block, :] = z
+            if lo + block < side:
+                rest = side - lo - block
+                ys = split2(y)
+                upd = dothi(y, y, TN)
+                updx = dothi(y, z, TN)
+                work[m, lo + block :, :] = work[m, lo + block :, :] - upd[lo + block :, :]
+                inv[m, lo + block :, :] = inv[m, lo + block :, :] - updx[lo + block :, :]
+            return 0
+        lax.fori_loop(0, count, one, 0)
+
+    def last(m, _):
+        out[m] = dothi(turned[m], inv[m], NT)
+        return 0
+    lax.fori_loop(0, count, last, 0)
+
+def tile_spec(side):
+    return pl.BlockSpec((1, side, side), lambda i: (i, 0, 0))
+def pair_spec(side):
+    return pl.BlockSpec((1, 2, side, side), lambda i: (i, 0, 0, 0))
+
+def soap_pre(first, stats, bases):
+    n, side = first.shape[0], first.shape[1]
+    t, p = tile_spec(side), pair_spec(side)
+    return pl.pallas_call(soap_pre_kernel, grid=(n,), in_specs=[t, p, p], out_specs=[t, p],
+        out_shape=[jax.ShapeDtypeStruct(first.shape, jnp.float32), jax.ShapeDtypeStruct(stats.shape, jnp.float32)],
+        name="soap_pre")(first, stats, bases)
+
+def soap_main(grad, master, first, second, stats, bases, rot_first, stats_rot):
+    n, side = first.shape[0], first.shape[1]
+    t, p = tile_spec(side), pair_spec(side)
+    f = jnp.float32
+    ts, ps = jax.ShapeDtypeStruct(first.shape, f), jax.ShapeDtypeStruct(stats.shape, f)
+    return pl.pallas_call(soap_main_kernel, grid=(n,), in_specs=[t, t, t, t, p, p, t, p],
+        out_specs=[t, t, t, p, p, p], out_shape=[ts, ts, ts, ps, ps, ps], name="soap_main")(
+        grad, master, first, second, stats, bases, rot_first, stats_rot)
+
+def chol_bases(turned, grams, block=32):
+    n, _, side, _ = turned.shape
+    shape = (2 * n, side, side)
+    out = pl.pallas_call(functools.partial(chol_kernel, block=block),
+        out_shape=jax.ShapeDtypeStruct(shape, jnp.float32),
+        scratch_shapes=[pltpu.VMEM(shape, jnp.float32), pltpu.VMEM(shape, jnp.float32), pltpu.VMEM((2*n, block, block), jnp.float32)],
+        compiler_params=pltpu.CompilerParams(vmem_limit_bytes=48 * 2**20), name="chol_bases")(
+        turned.reshape(shape), grams.reshape(shape))
+    return out.reshape(turned.shape)
+
+def soap(gradient, master, first, second, statistics, bases, block=32):
+    rot_first, stats_rot = soap_pre(first, statistics, bases)
+    nm, nf, ns, nst, turned, grams = soap_main(gradient, master, first, second, statistics, bases, rot_first, stats_rot)
+    return nf, ns, nm, nst, chol_bases(turned, grams, block)
+
+
+def permute_kernel(order, source, result):
+    result[...] = source[...]
+
+
+def permute_tiles(tiles, order):
+    count, side = tiles.shape[0], tiles.shape[-1]
+    return pl.pallas_call(
+        permute_kernel,
+        grid_spec=pltpu.PrefetchScalarGridSpec(
+            num_scalar_prefetch=1,
+            grid=(count,),
+            in_specs=[pl.BlockSpec((1, side, side), lambda i, order: (order[i], 0, 0))],
+            out_specs=pl.BlockSpec((1, side, side), lambda i, order: (i, 0, 0)),
+        ),
+        out_shape=jax.ShapeDtypeStruct(tiles.shape, tiles.dtype),
+        name="permute_tiles",
+    )(order, tiles)
 
 
 def shards(
@@ -257,7 +367,7 @@
         .set(jnp.arange(tile_count, dtype=jnp.int32))
     )
     gathered = lax.all_gather(master_tiles[0].astype(jnp.bfloat16), "dp", axis=0, tiled=True)
-    by_ident = jnp.take(gathered, inverse, axis=0)
+    by_ident = permute_tiles(gathered, inverse)
     (
         query_weight,
         key_weight,
@@ -450,7 +560,7 @@
     tile_terms = jnp.concatenate(
         [to_tiles(grad_item, tile_side) for grad_item in weight_grads], axis=0
     )
-    tile_terms = jnp.take(tile_terms, owner_list, axis=0)
+    tile_terms = permute_tiles(tile_terms, owner_list)
     owned_grads = lax.psum_scatter(tile_terms, "dp", scatter_dimension=0, tiled=True)
     shared_rows = (
         jnp.stack(
@@ -481,7 +591,7 @@
     vector_terms = jnp.concatenate([shared_rows, head_rows, inner_rows], axis=0).reshape(-1)
     owned_vector_terms = lax.psum_scatter(vector_terms, "dp", scatter_dimension=0, tiled=True)
     vector_grad = lax.psum(owned_vector_terms, "tensor")
-    new_first, new_second, new_master, new_stats, new_bases = soap_update(
+    new_first, new_second, new_master, new_stats, new_bases = soap(
         owned_grads, master_tiles[0], tile_first[0], tile_second[0], tile_stats[0], tile_bases[0]
     )
     new_vector_first = beta_one * vector_first + (1.0 - beta_one) * vector_grad

time: 2050 us -> 1280 us (0.62)
  other arithmetic: 858 us -> 52.6 us
  Pallas kernels: 0 us -> 183 us
  local copies, waits for them, and re-layouts: 247 us -> 179 us
  matrix products: 182 us -> 125 us
  waiting for transfers between devices: 652 us -> 628 us
    another operation x31 -> x4, other arithmetic: 776 us -> 0.01 us  [the longest x16 449 us: orthonormal(): factor = jnp.linalg.cholesky(gram_matrix)]
    pallas_call x0 -> x5, Pallas kernels: none -> 183 us  [the longest x1 84.6 us: chol_bases(): pl.pallas_call(functools.partial(chol_kernel, block=block), out_shape=jax...]
    dot_general x12 -> x0, matrix products: 34.3 us -> none  [the longest x2 6.65 us: rotate(): inner = jnp.einsum('nji,njk->nik', basis_left, middle, precision=highest)]
    another operation x10 -> x0, matrix products: 23.6 us -> none  [the longest x6 15.8 us: orthonormal(): jax.scipy.linalg.solve_triangular(factor, jnp.swapaxes(matrix, -1, -2), l...]
    all_gather x6, waiting for transfers between devices: 97.6 us -> 75.3 us  [spread(): return lax.all_gather(values, 'tensor', axis=1, tiled=True)]
  transfers between devices with their start and end apart: 15 -> 15, of which waited for: 14 -> 13; matrix products, arithmetic and copies ran while one was open for 14% -> 18% of each run, Pallas kernels for 0% -> 6%
where the time goes in v1:
time: 1280 us; the launch traced here: 1260 us
  waiting for transfers between devices  628 us (49%)
  Pallas kernels  183 us (14%)
  local copies, waits for them, and re-layouts  179 us (14%)
  matrix products  125 us (10%)
  blocking collectives  61 us (5%)
  other arithmetic  52.6 us (4%)
  between operations  17.9 us (1%)
  loops' own time  16.5 us (1%)
    reduce_scatter x5, waiting for transfers between devices, leave_branch(): lax.psum_scatter(partial_sum, 'tensor', scatter_dimension=1, tiled=True)  265 us
    unnamed x16, waiting for transfers between devices  160 us
    pallas_call x1, Pallas kernels, chol_bases(): pl.pallas_call(functools.partial(chol_kernel, block=block), out_shape=jax...  84.6 us
    all_gather x6, waiting for transfers between devices, spread(): return lax.all_gather(values, 'tensor', axis=1, tiled=True)  75.3 us
    pallas_call x2, Pallas kernels, permute_tiles(): pl.pallas_call(permute_kernel, grid_spec=pltpu.PrefetchScalarGridSpec(num...  71.4 us
    reduce_scatter x1, waiting for transfers between devices, shards(): lax.psum_scatter(tile_terms, 'dp', scatter_dimension=0, tiled=True)  56.1 us
    reduce_scatter x1, waiting for transfers between devices, shards(): lax.psum_scatter(part_normed_two, 'tensor', scatter_dimension=1, tiled=True)  53.2 us
    unnamed x2, blocking collectives  50.3 us
  transfers between devices with their start and end apart: 15, of which 13 were waited for; matrix products, arithmetic and copies ran while one was open for 18% of the time, Pallas kernels for 6%

profile of v1, /device:TPU:0, one launch (start us, length us, event | category | flops | bytes accessed | tf_op | source)
XLA Modules:
  0.0 1264.4 jit_solution(3911689541326852007)
XLA Ops:
  11.5 25.9 %all-reduce = bf16[14592]{0:T(1024)(128)(2,1)S(1)} all-reduce(bf16[14592]{0:T(1024)(128)(2,1)S(1)} %dynamic-update-slice), channel_id=1, replica_groups=mesh['dp'=8,'tensor'=4] {'dp'}, use_global_device_ids=true, to_apply=%add | all-reduce | flops 14592 | bytes 58368
  40.9 18.0 %all-gather.10.cloned.1.call-done.source = bf16[64,192,192]{2,1,0:T(8,128)(2,1)} async-done(((bf16[8,192,192]{2,1,0:T(8,128)(2,1)}), bf16[64,192,192]{2,1,0:T(8,128)(2,1)}) %all-gather.10.cloned.1.call-update) | async-done | bytes 4718608 | tf_op jit(solution)/shard_map/all_gather | solution.py:369
  58.9 34.6 %permute_tiles.2 = bf16[64,192,192]{2,1,0:T(8,128)(2,1)} custom-call(s32[64]{0:T(128)} %scatter_custom_fusion.order, bf16[64,192,192]{2,1,0:T(8,128)(2,1)} %all-gather.10.cloned.1.call-done.source), custom_call_target="tpu_custom_call" | custom-call | tf_op jit(solution)/shard_map/permute_tiles/pallas_call | solution.py:328
  93.5 3.1 slice_bitcast_fusion
  96.7 3.2 fusion.59
  110.3 10.6 while.62
  125.2 54.2 %reduce-scatter.8.cloned.1.call-done = f32[2,112,768]{2,1,0:T(8,128)} async-done(((f32[2,448,768]{2,1,0:T(8,128)}), f32[2,112,768]{2,1,0:T(8,128)}) %reduce-scatter.8.cloned.1.call-update) | async-done | bytes 688144 | tf_op jit(solution)/shard_map/reduce_scatter | solution.py:409
  182.2 5.1 copy.112
  187.3 5.6 reshape.692
  192.9 4.8 fusion.28
  197.7 3.8 reshape.693
  201.6 3.9 fusion.27
  213.1 2.5 all-gather.12.cloned.1.call-done
  215.6 2.7 fusion.61
  222.2 17.4 %while.63 = (s32[]{:T(128)}, bf16[2,448,192]{1,2,0:T(8,128)(2,1)}, f32[2,3,448]{2,1,0:T(4,128)S(1)}, s32[2]{0:T(128)S(1)}, bf16[2,1500,192]{1,2,0:T(8,128)(2,1)S...) while((s32[]{:T(128)}, bf16[2,448,192]{1,2,0:T(8,128)(2,1)}, ...), condition=%wide.region_13.14_spmd, body=%wide.region_10.13_spmd.sunk | while | flops 534324672 | bytes 28756896 | solution.py:134
  239.6 3.2 fusion.106
  242.9 53.2 %reduce-scatter.10.cloned.1.call-done = f32[2,112,768]{2,1,0:T(8,128)} async-done(((f32[2,448,768]{2,1,0:T(8,128)}), f32[2,112,768]{2,1,0:T(8,128)}) %reduce-scatter.10.cloned.1.call-update) | async-done | bytes 688144 | tf_op jit(solution)/shard_map/reduce_scatter | solution.py:409
  299.2 3.4 fusion.98
  304.9 4.4 reshape.701
  309.4 3.8 copy.118
  313.1 4.0 reshape.738
  317.2 15.7 %all-gather.14.cloned.1.call-done = bf16[2,448,768]{2,1,0:T(8,128)(2,1)} async-done(((bf16[2,112,768]{2,1,0:T(8,128)(2,1)}), bf16[2,448,768]{2,1,0:T(8,128)(2,1)}) %all-gather.14.cloned.1.call-update) | async-done | bytes 1376272 | tf_op jit(solution)/shard_map/all_gather | solution.py:403
  332.9 9.8 multiply_convert_fusion.2
  342.7 2.8 fusion.107
  345.6 53.2 %reduce-scatter.12.cloned.1.call-done = f32[2,112,768]{2,1,0:T(8,128)} async-done(((f32[2,448,768]{2,1,0:T(8,128)}), f32[2,112,768]{2,1,0:T(8,128)}) %reduce-scatter.12.cloned.1.call-update) | async-done | bytes 688144 | tf_op jit(solution)/shard_map/reduce_scatter | solution.py:409
  403.1 4.2 reshape.703
  407.3 4.0 reshape.739
  411.3 25.5 %all-gather.16.cloned.1.call-done = bf16[2,448,768]{2,1,0:T(8,128)(2,1)} async-done(((bf16[2,112,768]{2,1,0:T(8,128)(2,1)}), bf16[2,448,768]{2,1,0:T(8,128)(2,1)}) %all-gather.16.cloned.1.call-update) | async-done | bytes 1376272 | tf_op jit(solution)/shard_map/all_gather | solution.py:403
  436.8 7.4 convert_reduce_fusion
  444.3 2.8 fusion.108
  447.2 53.2 %reduce-scatter.14.cloned.1.call-done = f32[2,112,768]{2,1,0:T(8,128)} async-done(((f32[2,448,768]{2,1,0:T(8,128)}), f32[2,112,768]{2,1,0:T(8,128)}) %reduce-scatter.14.cloned.1.call-update) | async-done | bytes 688144 | tf_op jit(solution)/shard_map/reduce_scatter | solution.py:409
  502.6 3.9 convert_reduce_fusion.8
  508.7 31.6 %all-gather.18.cloned.1.call-done = bf16[2,448,768]{2,1,0:T(8,128)(2,1)} async-done(((bf16[2,112,768]{2,1,0:T(8,128)(2,1)}), bf16[2,448,768]{2,1,0:T(8,128)(2,1)}) %all-gather.18.cloned.1.call-update) | async-done | bytes 1376272 | tf_op jit(solution)/shard_map/all_gather | solution.py:403
  540.3 2.7 convolution_convert_fusion.2
  547.7 27.1 %while.64 = (s32[]{:T(128)}, bf16[2,448,192]{1,2,0:T(8,128)(2,1)}, bf16[2,1500,192]{1,2,0:T(8,128)(2,1)}, bf16[2,1500,192]{1,2,0:T(8,128)(2,1)}, s32[2]{0:T(128)...) while((s32[]{:T(128)}, bf16[2,448,192]{1,2,0:T(8,128)(2,1)}, ...), condition=%wide.region_27.28_spmd, body=%wide.region_25.27_spmd.sunk | while | flops 1315178752 | bytes 89786952 | solution.py:179
  551.9 2.7 multiply_reduce_fusion.17
  565.3 2.7 multiply_reduce_fusion.17
  574.8 3.2 fusion.109
  578.1 53.2 %reduce-scatter.16.cloned.1.call-done = f32[2,112,768]{2,1,0:T(8,128)} async-done(((f32[2,448,768]{2,1,0:T(8,128)}), f32[2,112,768]{2,1,0:T(8,128)}) %reduce-scatter.16.cloned.1.call-update) | async-done | bytes 688144 | tf_op jit(solution)/shard_map/reduce_scatter | solution.py:514
  635.2 2.6 copy.131
  641.2 2.5 fusion.112
  643.7 5.1 convolution_add_fusion
  648.9 8.2 reshape.711
  657.0 27.4 %copy.133 = f32[2,1500,768]{2,0,1:T(2,128)} copy(f32[2,1500,768]{2,1,0:T(8,128)} %reshape.711) | data formatting | bytes 18432000 | tf_op jit(solution)/shard_map/reshape | solution.py:512
  696.2 14.9 %while.65 = (s32[]{:T(128)}, bf16[2,448,192]{1,2,0:T(8,128)(2,1)S(1)}, bf16[2,448,192]{1,2,0:T(8,128)(2,1)}, bf16[2,448,192]{1,2,0:T(8,128)(2,1)}, s32[2]{0:T(12...) while((s32[]{:T(128)}, ...), condition=%wide.region_33.34_spmd, body=%wide.region_31.33_spmd.sunk | while | flops 392318080 | bytes 28281296 | solution.py:179
  722.7 8.2 fusion.39
  731.0 2.5 copy.145
  735.0 4.6 fusion.37
  741.2 2.6 copy.148
  743.8 5.0 fusion.113
  748.8 3.5 fusion.114
  754.7 4.0 convolution_bitcast_fusion.3
  759.9 4.7 convolution_bitcast_fusion.2
  773.7 2.5 convolution_dynamic-update-slice_fusion.3
  790.6 36.8 %permute_tiles.3 = f32[64,192,192]{2,1,0:T(8,128)} custom-call(s32[64]{0:T(128)} %order.1, f32[64,192,192]{2,1,0:T(8,128)} %constant_dynamic-update-slice_fusion.8.source), custom_call_target="tpu_custom_call" | custom-call | tf_op jit(solution)/shard_map/permute_tiles/pallas_call | solution.py:328
  830.1 10.0 soap_pre.1
  842.5 159.6 %all-reduce.5.cloned.1.call-done = f32[2,1500,768]{2,0,1:T(2,128)} async-done(((f32[2,1500,768]{2,0,1:T(2,128)}), f32[2,1500,768]{2,0,1:T(2,128)}) %all-reduce.5.cloned.1.call-update) | async-done | bytes 9216016
  1002.1 3.8 constant_dynamic-slice_fusion.17
  1005.9 51.6 %reduce-scatter.18.cloned.1.call-done = f32[2,112,768]{2,1,0:T(8,128)} async-done(((f32[2,448,768]{2,1,0:T(8,128)}), f32[2,112,768]{2,1,0:T(8,128)}) %reduce-scatter.18.cloned.1.call-update) | async-done | bytes 688144 | tf_op jit(solution)/shard_map/reduce_scatter | solution.py:409
  1059.3 24.3 %all-reduce.2 = f32[14592]{0:T(1024)S(1)} all-reduce(f32[14592]{0:T(1024)S(1)} %reshape.721), channel_id=10, replica_groups=mesh['dp'=8,'tensor'=4] {'dp'}, use_global_device_ids=true, to_apply=%region_55.56.clone | all-reduce | flops 14592 | bytes 116736
  1083.7 10.8 psum.7
  1097.4 56.1 %reduce-scatter.20.cloned.1.call-done.grad = f32[8,192,192]{2,1,0:T(8,128)} async-done(((f32[64,192,192]{2,1,0:T(8,128)}), f32[8,192,192]{2,1,0:T(8,128)}) %reduce-scatter.20.cloned.1.call-update) | async-done | bytes 1179664 | tf_op jit(solution)/shard_map/reduce_scatter | solution.py:564
  1153.5 17.4 %soap_main.1 = (f32[8,192,192]{2,1,0:T(8,128)}, f32[8,192,192]{2,1,0:T(8,128)}, f32[8,192,192]{2,1,0:T(8,128)}, f32[8,2,192,192]{3,2,1,0:T(8,128)}, f32[8,2,192,...) custom-call(f32[8,192,192]{2,1,0:T(8,128)} %reduce-scatter.20.cloned.1.call-done.grad, f32[8,192,192]{2,1,0:T(8,128)} %bitcast.525, ...), custom_call_target="tpu_custom_call" | custom-call | tf_op jit(solution)/shard_map/soap_main/pallas_call | solution.py:302
  1172.8 84.6 %chol_bases.1 = f32[16,192,192]{2,1,0:T(8,128)} custom-call(f32[16,192,192]{2,1,0:T(8,128)S(1)} %bitcast.487, f32[16,192,192]{2,1,0:T(8,128)} %bitcast.555), custom_call_target="tpu_custom_call" | custom-call | tf_op jit(solution)/shard_map/chol_bases/pallas_call | solution.py:309
  (505 shorter events, 173.4 us)
Async XLA Ops:
  7.2 30.2 %copy-start.11 = (bf16[2,112,768]{2,1,0:T(8,128)(2,1)S(1)}, bf16[2,112,768]{2,1,0:T(8,128)(2,1)}, u32[]{:S(2)}) copy-start(bf16[2,112,768]{2,1,0:T(8,128)(2,1)} %param.22) | copy-start | bytes 1032196
  7.2 32.3 %copy-start.101 = (s32[64]{0:T(128)S(1)}, s32[64]{0:T(128)}, u32[]{:S(2)}) copy-start(s32[64]{0:T(128)} %order.1) | copy-start | bytes 772
  7.2 51.7 %all-gather.10.cloned.1.call-start = ((), (), s32[]{:S(2)}) async-start(), calls=%async_computation.8 | async-start | bytes 7077888 | tf_op jit(solution)/shard_map/all_gather | solution.py:369
  9.7 86.9 %all-gather.8.cloned.1.call-start = ((), (), s32[]{:S(2)}) async-start(), calls=%async_computation.7 | async-start | bytes 1720320 | tf_op jit(solution)/shard_map/all_gather | solution.py:403
  37.8 55.7 %copy-start.91 = (f32[2,112]{1,0:T(2,128)}, f32[2,112]{1,0:T(2,128)S(1)}, u32[]{:S(2)}) copy-start(f32[2,112]{1,0:T(2,128)S(1)} %add_rsqrt_fusion.3) | copy-start | bytes 2692
  38.4 55.1 %copy-start.72 = (f32[768]{0:T(1024)}, f32[768]{0:T(1024)S(1)}, u32[]{:S(2)}) copy-start(f32[768]{0:T(1024)S(1)} %get-tuple-element.865) | copy-start | bytes 9220
  38.4 142.5 %copy-start.74 = (f32[768]{0:T(1024)}, f32[768]{0:T(1024)S(1)}, u32[]{:S(2)}) copy-start(f32[768]{0:T(1024)S(1)} %get-tuple-element.862) | copy-start | bytes 9220
  39.4 140.0 %reduce-scatter.8.cloned.1.call-start = ((), (), s32[]{:S(2)}) async-start(), calls=%async_computation.9 | async-start | bytes 3440640 | tf_op jit(solution)/shard_map/reduce_scatter | solution.py:409
  96.6 7.8 copy-start.36
  96.6 10.9 copy-start.26
  96.6 119.0 %copy-start.28 = (bf16[4,192,192]{2,1,0:T(8,128)(2,1)}, bf16[4,192,192]{2,1,0:T(8,128)(2,1)S(1)}, u32[]{:S(2)}) copy-start(bf16[4,192,192]{2,1,0:T(8,128)(2,1)S(1)} %get-tuple-element.849) | copy-start | bytes 884740
  96.7 6.4 copy-start.2
  104.4 5.9 copy-start.68
  104.4 5.9 copy-start.70
  125.2 90.4 %all-gather.12.cloned.1.call-start = ((), (), s32[]{:S(2)}) async-start(), calls=%async_computation.10 | async-start | bytes 1720320 | tf_op jit(solution)/shard_map/all_gather | solution.py:403
  180.7 6.6 copy-start.83
  180.9 6.3 copy-start.93
  181.9 114.2 %reduce-scatter.10.cloned.1.call-start = ((), (), s32[]{:S(2)}) async-start(), calls=%async_computation.11 | async-start | bytes 3440640 | tf_op jit(solution)/shard_map/reduce_scatter | solution.py:409
  187.3 5.6 copy-start.45
  242.8 90.0 %all-gather.14.cloned.1.call-start = ((), (), s32[]{:S(2)}) async-start(), calls=%async_computation.12 | async-start | bytes 1720320 | tf_op jit(solution)/shard_map/all_gather | solution.py:403
  299.1 99.6 %reduce-scatter.12.cloned.1.call-start = ((), (), s32[]{:S(2)}) async-start(), calls=%async_computation.13 | async-start | bytes 3440640 | tf_op jit(solution)/shard_map/reduce_scatter | solution.py:409
  299.2 137.6 %copy-start.77 = (f32[768]{0:T(1024)}, f32[768]{0:T(1024)S(1)}, u32[]{:S(2)}) copy-start(f32[768]{0:T(1024)S(1)} %dynamic-slice_reduce_fusion) | copy-start | bytes 9220
  332.9 9.8 copy-start.62
  345.5 53.3 %copy-start.85 = (f32[768]{0:T(1024)S(1)}, f32[768]{0:T(1024)}, u32[]{:S(2)}) copy-start(f32[768]{0:T(1024)} %get-tuple-element.858) | copy-start | bytes 9220
  345.5 55.0 %copy-start.76 = (f32[768]{0:T(1024)S(1)}, f32[768]{0:T(1024)}, u32[]{:S(2)}) copy-start(f32[768]{0:T(1024)} %get-tuple-element.856) | copy-start | bytes 9220
  345.5 91.3 %all-gather.16.cloned.1.call-start = ((), (), s32[]{:S(2)}) async-start(), calls=%async_computation.14 | async-start | bytes 1720320 | tf_op jit(solution)/shard_map/all_gather | solution.py:403
  403.1 97.3 %reduce-scatter.14.cloned.1.call-start = ((), (), s32[]{:S(2)}) async-start(), calls=%async_computation.15 | async-start | bytes 3440640 | tf_op jit(solution)/shard_map/reduce_scatter | solution.py:409
  436.8 7.4 copy-start.61
  447.1 55.5 %copy-start.95 = (f32[768]{0:T(1024)S(1)}, f32[768]{0:T(1024)}, u32[]{:S(2)}) copy-start(f32[768]{0:T(1024)} %get-tuple-element.857) | copy-start | bytes 9220
  447.1 93.2 %all-gather.18.cloned.1.call-start = ((), (), s32[]{:S(2)}) async-start(), calls=%async_computation.16 | async-start | bytes 1720320 | tf_op jit(solution)/shard_map/all_gather | solution.py:403
  506.5 124.8 %reduce-scatter.16.cloned.1.call-start = ((), (), s32[]{:S(2)}) async-start(), calls=%async_computation.17 | async-start | bytes 3440640 | tf_op jit(solution)/shard_map/reduce_scatter | solution.py:514
  574.8 56.5 %copy-start.75 = (f32[768]{0:T(1024)S(1)}, f32[768]{0:T(1024)}, u32[]{:S(2)}) copy-start(f32[768]{0:T(1024)} %copy-done.74) | copy-start | bytes 9220
  574.8 56.5 %copy-start.84 = (f32[2,112]{1,0:T(2,128)S(1)}, f32[2,112]{1,0:T(2,128)}, u32[]{:S(2)}) copy-start(f32[2,112]{1,0:T(2,128)} %copy-done.83) | copy-start | bytes 2692
  574.8 56.5 %copy-start.94 = (f32[2,112]{1,0:T(2,128)S(1)}, f32[2,112]{1,0:T(2,128)}, u32[]{:S(2)}) copy-start(f32[2,112]{1,0:T(2,128)} %copy-done.93) | copy-start | bytes 2692
  578.1 54.8 %copy-start.44 = (f32[2,112,768]{2,1,0:T(8,128)S(1)}, f32[2,112,768]{2,1,0:T(8,128)}, u32[]{:S(2)}) copy-start(f32[2,112,768]{2,1,0:T(8,128)} %get-tuple-element.815) | copy-start | bytes 2064388
  578.1 115.7 %all-gather.20.cloned.1.call-start = ((), (), s32[]{:S(2)}) async-start(), calls=%async_computation.18 | async-start | bytes 1720320 | tf_op jit(solution)/shard_map/all_gather | solution.py:403
  635.2 366.9 %all-reduce.5.cloned.1.call-start = ((), (), s32[]{:S(2)}) async-start(), calls=%async_computation.21 | async-start | bytes 18432000
  684.5 373.1 %reduce-scatter.18.cloned.1.call-start = ((), (), s32[]{:S(2)}) async-start(), calls=%async_computation.19 | async-start | bytes 3440640 | tf_op jit(solution)/shard_map/reduce_scatter | solution.py:409
  688.6 5.2 copy-start.63
  711.1 6.5 copy-start.27
  714.1 5.2 copy-start.29
  714.1 5.2 copy-start.37
  722.1 431.5 %reduce-scatter.20.cloned.1.call-start = ((), (), s32[]{:S(2)}) async-start(), calls=%async_computation.20 | async-start | bytes 14155776 | tf_op jit(solution)/shard_map/reduce_scatter | solution.py:564
  743.8 5.0 copy-start.55
  743.8 5.0 copy-start.57
  759.9 6.9 copy-start.14
  830.0 10.1 copy-start.88
  830.0 10.1 copy-start.87
  830.0 10.2 copy-start.86
  830.0 10.2 copy-start.99
  830.1 10.3 copy-start.96
  830.1 10.3 copy-start.90
  830.1 10.3 copy-start.89
  830.1 11.4 copy-start.23
  830.1 11.7 copy-start.31
  830.1 11.9 copy-start.49
  841.8 215.8 %copy-start.12 = (bf16[2,112,768]{2,1,0:T(8,128)(2,1)S(1)}, bf16[2,112,768]{2,1,0:T(8,128)(2,1)}, u32[]{:S(2)}) copy-start(bf16[2,112,768]{2,1,0:T(8,128)(2,1)} %param.22) | copy-start | bytes 1032196
  841.8 215.8 %copy-start.73 = (f32[768]{0:T(1024)S(1)}, f32[768]{0:T(1024)}, u32[]{:S(2)}) copy-start(f32[768]{0:T(1024)} %copy-done.72) | copy-start | bytes 9220
  841.8 215.8 %copy-start.82 = (f32[2,112]{1,0:T(2,128)S(1)}, f32[2,112]{1,0:T(2,128)}, u32[]{:S(2)}) copy-start(f32[2,112]{1,0:T(2,128)} %copy-done.81) | copy-start | bytes 2692
  841.8 215.8 %copy-start.92 = (f32[2,112]{1,0:T(2,128)S(1)}, f32[2,112]{1,0:T(2,128)}, u32[]{:S(2)}) copy-start(f32[2,112]{1,0:T(2,128)} %copy-done.91) | copy-start | bytes 2692
  842.4 252.1 %copy-start.80 = (f32[1824]{0:T(1024)S(1)}, f32[1824]{0:T(1024)}, u32[]{:S(2)}) copy-start(f32[1824]{0:T(1024)} %param.33) | copy-start | bytes 21892
  842.4 252.1 %copy-start.97 = (f32[1824]{0:T(1024)S(1)}, f32[1824]{0:T(1024)}, u32[]{:S(2)}) copy-start(f32[1824]{0:T(1024)} %param.34) | copy-start | bytes 21892
  842.4 252.1 %copy-start.98 = (f32[1824]{0:T(1024)S(1)}, f32[1824]{0:T(1024)}, u32[]{:S(2)}) copy-start(f32[1824]{0:T(1024)} %param.35) | copy-start | bytes 21892
  842.5 252.7 %copy-start.43 = (f32[2,112,768]{2,1,0:T(8,128)S(1)}, f32[2,112,768]{2,1,0:T(8,128)}, u32[]{:S(2)}) copy-start(f32[2,112,768]{2,1,0:T(8,128)} %get-tuple-element.818) | copy-start | bytes 2064388
  (63 other events, 155.6 us)
Sparse Core Ops, SparseCore 0:
  10.5 48.3 all-gather.9
  61.0 33.8 all-gather.7
  125.2 54.1 reduce-scatter.7
  182.0 33.5 all-gather.11
  243.0 53.0 reduce-scatter.9
  299.3 33.5 all-gather.13
  345.7 53.0 reduce-scatter.11
  403.2 33.5 all-gather.15
  447.2 53.0 reduce-scatter.13
  506.7 33.5 all-gather.17
  578.2 53.0 reduce-scatter.15
  635.3 33.5 all-gather.19
  684.6 317.4 all-reduce.4
  1004.4 53.1 reduce-scatter.17
  1061.3 92.1 reduce-scatter.19

commit v2 on v1

v2 whole, which is shorter than its diff:
```python
import functools

import jax
import jax.numpy as jnp
from jax import lax
from jax.experimental import pallas as pl
from jax.experimental.pallas import tpu as pltpu
from jax.sharding import PartitionSpec as P

HEAD = 64
FF = 3072
STEP = 5
LANES = 128
SLOT = 256
VM = 56 * 2**20
HI = lax.Precision.HIGHEST

norm_eps = 1e-05
beta_one = 0.9
beta_two = 0.95
adam_eps = 1e-08
rate_tiles = 0.05
rate_vectors = 0.3
score_scale = 0.125


def split2(a):
    hi = a.astype(jnp.bfloat16)
    lo = (a - hi.astype(jnp.float32)).astype(jnp.bfloat16)
    return hi, lo

def bdot(a, b, dims):
    return lax.dot_general(a, b, (dims, ((), ())), preferred_element_type=jnp.float32)

NN = ((1,), (0,)); TN = ((0,), (0,)); NT = ((1,), (1,))

def dot3(a, b, dims):
    (ah, al), (bh, bl) = a, b
    return bdot(ah, bh, dims) + (bdot(ah, bl, dims) + bdot(al, bh, dims))

def dothi(a, b, dims):
    return lax.dot_general(a, b, (dims, ((), ())), precision=HI, preferred_element_type=jnp.float32)

def soap_pre_kernel(first, stats, bases, rot_first, stats_rot):
    ql, qr = split2(bases[0, 0]), split2(bases[0, 1])
    inner = split2(dot3(ql, split2(first[0]), TN))
    rot_first[0] = dot3(inner, qr, NN)
    stats_rot[0, 0] = dot3(split2(stats[0, 0]), ql, NN)
    stats_rot[0, 1] = dot3(split2(stats[0, 1]), qr, NN)

def soap_main_kernel(grad, master, first, second, stats, bases, rot_first, stats_rot,
                     new_master, new_first, new_second, new_stats, turned, grams):
    g32 = grad[0].astype(jnp.float32)
    g, ql, qr = split2(g32), split2(bases[0, 0]), split2(bases[0, 1])
    new_first[0] = beta_one * first[0] + (1.0 - beta_one) * g32
    part_left = split2(dot3(ql, g, TN))
    rotated = dot3(part_left, qr, NN)
    fresh = beta_two * second[0] + (1.0 - beta_two) * rotated * rotated
    new_second[0] = fresh
    moment = (beta_one * rot_first[0] + (1.0 - beta_one) * rotated) / (1.0 - beta_one**STEP)
    step = moment / (jnp.sqrt(fresh / (1.0 - beta_two**STEP)) + adam_eps)
    back = split2(dot3(ql, split2(step), NN))
    new_master[0] = master[0] - rate_tiles * dot3(back, qr, NT)
    new_stats[0, 0] = beta_two * stats[0, 0] + (1.0 - beta_two) * dot3(g, g, NT)
    new_stats[0, 1] = beta_two * stats[0, 1] + (1.0 - beta_two) * dot3(g, g, TN)
    part_right = split2(dot3(g, qr, NN))
    for side, term in ((0, dot3(g, part_left, NT)), (1, dot3(g, part_right, TN))):
        side_turned = beta_two * stats_rot[0, side] + (1.0 - beta_two) * term
        turned[0, side] = side_turned
        halves = split2(side_turned)
        grams[0, side] = dot3(halves, halves, TN)

def chol_kernel(turned, grams, out, work, inv, fac, *, block):
    count, side = work.shape[0], work.shape[1]
    row = lax.broadcasted_iota(jnp.int32, (side, side), 0)
    col = lax.broadcasted_iota(jnp.int32, (side, side), 1)
    eye = (row == col).astype(jnp.float32)
    for m in range(count):
        work[m] = grams[m]
        inv[m] = eye
    brow = lax.broadcasted_iota(jnp.int32, (count, block, 2 * block), 1)
    bcol = lax.broadcasted_iota(jnp.int32, (count, block, 2 * block), 2)
    aug_eye = ((bcol - block) == brow).astype(jnp.float32)
    for k in range(side // block):
        lo = k * block
        diag = work[:, lo : lo + block, lo : lo + block]
        w = jnp.concatenate([diag, jnp.zeros_like(diag)], axis=2) + aug_eye
        for j in range(block - 1):
            piv = w[:, j : j + 1, :]
            ratio = w[:, :, j : j + 1] / w[:, j : j + 1, j : j + 1]
            w = w - jnp.where(brow > j, ratio * piv, 0.0)
        d = jnp.sum(jnp.where(brow == bcol, w, 0.0), axis=2, keepdims=True)
        fac[...] = w[:, :, block:] * lax.rsqrt(d)

        def one(m, _):
            x = fac[m]
            y = dothi(x, work[m, lo : lo + block, :], NN)
            z = dothi(x, inv[m, lo : lo + block, :], NN)
            inv[m, lo : lo + block, :] = z
            if lo + block < side:
                rest = side - lo - block
                ys = split2(y)
                upd = dothi(y, y, TN)
                updx = dothi(y, z, TN)
                work[m, lo + block :, :] = work[m, lo + block :, :] - upd[lo + block :, :]
                inv[m, lo + block :, :] = inv[m, lo + block :, :] - updx[lo + block :, :]
            return 0
        lax.fori_loop(0, count, one, 0)

    def last(m, _):
        out[m] = dothi(turned[m], inv[m], NT)
        return 0
    lax.fori_loop(0, count, last, 0)

def tile_spec(side):
    return pl.BlockSpec((1, side, side), lambda i: (i, 0, 0))
def pair_spec(side):
    return pl.BlockSpec((1, 2, side, side), lambda i: (i, 0, 0, 0))

def soap_pre(first, stats, bases):
    n, side = first.shape[0], first.shape[1]
    t, p = tile_spec(side), pair_spec(side)
    return pl.pallas_call(soap_pre_kernel, grid=(n,), in_specs=[t, p, p], out_specs=[t, p],
        out_shape=[jax.ShapeDtypeStruct(first.shape, jnp.float32), jax.ShapeDtypeStruct(stats.shape, jnp.float32)],
        name="soap_pre")(first, stats, bases)

def soap_main(grad, master, first, second, stats, bases, rot_first, stats_rot):
    n, side = first.shape[0], first.shape[1]
    t, p = tile_spec(side), pair_spec(side)
    f = jnp.float32
    ts, ps = jax.ShapeDtypeStruct(first.shape, f), jax.ShapeDtypeStruct(stats.shape, f)
    return pl.pallas_call(soap_main_kernel, grid=(n,), in_specs=[t, t, t, t, p, p, t, p],
        out_specs=[t, t, t, p, p, p], out_shape=[ts, ts, ts, ps, ps, ps], name="soap_main")(
        grad, master, first, second, stats, bases, rot_first, stats_rot)

def chol_bases(turned, grams, block=32):
    n, _, side, _ = turned.shape
    shape = (2 * n, side, side)
    out = pl.pallas_call(functools.partial(chol_kernel, block=block),
        out_shape=jax.ShapeDtypeStruct(shape, jnp.float32),
        scratch_shapes=[pltpu.VMEM(shape, jnp.float32), pltpu.VMEM(shape, jnp.float32), pltpu.VMEM((2*n, block, block), jnp.float32)],
        compiler_params=pltpu.CompilerParams(vmem_limit_bytes=48 * 2**20), name="chol_bases")(
        turned.reshape(shape), grams.reshape(shape))
    return out.reshape(turned.shape)

def soap(gradient, master, first, second, statistics, bases, block=32):
    rot_first, stats_rot = soap_pre(first, statistics, bases)
    nm, nf, ns, nst, turned, grams = soap_main(gradient, master, first, second, statistics, bases, rot_first, stats_rot)
    return nf, ns, nm, nst, chol_bases(turned, grams, block)


def head_pick(shape, head):
    lane = lax.broadcasted_iota(jnp.int32, shape, len(shape) - 1)
    return (lane >= HEAD) if head % 2 else (lane < HEAD)


def forward_heads(query, key, value, allowed, heads):
    blocks = []
    for first in range(0, heads, 2):
        span = slice(first * HEAD, first * HEAD + LANES)
        query_block, key_block, value_block = query[:, span], key[:, span], value[:, span]
        made = None
        for head in range(first, min(first + 2, heads)):
            own_query = jnp.where(head_pick(query_block.shape, head), query_block, jnp.zeros_like(query_block))
            scores = bdot(own_query, key_block, NT) * score_scale
            if allowed is not None:
                scores = jnp.where(allowed, scores, -1e30)
            weights = jnp.exp(scores - jnp.max(scores, axis=1, keepdims=True)).astype(jnp.bfloat16)
            own_value = jnp.where(head_pick(value_block.shape, head), value_block, jnp.ones_like(value_block))
            both = bdot(weights, own_value, NN)
            mixed = both / pltpu.roll(both, HEAD, 1)
            pick = head_pick(mixed.shape, head)
            made = jnp.where(pick, mixed, 0.0 if made is None else made)
        blocks.append(made.astype(jnp.bfloat16))
    return jnp.concatenate(blocks, axis=1)


def cross_forward_kernel(query, key, value, out, *, heads):
    out[0] = forward_heads(query[0], key[0], value[0], None, heads)


def self_forward_kernel(query, key, value, seg_col, seg_row, stamp_row, out, *, heads):
    rows = query.shape[1]
    at = lax.broadcasted_iota(jnp.int32, (rows, rows), 0)
    key_at = lax.broadcasted_iota(jnp.int32, (rows, rows), 1)
    allowed = (key_at <= at) & (seg_col[0] == seg_row[0]) & ((stamp_row[0] == 0) | (key_at == at))
    out[0] = forward_heads(query[0], key[0], value[0], allowed, heads)


def backward_head(query_block, key_block, key_turned, value_block, grad_block, mixed_block, allowed, head):
    pick = head_pick(query_block.shape, head)
    own_query = jnp.where(pick, query_block, jnp.zeros_like(query_block))
    own_grad = jnp.where(pick, grad_block, jnp.zeros_like(grad_block))
    scores = bdot(key_block, own_query, NT) * score_scale
    if allowed is not None:
        scores = jnp.where(allowed, scores, -1e30)
    weights = jnp.exp(scores - jnp.max(scores, axis=0, keepdims=True))
    probs = weights * (1.0 / jnp.sum(weights, axis=0, keepdims=True))
    grad_probs = bdot(value_block, own_grad, NT)
    row_dot = jnp.sum(probs * grad_probs, axis=0, keepdims=True)
    grad_scores = (probs * (grad_probs - row_dot)).astype(jnp.bfloat16)
    return probs.astype(jnp.bfloat16), grad_scores, bdot(key_turned, grad_scores, NN)


def backward_heads(query, key, value, grad, allowed, heads, probs_ref, scores_ref):
    blocks = []
    for first in range(0, heads, 2):
        span = slice(first * HEAD, first * HEAD + LANES)
        query_block, key_block, value_block, grad_block = query[:, span], key[:, span], value[:, span], grad[:, span]
        key_turned = key_block.T
        made = None
        for head in range(first, min(first + 2, heads)):
            probs, grad_scores, turned = backward_head(query_block, key_block, key_turned, value_block, grad_block, None, allowed, head)
            probs_ref[head] = probs
            scores_ref[head] = grad_scores
            row = lax.broadcasted_iota(jnp.int32, turned.shape, 0)
            pick = (row >= HEAD) if head % 2 else (row < HEAD)
            made = jnp.where(pick, turned, 0.0 if made is None else made)
        blocks.append((made.T * score_scale).astype(jnp.bfloat16))
    return jnp.concatenate(blocks, axis=1)


def key_value_grads(query, grad, heads, probs_ref, scores_ref):
    keys, values = [], []
    for first in range(0, heads, 2):
        span = slice(first * HEAD, first * HEAD + LANES)
        made_key = made_value = None
        for head in range(first, min(first + 2, heads)):
            grad_key = bdot(scores_ref[head], query[:, span], NN) * score_scale
            grad_value = bdot(probs_ref[head], grad[:, span], NN)
            pick = head_pick(grad_key.shape, head)
            made_key = jnp.where(pick, grad_key, 0.0 if made_key is None else made_key)
            made_value = jnp.where(pick, grad_value, 0.0 if made_value is None else made_value)
        keys.append(made_key.astype(jnp.bfloat16))
        values.append(made_value.astype(jnp.bfloat16))
    return jnp.concatenate(keys, axis=1), jnp.concatenate(values, axis=1)


def cross_backward_kernel(rank, query, key, value, grad, grad_query, grad_key, grad_value, probs_ref, scores_ref, *, heads):
    grad_query[0] = backward_heads(query[0], key[0], value[0], grad[0], None, heads, probs_ref, scores_ref)

    @pl.when(pl.program_id(1) == rank[0])
    def _():
        made = key_value_grads(query[0], grad[0], heads, probs_ref, scores_ref)
        grad_key[0], grad_value[0] = made


def self_backward_kernel(rank, query, key, value, grad, seg_col, seg_row, stamp_col, out, probs_ref, scores_ref, *, heads):
    rows = query.shape[1]
    key_at = lax.broadcasted_iota(jnp.int32, (rows, rows), 0)
    at = lax.broadcasted_iota(jnp.int32, (rows, rows), 1)
    allowed = (key_at <= at) & (seg_col[0] == seg_row[0]) & ((stamp_col[0] == 0) | (key_at == at))
    grad_query = backward_heads(query[0], key[0], value[0], grad[0], allowed, heads, probs_ref, scores_ref)
    grad_key, grad_value = key_value_grads(query[0], grad[0], heads, probs_ref, scores_ref)
    out[0] = jnp.concatenate([grad_query, grad_key, grad_value], axis=1)


def slot_spec(rows, offset):
    return pl.BlockSpec((1, rows, SLOT), lambda b, r: (b, 0, offset + r))


def self_forward(qkv, seg_col, seg_row, stamp_row, ranks, heads):
    seqs, rows, _ = qkv.shape
    col = pl.BlockSpec((1, rows, 1), lambda b, r: (b, 0, 0))
    row = pl.BlockSpec((1, 1, rows), lambda b, r: (b, 0, 0))
    return pl.pallas_call(
        functools.partial(self_forward_kernel, heads=heads),
        grid=(seqs, ranks),
        in_specs=[slot_spec(rows, 0), slot_spec(rows, ranks), slot_spec(rows, 2 * ranks), col, row, row],
        out_specs=slot_spec(rows, 0),
        out_shape=jax.ShapeDtypeStruct((seqs, rows, ranks * SLOT), jnp.bfloat16),
        compiler_params=pltpu.CompilerParams(vmem_limit_bytes=VM),
        name="self_forward",
    )(qkv, qkv, qkv, seg_col, seg_row, stamp_row)


def cross_forward(queries, keys_values, ranks, heads):
    seqs, rows, _ = queries.shape
    frames = keys_values.shape[1]
    return pl.pallas_call(
        functools.partial(cross_forward_kernel, heads=heads),
        grid=(seqs, ranks),
        in_specs=[slot_spec(rows, 0), slot_spec(frames, 0), slot_spec(frames, ranks)],
        out_specs=slot_spec(rows, 0),
        out_shape=jax.ShapeDtypeStruct((seqs, rows, ranks * SLOT), jnp.bfloat16),
        compiler_params=pltpu.CompilerParams(vmem_limit_bytes=VM),
        name="cross_forward",
    )(queries, keys_values, keys_values)


def ranked_spec(rows, offset):
    return pl.BlockSpec((1, rows, SLOT), lambda b, r, rank: (b, 0, offset + r))


def cross_backward(rank, queries, keys_values, grads, ranks, heads):
    seqs, rows, _ = queries.shape
    frames = keys_values.shape[1]
    kept = pl.BlockSpec((1, frames, SLOT), lambda b, r, rank: (b, 0, 0))
    bf = jnp.bfloat16
    return pl.pallas_call(
        functools.partial(cross_backward_kernel, heads=heads),
        grid_spec=pltpu.PrefetchScalarGridSpec(
            num_scalar_prefetch=1,
            grid=(seqs, ranks),
            in_specs=[ranked_spec(rows, 0), ranked_spec(frames, 0), ranked_spec(frames, ranks), ranked_spec(rows, 0)],
            out_specs=[ranked_spec(rows, 0), kept, kept],
            scratch_shapes=[pltpu.VMEM((heads, frames, rows), bf), pltpu.VMEM((heads, frames, rows), bf)],
        ),
        out_shape=[
            jax.ShapeDtypeStruct((seqs, rows, ranks * SLOT), bf),
            jax.ShapeDtypeStruct((seqs, frames, SLOT), bf),
            jax.ShapeDtypeStruct((seqs, frames, SLOT), bf),
        ],
        compiler_params=pltpu.CompilerParams(vmem_limit_bytes=VM),
        name="cross_backward",
    )(rank, queries, keys_values, keys_values, grads)


def self_backward(rank, qkv, grads, seg_col, seg_row, stamp_col, ranks, heads):
    seqs, rows, _ = qkv.shape
    bf = jnp.bfloat16
    own = lambda offset: pl.BlockSpec((1, rows, SLOT), lambda b, rank: (b, 0, offset + rank[0]))
    col = pl.BlockSpec((1, rows, 1), lambda b, rank: (b, 0, 0))
    row = pl.BlockSpec((1, 1, rows), lambda b, rank: (b, 0, 0))
    return pl.pallas_call(
        functools.partial(self_backward_kernel, heads=heads),
        grid_spec=pltpu.PrefetchScalarGridSpec(
            num_scalar_prefetch=1,
            grid=(seqs,),
            in_specs=[own(0), own(ranks), own(2 * ranks), own(0), col, row, col],
            out_specs=pl.BlockSpec((1, rows, 3 * SLOT), lambda b, rank: (b, 0, 0)),
            scratch_shapes=[pltpu.VMEM((heads, rows, rows), bf), pltpu.VMEM((heads, rows, rows), bf)],
        ),
        out_shape=jax.ShapeDtypeStruct((seqs, rows, 3 * SLOT), bf),
        compiler_params=pltpu.CompilerParams(vmem_limit_bytes=VM),
        name="self_backward",
    )(rank, qkv, qkv, qkv, grads, seg_col, seg_row, stamp_col)


def tile_sources():
    steps = []
    for base in (0, 4, 8, 16, 20, 12):
        for pair in range(2):
            steps.append([(pair * 2 + i // 4, base + i % 4) for i in range(8)])
    for base in (24, 28):
        for pair in range(2):
            steps.append([(pair * 2 + i // 4, base + i % 4) for i in range(8)])
    for half in range(2):
        for rank in range(4):
            steps.append([(rank, 32 + (half * 2 + i // 4) * 4 + i % 4) for i in range(8)])
    for rank in range(4):
        for half in range(2):
            steps.append([(rank, 48 + (half * 2 + i // 4) * 4 + i % 4) for i in range(8)])
    return steps


def assemble_kernel(table, *refs):
    tiles, (o_qkv, o_ckv, o_cq, o_wo, o_co, o_in, o_out) = refs[:8], refs[8:]
    step = pl.program_id(0)
    side = tiles[0].shape[1]

    def columns(out):
        gap = jnp.zeros((side, SLOT - side), jnp.bfloat16)
        for i in range(8):
            wide = jnp.concatenate([tiles[i][0], gap], axis=1)
            out[(i % 4) * side : (i % 4 + 1) * side, (i // 4) * SLOT : (i // 4 + 1) * SLOT] = wide

    def joined(half):
        return jnp.concatenate([tiles[half * 4 + i][0] for i in range(4)], axis=1)

    def padded_rows(out):
        for half in range(2):
            out[half * SLOT : half * SLOT + side, :] = joined(half)
            out[half * SLOT + side : (half + 1) * SLOT, :] = jnp.zeros((SLOT - side, 4 * side), jnp.bfloat16)

    def rows(out):
        for half in range(2):
            out[half * side : (half + 1) * side, :] = joined(half)

    for low, high, fill, out in (
        (0, 6, columns, o_qkv),
        (6, 10, columns, o_ckv),
        (10, 12, columns, o_cq),
        (12, 14, padded_rows, o_wo),
        (14, 16, padded_rows, o_co),
        (16, 24, rows, o_in),
        (24, 32, rows, o_out),
    ):
        pl.when((step >= low) & (step < high))(functools.partial(fill, out))


def assemble(table, tiles):
    side = tiles.shape[-1]
    width = 4 * side

    def tile_at(i):
        return pl.BlockSpec((1, side, side), lambda s, table: (table[s * 8 + i], 0, 0))

    def within(low, count):
        return lambda s: jnp.clip(s - low, 0, count - 1)

    a, b, c, d, e, f, g = [within(*x) for x in ((0, 6), (6, 4), (10, 2), (12, 2), (14, 2), (16, 8), (24, 8))]
    bf = jnp.bfloat16
    return pl.pallas_call(
        assemble_kernel,
        grid_spec=pltpu.PrefetchScalarGridSpec(
            num_scalar_prefetch=1,
            grid=(32,),
            in_specs=[tile_at(i) for i in range(8)],
            out_specs=[
                pl.BlockSpec((width, 2 * SLOT), lambda s, table: (0, a(s))),
                pl.BlockSpec((width, 2 * SLOT), lambda s, table: (0, b(s))),
                pl.BlockSpec((width, 2 * SLOT), lambda s, table: (0, c(s))),
                pl.BlockSpec((2 * SLOT, width), lambda s, table: (d(s), 0)),
                pl.BlockSpec((2 * SLOT, width), lambda s, table: (e(s), 0)),
                pl.BlockSpec((2 * side, width), lambda s, table: (f(s) // 4, f(s) % 4)),
                pl.BlockSpec((2 * side, width), lambda s, table: (g(s), 0)),
            ],
        ),
        out_shape=[
            jax.ShapeDtypeStruct((width, 12 * SLOT), bf),
            jax.ShapeDtypeStruct((width, 8 * SLOT), bf),
            jax.ShapeDtypeStruct((width, 4 * SLOT), bf),
            jax.ShapeDtypeStruct((4 * SLOT, width), bf),
            jax.ShapeDtypeStruct((4 * SLOT, width), bf),
            jax.ShapeDtypeStruct((width, 4 * width), bf),
            jax.ShapeDtypeStruct((4 * width, width), bf),
        ],
        compiler_params=pltpu.CompilerParams(vmem_limit_bytes=VM),
        name="assemble",
    )(table, *([tiles] * 8))


def weight_grads_kernel(
    rank, place, n1, dqkv, n2, dcq, frames, dk, dv, attended, b1, mixed, b2, n3, grad_up, active, b3, out
):
    side = out.shape[1]

    def slots(made, bases):
        for m, base in enumerate(bases):
            for i in range(4):
                out[place[base + i]] = made[i * side : (i + 1) * side, m * SLOT : m * SLOT + side].astype(jnp.bfloat16)

    def grid_of(made, base, rows):
        for i in range(rows):
            for j in range(4):
                tile = made[i * side : (i + 1) * side, j * side : (j + 1) * side]
                out[place[base + i * 4 + j]] = tile.astype(jnp.bfloat16)

    slots(bdot(n1[...], dqkv[...], TN), (0, 4, 8))
    slots(bdot(n2[...], dcq[...], TN), (12,))
    slots(bdot(frames[0], dk[0], TN) + bdot(frames[1], dk[1], TN), (16,))
    slots(bdot(frames[0], dv[0], TN) + bdot(frames[1], dv[1], TN), (20,))
    grid_of(bdot(attended[...], b1[...], TN), 24, 1)
    grid_of(bdot(mixed[...], b2[...], TN), 28, 1)
    grid_of(bdot(n3[...], grad_up[...], TN), 32, 4)
    grid_of(bdot(active[...], b3[...], TN), 48, 4)


def weight_grads(rank, place, side, n1, dqkv, n2, dcq, frames, dk, dv, attended, b1, mixed, b2, n3, grad_up, active, b3):
    def whole(x):
        return pl.BlockSpec(x.shape, lambda i, rank, place: (0,) * x.ndim)

    def own(x, width):
        return pl.BlockSpec((x.shape[0], width), lambda i, rank, place: (0, rank[0]))

    shape = (place.shape[0], side, side)
    return pl.pallas_call(
        weight_grads_kernel,
        grid_spec=pltpu.PrefetchScalarGridSpec(
            num_scalar_prefetch=2,
            grid=(1,),
            in_specs=[
                whole(n1), whole(dqkv), whole(n2), own(dcq, SLOT), whole(frames), whole(dk), whole(dv),
                own(attended, SLOT), whole(b1), own(mixed, SLOT), whole(b2), whole(n3),
                own(grad_up, 4 * side), own(active, 4 * side), whole(b3),
            ],
            out_specs=pl.BlockSpec(shape, lambda i, rank, place: (0, 0, 0)),
        ),
        out_shape=jax.ShapeDtypeStruct(shape, jnp.bfloat16),
        compiler_params=pltpu.CompilerParams(vmem_limit_bytes=60 * 2**20),
        name="weight_grads",
    )(rank, place, n1, dqkv, n2, dcq, frames, dk, dv, attended, b1, mixed, b2, n3, grad_up, active, b3)


def frames_kernel(frames, weight, bias, out):
    out[0] = (bdot(frames[0], weight[...], NN) + bias[...]).astype(jnp.bfloat16)


def frame_projection(frames, weight, bias):
    seqs, count, width = frames.shape
    total = weight.shape[1]
    return pl.pallas_call(
        frames_kernel,
        grid=(seqs, total // 512),
        in_specs=[
            pl.BlockSpec((1, count, width), lambda b, c: (b, 0, 0)),
            pl.BlockSpec((width, 512), lambda b, c: (0, c)),
            pl.BlockSpec((1, 512), lambda b, c: (0, c)),
        ],
        out_specs=pl.BlockSpec((1, count, 512), lambda b, c: (b, 0, c)),
        out_shape=jax.ShapeDtypeStruct((seqs, count, total), jnp.bfloat16),
        compiler_params=pltpu.CompilerParams(vmem_limit_bytes=VM),
        name="frame_projection",
    )(frames, weight, bias[None])


def frames_back_kernel(rank, dk, dv, key_weight, value_weight, out, *, parts):
    made = bdot(dk[0], key_weight[...], NT) + bdot(dv[0], value_weight[...], NT)
    share = made.shape[0] // parts
    for part in range(parts):
        piece = made[part * share : (part + 1) * share]
        out[part, 0] = jnp.concatenate([piece, jnp.zeros((out.shape[2] - share, piece.shape[1]), jnp.float32)], axis=0).astype(jnp.bfloat16)


def frames_back(rank, dk, dv, weight, parts):
    seqs, count, slot = dk.shape
    width = weight.shape[0]
    padded = -(-(count // parts) // 16) * 16
    own = pl.BlockSpec((1, count, slot), lambda b, rank: (b, 0, 0))
    return pl.pallas_call(
        functools.partial(frames_back_kernel, parts=parts),
        grid_spec=pltpu.PrefetchScalarGridSpec(
            num_scalar_prefetch=1,
            grid=(seqs,),
            in_specs=[
                own, own,
                pl.BlockSpec((width, slot), lambda b, rank: (0, rank[0])),
                pl.BlockSpec((width, slot), lambda b, rank: (0, parts + rank[0])),
            ],
            out_specs=pl.BlockSpec((parts, 1, padded, width), lambda b, rank: (0, b, 0, 0)),
        ),
        out_shape=jax.ShapeDtypeStruct((parts, seqs, padded, width), jnp.bfloat16),
        compiler_params=pltpu.CompilerParams(vmem_limit_bytes=VM),
        name="frames_back",
    )(rank, dk, dv, weight, weight)


def product(left_part, right_part):
    return jnp.dot(left_part, right_part, preferred_element_type=jnp.float32)


def times_transpose(left_part, right_part):
    return lax.dot_general(left_part, right_part, (NT, ((), ())), preferred_element_type=jnp.float32)


def unit_rows(values):
    centre = jnp.mean(values, axis=-1, keepdims=True)
    centred = values - centre
    inverse = lax.rsqrt(jnp.mean(centred * centred, axis=-1, keepdims=True) + norm_eps)
    return centred * inverse, inverse


def normalize(values, gain, shift):
    return unit_rows(values)[0] * gain + shift


def normalize_back(values, gain, grads):
    unit, inverse = unit_rows(values)
    scaled = grads * gain
    result = inverse * (
        scaled
        - jnp.mean(scaled, axis=-1, keepdims=True)
        - unit * jnp.mean(scaled * unit, axis=-1, keepdims=True)
    )
    return result, jnp.sum(grads * unit, axis=0), jnp.sum(grads, axis=0)


def gelu_pair(value):
    size = jnp.abs(value) * 0.7071067811865476
    bell = jnp.exp(-size * size)
    t = 1.0 / (1.0 + 0.3275911 * size)
    poly = t * (0.254829592 + t * (-0.284496736 + t * (1.421413741 + t * (-1.453152027 + t * 1.061405429))))
    tail = 0.5 * poly * bell
    level = jnp.where(value >= 0, 1.0 - tail, tail)
    return value * level, level + value * bell * 0.3989422804014327


def spread_heads(rows, ranks):
    lead = rows.shape[0]
    side = rows.shape[1] // ranks
    return jnp.pad(rows.reshape(lead, ranks, side), ((0, 0), (0, 0), (0, SLOT - side))).reshape(lead, ranks * SLOT)


def shards(
    hidden_in, frames, cotangent, segments, stamps, owner_list, master_tiles, tile_first, tile_second,
    tile_stats, tile_bases, master_vectors, vector_first, vector_second,
):
    f32, bf16 = jnp.float32, jnp.bfloat16
    ranks, groups = lax.axis_size("tensor"), lax.axis_size("dp")
    rank, group = lax.axis_index("tensor"), lax.axis_index("dp")
    seqs, local_rows, width = hidden_in.shape
    rows = local_rows * ranks
    tokens = seqs * rows
    own_tiles, side = master_tiles.shape[1], master_tiles.shape[-1]
    heads = side // HEAD
    rank_ref = rank.astype(jnp.int32)[None]

    both = lax.all_gather(jnp.stack([hidden_in, cotangent]), "tensor", axis=2, tiled=True)
    hidden = both[0].reshape(tokens, width).astype(f32)
    top_grad = both[1].reshape(tokens, width).astype(f32)
    gathered = lax.all_gather(master_tiles[0].astype(bf16), ("dp", "tensor"), axis=0, tiled=True)
    vectors = lax.all_gather(master_vectors.astype(bf16), "dp", axis=0, tiled=True).astype(f32).reshape(19, width)

    count = owner_list.shape[0]
    position = jnp.arange(count, dtype=jnp.int32)
    place = jnp.sum(jnp.where(owner_list[None, :] == position[:, None], position[None, :], 0), axis=1)
    steps = tile_sources()
    source_rank = jnp.array([r for step in steps for r, _ in step], jnp.int32)
    source_ident = jnp.array([t for step in steps for _, t in step], jnp.int32)
    found = jnp.sum(jnp.where(owner_list[None, :] == source_ident[:, None], position[None, :], 0), axis=1)
    table = (found // own_tiles * ranks + source_rank) * own_tiles + found % own_tiles
    w_qkv, c_kv, c_q, w_o, c_o, w_in, w_out = assemble(table, gathered)

    head_bias = spread_heads(vectors[11:15], ranks)
    none = jnp.zeros_like(head_bias[0])
    inner_bias = vectors[15:19].reshape(-1)
    seg_col, seg_row = segments[:, :, None], segments[:, None, :]
    stamp_col, stamp_row = stamps[:, :, None], stamps[:, None, :]

    def split(values):
        return values.reshape(seqs, rows, values.shape[-1])

    def flat(values):
        return values.reshape(tokens, values.shape[-1])

    def own_rows(values):
        return lax.dynamic_slice_in_dim(split(values), rank * local_rows, local_rows, axis=1)

    keys_values = frame_projection(frames, c_kv, jnp.concatenate([none, head_bias[3]]))
    n1 = normalize(hidden, vectors[0], vectors[1]).astype(bf16)
    qkv = split((product(n1, w_qkv) + jnp.concatenate([head_bias[0], none, head_bias[1]])).astype(bf16))
    attended = flat(self_forward(qkv, seg_col, seg_row, stamp_row, ranks, heads))
    first_sum = hidden + product(attended, w_o) + vectors[8]
    n2 = normalize(first_sum, vectors[2], vectors[3]).astype(bf16)
    cross_queries = split((product(n2, c_q) + head_bias[2]).astype(bf16))
    mixed = flat(cross_forward(cross_queries, keys_values, ranks, heads))
    second_sum = first_sum + product(mixed, c_o) + vectors[9]
    n3 = normalize(second_sum, vectors[4], vectors[5]).astype(bf16)
    active, slope = gelu_pair(product(n3, w_in) + inner_bias)
    active, slope = active.astype(bf16), slope.astype(bf16)
    third_sum = second_sum + product(active, w_out) + vectors[10]
    block_out = own_rows(normalize(third_sum, vectors[6], vectors[7]))

    grad_third, gain_final, shift_final = normalize_back(third_sum, vectors[6], top_grad)
    b3 = grad_third.astype(bf16)
    grad_up = (times_transpose(b3, w_out) * slope.astype(f32)).astype(bf16)
    back, gain_three, shift_three = normalize_back(second_sum, vectors[4], times_transpose(grad_up, w_in))
    grad_second = grad_third + back
    b2 = grad_second.astype(bf16)
    grad_mixed = split(times_transpose(b2, c_o).astype(bf16))
    dcq, dk, dv = cross_backward(rank_ref, cross_queries, keys_values, grad_mixed, ranks, heads)
    dcq = flat(dcq)
    frames_part = frames_back(rank_ref, dk, dv, c_kv, ranks)
    frames_sum = lax.psum_scatter(
        frames_part.reshape(ranks * seqs, frames_part.shape[2], width), "tensor", scatter_dimension=0, tiled=True
    )
    frames_grad = frames_sum[:, : frames.shape[1] // ranks].astype(f32)
    back, gain_two, shift_two = normalize_back(first_sum, vectors[2], times_transpose(dcq, c_q))
    grad_first = grad_second + back
    b1 = grad_first.astype(bf16)
    grad_attended = split(times_transpose(b1, w_o).astype(bf16))
    dqkv = flat(self_backward(rank_ref, qkv, grad_attended, seg_col, seg_row, stamp_col, ranks, heads))

    own_weight = lax.dynamic_slice_in_dim(w_qkv.reshape(width, 3, ranks * SLOT), rank * SLOT, SLOT, axis=2)
    part_one = times_transpose(dqkv, own_weight.reshape(width, 3 * SLOT))
    unit_one, _ = unit_rows(hidden)
    gain_one, shift_one = jnp.sum(part_one * unit_one, axis=0), jnp.sum(part_one, axis=0)
    grad_one = lax.psum_scatter(split(part_one.astype(bf16)), "tensor", scatter_dimension=1, tiled=True).astype(f32)
    back, _, _ = normalize_back(
        hidden_in.astype(f32).reshape(-1, width), vectors[0], grad_one.reshape(-1, width)
    )
    input_grad = own_rows(grad_first) + back.reshape(hidden_in.shape)

    tile_terms = weight_grads(
        rank_ref, place, side, n1, dqkv, n2, dcq, frames, dk, dv, attended, b1, mixed, b2, n3, grad_up, active, b3
    )
    owned_grads = lax.psum_scatter(tile_terms, "dp", scatter_dimension=0, tiled=True)

    def total(values):
        return jnp.sum(values.astype(f32), axis=tuple(range(values.ndim - 1)))

    same = jnp.stack(
        [gain_two, shift_two, gain_three, shift_three, gain_final, shift_final, total(b1), total(b2), total(b3)]
    )
    query_sum = total(dcq).reshape(ranks, SLOT)[:, :side].reshape(1, width)
    up_sum = total(grad_up).reshape(4, width)
    even = 1.0 / ranks
    dqkv_sum = total(dqkv)
    own_sums = jnp.stack([dqkv_sum[:side], dqkv_sum[2 * SLOT : 2 * SLOT + side], total(dv)[:side]])
    own_sums = lax.dynamic_update_slice(jnp.zeros((3, width), f32), own_sums, (0, rank * side))
    vector_terms = jnp.concatenate(
        [gain_one[None], shift_one[None], same * even, own_sums[:2], query_sum * even, own_sums[2:], up_sum * even]
    )
    vector_sums = lax.psum(vector_terms.reshape(-1), ("dp", "tensor"))
    length = master_vectors.shape[0]
    vector_grad = lax.dynamic_slice_in_dim(vector_sums, group * length, length)

    new_first, new_second, new_master, new_stats, new_bases = soap(
        owned_grads, master_tiles[0], tile_first[0], tile_second[0], tile_stats[0], tile_bases[0]
    )
    new_vector_first = beta_one * vector_first + (1.0 - beta_one) * vector_grad
    new_vector_second = beta_two * vector_second + (1.0 - beta_two) * vector_grad * vector_grad
    new_vectors = master_vectors - rate_vectors * (new_vector_first / (1.0 - beta_one**STEP)) / (
        jnp.sqrt(new_vector_second / (1.0 - beta_two**STEP)) + adam_eps
    )
    return (
        block_out, input_grad, frames_grad, new_master[None], new_first[None], new_second[None],
        new_stats[None], new_bases[None], new_vectors, new_vector_first, new_vector_second,
    )


def solution(mesh):
    rows, seqs, tiles, pairs = (
        P("dp", "tensor", None), P("dp", None), P("tensor", "dp", None, None), P("tensor", "dp", None, None, None)
    )
    line = P("dp")
    in_specs = (
        rows, P("dp", None, None), rows, seqs, seqs, P(), tiles, tiles, tiles, pairs, pairs, line, line, line
    )
    out_specs = (rows, rows, rows, tiles, tiles, tiles, pairs, pairs, line, line, line)
    return jax.shard_map(shards, mesh=mesh, in_specs=in_specs, out_specs=out_specs, check_vma=False)
```

time: 1280 us -> 712 us (0.56)
  waiting for transfers between devices: 628 us -> 173 us
  local copies, waits for them, and re-layouts: 179 us -> 35.6 us
  Pallas kernels: 183 us -> 300 us
  matrix products: 125 us -> 78.9 us
  other arithmetic: 52.6 us -> 33.2 us
  loops' own time: 16.5 us -> 0 us
    reduce_scatter x6 -> x2, waiting for transfers between devices: 319 us -> 0.01 us  [the longest x1 0.01 us: shards(): lax.psum_scatter(split(part_one.astype(bf16)), 'tensor', scatter_dimensio...]
    unnamed x16 -> x5, waiting for transfers between devices: 160 us -> 0.08 us
    pallas_call x2 -> x8, Pallas kernels: 71.4 us -> 188 us  [the longest x1 65.9 us: cross_backward(): pl.pallas_call(functools.partial(cross_backward_kernel, heads=heads), gri...]
    reshape x25 -> x2, local copies, waits for them, and re-layouts: 85.6 us -> 0.02 us  [the longest x1 0.01 us: shards(): query_sum = total(dcq).reshape(ranks, SLOT)[:, :side].reshape(1, width)]
    all_gather x7 -> x2, waiting for transfers between devices: 93.4 us -> 171 us  [the longest x1 150 us: shards(): lax.all_gather(master_tiles[0].astype(bf16), ('dp', 'tensor'), axis=0, ti...]
    reduce_scatter x1, waiting for transfers between devices: 56.1 us -> 1.85 us  [shards(): lax.psum_scatter(tile_terms, 'dp', scatter_dimension=0, tiled=True)]
    dot_general x48 -> x6, matrix products: 89.6 us -> 38.1 us  [times_transpose(): lax.dot_general(left_part, right_part, (NT, ((), ())), preferred_element_...]
    psum x1, blocking collectives: 10.8 us -> 39.3 us  [shards(): vector_sums = lax.psum(vector_terms.reshape(-1), ('dp', 'tensor'))]
  transfers between devices with their start and end apart: 15 -> 5, of which waited for: 13 -> 3; matrix products, arithmetic and copies ran while one was open for 18% -> 5% of each run, Pallas kernels for 6% -> 20%
where the time goes in v2:
time: 712 us; the launch traced here: 702 us
  Pallas kernels  300 us (42%)
  waiting for transfers between devices  173 us (24%)
  matrix products  78.9 us (11%)
  blocking collectives  65.6 us (9%)
  local copies, waits for them, and re-layouts  35.6 us (5%)
  other arithmetic  33.2 us (5%)
  between operations  15.3 us (2%)
    all_gather x1, waiting for transfers between devices, shards(): lax.all_gather(master_tiles[0].astype(bf16), ('dp', 'tensor'), axis=0, ti...  150 us
    pallas_call x1, Pallas kernels, chol_bases(): pl.pallas_call(functools.partial(chol_kernel, block=block), out_shape=jax...  84.5 us
    pallas_call x1, Pallas kernels, cross_backward(): pl.pallas_call(functools.partial(cross_backward_kernel, heads=heads), gri...  65.9 us
    dot_general x6, matrix products, product(): return jnp.dot(left_part, right_part, preferred_element_type=jnp.float32)  40.8 us
    psum x1, blocking collectives, shards(): vector_sums = lax.psum(vector_terms.reshape(-1), ('dp', 'tensor'))  39.3 us
    dot_general x6, matrix products, times_transpose(): lax.dot_general(left_part, right_part, (NT, ((), ())), preferred_element_...  38.1 us
    pallas_call x1, Pallas kernels, cross_forward(): pl.pallas_call(functools.partial(cross_forward_kernel, heads=heads), grid...  29.5 us
    pallas_call x1, Pallas kernels, assemble(): pl.pallas_call(assemble_kernel, grid_spec=pltpu.PrefetchScalarGridSpec(nu...  29.4 us
  transfers between devices with their start and end apart: 5, of which 3 were waited for; matrix products, arithmetic and copies ran while one was open for 5% of the time, Pallas kernels for 20%

profile of v2, /device:TPU:0, one launch (start us, length us, event | category | flops | bytes accessed | tf_op | source)
XLA Modules:
  0.0 701.9 jit_solution(8488803594995547550)
XLA Ops:
  7.3 2.1 pad_maximum_fusion
  9.5 1.0 bitcast_convert_fusion
  12.1 26.3 %all-reduce.2 = bf16[14592]{0:T(1024)(128)(2,1)S(1)} all-reduce(bf16[14592]{0:T(1024)(128)(2,1)S(1)} %dynamic-update-slice), channel_id=1, replica_groups=mesh['dp'=8,'tensor'=4] {'dp'}, use_global_device_ids=true, to_apply=%add.2 | all-reduce | flops 14592 | bytes 58368
  39.1 1.0 copy.44.seg_col
  40.8 5.1 copy.45.frames
  45.8 1.0 copy.47.stamp_col
  48.7 21.2 %all-gather.3.cloned.1.call-done = bf16[2,2,448,768]{3,2,1,0:T(8,128)(2,1)} async-done(((bf16[2,2,112,768]{3,2,1,0:T(8,128)(2,1)}), bf16[2,2,448,768]{3,2,1,0:T(8,128)(2,1)}) %all-gather.3.cloned.1.call-update) | async-done | bytes 2752528 | tf_op jit(solution)/shard_map/all_gather | solution.py:599
  69.9 1.6 convert_reduce_fusion.4
  71.6 3.6 convert_reduce_fusion.3
  75.3 1.7 fusion.14.n1
  77.1 149.7 %all-gather.5.cloned.1.call-done.refs_0_.refs_1_.refs_2_.refs_3_.refs_4_.refs_5_.refs_6_.refs_7_ = bf16[256,192,192]{2,1,0:T(8,128)(2,1)} async-done(((bf16[8,192,192]{2,1,0:T(8,128)(2,1)}), bf16[256,192,192]{2,1,0:T(8,128)(2,1)}) %all-gather.5.cloned.1.call-update) | async-done | bytes 18874384 | tf_op jit(solution)/shard_map/all_gather | solution.py:602
  226.8 29.4 %assemble.1 = (bf16[768,3072]{1,0:T(8,128)(2,1)}, bf16[768,2048]{1,0:T(8,128)(2,1)}, bf16[768,1024]{1,0:T(8,128)(2,1)}, bf16[1024,768]{1,0:T(8,128)(2,1)}, bf16[...) custom-call(s32[256]{0:T(256)} %fusion.32.table, ...), custom_call_target="tpu_custom_call" | custom-call | tf_op jit(solution)/shard_map/assemble/pallas_call | solution.py:404
  256.2 6.7 copy.48
  262.9 9.6 %add_convert_fusion.1 = bf16[896,3072]{1,0:T(8,128)(2,1)} fusion(f32[3072]{0:T(1024)S(1)} %pad_maximum_fusion.1, bf16[896,768]{1,0:T(8,128)(2,1)} %fusion.14.n1, bf16[768,3072]{1,0:T(8,128)(2,1)} %get-tuple-element.29), kind=kOutput, calls=%fused_computation.7 | convolution fusion | flops 4233363456 | bytes 11612160 | tf_op jit(solution)/shard_map/dot_general | solution.py:540
  272.5 14.0 %self_forward.1 = bf16[2,448,1024]{2,1,0:T(8,128)(2,1)} custom-call(bf16[2,448,3072]{2,1,0:T(8,128)(2,1)} %bitcast.113, bf16[2,448,3072]{2,1,0:T(8,128)(2,1)} %bitcast.114, bf16[2,448,3072]{2,1,0:T(8,128)(2,1)} %bitcast.115, s32[2,448,1]{2,1,0:T(8,128)} %copy.44.seg_col, s32[2,1,448]{2,1,0:T(1,128)} %broadcast_in_dim.56.seg_row, ...), custom_call_target="tpu_custom_call" | custom-call | tf_op jit(solution)/shard_map/self_forward/pallas_call | solution.py:266
  286.4 3.7 fusion.40
  291.1 0.9 copy-done.37
  292.0 2.8 add_convert_fusion.2
  294.8 16.0 %frame_projection.1.key.value = bf16[2,1500,2048]{2,1,0:T(8,128)(2,1)} custom-call(bf16[2,1500,768]{2,1,0:T(8,128)(2,1)} %copy.45.frames, bf16[768,2048]{1,0:T(8,128)(2,1)} %get-tuple-element.32.weight.key_weight.value_weight, f32[1,2048]{1,0:T(1,128)} %bitcast.149), custom_call_target="tpu_custom_call" | custom-call | tf_op jit(solution)/shard_map/frame_projection/pallas_call | solution.py:493
  310.8 29.5 %cross_forward.1 = bf16[2,448,1024]{2,1,0:T(8,128)(2,1)} custom-call(bf16[2,448,1024]{2,1,0:T(8,128)(2,1)} %bitcast.132, bf16[2,1500,2048]{2,1,0:T(8,128)(2,1)} %frame_projection.1.key.value, bf16[2,1500,2048]{2,1,0:T(8,128)(2,1)} %frame_projection.1.key.value), custom_call_target="tpu_custom_call" | custom-call | tf_op jit(solution)/shard_map/cross_forward/pallas_call | solution.py:280
  340.3 3.6 fusion.41
  345.0 16.5 %multiply_convert_fusion.1 = (bf16[896,3072]{1,0:T(8,128)(2,1)S(1)}, f32[896,3072]{1,0:T(8,128)}) fusion(f32[3072]{0:T(1024)S(1)} %get-tuple-element.110, bf16[896,768]{1,0:T(8,128)(2,1)S(1)} %add_convert_fusion.3.n3, bf16[768,3072]{1,0:T(8,128)(2,1)} %get-tuple-element.34), kind=kOutput, calls=%fused_computation.6 | convolution fusion | flops 4293918720 | bytes 22622208 | tf_op jit(solution)/shard_map/dot_general | solution.py:540
  361.5 4.6 fusion.42
  366.7 1.7 fusion.7
  368.3 1.7 convert_reduce_fusion.6
  370.0 17.5 %convert_reduce_fusion = (f32[3072]{0:T(1024)}, bf16[896,3072]{1,0:T(8,128)(2,1)S(1)}) fusion(f32[896,3072]{1,0:T(8,128)} %get-tuple-element.123, f32[3072]{0:T(1024)S(1)} %get-tuple-element.110, bf16[896,768]{1,0:T(8,128)(2,1)S(1)} %get-tuple-element.90.b3, bf16[3072,768]{1,0:T(8,128)(2,1)} %get-tuple-element.35), kind=kOutput, calls=%fused_computation.3 | convolution fusion | flops 4313183232 | bytes 22634496 | tf_op jit(solution)/shard_map/dot_general | solution.py:544
  387.6 5.6 multiply_reduce_fusion
  393.2 4.4 convert_reduce_fusion.7
  397.6 2.9 convolution_convert_fusion.1
  400.5 65.9 %cross_backward.1 = (bf16[2,448,1024]{2,1,0:T(8,128)(2,1)}, bf16[2,1500,256]{2,1,0:T(8,128)(2,1)}, bf16[2,1500,256]{2,1,0:T(8,128)(2,1)}) custom-call(s32[1]{0:T(128)} %bitcast.13.rank, bf16[2,448,1024]{2,1,0:T(8,128)(2,1)} %bitcast.133, bf16[2,1500,2048]{2,1,0:T(8,128)(2,1)} %frame_projection.1.key.value, bf16[2,1500,2048]{2,1,0:T(8,128)(2,1)} %frame_projection.1.key.value, ...), custom_call_target="tpu_custom_call" | custom-call | tf_op jit(solution)/shard_map/cross_backward/pallas_call | solution.py:300
  466.4 4.9 multiply_reduce_fusion.1
  471.3 3.2 convert_reduce_fusion.8
  474.6 2.8 convolution_convert_fusion
  477.4 8.3 %self_backward.1 = bf16[2,448,768]{2,1,0:T(8,128)(2,1)} custom-call(s32[1]{0:T(128)} %bitcast.13.rank, bf16[2,448,3072]{2,1,0:T(8,128)(2,1)} %bitcast.116, bf16[2,448,3072]{2,1,0:T(8,128)(2,1)} %bitcast.117, bf16[2,448,3072]{2,1,0:T(8,128)(2,1)} %bitcast.118, bf16[2,448,1024]{2,1,0:T(8,128)(2,1)} %bitcast.143, s32[2,448,1]{2,1,0:T(8,128)} %copy.44.seg_col, ...), custom_call_target="tpu_custom_call" | custom-call | tf_op jit(solution)/shard_map/self_backward/pallas_call | solution.py:325
  485.7 1.3 constant_dynamic-slice_fusion
  487.0 4.4 fusion.34
  491.5 0.7 select_reduce_fusion.1.place
  492.2 18.7 %weight_grads.1 = bf16[64,192,192]{2,1,0:T(8,128)(2,1)} custom-call(s32[1]{0:T(128)} %bitcast.13.rank, s32[64]{0:T(128)} %select_reduce_fusion.1.place, bf16[896,768]{1,0:T(8,128)(2,1)} %fusion.14.n1, bf16[896,768]{1,0:T(8,128)(2,1)} %bitcast.125, bf16[896,768]{1,0:T(8,128)(2,1)} %copy-done.8, bf16[896,1024]{1,0:T(8,128)(2,1)} %bitcast.135, ...), custom_call_target="tpu_custom_call" | custom-call | tf_op jit(solution)/shard_map/weight_grads/pallas_call | solution.py:468
  511.0 6.1 frames_back.1
  517.1 10.0 %soap_pre.1 = (f32[8,192,192]{2,1,0:T(8,128)}, f32[8,2,192,192]{3,2,1,0:T(8,128)}) custom-call(f32[8,192,192]{2,1,0:T(8,128)} %bitcast.137, f32[8,2,192,192]{3,2,1,0:T(8,128)} %bitcast.120, f32[8,2,192,192]{3,2,1,0:T(8,128)} %bitcast.122), custom_call_target="tpu_custom_call" | custom-call | tf_op jit(solution)/shard_map/soap_pre/pallas_call | solution.py:123
  527.9 0.6 add_rsqrt_fusion.4
  528.6 1.3 stack.59
  530.9 0.7 stack.60
  531.6 0.7 stack.54
  532.3 0.7 stack.55
  532.9 0.7 stack.61
  533.6 0.7 stack.56
  534.3 0.7 stack.57
  535.0 0.7 stack.62
  535.7 0.7 stack.58
  536.4 0.7 broadcast_in_dim.114
  537.1 0.7 broadcast_in_dim.115
  538.2 0.7 broadcast_multiply_fusion.1
  539.3 39.3 %psum.7 = f32[14592]{0:T(1024)S(1)} all-reduce(f32[14592]{0:T(1024)S(1)} %reshape.355), channel_id=1, replica_groups=mesh['dp'=8,'tensor'=4] {'dp','tensor'}, use_global_device_ids=true, to_apply=%region_38.39 | all-reduce | flops 14592 | bytes 116736 | tf_op jit(solution)/shard_map/psum | solution.py:695
  578.6 2.0 constant_dynamic-slice_fusion.1
  580.7 0.7 divide_subtract_fusion
  581.4 1.3 fusion.26
  582.7 2.3 fusion.24
  585.0 1.9 reduce-scatter.8.cloned.1.call-done.grad
  586.9 17.9 %soap_main.1 = (f32[8,192,192]{2,1,0:T(8,128)}, f32[8,192,192]{2,1,0:T(8,128)}, f32[8,192,192]{2,1,0:T(8,128)}, f32[8,2,192,192]{3,2,1,0:T(8,128)}, f32[8,2,192,...) custom-call(bf16[8,192,192]{2,1,0:T(8,128)(2,1)} %reduce-scatter.8.cloned.1.call-done.grad, f32[8,192,192]{2,1,0:T(8,128)} %bitcast.136, ...), custom_call_target="tpu_custom_call" | custom-call | tf_op jit(solution)/shard_map/soap_main/pallas_call | solution.py:132
  604.7 1.9 copy-done
  606.6 84.5 %chol_bases.1 = f32[16,192,192]{2,1,0:T(8,128)} custom-call(f32[16,192,192]{2,1,0:T(8,128)S(1)} %bitcast.112, f32[16,192,192]{2,1,0:T(8,128)} %bitcast.142), custom_call_target="tpu_custom_call" | custom-call | tf_op jit(solution)/shard_map/chol_bases/pallas_call | solution.py:139
  691.2 1.4 slice_convert_fusion
  692.6 2.6 copy.50
  (164 shorter events, 9.8 us)
Async XLA Ops:
  7.2 3.4 copy-start.39
  7.2 2.3 copy-start.7
  7.2 3.3 copy-start.17
  7.2 31.3 %copy-start.22 = (s32[2,448]{1,0:T(2,128)S(1)}, s32[2,448]{1,0:T(2,128)}, u32[]{:S(2)}) copy-start(s32[2,448]{1,0:T(2,128)} %param.19) | copy-start | bytes 10756
  7.2 62.7 %all-gather.3.cloned.1.call-start = ((), (), s32[]{:S(2)}) async-start(), calls=%async_computation.3 | async-start | bytes 3440640 | tf_op jit(solution)/shard_map/all_gather | solution.py:599
  7.3 32.9 %copy-start.23 = (s32[2,448]{1,0:T(2,128)S(1)}, s32[2,448]{1,0:T(2,128)}, u32[]{:S(2)}) copy-start(s32[2,448]{1,0:T(2,128)} %param.20) | copy-start | bytes 10756
  9.4 217.4 %all-gather.5.cloned.1.call-start = ((), (), s32[]{:S(2)}) async-start(), calls=%async_computation.4 | async-start | bytes 25952256 | tf_op jit(solution)/shard_map/all_gather | solution.py:602
  10.4 570.9 %reduce-scatter.4.cloned.1.call-start = ((), (), s32[]{:S(2)}) async-start(), calls=%async_computation.5 | async-start | bytes 1720320 | tf_op jit(solution)/shard_map/reduce_scatter | solution.py:669
  40.7 6.7 copy-start.33
  40.7 6.7 copy-start.34
  40.7 6.8 copy-start.32
  48.7 26.7 %copy-start.15 = (f32[768]{0:T(1024)}, f32[768]{0:T(1024)S(1)}, u32[]{:S(2)}) copy-start(f32[768]{0:T(1024)S(1)} %get-tuple-element.108) | copy-start | bytes 9220
  71.6 3.8 copy-start.24
  71.6 3.8 copy-start.1
  75.3 1.8 copy-start.26
  272.5 14.0 %slice-start = ((bf16[2,2,448,768]{3,2,1,0:T(8,128)(2,1)}), bf16[1,2,448,768]{3,2,1,0:T(8,128)(2,1)S(1)}, s32[]{:S(2)}) async-start(bf16[2,2,448,768]{3,2,1,0:T(8,128)(2,1)} %all-gather.3.cloned.1.call-done), calls=%async_computation.8 | async-start | bytes 2752512 | tf_op jit(solution)/shard_map/slice | solution.py:600
  290.5 1.4 copy-start.37
  291.1 3.7 copy-start.8
  344.5 17.0 %slice-start.3 = ((s8[4718592]{0:T(1024)(128)(4,1)}), s8[4194304]{0:T(1024)(128)(4,1)S(1)}, s32[]{:S(2)}) async-start(s8[4718592]{0:T(1024)(128)(4,1)} %bitcast.161), calls=%async_computation.11 | async-start | bytes 8388608
  345.0 16.5 %copy-start.9 = (bf16[896,768]{1,0:T(8,128)(2,1)}, bf16[896,768]{1,0:T(8,128)(2,1)S(1)}, u32[]{:S(2)}) copy-start(bf16[896,768]{1,0:T(8,128)(2,1)S(1)} %add_convert_fusion.3.n3) | copy-start | bytes 4128772
  345.0 16.5 %slice-start.4 = ((s8[4718592]{0:T(1024)(128)(4,1)}), s8[524288]{0:T(1024)(128)(4,1)S(1)}, s32[]{:S(2)}) async-start(s8[4718592]{0:T(1024)(128)(4,1)} %bitcast.161), calls=%async_computation.12 | async-start | bytes 1048576
  361.5 4.7 copy-start.11
  368.3 19.2 %slice-start.1 = ((s8[4718592]{0:T(1024)(128)(4,1)}), s8[4194304]{0:T(1024)(128)(4,1)S(1)}, s32[]{:S(2)}) async-start(s8[4718592]{0:T(1024)(128)(4,1)} %bitcast.159), calls=%async_computation.9 | async-start | bytes 8388608
  370.0 17.6 %copy-start.10 = (bf16[896,768]{1,0:T(8,128)(2,1)}, bf16[896,768]{1,0:T(8,128)(2,1)S(1)}, u32[]{:S(2)}) copy-start(bf16[896,768]{1,0:T(8,128)(2,1)S(1)} %get-tuple-element.90.b3) | copy-start | bytes 4128772
  370.0 17.6 %slice-start.2 = ((s8[4718592]{0:T(1024)(128)(4,1)}), s8[524288]{0:T(1024)(128)(4,1)S(1)}, s32[]{:S(2)}) async-start(s8[4718592]{0:T(1024)(128)(4,1)} %bitcast.159), calls=%async_computation.10 | async-start | bytes 1048576
  387.5 5.6 copy-start.12
  387.6 5.6 copy-start.21
  393.2 4.5 copy-start.38
  397.6 2.9 copy-start.13
  466.4 4.9 copy-start.4
  471.3 3.2 copy-start.36
  474.6 2.8 copy-start.14
  477.4 9.6 %copy-start.25 = (f32[896]{0:T(1024)S(1)}, f32[896]{0:T(1024)}, u32[]{:S(2)}) copy-start(f32[896]{0:T(1024)} %copy-done.24) | copy-start | bytes 10756
  477.4 9.6 %copy-start.27 = (f32[896]{0:T(1024)S(1)}, f32[896]{0:T(1024)}, u32[]{:S(2)}) copy-start(f32[896]{0:T(1024)} %copy-done.26) | copy-start | bytes 10756
  487.0 4.5 copy-start.35
  491.5 95.4 %reduce-scatter.8.cloned.1.call-start = ((), (), s32[]{:S(2)}) async-start(), calls=%async_computation.7 | async-start | bytes 7077888 | tf_op jit(solution)/shard_map/reduce_scatter | solution.py:678
  510.9 180.3 %reduce-scatter.6.cloned.1.call-start = ((), (), s32[]{:S(2)}) async-start(), calls=%async_computation.6 | async-start | bytes 5898240 | tf_op jit(solution)/shard_map/reduce_scatter | solution.py:655
  517.0 10.0 %copy-start.5 = (bf16[2,112,768]{2,1,0:T(8,128)(2,1)S(1)}, bf16[2,112,768]{2,1,0:T(8,128)(2,1)}, u32[]{:S(2)}) copy-start(bf16[2,112,768]{2,1,0:T(8,128)(2,1)} %param.16) | copy-start | bytes 1032196
  517.1 12.8 %copy-start.3 = (bf16[2,448,768]{2,1,0:T(8,128)(2,1)S(1)}, bf16[2,448,768]{2,1,0:T(8,128)(2,1)}, u32[]{:S(2)}) copy-start(bf16[2,448,768]{2,1,0:T(8,128)(2,1)} %self_backward.1) | copy-start | bytes 4128772
  527.1 3.0 copy-start.2
  527.1 10.7 %copy-start.6 = (bf16[2,448,1024]{2,1,0:T(8,128)(2,1)S(1)}, bf16[2,448,1024]{2,1,0:T(8,128)(2,1)}, u32[]{:S(2)}) copy-start(bf16[2,448,1024]{2,1,0:T(8,128)(2,1)} %get-tuple-element.36) | copy-start | bytes 5505028
  527.2 0.5 copy-start.19
  530.1 8.8 %copy-start.28 = (f32[1,768]{1,0:T(1,128)S(1)}, f32[1,768]{1,0:T(1,128)}, u32[]{:S(2)}) copy-start(f32[1,768]{1,0:T(1,128)} %stack.59) | copy-start | bytes 9220
  530.1 50.5 %copy-start.18 = (f32[1824]{0:T(1024)S(1)}, f32[1824]{0:T(1024)}, u32[]{:S(2)}) copy-start(f32[1824]{0:T(1024)} %param.27) | copy-start | bytes 21892
  530.1 50.5 %copy-start.30 = (f32[1824]{0:T(1024)S(1)}, f32[1824]{0:T(1024)}, u32[]{:S(2)}) copy-start(f32[1824]{0:T(1024)} %param.28) | copy-start | bytes 21892
  530.1 50.5 %copy-start.31 = (f32[1824]{0:T(1024)S(1)}, f32[1824]{0:T(1024)}, u32[]{:S(2)}) copy-start(f32[1824]{0:T(1024)} %param.29) | copy-start | bytes 21892
  530.1 51.2 %copy-start.16 = (f32[768]{0:T(1024)S(1)}, f32[768]{0:T(1024)}, u32[]{:S(2)}) copy-start(f32[768]{0:T(1024)} %copy-done.15) | copy-start | bytes 9220
  530.1 51.2 %copy-start.20 = (f32[2,112]{1,0:T(2,128)S(1)}, f32[2,112]{1,0:T(2,128)}, u32[]{:S(2)}) copy-start(f32[2,112]{1,0:T(2,128)} %copy-done.19) | copy-start | bytes 2692
  530.2 51.2 %copy-start.29 = (f32[2,112]{1,0:T(2,128)S(1)}, f32[2,112]{1,0:T(2,128)}, u32[]{:S(2)}) copy-start(f32[2,112]{1,0:T(2,128)} %add_rsqrt_fusion.4) | copy-start | bytes 2692
  604.7 1.9 copy-start
Sparse Core Ops, SparseCore 0:
  10.2 59.6 all-gather.2
  73.3 153.4 all-gather.4
  491.6 30.4 reduce-scatter.3
  525.6 61.1 reduce-scatter.7
  589.0 85.0 reduce-scatter.5

commit v3 on v2

--- a/solution.py
+++ b/solution.py
@@ -70,20 +70,20 @@
         halves = split2(side_turned)
         grams[0, side] = dot3(halves, halves, TN)
 
-def chol_kernel(turned, grams, out, work, inv, fac, *, block):
+def chol_kernel(turned, grams, out, work, fac, *, block, unroll, passes):
     count, side = work.shape[0], work.shape[1]
-    row = lax.broadcasted_iota(jnp.int32, (side, side), 0)
-    col = lax.broadcasted_iota(jnp.int32, (side, side), 1)
-    eye = (row == col).astype(jnp.float32)
+    wide = work.shape[2] // 2
     for m in range(count):
-        work[m] = grams[m]
-        inv[m] = eye
+        work[m, :, :side] = grams[m]
+        work[m, :, side:wide] = jnp.zeros((side, wide - side), jnp.float32)
+        work[m, :, wide : wide + side] = turned[m].T
+        work[m, :, wide + side :] = jnp.zeros((side, wide - side), jnp.float32)
     brow = lax.broadcasted_iota(jnp.int32, (count, block, 2 * block), 1)
     bcol = lax.broadcasted_iota(jnp.int32, (count, block, 2 * block), 2)
     aug_eye = ((bcol - block) == brow).astype(jnp.float32)
     for k in range(side // block):
-        lo = k * block
-        diag = work[:, lo : lo + block, lo : lo + block]
+        lo, hi = k * block, (k + 1) * block
+        diag = work[:, lo:hi, lo:hi]
         w = jnp.concatenate([diag, jnp.zeros_like(diag)], axis=2) + aug_eye
         for j in range(block - 1):
             piv = w[:, j : j + 1, :]
@@ -92,25 +92,25 @@
         d = jnp.sum(jnp.where(brow == bcol, w, 0.0), axis=2, keepdims=True)
         fac[...] = w[:, :, block:] * lax.rsqrt(d)
 
-        def one(m, _):
-            x = fac[m]
-            y = dothi(x, work[m, lo : lo + block, :], NN)
-            z = dothi(x, inv[m, lo : lo + block, :], NN)
-            inv[m, lo : lo + block, :] = z
-            if lo + block < side:
-                rest = side - lo - block
-                ys = split2(y)
-                upd = dothi(y, y, TN)
-                updx = dothi(y, z, TN)
-                work[m, lo + block :, :] = work[m, lo + block :, :] - upd[lo + block :, :]
-                inv[m, lo + block :, :] = inv[m, lo + block :, :] - updx[lo + block :, :]
+        def several(i, _):
+            for u in range(unroll):
+                m = i * unroll + u
+                if passes == 6:
+                    y = dothi(fac[m], work[m, lo:hi, :], NN)
+                else:
+                    y = dot3(split2(fac[m]), split2(work[m, lo:hi, :]), NN)
+                work[m, lo:hi, :] = y
+                if hi < side:
+                    turn = y[:, :side].T[hi:]
+                    if passes == 6:
+                        step = dothi(turn, y, NN)
+                    else:
+                        step = dot3(split2(turn), split2(y), NN)
+                    work[m, hi:, :] = work[m, hi:, :] - step
             return 0
-        lax.fori_loop(0, count, one, 0)
-
-    def last(m, _):
-        out[m] = dothi(turned[m], inv[m], NT)
-        return 0
-    lax.fori_loop(0, count, last, 0)
+        lax.fori_loop(0, count // unroll, several, 0)
+    for m in range(count):
+        out[m] = work[m, :, wide : wide + side].T
 
 def tile_spec(side):
     return pl.BlockSpec((1, side, side), lambda i: (i, 0, 0))
@@ -133,20 +133,22 @@
         out_specs=[t, t, t, p, p, p], out_shape=[ts, ts, ts, ps, ps, ps], name="soap_main")(
         grad, master, first, second, stats, bases, rot_first, stats_rot)
 
-def chol_bases(turned, grams, block=32):
+def chol_bases(turned, grams, block=64, unroll=4, passes=3):
     n, _, side, _ = turned.shape
     shape = (2 * n, side, side)
-    out = pl.pallas_call(functools.partial(chol_kernel, block=block),
+    unroll = min(unroll, 2 * n)
+    out = pl.pallas_call(functools.partial(chol_kernel, block=block, unroll=unroll, passes=passes),
         out_shape=jax.ShapeDtypeStruct(shape, jnp.float32),
-        scratch_shapes=[pltpu.VMEM(shape, jnp.float32), pltpu.VMEM(shape, jnp.float32), pltpu.VMEM((2*n, block, block), jnp.float32)],
+        scratch_shapes=[pltpu.VMEM((2 * n, side, 512), jnp.float32), pltpu.VMEM((2*n, block, block), jnp.float32)],
         compiler_params=pltpu.CompilerParams(vmem_limit_bytes=48 * 2**20), name="chol_bases")(
         turned.reshape(shape), grams.reshape(shape))
     return out.reshape(turned.shape)
 
-def soap(gradient, master, first, second, statistics, bases, block=32):
+
+def soap(gradient, master, first, second, statistics, bases):
     rot_first, stats_rot = soap_pre(first, statistics, bases)
     nm, nf, ns, nst, turned, grams = soap_main(gradient, master, first, second, statistics, bases, rot_first, stats_rot)
-    return nf, ns, nm, nst, chol_bases(turned, grams, block)
+    return nf, ns, nm, nst, chol_bases(turned, grams)
 
 
 def head_pick(shape, head):
@@ -154,70 +156,101 @@
     return (lane >= HEAD) if head % 2 else (lane < HEAD)
 
 
-def forward_heads(query, key, value, allowed, heads):
-    blocks = []
-    for first in range(0, heads, 2):
-        span = slice(first * HEAD, first * HEAD + LANES)
-        query_block, key_block, value_block = query[:, span], key[:, span], value[:, span]
-        made = None
-        for head in range(first, min(first + 2, heads)):
-            own_query = jnp.where(head_pick(query_block.shape, head), query_block, jnp.zeros_like(query_block))
-            scores = bdot(own_query, key_block, NT) * score_scale
-            if allowed is not None:
-                scores = jnp.where(allowed, scores, -1e30)
-            weights = jnp.exp(scores - jnp.max(scores, axis=1, keepdims=True)).astype(jnp.bfloat16)
-            own_value = jnp.where(head_pick(value_block.shape, head), value_block, jnp.ones_like(value_block))
-            both = bdot(weights, own_value, NN)
-            mixed = both / pltpu.roll(both, HEAD, 1)
-            pick = head_pick(mixed.shape, head)
-            made = jnp.where(pick, mixed, 0.0 if made is None else made)
-        blocks.append(made.astype(jnp.bfloat16))
-    return jnp.concatenate(blocks, axis=1)
-
-
-def cross_forward_kernel(query, key, value, out, *, heads):
-    out[0] = forward_heads(query[0], key[0], value[0], None, heads)
-
-
-def self_forward_kernel(query, key, value, seg_col, seg_row, stamp_row, out, *, heads):
+def forward_heads(query, key, value, allowed, heads, chunk):
+    rows = query.shape[0]
+    units = [(low, head) for low in range(0, rows, chunk) for head in range(heads)]
+    spans = [slice(head // 2 * LANES, head // 2 * LANES + LANES) for head in range(heads)]
+    own_values = []
+    for head in range(heads):
+        block = value[:, spans[head]]
+        own_values.append(jnp.where(head_pick(block.shape, head), block, jnp.ones_like(block)))
+
+    def scores_of(unit):
+        low, head = unit
+        block = query[low : low + chunk, spans[head]]
+        own = jnp.where(head_pick(block.shape, head), block, jnp.zeros_like(block)) * jnp.bfloat16(score_scale)
+        return bdot(own, key[:, spans[head]], NT)
+
+    done, logs = {}, {}
+    ahead = scores_of(units[0])
+    for i, (low, head) in enumerate(units):
+        scores = ahead
+        if i + 1 < len(units):
+            ahead = scores_of(units[i + 1])
+        if allowed is not None:
+            scores = jnp.where(allowed[low : low + chunk], scores, -1e30)
+        top = jnp.max(scores, axis=1, keepdims=True)
+        weights = jnp.exp(scores - top).astype(jnp.bfloat16)
+        both = bdot(weights, own_values[head], NN)
+        turned = pltpu.roll(both, HEAD, 1)
+        pick = head_pick(both.shape, head)
+        done[low, head] = both / turned
+        logs[low, head] = top + jnp.log(jnp.where(pick, turned, both))
+    columns, lines = [], []
+    for low in range(0, rows, chunk):
+        blocks = []
+        lane = lax.broadcasted_iota(jnp.int32, (chunk, LANES), 1)
+        line = jnp.zeros((chunk, LANES), jnp.float32)
+        for first in range(0, heads, 2):
+            other = done[low, first + 1] if first + 1 < heads else 0.0
+            blocks.append(jnp.where(lane < HEAD, done[low, first], other).astype(jnp.bfloat16))
+        for head in range(heads):
+            line = jnp.where(lane == head, logs[low, head], line)
+        columns.append(jnp.concatenate(blocks, axis=1))
+        lines.append(line)
+    return jnp.concatenate(columns, axis=0), jnp.concatenate(lines, axis=0).T[:8]
+
+
+def cross_forward_kernel(query, key, value, out, logs, *, heads, chunk):
+    out[0], logs[0, 0] = forward_heads(query[0], key[0], value[0], None, heads, chunk)
+
+
+def self_forward_kernel(query, key, value, seg_col, seg_row, stamp_row, out, logs, *, heads, chunk):
     rows = query.shape[1]
     at = lax.broadcasted_iota(jnp.int32, (rows, rows), 0)
     key_at = lax.broadcasted_iota(jnp.int32, (rows, rows), 1)
     allowed = (key_at <= at) & (seg_col[0] == seg_row[0]) & ((stamp_row[0] == 0) | (key_at == at))
-    out[0] = forward_heads(query[0], key[0], value[0], allowed, heads)
-
-
-def backward_head(query_block, key_block, key_turned, value_block, grad_block, mixed_block, allowed, head):
-    pick = head_pick(query_block.shape, head)
-    own_query = jnp.where(pick, query_block, jnp.zeros_like(query_block))
-    own_grad = jnp.where(pick, grad_block, jnp.zeros_like(grad_block))
-    scores = bdot(key_block, own_query, NT) * score_scale
-    if allowed is not None:
-        scores = jnp.where(allowed, scores, -1e30)
-    weights = jnp.exp(scores - jnp.max(scores, axis=0, keepdims=True))
-    probs = weights * (1.0 / jnp.sum(weights, axis=0, keepdims=True))
-    grad_probs = bdot(value_block, own_grad, NT)
-    row_dot = jnp.sum(probs * grad_probs, axis=0, keepdims=True)
-    grad_scores = (probs * (grad_probs - row_dot)).astype(jnp.bfloat16)
-    return probs.astype(jnp.bfloat16), grad_scores, bdot(key_turned, grad_scores, NN)
-
-
-def backward_heads(query, key, value, grad, allowed, heads, probs_ref, scores_ref):
-    blocks = []
-    for first in range(0, heads, 2):
-        span = slice(first * HEAD, first * HEAD + LANES)
-        query_block, key_block, value_block, grad_block = query[:, span], key[:, span], value[:, span], grad[:, span]
-        key_turned = key_block.T
-        made = None
-        for head in range(first, min(first + 2, heads)):
-            probs, grad_scores, turned = backward_head(query_block, key_block, key_turned, value_block, grad_block, None, allowed, head)
-            probs_ref[head] = probs
-            scores_ref[head] = grad_scores
-            row = lax.broadcasted_iota(jnp.int32, turned.shape, 0)
-            pick = (row >= HEAD) if head % 2 else (row < HEAD)
-            made = jnp.where(pick, turned, 0.0 if made is None else made)
-        blocks.append((made.T * score_scale).astype(jnp.bfloat16))
-    return jnp.concatenate(blocks, axis=1)
+    out[0], logs[0, 0] = forward_heads(query[0], key[0], value[0], allowed, heads, chunk)
+
+
+def backward_heads(query, key, value, grad, mixed, logs, allowed, heads, chunk, probs_ref, scores_ref):
+    keys = key.shape[0]
+    spans = [slice(head // 2 * LANES, head // 2 * LANES + LANES) for head in range(heads)]
+    products = (grad.astype(jnp.float32) * mixed.astype(jnp.float32)).T
+    own_query, own_grad, turned, dots, total = [], [], [], [], [None] * heads
+    for head in range(heads):
+        pick = head_pick((query.shape[0], LANES), head)
+        zero = jnp.zeros((query.shape[0], LANES), jnp.bfloat16)
+        own_query.append(jnp.where(pick, query[:, spans[head]], zero) * jnp.bfloat16(score_scale))
+        own_grad.append(jnp.where(pick, grad[:, spans[head]], zero))
+        dots.append(jnp.sum(products[head * HEAD : (head + 1) * HEAD], axis=0, keepdims=True))
+        if head % 2 == 0:
+            turned.append(key[:, spans[head]].T)
+    units = [(low, head) for low in range(0, keys, chunk) for head in range(heads)]
+
+    def products_of(unit):
+        low, head = unit
+        high = min(low + chunk, keys)
+        return bdot(key[low:high, spans[head]], own_query[head], NT), bdot(value[low:high, spans[head]], own_grad[head], NT)
+
+    ahead = products_of(units[0])
+    for i, (low, head) in enumerate(units):
+        high = min(low + chunk, keys)
+        scores, grad_probs = ahead
+        if i + 1 < len(units):
+            ahead = products_of(units[i + 1])
+        if allowed is not None:
+            scores = jnp.where(allowed[low:high], scores, -1e30)
+        probs = jnp.exp(scores - logs[head : head + 1])
+        grad_scores = (probs * (grad_probs - dots[head])).astype(jnp.bfloat16)
+        probs_ref[head, low:high] = probs.astype(jnp.bfloat16)
+        scores_ref[head, low:high] = grad_scores
+        half = head % 2 * HEAD
+        term = bdot(turned[head // 2][half : half + HEAD, low:high], grad_scores, NN)
+        total[head] = term if total[head] is None else total[head] + term
+    if heads % 2:
+        total.append(jnp.zeros_like(total[0]))
+    return (jnp.concatenate(total, axis=0).T * score_scale).astype(jnp.bfloat16)
 
 
 def key_value_grads(query, grad, heads, probs_ref, scores_ref):
@@ -236,8 +269,12 @@
     return jnp.concatenate(keys, axis=1), jnp.concatenate(values, axis=1)
 
 
-def cross_backward_kernel(rank, query, key, value, grad, grad_query, grad_key, grad_value, probs_ref, scores_ref, *, heads):
-    grad_query[0] = backward_heads(query[0], key[0], value[0], grad[0], None, heads, probs_ref, scores_ref)
+def cross_backward_kernel(
+    rank, query, key, value, grad, mixed, logs, grad_query, grad_key, grad_value, probs_ref, scores_ref, *, heads, chunk
+):
+    grad_query[0] = backward_heads(
+        query[0], key[0], value[0], grad[0], mixed[0], logs[0, 0], None, heads, chunk, probs_ref, scores_ref
+    )
 
     @pl.when(pl.program_id(1) == rank[0])
     def _():
@@ -245,12 +282,16 @@
         grad_key[0], grad_value[0] = made
 
 
-def self_backward_kernel(rank, query, key, value, grad, seg_col, seg_row, stamp_col, out, probs_ref, scores_ref, *, heads):
+def self_backward_kernel(
+    rank, query, key, value, grad, mixed, logs, seg_col, seg_row, stamp_col, out, probs_ref, scores_ref, *, heads, chunk
+):
     rows = query.shape[1]
     key_at = lax.broadcasted_iota(jnp.int32, (rows, rows), 0)
     at = lax.broadcasted_iota(jnp.int32, (rows, rows), 1)
     allowed = (key_at <= at) & (seg_col[0] == seg_row[0]) & ((stamp_col[0] == 0) | (key_at == at))
-    grad_query = backward_heads(query[0], key[0], value[0], grad[0], allowed, heads, probs_ref, scores_ref)
+    grad_query = backward_heads(
+        query[0], key[0], value[0], grad[0], mixed[0], logs[0, 0], allowed, heads, chunk, probs_ref, scores_ref
+    )
     grad_key, grad_value = key_value_grads(query[0], grad[0], heads, probs_ref, scores_ref)
     out[0] = jnp.concatenate([grad_query, grad_key, grad_value], axis=1)
 
@@ -259,30 +300,36 @@
     return pl.BlockSpec((1, rows, SLOT), lambda b, r: (b, 0, offset + r))
 
 
-def self_forward(qkv, seg_col, seg_row, stamp_row, ranks, heads):
+def self_forward(qkv, seg_col, seg_row, stamp_row, ranks, heads, chunk=448):
     seqs, rows, _ = qkv.shape
     col = pl.BlockSpec((1, rows, 1), lambda b, r: (b, 0, 0))
     row = pl.BlockSpec((1, 1, rows), lambda b, r: (b, 0, 0))
     return pl.pallas_call(
-        functools.partial(self_forward_kernel, heads=heads),
+        functools.partial(self_forward_kernel, heads=heads, chunk=chunk),
         grid=(seqs, ranks),
         in_specs=[slot_spec(rows, 0), slot_spec(rows, ranks), slot_spec(rows, 2 * ranks), col, row, row],
-        out_specs=slot_spec(rows, 0),
-        out_shape=jax.ShapeDtypeStruct((seqs, rows, ranks * SLOT), jnp.bfloat16),
+        out_specs=[slot_spec(rows, 0), pl.BlockSpec((1, 1, 8, rows), lambda b, r: (b, r, 0, 0))],
+        out_shape=[
+            jax.ShapeDtypeStruct((seqs, rows, ranks * SLOT), jnp.bfloat16),
+            jax.ShapeDtypeStruct((seqs, ranks, 8, rows), jnp.float32),
+        ],
         compiler_params=pltpu.CompilerParams(vmem_limit_bytes=VM),
         name="self_forward",
     )(qkv, qkv, qkv, seg_col, seg_row, stamp_row)
 
 
-def cross_forward(queries, keys_values, ranks, heads):
+def cross_forward(queries, keys_values, ranks, heads, chunk=448):
     seqs, rows, _ = queries.shape
     frames = keys_values.shape[1]
     return pl.pallas_call(
-        functools.partial(cross_forward_kernel, heads=heads),
+        functools.partial(cross_forward_kernel, heads=heads, chunk=chunk),
         grid=(seqs, ranks),
         in_specs=[slot_spec(rows, 0), slot_spec(frames, 0), slot_spec(frames, ranks)],
-        out_specs=slot_spec(rows, 0),
-        out_shape=jax.ShapeDtypeStruct((seqs, rows, ranks * SLOT), jnp.bfloat16),
+        out_specs=[slot_spec(rows, 0), pl.BlockSpec((1, 1, 8, rows), lambda b, r: (b, r, 0, 0))],
+        out_shape=[
+            jax.ShapeDtypeStruct((seqs, rows, ranks * SLOT), jnp.bfloat16),
+            jax.ShapeDtypeStruct((seqs, ranks, 8, rows), jnp.float32),
+        ],
         compiler_params=pltpu.CompilerParams(vmem_limit_bytes=VM),
         name="cross_forward",
     )(queries, keys_values, keys_values)
@@ -292,17 +339,20 @@
     return pl.BlockSpec((1, rows, SLOT), lambda b, r, rank: (b, 0, offset + r))
 
 
-def cross_backward(rank, queries, keys_values, grads, ranks, heads):
+def cross_backward(rank, queries, keys_values, grads, mixed, logs, ranks, heads, chunk=512):
     seqs, rows, _ = queries.shape
     frames = keys_values.shape[1]
     kept = pl.BlockSpec((1, frames, SLOT), lambda b, r, rank: (b, 0, 0))
     bf = jnp.bfloat16
     return pl.pallas_call(
-        functools.partial(cross_backward_kernel, heads=heads),
+        functools.partial(cross_backward_kernel, heads=heads, chunk=chunk),
         grid_spec=pltpu.PrefetchScalarGridSpec(
             num_scalar_prefetch=1,
             grid=(seqs, ranks),
-            in_specs=[ranked_spec(rows, 0), ranked_spec(frames, 0), ranked_spec(frames, ranks), ranked_spec(rows, 0)],
+            in_specs=[
+                ranked_spec(rows, 0), ranked_spec(frames, 0), ranked_spec(frames, ranks), ranked_spec(rows, 0), ranked_spec(rows, 0),
+                pl.BlockSpec((1, 1, 8, rows), lambda b, r, rank: (b, r, 0, 0)),
+            ],
             out_specs=[ranked_spec(rows, 0), kept, kept],
             scratch_shapes=[pltpu.VMEM((heads, frames, rows), bf), pltpu.VMEM((heads, frames, rows), bf)],
         ),
@@ -313,122 +363,176 @@
         ],
         compiler_params=pltpu.CompilerParams(vmem_limit_bytes=VM),
         name="cross_backward",
-    )(rank, queries, keys_values, keys_values, grads)
-
-
-def self_backward(rank, qkv, grads, seg_col, seg_row, stamp_col, ranks, heads):
+    )(rank, queries, keys_values, keys_values, grads, mixed, logs)
+
+
+def self_backward(rank, qkv, grads, mixed, logs, seg_col, seg_row, stamp_col, ranks, heads, chunk=224):
     seqs, rows, _ = qkv.shape
     bf = jnp.bfloat16
     own = lambda offset: pl.BlockSpec((1, rows, SLOT), lambda b, rank: (b, 0, offset + rank[0]))
     col = pl.BlockSpec((1, rows, 1), lambda b, rank: (b, 0, 0))
     row = pl.BlockSpec((1, 1, rows), lambda b, rank: (b, 0, 0))
     return pl.pallas_call(
-        functools.partial(self_backward_kernel, heads=heads),
+        functools.partial(self_backward_kernel, heads=heads, chunk=chunk),
         grid_spec=pltpu.PrefetchScalarGridSpec(
             num_scalar_prefetch=1,
             grid=(seqs,),
-            in_specs=[own(0), own(ranks), own(2 * ranks), own(0), col, row, col],
+            in_specs=[
+                own(0), own(ranks), own(2 * ranks), own(0), own(0),
+                pl.BlockSpec((1, 1, 8, rows), lambda b, rank: (b, rank[0], 0, 0)), col, row, col,
+            ],
             out_specs=pl.BlockSpec((1, rows, 3 * SLOT), lambda b, rank: (b, 0, 0)),
             scratch_shapes=[pltpu.VMEM((heads, rows, rows), bf), pltpu.VMEM((heads, rows, rows), bf)],
         ),
         out_shape=jax.ShapeDtypeStruct((seqs, rows, 3 * SLOT), bf),
         compiler_params=pltpu.CompilerParams(vmem_limit_bytes=VM),
         name="self_backward",
-    )(rank, qkv, qkv, qkv, grads, seg_col, seg_row, stamp_col)
-
-
-def tile_sources():
-    steps = []
-    for base in (0, 4, 8, 16, 20, 12):
-        for pair in range(2):
-            steps.append([(pair * 2 + i // 4, base + i % 4) for i in range(8)])
-    for base in (24, 28):
-        for pair in range(2):
-            steps.append([(pair * 2 + i // 4, base + i % 4) for i in range(8)])
-    for half in range(2):
+    )(rank, qkv, qkv, qkv, grads, mixed, logs, seg_col, seg_row, stamp_col)
+
+
+def pack_kernel(tiles, line, out):
+    side = tiles.shape[1]
+    half, extra = side // 2, side - LANES
+    for i in range(tiles.shape[0]):
+        tile = tiles[i].astype(jnp.bfloat16)
+        low = i * (side + half)
+        out[low : low + side] = tile[:, :LANES]
+        out[low + side : low + side + half] = jnp.concatenate([tile[:half, LANES:], tile[half:, LANES:]], axis=1)
+    out[out.shape[0] - line.shape[0] :] = line[...].astype(jnp.bfloat16)
+
+
+def pack(tiles, line):
+    count, side, _ = tiles.shape
+    rows = count * (side + side // 2) + line.shape[0]
+    return pl.pallas_call(
+        pack_kernel, out_shape=jax.ShapeDtypeStruct((rows, LANES), jnp.bfloat16), name="pack"
+    )(tiles, line)
+
+
+def gather_plane(held, flips, axis):
+    cut = held.shape[1] // 32 * 16
+    across = lax.ppermute(held, axis, flips(2))
+    along = lax.ppermute(held, axis, flips(4))
+    corner_low = lax.ppermute(across[:, :cut], axis, flips(4))
+    corner_high = lax.ppermute(along[:, cut:], axis, flips(2))
+    even = jnp.concatenate([held, across, along, jnp.concatenate([corner_low, corner_high], axis=1)], axis=0)
+    return even, lax.ppermute(even, axis, flips(1))
+
+
+def gather_blocks(block, ranks, groups):
+    if ranks == 4 and groups == 8:
+        flips = lambda bits: [(i, i ^ bits) for i in range(groups)]
+        turn = lambda step: [(i, (i + step) % ranks) for i in range(ranks)]
+        one, three, two = [lax.ppermute(block, "tensor", turn(step)) for step in (1, 3, 2)]
+        arrays, where = [], []
+        for step, held in ((0, block), (1, one), (3, three), (2, two)):
+            for parity, array in enumerate(gather_plane(held[None], flips, "dp")):
+                arrays.append(array)
+                where.append([(step, 2 * k + parity) for k in range(4)])
+        return arrays, where, two
+    return [lax.all_gather(block, ("dp", "tensor"), axis=0)], None, None
+
+
+def assemble_kernel(target, *refs, sources, own_tiles, tile_rows):
+    ins, outs = refs[:sources], refs[sources : sources + 7]
+    staging, (f_qkv, f_ckv, f_cq, f_wo, f_co, f_in, f_out), arrived, sent = refs[sources + 7], refs[sources + 8 : -2], refs[-2], refs[-1]
+    side = tile_rows * 2 // 3
+    half = side // 2
+    at = 0
+    for source in ins:
+        blocks = source.shape[0]
+
+        def fetch(k, _, source=source, at=at):
+            for slot in range(own_tiles):
+                pltpu.make_async_copy(
+                    source.at[k, pl.ds(slot * tile_rows, tile_rows)],
+                    staging.at[target[at + k * own_tiles + slot]],
+                    arrived,
+                ).start()
+            return 0
+
+        lax.fori_loop(0, blocks, fetch, 0)
+        at += blocks * own_tiles
+    pltpu.make_async_copy(staging, staging, arrived).wait()
+
+    def parts(rank, ident):
+        packed = staging.at[rank * 64 + ident]
+        low = packed[side:]
+        return packed[:side], jnp.concatenate([low[:, : side - LANES], low[:, side - LANES :]], axis=0)
+
+    def columns(out, base, offset):
         for rank in range(4):
-            steps.append([(rank, 32 + (half * 2 + i // 4) * 4 + i % 4) for i in range(8)])
+            for i in range(4):
+                main, rest = parts(rank, base + i)
+                rest = jnp.concatenate([rest, jnp.zeros((side, SLOT - side), jnp.bfloat16)], axis=1)
+                out[i * side : (i + 1) * side, offset + rank * SLOT : offset + (rank + 1) * SLOT] = jnp.concatenate([main, rest], axis=1)
+
+    def joined(rank, base):
+        pieces = []
+        for i in range(4):
+            pieces.extend(parts(rank, base + i))
+        return jnp.concatenate(pieces, axis=1)
+
+    def padded_rows(out, base):
+        for rank in range(4):
+            out[rank * SLOT : rank * SLOT + side, :] = joined(rank, base)
+            out[rank * SLOT + side : (rank + 1) * SLOT, :] = jnp.zeros((SLOT - side, 4 * side), jnp.bfloat16)
+
+    copies = []
+
+    def send(i, held):
+        copy = pltpu.make_async_copy(held, outs[i], sent.at[i])
+        copy.start()
+        copies.append(copy)
+
+    for m, base in enumerate((0, 4, 8)):
+        columns(f_qkv, base, m * 4 * SLOT)
+    send(0, f_qkv)
+    for m, base in enumerate((16, 20)):
+        columns(f_ckv, base, m * 4 * SLOT)
+    send(1, f_ckv)
+    columns(f_cq, 12, 0)
+    send(2, f_cq)
+    padded_rows(f_wo, 24)
+    send(3, f_wo)
+    padded_rows(f_co, 28)
+    send(4, f_co)
     for rank in range(4):
-        for half in range(2):
-            steps.append([(rank, 48 + (half * 2 + i // 4) * 4 + i % 4) for i in range(8)])
-    return steps
-
-
-def assemble_kernel(table, *refs):
-    tiles, (o_qkv, o_ckv, o_cq, o_wo, o_co, o_in, o_out) = refs[:8], refs[8:]
-    step = pl.program_id(0)
-    side = tiles[0].shape[1]
-
-    def columns(out):
-        gap = jnp.zeros((side, SLOT - side), jnp.bfloat16)
-        for i in range(8):
-            wide = jnp.concatenate([tiles[i][0], gap], axis=1)
-            out[(i % 4) * side : (i % 4 + 1) * side, (i // 4) * SLOT : (i // 4 + 1) * SLOT] = wide
-
-    def joined(half):
-        return jnp.concatenate([tiles[half * 4 + i][0] for i in range(4)], axis=1)
-
-    def padded_rows(out):
-        for half in range(2):
-            out[half * SLOT : half * SLOT + side, :] = joined(half)
-            out[half * SLOT + side : (half + 1) * SLOT, :] = jnp.zeros((SLOT - side, 4 * side), jnp.bfloat16)
-
-    def rows(out):
-        for half in range(2):
-            out[half * side : (half + 1) * side, :] = joined(half)
-
-    for low, high, fill, out in (
-        (0, 6, columns, o_qkv),
-        (6, 10, columns, o_ckv),
-        (10, 12, columns, o_cq),
-        (12, 14, padded_rows, o_wo),
-        (14, 16, padded_rows, o_co),
-        (16, 24, rows, o_in),
-        (24, 32, rows, o_out),
-    ):
-        pl.when((step >= low) & (step < high))(functools.partial(fill, out))
-
-
-def assemble(table, tiles):
-    side = tiles.shape[-1]
+        for i in range(4):
+            f_in[i * side : (i + 1) * side, rank * 4 * side : (rank + 1) * 4 * side] = joined(rank, 32 + 4 * i)
+    send(5, f_in)
+    for rank in range(4):
+        for i in range(4):
+            f_out[(rank * 4 + i) * side : (rank * 4 + i + 1) * side, :] = joined(rank, 48 + 4 * i)
+    send(6, f_out)
+    for copy in copies:
+        copy.wait()
+
+
+def assemble(target, arrays, own_tiles, side):
     width = 4 * side
-
-    def tile_at(i):
-        return pl.BlockSpec((1, side, side), lambda s, table: (table[s * 8 + i], 0, 0))
-
-    def within(low, count):
-        return lambda s: jnp.clip(s - low, 0, count - 1)
-
-    a, b, c, d, e, f, g = [within(*x) for x in ((0, 6), (6, 4), (10, 2), (12, 2), (14, 2), (16, 8), (24, 8))]
+    tile_rows = side + side // 2
     bf = jnp.bfloat16
+    shapes = [
+        (width, 12 * SLOT), (width, 8 * SLOT), (width, 4 * SLOT), (4 * SLOT, width), (4 * SLOT, width),
+        (width, 4 * width), (4 * width, width),
+    ]
+    anywhere = pl.BlockSpec(memory_space=pl.ANY)
     return pl.pallas_call(
-        assemble_kernel,
+        functools.partial(assemble_kernel, sources=len(arrays), own_tiles=own_tiles, tile_rows=tile_rows),
         grid_spec=pltpu.PrefetchScalarGridSpec(
             num_scalar_prefetch=1,
-            grid=(32,),
-            in_specs=[tile_at(i) for i in range(8)],
-            out_specs=[
-                pl.BlockSpec((width, 2 * SLOT), lambda s, table: (0, a(s))),
-                pl.BlockSpec((width, 2 * SLOT), lambda s, table: (0, b(s))),
-                pl.BlockSpec((width, 2 * SLOT), lambda s, table: (0, c(s))),
-                pl.BlockSpec((2 * SLOT, width), lambda s, table: (d(s), 0)),
-                pl.BlockSpec((2 * SLOT, width), lambda s, table: (e(s), 0)),
-                pl.BlockSpec((2 * side, width), lambda s, table: (f(s) // 4, f(s) % 4)),
-                pl.BlockSpec((2 * side, width), lambda s, table: (g(s), 0)),
-            ],
+            grid=(1,),
+            in_specs=[anywhere] * len(arrays),
+            out_specs=[anywhere] * 7,
+            scratch_shapes=[pltpu.VMEM((256, tile_rows, LANES), bf)]
+            + [pltpu.VMEM(shape, bf) for shape in shapes]
+            + [pltpu.SemaphoreType.DMA, pltpu.SemaphoreType.DMA((7,))],
         ),
-        out_shape=[
-            jax.ShapeDtypeStruct((width, 12 * SLOT), bf),
-            jax.ShapeDtypeStruct((width, 8 * SLOT), bf),
-            jax.ShapeDtypeStruct((width, 4 * SLOT), bf),
-            jax.ShapeDtypeStruct((4 * SLOT, width), bf),
-            jax.ShapeDtypeStruct((4 * SLOT, width), bf),
-            jax.ShapeDtypeStruct((width, 4 * width), bf),
-            jax.ShapeDtypeStruct((4 * width, width), bf),
-        ],
-        compiler_params=pltpu.CompilerParams(vmem_limit_bytes=VM),
+        out_shape=[jax.ShapeDtypeStruct(shape, bf) for shape in shapes],
+        compiler_params=pltpu.CompilerParams(vmem_limit_bytes=56 * 2**20),
         name="assemble",
-    )(table, *([tiles] * 8))
+    )(target, *arrays)
 
 
 def weight_grads_kernel(
@@ -596,21 +700,40 @@
     heads = side // HEAD
     rank_ref = rank.astype(jnp.int32)[None]
 
-    both = lax.all_gather(jnp.stack([hidden_in, cotangent]), "tensor", axis=2, tiled=True)
-    hidden = both[0].reshape(tokens, width).astype(f32)
-    top_grad = both[1].reshape(tokens, width).astype(f32)
-    gathered = lax.all_gather(master_tiles[0].astype(bf16), ("dp", "tensor"), axis=0, tiled=True)
-    vectors = lax.all_gather(master_vectors.astype(bf16), "dp", axis=0, tiled=True).astype(f32).reshape(19, width)
+    length = master_vectors.shape[0]
+    line_rows = -(-length // (16 * LANES)) * 16
+    line = jnp.pad(master_vectors, (0, line_rows * LANES - length)).reshape(line_rows, LANES)
+    block = pack(master_tiles[0], line)
+    arrays, where, last = gather_blocks(block, ranks, groups)
+    if where is None:
+        source_rank = jnp.tile(jnp.arange(ranks, dtype=jnp.int32), groups)
+        source_group = jnp.repeat(jnp.arange(groups, dtype=jnp.int32), ranks)
+        lines = arrays[0].reshape(groups, ranks, -1, LANES)[:, 0, -line_rows:].reshape(groups, -1)[:, :length]
+    else:
+        steps = jnp.array([step for array in where for step, _ in array], jnp.int32)
+        bits = jnp.array([bit for array in where for _, bit in array], jnp.int32)
+        source_rank = (rank - steps) % ranks
+        source_group = group ^ bits
+        lines = jnp.concatenate([array[:, -line_rows:] for array in arrays[:2]], axis=0).reshape(groups, -1)[:, :length]
+        spots = source_group[:groups]
+        order = jnp.arange(groups, dtype=jnp.int32)
+        lines = jnp.sum(jnp.where((spots[None] == order[:, None])[:, :, None], lines[None].astype(f32), 0.0), axis=1)
+    vectors = lines.astype(f32).reshape(19, width)
 
     count = owner_list.shape[0]
     position = jnp.arange(count, dtype=jnp.int32)
     place = jnp.sum(jnp.where(owner_list[None, :] == position[:, None], position[None, :], 0), axis=1)
-    steps = tile_sources()
-    source_rank = jnp.array([r for step in steps for r, _ in step], jnp.int32)
-    source_ident = jnp.array([t for step in steps for _, t in step], jnp.int32)
-    found = jnp.sum(jnp.where(owner_list[None, :] == source_ident[:, None], position[None, :], 0), axis=1)
-    table = (found // own_tiles * ranks + source_rank) * own_tiles + found % own_tiles
-    w_qkv, c_kv, c_q, w_o, c_o, w_in, w_out = assemble(table, gathered)
+    spot = (source_group[:, None] * own_tiles + jnp.arange(own_tiles, dtype=jnp.int32)[None]).reshape(-1)
+    ident = jnp.sum(jnp.where(spot[:, None] == position[None, :], owner_list[None, :], 0), axis=1)
+    target = jnp.repeat(source_rank, own_tiles) * count + ident
+    w_qkv, c_kv, c_q, w_o, c_o, w_in, w_out = assemble(target, arrays, own_tiles, side)
+
+    rows_in = jnp.stack([hidden_in, cotangent])
+    if where is not None:
+        rows_in, _ = lax.optimization_barrier((rows_in, last))
+    both = lax.all_gather(rows_in, "tensor", axis=2, tiled=True)
+    hidden = both[0].reshape(tokens, width).astype(f32)
+    top_grad = both[1].reshape(tokens, width).astype(f32)
 
     head_bias = spread_heads(vectors[11:15], ranks)
     none = jnp.zeros_like(head_bias[0])
@@ -630,11 +753,13 @@
     keys_values = frame_projection(frames, c_kv, jnp.concatenate([none, head_bias[3]]))
     n1 = normalize(hidden, vectors[0], vectors[1]).astype(bf16)
     qkv = split((product(n1, w_qkv) + jnp.concatenate([head_bias[0], none, head_bias[1]])).astype(bf16))
-    attended = flat(self_forward(qkv, seg_col, seg_row, stamp_row, ranks, heads))
+    attended, self_logs = self_forward(qkv, seg_col, seg_row, stamp_row, ranks, heads)
+    attended = flat(attended)
     first_sum = hidden + product(attended, w_o) + vectors[8]
     n2 = normalize(first_sum, vectors[2], vectors[3]).astype(bf16)
     cross_queries = split((product(n2, c_q) + head_bias[2]).astype(bf16))
-    mixed = flat(cross_forward(cross_queries, keys_values, ranks, heads))
+    mixed, cross_logs = cross_forward(cross_queries, keys_values, ranks, heads)
+    mixed = flat(mixed)
     second_sum = first_sum + product(mixed, c_o) + vectors[9]
     n3 = normalize(second_sum, vectors[4], vectors[5]).astype(bf16)
     active, slope = gelu_pair(product(n3, w_in) + inner_bias)
@@ -649,7 +774,9 @@
     grad_second = grad_third + back
     b2 = grad_second.astype(bf16)
     grad_mixed = split(times_transpose(b2, c_o).astype(bf16))
-    dcq, dk, dv = cross_backward(rank_ref, cross_queries, keys_values, grad_mixed, ranks, heads)
+    dcq, dk, dv = cross_backward(
+        rank_ref, cross_queries, keys_values, grad_mixed, split(mixed), cross_logs, ranks, heads
+    )
     dcq = flat(dcq)
     frames_part = frames_back(rank_ref, dk, dv, c_kv, ranks)
     frames_sum = lax.psum_scatter(
@@ -660,7 +787,11 @@
     grad_first = grad_second + back
     b1 = grad_first.astype(bf16)
     grad_attended = split(times_transpose(b1, w_o).astype(bf16))
-    dqkv = flat(self_backward(rank_ref, qkv, grad_attended, seg_col, seg_row, stamp_col, ranks, heads))
+    dqkv = flat(
+        self_backward(
+            rank_ref, qkv, grad_attended, split(attended), self_logs, seg_col, seg_row, stamp_col, ranks, heads
+        )
+    )
 
     own_weight = lax.dynamic_slice_in_dim(w_qkv.reshape(width, 3, ranks * SLOT), rank * SLOT, SLOT, axis=2)
     part_one = times_transpose(dqkv, own_weight.reshape(width, 3 * SLOT))
@@ -693,7 +824,6 @@
         [gain_one[None], shift_one[None], same * even, own_sums[:2], query_sum * even, own_sums[2:], up_sum * even]
     )
     vector_sums = lax.psum(vector_terms.reshape(-1), ("dp", "tensor"))
-    length = master_vectors.shape[0]
     vector_grad = lax.dynamic_slice_in_dim(vector_sums, group * length, length)
 
     new_first, new_second, new_master, new_stats, new_bases = soap(

time: 712 us -> 588 us (0.83)
  Pallas kernels: 300 us -> 209 us
  waiting for transfers between devices: 173 us -> 109 us
  starting transfers between devices: 0.21 us -> 28.4 us
  blocking collectives: 65.6 us -> 42.9 us
  other arithmetic: 33.2 us -> 46.8 us
  local copies, waits for them, and re-layouts: 35.6 us -> 47 us
    all_gather x2 -> x1, waiting for transfers between devices: 171 us -> 0.01 us  [shards(): both = lax.all_gather(rows_in, 'tensor', axis=2, tiled=True)]
    pallas_call x6 -> x7, Pallas kernels: 232 us -> 141 us  [the longest x1 38.5 us: chol_bases(): pl.pallas_call(functools.partial(chol_kernel, block=block, unroll=unroll,...]
    ppermute x0 -> x23, waiting for transfers between devices: none -> 77.7 us  [the longest x3 33.2 us: gather_blocks(): lax.ppermute(block, 'tensor', turn(step))]
    reduce_scatter x1, waiting for transfers between devices: 0.01 us -> 29.1 us  [shards(): lax.psum_scatter(frames_part.reshape(ranks * seqs, frames_part.shape[2],...]
    ppermute x0 -> x23, starting transfers between devices: none -> 28 us  [the longest x3 7.86 us: gather_blocks(): lax.ppermute(block, 'tensor', turn(step))]
    unnamed x1 -> x0, blocking collectives: 26.3 us -> none
    concatenate x0 -> x4, other arithmetic: none -> 16 us  [gather_plane(): jnp.concatenate([held, across, along, jnp.concatenate([corner_low, corner...]
    unnamed x98 -> x134, local copies, waits for them, and re-layouts: 12 us -> 14.5 us
  transfers between devices with their start and end apart: 5 -> 27, of which waited for: 3 -> 8; matrix products, arithmetic and copies ran while one was open for 5% -> 10% of each run, Pallas kernels for 20% -> 22%
where the time goes in v3:
time: 588 us; the launch traced here: 577 us
  Pallas kernels  209 us (36%)
  waiting for transfers between devices  109 us (19%)
  matrix products  78.2 us (13%)
  local copies, waits for them, and re-layouts  47 us (8%)
  other arithmetic  46.8 us (8%)
  blocking collectives  42.9 us (7%)
  starting transfers between devices  28.4 us (5%)
  between operations  14.8 us (3%)
    psum x1, blocking collectives, shards(): vector_sums = lax.psum(vector_terms.reshape(-1), ('dp', 'tensor'))  42.9 us
    dot_general x6, matrix products, product(): return jnp.dot(left_part, right_part, preferred_element_type=jnp.float32)  40.3 us
    pallas_call x1, Pallas kernels, chol_bases(): pl.pallas_call(functools.partial(chol_kernel, block=block, unroll=unroll,...  38.5 us
    dot_general x6, matrix products, times_transpose(): lax.dot_general(left_part, right_part, (NT, ((), ())), preferred_element_...  38 us
    pallas_call x1, Pallas kernels, cross_backward(): pl.pallas_call(functools.partial(cross_backward_kernel, heads=heads, chun...  37.6 us
    ppermute x3, waiting for transfers between devices, gather_blocks(): lax.ppermute(block, 'tensor', turn(step))  33.2 us
    reduce_scatter x1, waiting for transfers between devices, shards(): lax.psum_scatter(frames_part.reshape(ranks * seqs, frames_part.shape[2],...  29.1 us
    ppermute x4, waiting for transfers between devices, gather_plane(): corner_low = lax.ppermute(across[:, :cut], axis, flips(4))  26.1 us
  transfers between devices with their start and end apart: 27, of which 8 were waited for; matrix products, arithmetic and copies ran while one was open for 10% of the time, Pallas kernels for 22%

profile of v3, /device:TPU:0, one launch (start us, length us, event | category | flops | bytes accessed | tf_op | source)
XLA Modules:
  0.0 576.6 jit_solution(2134993904345200171)
XLA Ops:
  7.2 1.4 pad_bitcast_fusion.line
  8.6 2.3 pack.1
  10.9 4.0 collective-permute-start
  15.0 1.5 collective-permute-start.1
  16.5 1.6 collective-permute-start.6
  18.1 1.5 collective-permute-start.2
  19.6 2.2 collective-permute-start.12
  21.8 33.2 %collective-permute-done = bf16[2320,128]{1,0:T(8,128)(2,1)S(1)} collective-permute-done((bf16[2320,128]{1,0:T(8,128)(2,1)}, bf16[2320,128]{1,0:T(8,128)(2,1)S(1)}, u32[]{:S(2)}, u32[]{:S(2)}) %collective-permute-start) | collective-permute-done | bytes 593952 | tf_op jit(solution)/shard_map/ppermute | solution.py:426
  55.0 1.8 collective-permute-start.19
  56.8 1.5 collective-permute-start.18
  58.9 1.6 collective-permute-start.3
  61.7 26.1 %collective-permute-done.3 = bf16[1,1152,128]{2,1,0:T(8,128)(2,1)S(1)} collective-permute-done((bf16[1,1152,128]{2,1,0:T(8,128)(2,1)S(1)}, bf16[1,1152,128]{2,1,0:T(8,128)(2,1)S(1)}, u32[]{:S(2)}, u32[]{:S(2)}) %collective-permute-start.3) | collective-permute-done | bytes 294944 | tf_op jit(solution)/shard_map/ppermute | solution.py:416
  89.0 1.6 collective-permute-start.14
  93.2 1.6 collective-permute-start.21
  96.1 2.4 maximum_maximum_fusion.refs_0_
  98.6 5.9 %collective-permute-done.7 = bf16[1,2320,128]{2,1,0:T(8,128)(2,1)} collective-permute-done((bf16[1,2320,128]{2,1,0:T(8,128)(2,1)}, bf16[1,2320,128]{2,1,0:T(8,128)(2,1)}, u32[]{:S(2)}, u32[]{:S(2)}) %collective-permute-start.7) | collective-permute-done | bytes 593952 | tf_op jit(solution)/shard_map/ppermute | solution.py:414
  107.8 9.4 %collective-permute-done.13 = bf16[1,2320,128]{2,1,0:T(8,128)(2,1)} collective-permute-done((bf16[1,2320,128]{2,1,0:T(8,128)(2,1)}, bf16[1,2320,128]{2,1,0:T(8,128)(2,1)}, u32[]{:S(2)}, u32[]{:S(2)}) %collective-permute-start.13) | collective-permute-done | bytes 593952 | tf_op jit(solution)/shard_map/ppermute | solution.py:414
  119.5 1.6 collective-permute-start.16
  121.0 2.5 collective-permute-done.21
  124.8 4.4 maximum_maximum_fusion.3.refs_6_
  129.6 4.5 maximum_maximum_fusion.1.refs_2_
  134.3 4.6 maximum_maximum_fusion.2.refs_4_
  139.7 5.1 copy.45.frames
  151.2 16.9 %assemble.1 = (bf16[768,3072]{1,0:T(8,128)(2,1)}, bf16[768,2048]{1,0:T(8,128)(2,1)}, bf16[768,1024]{1,0:T(8,128)(2,1)}, bf16[1024,768]{1,0:T(8,128)(2,1)}, bf16[...) custom-call(s32[256]{0:T(256)} %add.271.target, bf16[4,2320,128]{2,1,0:T(8,128)(2,1)} %copy-done.11, ...), custom_call_target="tpu_custom_call" | custom-call | tf_op jit(solution)/shard_map/assemble/pallas_call | solution.py:521
  168.1 6.6 %copy.48 = bf16[768,3072]{0,1:T(8,128)(2,1)} copy(bf16[768,3072]{1,0:T(8,128)(2,1)} %get-tuple-element.35) | data formatting | bytes 9437184 | tf_op jit(solution)/shard_map/assemble/pallas_call | solution.py:521
  174.7 16.5 %frame_projection.1.key.value = bf16[2,1500,2048]{2,1,0:T(8,128)(2,1)} custom-call(bf16[2,1500,768]{2,1,0:T(8,128)(2,1)} %copy.45.frames, bf16[768,2048]{1,0:T(8,128)(2,1)} %get-tuple-element.39.weight.key_weight.value_weight, f32[1,2048]{1,0:T(1,128)} %bitcast.167), custom_call_target="tpu_custom_call" | custom-call | tf_op jit(solution)/shard_map/frame_projection/pallas_call | solution.py:597
  191.2 2.4 constant_dynamic-slice_fusion
  193.6 1.7 convert_reduce_fusion.4
  195.5 3.4 convert_reduce_fusion.3
  199.6 9.1 %add_convert_fusion.1 = bf16[896,3072]{1,0:T(8,128)(2,1)} fusion(f32[3072]{0:T(1024)S(1)} %pad_maximum_fusion.1, bf16[896,768]{1,0:T(8,128)(2,1)S(1)} %fusion.14.n1, bf16[768,3072]{1,0:T(8,128)(2,1)} %get-tuple-element.35), kind=kOutput, calls=%fused_computation.7 | convolution fusion | flops 4233363456 | bytes 11612160 | tf_op jit(solution)/shard_map/dot_general | solution.py:644
  208.7 12.5 %self_forward.1 = (bf16[2,448,1024]{2,1,0:T(8,128)(2,1)}, f32[2,4,8,448]{3,2,1,0:T(8,128)}) custom-call(bf16[2,448,3072]{2,1,0:T(8,128)(2,1)} %bitcast.123, bf16[2,448,3072]{2,1,0:T(8,128)(2,1)} %bitcast.124, bf16[2,448,3072]{2,1,0:T(8,128)(2,1)} %bitcast.125, s32[2,448,1]{2,1,0:T(8,128)} %copy.44.seg_col, s32[2,1,448]{2,1,0:T(1,128)} %broadcast_in_dim.151.seg_row, ...), custom_call_target="tpu_custom_call" | custom-call | tf_op jit(solution)/shard_map/self_forward/pallas_call | solution.py:307
  221.2 1.3 slice-done
  222.5 3.6 fusion.40
  227.2 1.9 copy-done.54
  229.1 2.9 add_convert_fusion.2
  231.9 25.5 %cross_forward.1 = (bf16[2,448,1024]{2,1,0:T(8,128)(2,1)}, f32[2,4,8,448]{3,2,1,0:T(8,128)}) custom-call(bf16[2,448,1024]{2,1,0:T(8,128)(2,1)} %bitcast.138, bf16[2,1500,2048]{2,1,0:T(8,128)(2,1)} %frame_projection.1.key.value, bf16[2,1500,2048]{2,1,0:T(8,128)(2,1)} %frame_projection.1.key.value), custom_call_target="tpu_custom_call" | custom-call | tf_op jit(solution)/shard_map/cross_forward/pallas_call | solution.py:324
  257.4 3.2 fusion.41
  261.6 16.9 %multiply_convert_fusion.1 = (bf16[896,3072]{1,0:T(8,128)(2,1)S(1)}, f32[896,3072]{1,0:T(8,128)}) fusion(f32[3072]{0:T(1024)S(1)} %add.293, bf16[896,768]{1,0:T(8,128)(2,1)S(1)} %add_convert_fusion.3.n3, bf16[768,3072]{1,0:T(8,128)(2,1)} %get-tuple-element.42), kind=kOutput, calls=%fused_computation.6 | convolution fusion | flops 4293918720 | bytes 22622208 | tf_op jit(solution)/shard_map/dot_general | solution.py:644
  278.6 4.6 fusion.42
  285.0 1.6 fusion.7
  286.7 2.9 convert_reduce_fusion.6
  289.5 17.8 %convert_reduce_fusion = (f32[3072]{0:T(1024)}, bf16[896,3072]{1,0:T(8,128)(2,1)S(1)}) fusion(f32[896,3072]{1,0:T(8,128)} %get-tuple-element.135, f32[3072]{0:T(1024)S(1)} %add.293, bf16[896,768]{1,0:T(8,128)(2,1)S(1)} %get-tuple-element.111.b3, bf16[3072,768]{1,0:T(8,128)(2,1)} %get-tuple-element.43), kind=kOutput, calls=%fused_computation.3 | convolution fusion | flops 4313183232 | bytes 22634496 | tf_op jit(solution)/shard_map/dot_general | solution.py:648
  307.4 5.6 multiply_reduce_fusion
  313.1 4.4 convert_reduce_fusion.7
  317.5 2.9 convolution_convert_fusion.1
  320.4 37.6 %cross_backward.1 = (bf16[2,448,1024]{2,1,0:T(8,128)(2,1)}, bf16[2,1500,256]{2,1,0:T(8,128)(2,1)}, bf16[2,1500,256]{2,1,0:T(8,128)(2,1)}) custom-call(s32[1]{0:T(128)} %bitcast.17.rank, bf16[2,448,1024]{2,1,0:T(8,128)(2,1)} %bitcast.139, bf16[2,1500,2048]{2,1,0:T(8,128)(2,1)} %frame_projection.1.key.value, bf16[2,1500,2048]{2,1,0:T(8,128)(2,1)} %frame_projection.1.key.value, ...), custom_call_target="tpu_custom_call" | custom-call | tf_op jit(solution)/shard_map/cross_backward/pallas_call | solution.py:347
  358.1 4.4 multiply_reduce_fusion.1
  362.5 2.9 convert_reduce_fusion.8
  365.4 2.9 convolution_convert_fusion
  368.2 7.2 %self_backward.1 = bf16[2,448,768]{2,1,0:T(8,128)(2,1)} custom-call(s32[1]{0:T(128)} %bitcast.17.rank, bf16[2,448,3072]{2,1,0:T(8,128)(2,1)} %bitcast.126, bf16[2,448,3072]{2,1,0:T(8,128)(2,1)} %bitcast.127, bf16[2,448,3072]{2,1,0:T(8,128)(2,1)} %bitcast.128, bf16[2,448,1024]{2,1,0:T(8,128)(2,1)} %bitcast.158, ...), custom_call_target="tpu_custom_call" | custom-call | tf_op jit(solution)/shard_map/self_backward/pallas_call | solution.py:375
  375.4 4.4 fusion.35
  380.7 18.7 %weight_grads.1 = bf16[64,192,192]{2,1,0:T(8,128)(2,1)} custom-call(s32[1]{0:T(128)} %bitcast.17.rank, s32[64]{0:T(128)} %select_reduce_fusion.2.place, bf16[896,768]{1,0:T(8,128)(2,1)} %copy-done.15, bf16[896,768]{1,0:T(8,128)(2,1)} %bitcast.135, bf16[896,768]{1,0:T(8,128)(2,1)} %copy-done.16, bf16[896,1024]{1,0:T(8,128)(2,1)} %bitcast.141, ...), custom_call_target="tpu_custom_call" | custom-call | tf_op jit(solution)/shard_map/weight_grads/pallas_call | solution.py:572
  399.5 5.9 %frames_back.1 = bf16[4,2,384,768]{3,2,1,0:T(8,128)(2,1)} custom-call(s32[1]{0:T(128)} %bitcast.17.rank, bf16[2,1500,256]{2,1,0:T(8,128)(2,1)} %get-tuple-element.47.dk, bf16[2,1500,256]{2,1,0:T(8,128)(2,1)} %get-tuple-element.48.dv, bf16[768,2048]{1,0:T(8,128)(2,1)} %get-tuple-element.39.weight.key_weight.value_weight, ...), custom_call_target="tpu_custom_call" | custom-call | tf_op jit(solution)/shard_map/frames_back/pallas_call | solution.py:625
  405.4 10.0 %soap_pre.1 = (f32[8,192,192]{2,1,0:T(8,128)}, f32[8,2,192,192]{3,2,1,0:T(8,128)}) custom-call(f32[8,192,192]{2,1,0:T(8,128)} %bitcast.148, f32[8,2,192,192]{3,2,1,0:T(8,128)} %bitcast.130, f32[8,2,192,192]{3,2,1,0:T(8,128)} %bitcast.132), custom_call_target="tpu_custom_call" | custom-call | tf_op jit(solution)/shard_map/soap_pre/pallas_call | solution.py:123
  427.1 42.9 %psum.7 = f32[14592]{0:T(1024)S(1)} all-reduce(f32[14592]{0:T(1024)S(1)} %reshape.377), channel_id=1, replica_groups=mesh['dp'=8,'tensor'=4] {'dp','tensor'}, use_global_device_ids=true, to_apply=%region_39.40 | all-reduce | flops 14592 | bytes 116736 | tf_op jit(solution)/shard_map/psum | solution.py:826
  469.9 2.0 constant_dynamic-slice_fusion.1
  474.0 2.4 fusion.24
  476.3 2.1 reduce-scatter.8.cloned.1.call-done.grad
  478.5 17.8 %soap_main.1 = (f32[8,192,192]{2,1,0:T(8,128)}, f32[8,192,192]{2,1,0:T(8,128)}, f32[8,192,192]{2,1,0:T(8,128)}, f32[8,2,192,192]{3,2,1,0:T(8,128)}, f32[8,2,192,...) custom-call(bf16[8,192,192]{2,1,0:T(8,128)(2,1)} %reduce-scatter.8.cloned.1.call-done.grad, f32[8,192,192]{2,1,0:T(8,128)} %bitcast.147, ...), custom_call_target="tpu_custom_call" | custom-call | tf_op jit(solution)/shard_map/soap_main/pallas_call | solution.py:132
  496.3 1.9 copy-done
  498.2 38.5 %chol_bases.1 = f32[16,192,192]{2,1,0:T(8,128)} custom-call(f32[16,192,192]{2,1,0:T(8,128)S(1)} %bitcast.122, f32[16,192,192]{2,1,0:T(8,128)} %bitcast.153), custom_call_target="tpu_custom_call" | custom-call | tf_op jit(solution)/shard_map/chol_bases/pallas_call | solution.py:140
  536.8 29.1 %reduce-scatter.6.cloned.1.call-done = bf16[2,384,768]{2,1,0:T(8,128)(2,1)} async-done(((bf16[8,384,768]{2,1,0:T(8,128)(2,1)}), bf16[2,384,768]{2,1,0:T(8,128)(2,1)}) %reduce-scatter.6.cloned.1.call-update) | async-done | bytes 1179664 | tf_op jit(solution)/shard_map/reduce_scatter | solution.py:782
  565.9 1.4 slice_convert_fusion
  567.3 2.6 copy.50
  (268 shorter events, 40.4 us)
Async XLA Ops:
  7.2 84.0 %copy-start.12 = (bf16[2,112,768]{2,1,0:T(8,128)(2,1)S(1)}, bf16[2,112,768]{2,1,0:T(8,128)(2,1)}, u32[]{:S(2)}) copy-start(bf16[2,112,768]{2,1,0:T(8,128)(2,1)} %param.16) | copy-start | bytes 1032196
  7.2 84.0 %copy-start.33 = (bf16[2,112,768]{2,1,0:T(8,128)(2,1)S(1)}, bf16[2,112,768]{2,1,0:T(8,128)(2,1)}, u32[]{:S(2)}) copy-start(bf16[2,112,768]{2,1,0:T(8,128)(2,1)} %param.18) | copy-start | bytes 1032196
  7.2 186.4 %all-gather.2.cloned.1.call-start = ((), (), s32[]{:S(2)}) async-start(), calls=%async_computation.3 | async-start | bytes 3440640 | tf_op jit(solution)/shard_map/all_gather | solution.py:734
  10.9 85.2 %copy-start.23 = (bf16[2320,128]{1,0:T(8,128)(2,1)S(1)}, bf16[2320,128]{1,0:T(8,128)(2,1)}, u32[]{:S(2)}) copy-start(bf16[2320,128]{1,0:T(8,128)(2,1)} %pack.1) | copy-start | bytes 1781764
  10.9 44.1 %collective-permute-start = (bf16[2320,128]{1,0:T(8,128)(2,1)}, bf16[2320,128]{1,0:T(8,128)(2,1)S(1)}, u32[]{:S(2)}, u32[]{:S(2)}) collective-permute-start(bf16[2320,128]{1,0:T(8,128)(2,1)} %pack.1), channel_id=1, source_target_pairs={{0,2},{1,3},{2,0},{3,1},{4,6},{5,7},{6,4},{7,5},{8,10},{9,11},{10,... | collective-permute-start | bytes 1781768 | tf_op jit(solution)/shard_map/ppermute | solution.py:426
  15.0 41.8 %collective-permute-start.1 = (bf16[1,2320,128]{2,1,0:T(8,128)(2,1)}, bf16[1,2320,128]{2,1,0:T(8,128)(2,1)S(1)}, u32[]{:S(2)}, u32[]{:S(2)}) collective-permute-start(bf16[1,2320,128]{2,1,0:T(8,128)(2,1)} %bitcast.154), channel_id=1, source_target_pairs={{0,8},{4,12},{8,0},{12,4},{16,24},{20,28},{24,16},{28,20},{1,9},{5... | collective-permute-start | bytes 1781768 | tf_op jit(solution)/shard_map/ppermute | solution.py:414
  16.5 41.8 %collective-permute-start.6 = (bf16[2320,128]{1,0:T(8,128)(2,1)}, bf16[2320,128]{1,0:T(8,128)(2,1)}, u32[]{:S(2)}, u32[]{:S(2)}) collective-permute-start(bf16[2320,128]{1,0:T(8,128)(2,1)} %pack.1), channel_id=1, source_target_pairs={{0,1},{1,2},{2,3},{3,0},{4,5},{5,6},{6,7},{7,4},{8,9},{9,10},{10,1... | collective-permute-start | bytes 1781768 | tf_op jit(solution)/shard_map/ppermute | solution.py:426
  18.1 40.8 %collective-permute-start.2 = (bf16[1,2320,128]{2,1,0:T(8,128)(2,1)}, bf16[1,2320,128]{2,1,0:T(8,128)(2,1)S(1)}, u32[]{:S(2)}, u32[]{:S(2)}) collective-permute-start(bf16[1,2320,128]{2,1,0:T(8,128)(2,1)} %bitcast.155), channel_id=1, source_target_pairs={{0,16},{4,20},{8,24},{12,28},{16,0},{20,4},{24,8},{28,12},{1,17},{... | collective-permute-start | bytes 1781768 | tf_op jit(solution)/shard_map/ppermute | solution.py:415
  19.6 41.6 %collective-permute-start.12 = (bf16[2320,128]{1,0:T(8,128)(2,1)}, bf16[2320,128]{1,0:T(8,128)(2,1)}, u32[]{:S(2)}, u32[]{:S(2)}) collective-permute-start(bf16[2320,128]{1,0:T(8,128)(2,1)} %pack.1), channel_id=1, source_target_pairs={{0,3},{1,0},{2,1},{3,2},{4,7},{5,4},{6,5},{7,6},{8,11},{9,8},{10,9... | collective-permute-start | bytes 1781768 | tf_op jit(solution)/shard_map/ppermute | solution.py:426
  55.0 34.0 %copy-start.31 = (bf16[2320,128]{1,0:T(8,128)(2,1)}, bf16[2320,128]{1,0:T(8,128)(2,1)S(1)}, u32[]{:S(2)}) copy-start(bf16[2320,128]{1,0:T(8,128)(2,1)S(1)} %collective-permute-done) | copy-start | bytes 1781764
  55.0 34.0 %collective-permute-start.19 = (bf16[1,2320,128]{2,1,0:T(8,128)(2,1)S(1)}, bf16[1,2320,128]{2,1,0:T(8,128)(2,1)S(1)}, u32[]{:S(2)}, u32[]{:S(2)}) collective-permute-start(bf16[1,2320,128]{2,1,0:T(8,128)(2,1)S(1)} %bitcast.162), channel_id=1, source_target_pairs={{0,16},{4,20},{8,24},{12,28},{16,0},{20,4},{24,8},{28,12},{1,17},{... | collective-permute-start | bytes 1781768 | tf_op jit(solution)/shard_map/ppermute | solution.py:415
  56.8 32.2 %copy-start.29 = (bf16[1,2320,128]{2,1,0:T(8,128)(2,1)}, bf16[1,2320,128]{2,1,0:T(8,128)(2,1)S(1)}, u32[]{:S(2)}) copy-start(bf16[1,2320,128]{2,1,0:T(8,128)(2,1)S(1)} %collective-permute-done.1) | copy-start | bytes 1781764
  56.8 33.8 %collective-permute-start.18 = (bf16[1,2320,128]{2,1,0:T(8,128)(2,1)S(1)}, bf16[1,2320,128]{2,1,0:T(8,128)(2,1)}, u32[]{:S(2)}, u32[]{:S(2)}) collective-permute-start(bf16[1,2320,128]{2,1,0:T(8,128)(2,1)S(1)} %bitcast.163), channel_id=1, source_target_pairs={{0,8},{4,12},{8,0},{12,4},{16,24},{20,28},{24,16},{28,20},{1,9},{5... | collective-permute-start | bytes 1781768 | tf_op jit(solution)/shard_map/ppermute | solution.py:414
  58.3 36.4 %collective-permute-start.8 = (bf16[1,2320,128]{2,1,0:T(8,128)(2,1)}, bf16[1,2320,128]{2,1,0:T(8,128)(2,1)S(1)}, u32[]{:S(2)}, u32[]{:S(2)}) collective-permute-start(bf16[1,2320,128]{2,1,0:T(8,128)(2,1)} %bitcast.6), channel_id=1, source_target_pairs={{0,16},{4,20},{8,24},{12,28},{16,0},{20,4},{24,8},{28,12},{1,17},{... | collective-permute-start | bytes 1781768 | tf_op jit(solution)/shard_map/ppermute | solution.py:415
  58.9 35.9 %copy-start.28 = (bf16[1,2320,128]{2,1,0:T(8,128)(2,1)}, bf16[1,2320,128]{2,1,0:T(8,128)(2,1)S(1)}, u32[]{:S(2)}) copy-start(bf16[1,2320,128]{2,1,0:T(8,128)(2,1)S(1)} %collective-permute-done.2) | copy-start | bytes 1781764
  58.9 29.0 %collective-permute-start.3 = (bf16[1,1152,128]{2,1,0:T(8,128)(2,1)S(1)}, bf16[1,1152,128]{2,1,0:T(8,128)(2,1)S(1)}, u32[]{:S(2)}, u32[]{:S(2)}) collective-permute-start(bf16[1,1152,128]{2,1,0:T(8,128)(2,1)S(1)} %slice.161), channel_id=1, source_target_pairs={{0,16},{4,20},{8,24},{12,28},{16,0},{20,4},{24,8},{28,12},{1,17},{... | collective-permute-start | bytes 884744 | tf_op jit(solution)/shard_map/ppermute | solution.py:416
  61.2 32.0 %collective-permute-start.4 = (bf16[1,1168,128]{2,1,0:T(8,128)(2,1)}, bf16[1,1168,128]{2,1,0:T(8,128)(2,1)}, u32[]{:S(2)}, u32[]{:S(2)}) collective-permute-start(bf16[1,1168,128]{2,1,0:T(8,128)(2,1)} %slice.162), channel_id=1, source_target_pairs={{0,8},{4,12},{8,0},{12,4},{16,24},{20,28},{24,16},{28,20},{1,9},{5... | collective-permute-start | bytes 897032 | tf_op jit(solution)/shard_map/ppermute | solution.py:417
  87.8 16.7 %collective-permute-start.7 = (bf16[1,2320,128]{2,1,0:T(8,128)(2,1)}, bf16[1,2320,128]{2,1,0:T(8,128)(2,1)}, u32[]{:S(2)}, u32[]{:S(2)}) collective-permute-start(bf16[1,2320,128]{2,1,0:T(8,128)(2,1)} %bitcast.6), channel_id=1, source_target_pairs={{0,8},{4,12},{8,0},{12,4},{16,24},{20,28},{24,16},{28,20},{1,9},{5... | collective-permute-start | bytes 1781768 | tf_op jit(solution)/shard_map/ppermute | solution.py:414
  89.0 16.5 %collective-permute-start.14 = (bf16[1,2320,128]{2,1,0:T(8,128)(2,1)}, bf16[1,2320,128]{2,1,0:T(8,128)(2,1)}, u32[]{:S(2)}, u32[]{:S(2)}) collective-permute-start(bf16[1,2320,128]{2,1,0:T(8,128)(2,1)} %bitcast.7), channel_id=1, source_target_pairs={{0,16},{4,20},{8,24},{12,28},{16,0},{20,4},{24,8},{28,12},{1,17},{... | collective-permute-start | bytes 1781768 | tf_op jit(solution)/shard_map/ppermute | solution.py:415
  90.6 26.6 %collective-permute-start.13 = (bf16[1,2320,128]{2,1,0:T(8,128)(2,1)}, bf16[1,2320,128]{2,1,0:T(8,128)(2,1)}, u32[]{:S(2)}, u32[]{:S(2)}) collective-permute-start(bf16[1,2320,128]{2,1,0:T(8,128)(2,1)} %bitcast.7), channel_id=1, source_target_pairs={{0,8},{4,12},{8,0},{12,4},{16,24},{20,28},{24,16},{28,20},{1,9},{5... | collective-permute-start | bytes 1781768 | tf_op jit(solution)/shard_map/ppermute | solution.py:414
  92.1 380.6 %reduce-scatter.4.cloned.1.call-start = ((), (), s32[]{:S(2)}) async-start(), calls=%async_computation.4 | async-start | bytes 1720320 | tf_op jit(solution)/shard_map/reduce_scatter | solution.py:800
  93.2 31.6 %copy-start.32 = (bf16[2320,128]{1,0:T(8,128)(2,1)S(1)}, bf16[2320,128]{1,0:T(8,128)(2,1)}, u32[]{:S(2)}) copy-start(bf16[2320,128]{1,0:T(8,128)(2,1)} %copy-done.31) | copy-start | bytes 1781764
  93.2 30.3 %collective-permute-start.21 = (bf16[1,1168,128]{2,1,0:T(8,128)(2,1)S(1)}, bf16[1,1168,128]{2,1,0:T(8,128)(2,1)S(1)}, u32[]{:S(2)}, u32[]{:S(2)}) collective-permute-start(bf16[1,1168,128]{2,1,0:T(8,128)(2,1)S(1)} %slice.173), channel_id=1, source_target_pairs={{0,8},{4,12},{8,0},{12,4},{16,24},{20,28},{24,16},{28,20},{1,9},{5... | collective-permute-start | bytes 897032 | tf_op jit(solution)/shard_map/ppermute | solution.py:417
  95.6 23.9 %collective-permute-start.20 = (bf16[1,1152,128]{2,1,0:T(8,128)(2,1)S(1)}, bf16[1,1152,128]{2,1,0:T(8,128)(2,1)S(1)}, u32[]{:S(2)}, u32[]{:S(2)}) collective-permute-start(bf16[1,1152,128]{2,1,0:T(8,128)(2,1)S(1)} %slice.172), channel_id=1, source_target_pairs={{0,16},{4,20},{8,24},{12,28},{16,0},{20,4},{24,8},{28,12},{1,17},{... | collective-permute-start | bytes 884744 | tf_op jit(solution)/shard_map/ppermute | solution.py:416
  96.1 8.4 %copy-start.25 = (bf16[1,2320,128]{2,1,0:T(8,128)(2,1)S(1)}, bf16[1,2320,128]{2,1,0:T(8,128)(2,1)}, u32[]{:S(2)}) copy-start(bf16[1,2320,128]{2,1,0:T(8,128)(2,1)} %copy-done.24) | copy-start | bytes 1781764
  96.1 28.7 %copy-start.27 = (bf16[1,2320,128]{2,1,0:T(8,128)(2,1)S(1)}, bf16[1,2320,128]{2,1,0:T(8,128)(2,1)}, u32[]{:S(2)}) copy-start(bf16[1,2320,128]{2,1,0:T(8,128)(2,1)} %copy-done.26) | copy-start | bytes 1781764
  98.5 50.2 %copy-start.11 = (bf16[4,2320,128]{2,1,0:T(8,128)(2,1)}, bf16[4,2320,128]{2,1,0:T(8,128)(2,1)S(1)}, u32[]{:S(2)}) copy-start(bf16[4,2320,128]{2,1,0:T(8,128)(2,1)S(1)} %maximum_maximum_fusion.refs_0_) | copy-start | bytes 7127044
  104.5 44.2 %collective-permute-start.5 = (bf16[4,2320,128]{2,1,0:T(8,128)(2,1)S(1)}, bf16[4,2320,128]{2,1,0:T(8,128)(2,1)}, u32[]{:S(2)}, u32[]{:S(2)}) collective-permute-start(bf16[4,2320,128]{2,1,0:T(8,128)(2,1)S(1)} %maximum_maximum_fusion.refs_0_), channel_id=1, source_target_pairs={{0,4},{4,0},{8,12},{12,8},{16,20},{20,16},{24,28},{28,24},{1,5},{5... | collective-permute-start | bytes 7127048 | tf_op jit(solution)/shard_map/ppermute | solution.py:419
  105.5 24.1 %collective-permute-start.10 = (bf16[1,1168,128]{2,1,0:T(8,128)(2,1)S(1)}, bf16[1,1168,128]{2,1,0:T(8,128)(2,1)S(1)}, u32[]{:S(2)}, u32[]{:S(2)}) collective-permute-start(bf16[1,1168,128]{2,1,0:T(8,128)(2,1)S(1)} %slice.169), channel_id=1, source_target_pairs={{0,8},{4,12},{8,0},{12,4},{16,24},{20,28},{24,16},{28,20},{1,9},{5... | collective-permute-start | bytes 897032 | tf_op jit(solution)/shard_map/ppermute | solution.py:417
  117.2 12.0 %collective-permute-start.9 = (bf16[1,1152,128]{2,1,0:T(8,128)(2,1)S(1)}, bf16[1,1152,128]{2,1,0:T(8,128)(2,1)S(1)}, u32[]{:S(2)}, u32[]{:S(2)}) collective-permute-start(bf16[1,1152,128]{2,1,0:T(8,128)(2,1)S(1)} %slice.168), channel_id=1, source_target_pairs={{0,16},{4,20},{8,24},{12,28},{16,0},{20,4},{24,8},{28,12},{1,17},{... | collective-permute-start | bytes 884744 | tf_op jit(solution)/shard_map/ppermute | solution.py:416
  119.5 14.8 %collective-permute-start.16 = (bf16[1,1168,128]{2,1,0:T(8,128)(2,1)S(1)}, bf16[1,1168,128]{2,1,0:T(8,128)(2,1)S(1)}, u32[]{:S(2)}, u32[]{:S(2)}) collective-permute-start(bf16[1,1168,128]{2,1,0:T(8,128)(2,1)S(1)} %slice.171), channel_id=1, source_target_pairs={{0,8},{4,12},{8,0},{12,4},{16,24},{20,28},{24,16},{28,20},{1,9},{5... | collective-permute-start | bytes 897032 | tf_op jit(solution)/shard_map/ppermute | solution.py:417
  123.5 10.7 %collective-permute-start.15 = (bf16[1,1152,128]{2,1,0:T(8,128)(2,1)S(1)}, bf16[1,1152,128]{2,1,0:T(8,128)(2,1)S(1)}, u32[]{:S(2)}, u32[]{:S(2)}) collective-permute-start(bf16[1,1152,128]{2,1,0:T(8,128)(2,1)S(1)} %slice.170), channel_id=1, source_target_pairs={{0,16},{4,20},{8,24},{12,28},{16,0},{20,4},{24,8},{28,12},{1,17},{... | collective-permute-start | bytes 884744 | tf_op jit(solution)/shard_map/ppermute | solution.py:416
  129.2 22.0 %collective-permute-start.22 = (bf16[4,2320,128]{2,1,0:T(8,128)(2,1)}, bf16[4,2320,128]{2,1,0:T(8,128)(2,1)}, u32[]{:S(2)}, u32[]{:S(2)}) collective-permute-start(bf16[4,2320,128]{2,1,0:T(8,128)(2,1)} %maximum_maximum_fusion.3.refs_6_), channel_id=1, source_target_pairs={{0,4},{4,0},{8,12},{12,8},{16,20},{20,16},{24,28},{28,24},{1,5},{5... | collective-permute-start | bytes 7127048 | tf_op jit(solution)/shard_map/ppermute | solution.py:419
  134.2 17.1 %collective-permute-start.11 = (bf16[4,2320,128]{2,1,0:T(8,128)(2,1)}, bf16[4,2320,128]{2,1,0:T(8,128)(2,1)}, u32[]{:S(2)}, u32[]{:S(2)}) collective-permute-start(bf16[4,2320,128]{2,1,0:T(8,128)(2,1)} %maximum_maximum_fusion.1.refs_2_), channel_id=1, source_target_pairs={{0,4},{4,0},{8,12},{12,8},{16,20},{20,16},{24,28},{28,24},{1,5},{5... | collective-permute-start | bytes 7127048 | tf_op jit(solution)/shard_map/ppermute | solution.py:419
  138.9 12.4 %collective-permute-start.17 = (bf16[4,2320,128]{2,1,0:T(8,128)(2,1)}, bf16[4,2320,128]{2,1,0:T(8,128)(2,1)}, u32[]{:S(2)}, u32[]{:S(2)}) collective-permute-start(bf16[4,2320,128]{2,1,0:T(8,128)(2,1)} %maximum_maximum_fusion.2.refs_4_), channel_id=1, source_target_pairs={{0,4},{4,0},{8,12},{12,8},{16,20},{20,16},{24,28},{28,24},{1,5},{5... | collective-permute-start | bytes 7127048 | tf_op jit(solution)/shard_map/ppermute | solution.py:419
  139.7 8.3 %copy-start.50 = (s32[64]{0:T(128)S(1)}, s32[64]{0:T(128)}, u32[]{:S(2)}) copy-start(s32[64]{0:T(128)} %param.21) | copy-start | bytes 772
  151.2 47.8 %copy-start.35 = (f32[768]{0:T(1024)}, f32[768]{0:T(1024)S(1)}, u32[]{:S(2)}) copy-start(f32[768]{0:T(1024)S(1)} %get-tuple-element.106) | copy-start | bytes 9220
  199.0 9.7 %copy-start.45 = (f32[896]{0:T(1024)}, f32[896]{0:T(1024)S(1)}, u32[]{:S(2)}) copy-start(f32[896]{0:T(1024)S(1)} %rsqrt.48) | copy-start | bytes 10756
  199.6 9.1 %copy-start.15 = (bf16[896,768]{1,0:T(8,128)(2,1)}, bf16[896,768]{1,0:T(8,128)(2,1)S(1)}, u32[]{:S(2)}) copy-start(bf16[896,768]{1,0:T(8,128)(2,1)S(1)} %fusion.14.n1) | copy-start | bytes 4128772
  226.2 31.2 %copy-start.6 = (f32[896,768]{1,0:T(8,128)}, f32[896,768]{1,0:T(8,128)S(1)}, u32[]{:S(2)}) copy-start(f32[896,768]{1,0:T(8,128)S(1)} %get-tuple-element.131) | copy-start | bytes 8257540
  231.9 25.5 %copy-start.56 = (bf16[1024,768]{1,0:T(8,128)(2,1)S(1)}, bf16[1024,768]{1,0:T(8,128)(2,1)}, u32[]{:S(2)}) copy-start(bf16[1024,768]{1,0:T(8,128)(2,1)} %get-tuple-element.41) | copy-start | bytes 4718596
  260.6 17.9 %copy-start.4 = (f32[896,768]{1,0:T(8,128)}, f32[896,768]{1,0:T(8,128)S(1)}, u32[]{:S(2)}) copy-start(f32[896,768]{1,0:T(8,128)S(1)} %get-tuple-element.133) | copy-start | bytes 8257540
  261.1 17.4 %slice-start.3 = ((s8[4718592]{0:T(1024)(128)(4,1)}), s8[4194304]{0:T(1024)(128)(4,1)S(1)}, s32[]{:S(2)}) async-start(s8[4718592]{0:T(1024)(128)(4,1)} %bitcast.180), calls=%async_computation.10 | async-start | bytes 8388608
  261.6 16.9 %copy-start.17 = (bf16[896,768]{1,0:T(8,128)(2,1)}, bf16[896,768]{1,0:T(8,128)(2,1)S(1)}, u32[]{:S(2)}) copy-start(bf16[896,768]{1,0:T(8,128)(2,1)S(1)} %add_convert_fusion.3.n3) | copy-start | bytes 4128772
  261.6 16.9 %slice-start.4 = ((s8[4718592]{0:T(1024)(128)(4,1)}), s8[524288]{0:T(1024)(128)(4,1)S(1)}, s32[]{:S(2)}) async-start(s8[4718592]{0:T(1024)(128)(4,1)} %bitcast.180), calls=%async_computation.11 | async-start | bytes 1048576
  286.7 20.7 %slice-start.1 = ((s8[4718592]{0:T(1024)(128)(4,1)}), s8[4194304]{0:T(1024)(128)(4,1)S(1)}, s32[]{:S(2)}) async-start(s8[4718592]{0:T(1024)(128)(4,1)} %bitcast.178), calls=%async_computation.8 | async-start | bytes 8388608
  289.5 17.9 %copy-start.18 = (bf16[896,768]{1,0:T(8,128)(2,1)}, bf16[896,768]{1,0:T(8,128)(2,1)S(1)}, u32[]{:S(2)}) copy-start(bf16[896,768]{1,0:T(8,128)(2,1)S(1)} %get-tuple-element.111.b3) | copy-start | bytes 4128772
  289.5 17.9 %copy-start.5 = (f32[896,768]{1,0:T(8,128)S(1)}, f32[896,768]{1,0:T(8,128)}, u32[]{:S(2)}) copy-start(f32[896,768]{1,0:T(8,128)} %copy-done.4) | copy-start | bytes 8257540
  289.5 17.9 %slice-start.2 = ((s8[4718592]{0:T(1024)(128)(4,1)}), s8[524288]{0:T(1024)(128)(4,1)S(1)}, s32[]{:S(2)}) async-start(s8[4718592]{0:T(1024)(128)(4,1)} %bitcast.178), calls=%async_computation.9 | async-start | bytes 1048576
  320.4 37.6 %copy-start.7 = (f32[896,768]{1,0:T(8,128)S(1)}, f32[896,768]{1,0:T(8,128)}, u32[]{:S(2)}) copy-start(f32[896,768]{1,0:T(8,128)} %copy-done.6) | copy-start | bytes 8257540
  320.4 37.7 %copy-start.55 = (bf16[768,1024]{1,0:T(8,128)(2,1)S(1)}, bf16[768,1024]{1,0:T(8,128)(2,1)}, u32[]{:S(2)}) copy-start(bf16[768,1024]{1,0:T(8,128)(2,1)} %get-tuple-element.38) | copy-start | bytes 4718596
  368.2 7.2 %copy-start.44 = (f32[896]{0:T(1024)S(1)}, f32[896]{0:T(1024)}, u32[]{:S(2)}) copy-start(f32[896]{0:T(1024)} %copy-done.43) | copy-start | bytes 10756
  368.2 7.2 %copy-start.46 = (f32[896]{0:T(1024)S(1)}, f32[896]{0:T(1024)}, u32[]{:S(2)}) copy-start(f32[896]{0:T(1024)} %copy-done.45) | copy-start | bytes 10756
  379.8 98.6 %reduce-scatter.8.cloned.1.call-start = ((), (), s32[]{:S(2)}) async-start(), calls=%async_computation.6 | async-start | bytes 7077888 | tf_op jit(solution)/shard_map/reduce_scatter | solution.py:809
  399.4 166.4 %reduce-scatter.6.cloned.1.call-start = ((), (), s32[]{:S(2)}) async-start(), calls=%async_computation.5 | async-start | bytes 5898240 | tf_op jit(solution)/shard_map/reduce_scatter | solution.py:782
  405.4 10.0 %copy-start.13 = (bf16[2,112,768]{2,1,0:T(8,128)(2,1)S(1)}, bf16[2,112,768]{2,1,0:T(8,128)(2,1)}, u32[]{:S(2)}) copy-start(bf16[2,112,768]{2,1,0:T(8,128)(2,1)} %param.16) | copy-start | bytes 1032196
  405.4 11.6 %copy-start.9 = (bf16[2,448,768]{2,1,0:T(8,128)(2,1)S(1)}, bf16[2,448,768]{2,1,0:T(8,128)(2,1)}, u32[]{:S(2)}) copy-start(bf16[2,448,768]{2,1,0:T(8,128)(2,1)} %self_backward.1) | copy-start | bytes 4128772
  415.4 10.1 %copy-start.14 = (bf16[2,448,1024]{2,1,0:T(8,128)(2,1)S(1)}, bf16[2,448,1024]{2,1,0:T(8,128)(2,1)}, u32[]{:S(2)}) copy-start(bf16[2,448,1024]{2,1,0:T(8,128)(2,1)} %get-tuple-element.45) | copy-start | bytes 5505028
  417.2 54.7 %copy-start.37 = (f32[1824]{0:T(1024)S(1)}, f32[1824]{0:T(1024)}, u32[]{:S(2)}) copy-start(f32[1824]{0:T(1024)} %param.27) | copy-start | bytes 21892
  417.2 54.7 %copy-start.48 = (f32[1824]{0:T(1024)S(1)}, f32[1824]{0:T(1024)}, u32[]{:S(2)}) copy-start(f32[1824]{0:T(1024)} %param.28) | copy-start | bytes 21892
  417.2 54.7 %copy-start.49 = (f32[1824]{0:T(1024)S(1)}, f32[1824]{0:T(1024)}, u32[]{:S(2)}) copy-start(f32[1824]{0:T(1024)} %param.29) | copy-start | bytes 21892
  417.3 55.4 %copy-start.36 = (f32[768]{0:T(1024)S(1)}, f32[768]{0:T(1024)}, u32[]{:S(2)}) copy-start(f32[768]{0:T(1024)} %copy-done.35) | copy-start | bytes 9220
  417.3 55.4 %copy-start.39 = (f32[2,112]{1,0:T(2,128)S(1)}, f32[2,112]{1,0:T(2,128)}, u32[]{:S(2)}) copy-start(f32[2,112]{1,0:T(2,128)} %copy-done.38) | copy-start | bytes 2692
  417.3 55.4 %copy-start.47 = (f32[2,112]{1,0:T(2,128)S(1)}, f32[2,112]{1,0:T(2,128)}, u32[]{:S(2)}) copy-start(f32[2,112]{1,0:T(2,128)} %add_rsqrt_fusion.4) | copy-start | bytes 2692
  (27 other events, 106.8 us)
Sparse Core Ops, SparseCore 0:
  92.2 57.5 all-gather.1
  379.9 33.7 reduce-scatter.3
  417.5 60.9 reduce-scatter.7
  480.6 85.2 reduce-scatter.5

commit v4 on v3

--- a/solution.py
+++ b/solution.py
@@ -5,6 +5,7 @@
 from jax import lax
 from jax.experimental import pallas as pl
 from jax.experimental.pallas import tpu as pltpu
+from jax.experimental.layout import Layout, with_layout_constraint
 from jax.sharding import PartitionSpec as P
 
 HEAD = 64
@@ -50,7 +51,10 @@
 
 def soap_main_kernel(grad, master, first, second, stats, bases, rot_first, stats_rot,
                      new_master, new_first, new_second, new_stats, turned, grams):
-    g32 = grad[0].astype(jnp.float32)
+    side = master.shape[1]
+    rest = grad[side:]
+    rest = jnp.concatenate([rest[:, : side - LANES], rest[:, side - LANES :]], axis=0)
+    g32 = jnp.concatenate([grad[:side], rest], axis=1)
     g, ql, qr = split2(g32), split2(bases[0, 0]), split2(bases[0, 1])
     new_first[0] = beta_one * first[0] + (1.0 - beta_one) * g32
     part_left = split2(dot3(ql, g, TN))
@@ -129,7 +133,7 @@
     t, p = tile_spec(side), pair_spec(side)
     f = jnp.float32
     ts, ps = jax.ShapeDtypeStruct(first.shape, f), jax.ShapeDtypeStruct(stats.shape, f)
-    return pl.pallas_call(soap_main_kernel, grid=(n,), in_specs=[t, t, t, t, p, p, t, p],
+    return pl.pallas_call(soap_main_kernel, grid=(n,), in_specs=[pl.BlockSpec((side + side // 2, LANES), lambda i: (i, 0)), t, t, t, p, p, t, p],
         out_specs=[t, t, t, p, p, p], out_shape=[ts, ts, ts, ps, ps, ps], name="soap_main")(
         grad, master, first, second, stats, bases, rot_first, stats_rot)
 
@@ -145,8 +149,7 @@
     return out.reshape(turned.shape)
 
 
-def soap(gradient, master, first, second, statistics, bases):
-    rot_first, stats_rot = soap_pre(first, statistics, bases)
+def soap(gradient, master, first, second, statistics, bases, rot_first, stats_rot):
     nm, nf, ns, nst, turned, grams = soap_main(gradient, master, first, second, statistics, bases, rot_first, stats_rot)
     return nf, ns, nm, nst, chol_bases(turned, grams)
 
@@ -409,28 +412,37 @@
     )(tiles, line)
 
 
-def gather_plane(held, flips, axis):
-    cut = held.shape[1] // 32 * 16
-    across = lax.ppermute(held, axis, flips(2))
-    along = lax.ppermute(held, axis, flips(4))
-    corner_low = lax.ppermute(across[:, :cut], axis, flips(4))
-    corner_high = lax.ppermute(along[:, cut:], axis, flips(2))
-    even = jnp.concatenate([held, across, along, jnp.concatenate([corner_low, corner_high], axis=1)], axis=0)
-    return even, lax.ppermute(even, axis, flips(1))
-
-
-def gather_blocks(block, ranks, groups):
-    if ranks == 4 and groups == 8:
-        flips = lambda bits: [(i, i ^ bits) for i in range(groups)]
-        turn = lambda step: [(i, (i + step) % ranks) for i in range(ranks)]
-        one, three, two = [lax.ppermute(block, "tensor", turn(step)) for step in (1, 3, 2)]
-        arrays, where = [], []
-        for step, held in ((0, block), (1, one), (3, three), (2, two)):
-            for parity, array in enumerate(gather_plane(held[None], flips, "dp")):
-                arrays.append(array)
-                where.append([(step, 2 * k + parity) for k in range(4)])
-        return arrays, where, two
-    return [lax.all_gather(block, ("dp", "tensor"), axis=0)], None, None
+def gather_blocks(block, ranks, groups, ready):
+    if ranks != 4 or groups != 8:
+        return [lax.all_gather(block, ("dp", "tensor"), axis=0)], None, None, ready
+
+    def flip(values, bits):
+        return lax.ppermute(values, "dp", [(i, i ^ bits) for i in range(groups)])
+
+    def turn(values, step):
+        return lax.ppermute(values, "tensor", [(i, (i + step) % ranks) for i in range(ranks)])
+
+    cut = block.shape[0] // 32 * 16
+    one, three = turn(block, 1), turn(block, 3)
+    held = block[None]
+    sides = flip(held, 2), flip(held, 4)
+    later, _ = lax.optimization_barrier((block, sides))
+    two = turn(later, 2)
+    units, before = [(0, held, sides)], sides
+    for step, values in ((1, one), (3, three), (2, two)):
+        if step == 1:
+            values, ready = lax.optimization_barrier((values, ready))
+        held, _ = lax.optimization_barrier((values[None], before))
+        before = flip(held, 2), flip(held, 4)
+        units.append((step, held, before))
+    arrays, where = [], []
+    for step, held, (across, along) in units:
+        low, high = flip(across[:, :cut], 4), flip(along[:, cut:], 2)
+        even = jnp.concatenate([held, across, along, jnp.concatenate([low, high], axis=1)], axis=0)
+        for parity, array in enumerate((even, flip(even, 1))):
+            arrays.append(array)
+            where.append([(step, 2 * k + parity) for k in range(4)])
+    return arrays, where, two, ready
 
 
 def assemble_kernel(target, *refs, sources, own_tiles, tile_rows):
@@ -536,20 +548,27 @@
 
 
 def weight_grads_kernel(
-    rank, place, n1, dqkv, n2, dcq, frames, dk, dv, attended, b1, mixed, b2, n3, grad_up, active, b3, out
+    rank, slot, sub, n1, dqkv, n2, dcq, frames, dk, dv, attended, b1, mixed, b2, n3, grad_up, active, b3, lines, out, *, side
 ):
-    side = out.shape[1]
+    half = side // 2
+    tile_rows = side + half
+
+    def keep(tile, ident):
+        tile = tile.astype(jnp.bfloat16)
+        at = pl.multiple_of(sub[ident] * tile_rows, 32)
+        out[slot[ident], pl.ds(at, side)] = tile[:, :LANES]
+        rest = tile[:, LANES:]
+        out[slot[ident], pl.ds(at + side, half)] = jnp.concatenate([rest[:half], rest[half:]], axis=1)
 
     def slots(made, bases):
         for m, base in enumerate(bases):
             for i in range(4):
-                out[place[base + i]] = made[i * side : (i + 1) * side, m * SLOT : m * SLOT + side].astype(jnp.bfloat16)
+                keep(made[i * side : (i + 1) * side, m * SLOT : m * SLOT + side], base + i)
 
     def grid_of(made, base, rows):
         for i in range(rows):
             for j in range(4):
-                tile = made[i * side : (i + 1) * side, j * side : (j + 1) * side]
-                out[place[base + i * 4 + j]] = tile.astype(jnp.bfloat16)
+                keep(made[i * side : (i + 1) * side, j * side : (j + 1) * side], base + i * 4 + j)
 
     slots(bdot(n1[...], dqkv[...], TN), (0, 4, 8))
     slots(bdot(n2[...], dcq[...], TN), (12,))
@@ -559,32 +578,83 @@
     grid_of(bdot(mixed[...], b2[...], TN), 28, 1)
     grid_of(bdot(n3[...], grad_up[...], TN), 32, 4)
     grid_of(bdot(active[...], b3[...], TN), 48, 4)
-
-
-def weight_grads(rank, place, side, n1, dqkv, n2, dcq, frames, dk, dv, attended, b1, mixed, b2, n3, grad_up, active, b3):
+    for i in range(out.shape[0]):
+        out[i, out.shape[1] - lines.shape[1] :] = lines[i].astype(jnp.bfloat16)
+
+
+def weight_grads(rank, slot, sub, side, groups, own_tiles, lines, n1, dqkv, n2, dcq, frames, dk, dv, attended, b1, mixed, b2, n3, grad_up, active, b3):
     def whole(x):
-        return pl.BlockSpec(x.shape, lambda i, rank, place: (0,) * x.ndim)
+        return pl.BlockSpec(x.shape, lambda i, rank, slot, sub: (0,) * x.ndim)
 
     def own(x, width):
-        return pl.BlockSpec((x.shape[0], width), lambda i, rank, place: (0, rank[0]))
-
-    shape = (place.shape[0], side, side)
+        return pl.BlockSpec((x.shape[0], width), lambda i, rank, slot, sub: (0, rank[0]))
+
+    def fitted(x):
+        return own(x, 4 * side) if x.shape[1] > 4 * side else whole(x)
+
+    shape = (groups, own_tiles * (side + side // 2) + lines.shape[1], LANES)
     return pl.pallas_call(
-        weight_grads_kernel,
+        functools.partial(weight_grads_kernel, side=side),
         grid_spec=pltpu.PrefetchScalarGridSpec(
-            num_scalar_prefetch=2,
+            num_scalar_prefetch=3,
             grid=(1,),
             in_specs=[
                 whole(n1), whole(dqkv), whole(n2), own(dcq, SLOT), whole(frames), whole(dk), whole(dv),
                 own(attended, SLOT), whole(b1), own(mixed, SLOT), whole(b2), whole(n3),
-                own(grad_up, 4 * side), own(active, 4 * side), whole(b3),
+                fitted(grad_up), fitted(active), whole(b3), whole(lines),
             ],
-            out_specs=pl.BlockSpec(shape, lambda i, rank, place: (0, 0, 0)),
+            out_specs=pl.BlockSpec(shape, lambda i, rank, slot, sub: (0, 0, 0)),
         ),
         out_shape=jax.ShapeDtypeStruct(shape, jnp.bfloat16),
         compiler_params=pltpu.CompilerParams(vmem_limit_bytes=60 * 2**20),
         name="weight_grads",
-    )(rank, place, n1, dqkv, n2, dcq, frames, dk, dv, attended, b1, mixed, b2, n3, grad_up, active, b3)
+    )(rank, slot, sub, n1, dqkv, n2, dcq, frames, dk, dv, attended, b1, mixed, b2, n3, grad_up, active, b3, lines)
+
+
+def scatter_blocks(blocks, ranks, groups):
+    f32, bf16 = jnp.float32, jnp.bfloat16
+    if groups != 8:
+        return lax.psum_scatter(blocks, "dp", scatter_dimension=0, tiled=True)[0].astype(f32)
+
+    def sent(values, bits):
+        return lax.ppermute(values.astype(bf16), "dp", [(i, i ^ bits) for i in range(groups)]).astype(f32)
+
+    half = groups // 2
+    cut = blocks.shape[1] // 32 * 16
+    chip = (blocks[:half].astype(f32) + sent(blocks[half:], 1)).astype(bf16)
+    low, high = chip[:, :cut], chip[:, cut:]
+    low_x, high_y = sent(jnp.stack([low[1], low[3]]), 2), sent(high[2:], 4)
+    low = jnp.stack([low[0], low[2]]).astype(f32) + low_x
+    high = high[:2].astype(f32) + high_y
+    low_y, high_x = sent(low[1], 4), sent(high[1], 2)
+    return jnp.concatenate([low[0] + low_y, high[0] + high_x], axis=0)
+
+
+def first_back_kernel(rank, dqkv, query_weight, key_weight, value_weight, hidden, out, sums):
+    weights = jnp.concatenate([query_weight[...], key_weight[...], value_weight[...]], axis=1)
+    made = bdot(dqkv[...], weights, NT)
+    unit, _ = unit_rows(hidden[...])
+    sums[0:1] = jnp.sum(made * unit, axis=0, keepdims=True)
+    sums[1:2] = jnp.sum(made, axis=0, keepdims=True)
+    out[...] = made.astype(jnp.bfloat16)
+
+
+def first_back(rank, dqkv, weight, hidden, ranks):
+    tokens, width = hidden.shape
+    own = lambda offset: pl.BlockSpec((width, SLOT), lambda i, rank: (0, offset + rank[0]))
+    whole = lambda shape: pl.BlockSpec(shape, lambda i, rank: (0, 0))
+    return pl.pallas_call(
+        first_back_kernel,
+        grid_spec=pltpu.PrefetchScalarGridSpec(
+            num_scalar_prefetch=1,
+            grid=(1,),
+            in_specs=[whole(dqkv.shape), own(0), own(ranks), own(2 * ranks), whole(hidden.shape)],
+            out_specs=[whole((tokens, width)), whole((2, width))],
+        ),
+        out_shape=[jax.ShapeDtypeStruct((tokens, width), jnp.bfloat16), jax.ShapeDtypeStruct((2, width), jnp.float32)],
+        compiler_params=pltpu.CompilerParams(vmem_limit_bytes=VM),
+        name="first_back",
+    )(rank, dqkv, weight, weight, weight, hidden)
 
 
 def frames_kernel(frames, weight, bias, out):
@@ -680,6 +750,100 @@
     return value * level, level + value * bell * 0.3989422804014327
 
 
+def middle_kernel(
+    rank, mixed, first_sum, top_grad, c_o, w_in, w_out, vectors, inner_bias,
+    block_out, grad_out, grad_mixed, n3_out, b2_out, b3_out, active_out, up_out, sums, up_sums, acts, slopes, ups,
+):
+    f32, bf16 = jnp.float32, jnp.bfloat16
+    width = first_sum.shape[1]
+    parts = acts.shape[0]
+    row = lambda i: vectors[i : i + 1]
+    cut = lambda i: slice(i * width, (i + 1) * width)
+    fold = lambda values: jnp.sum(values, axis=0, keepdims=True)
+
+    def back(unit, inverse, scaled):
+        centre = jnp.mean(scaled, axis=-1, keepdims=True)
+        return inverse * (scaled - centre - unit * jnp.mean(scaled * unit, axis=-1, keepdims=True))
+
+    second_sum = first_sum[...] + bdot(mixed[...], c_o[...], NN) + row(9)
+    unit, inverse = unit_rows(second_sum)
+    n3 = (unit * row(4) + row(5)).astype(bf16)
+    n3_out[...] = n3
+    third_sum = second_sum + row(10)
+    for i in range(parts):
+        value, slope = gelu_pair(bdot(n3, w_in[:, cut(i)], NN) + inner_bias[:, cut(i)])
+        acts[i] = value.astype(bf16)
+        slopes[i] = slope.astype(bf16)
+        third_sum = third_sum + bdot(acts[i], w_out[cut(i)], NN)
+    active_out[...] = acts[rank[0]]
+    last, last_inverse = unit_rows(third_sum)
+    block_out[...] = last * row(6) + row(7)
+    grads = top_grad[...].astype(f32)
+    grad_third = back(last, last_inverse, grads * row(6))
+    b3 = grad_third.astype(bf16)
+    b3_out[...] = b3
+    grad_normed, ups_now = None, []
+    for i in range(parts):
+        grad_up = (bdot(b3, w_out[cut(i)], NT) * slopes[i].astype(f32)).astype(bf16)
+        ups[i] = grad_up
+        ups_now.append(fold(grad_up.astype(f32)))
+        term = bdot(grad_up, w_in[:, cut(i)], NT)
+        grad_normed = term if grad_normed is None else grad_normed + term
+    up_out[...] = ups[rank[0]]
+    grad_second = grad_third + back(unit, inverse, grad_normed * row(4))
+    grad_out[...] = grad_second
+    b2 = grad_second.astype(bf16)
+    b2_out[...] = b2
+    grad_mixed[...] = bdot(b2, c_o[...], NT).astype(bf16)
+    now = jnp.concatenate(
+        [
+            fold(grad_normed * unit), fold(grad_normed), fold(grads * last), fold(grads),
+            fold(b2.astype(f32)), fold(b3.astype(f32)), jnp.zeros((2, width), f32),
+        ],
+        axis=0,
+    )
+    ups_all = jnp.concatenate(ups_now, axis=0)
+    start = pl.program_id(0) == 0
+
+    @pl.when(start)
+    def _():
+        sums[...] = now
+        up_sums[...] = ups_all
+
+    @pl.when(jnp.logical_not(start))
+    def _():
+        sums[...] += now
+        up_sums[...] += ups_all
+
+
+def middle(rank, mixed, first_sum, top_grad, c_o, w_in, w_out, vectors, inner_bias, block=224):
+    f32, bf16 = jnp.float32, jnp.bfloat16
+    tokens, width = first_sum.shape
+    slots, hidden = mixed.shape[1], w_in.shape[1]
+    parts = hidden // width
+    rows = lambda size: pl.BlockSpec((block, size), lambda i, rank: (i, 0))
+    once = lambda x: pl.BlockSpec(x.shape, lambda i, rank: (0, 0), pipeline_mode=pl.Buffered(1))
+    total = lambda count: pl.BlockSpec((count, width), lambda i, rank: (0, 0))
+    out = lambda size, kind: jax.ShapeDtypeStruct((tokens, size), kind)
+    return pl.pallas_call(
+        middle_kernel,
+        grid_spec=pltpu.PrefetchScalarGridSpec(
+            num_scalar_prefetch=1,
+            grid=(tokens // block,),
+            in_specs=[
+                rows(slots), rows(width), rows(width), once(c_o), once(w_in), once(w_out), once(vectors), once(inner_bias),
+            ],
+            out_specs=[rows(width), rows(width), rows(slots)] + [rows(width)] * 5 + [total(8), total(parts)],
+            scratch_shapes=[pltpu.VMEM((parts, block, width), bf16)] * 3,
+        ),
+        out_shape=[out(width, f32), out(width, f32), out(slots, bf16)]
+        + [out(width, bf16)] * 5
+        + [jax.ShapeDtypeStruct((8, width), f32), jax.ShapeDtypeStruct((parts, width), f32)],
+        compiler_params=pltpu.CompilerParams(vmem_limit_bytes=VM),
+        name="middle",
+    )(rank, mixed, first_sum, top_grad, c_o, w_in, w_out, vectors, inner_bias)
+
+
 def spread_heads(rows, ranks):
     lead = rows.shape[0]
     side = rows.shape[1] // ranks
@@ -704,7 +868,9 @@
     line_rows = -(-length // (16 * LANES)) * 16
     line = jnp.pad(master_vectors, (0, line_rows * LANES - length)).reshape(line_rows, LANES)
     block = pack(master_tiles[0], line)
-    arrays, where, last = gather_blocks(block, ranks, groups)
+    ready = soap_pre(tile_first[0], tile_stats[0], tile_bases[0])
+    frames = with_layout_constraint(frames, Layout(major_to_minor=(0, 1, 2)))
+    arrays, where, last, (ready, frames) = gather_blocks(block, ranks, groups, (ready, frames))
     if where is None:
         source_rank = jnp.tile(jnp.arange(ranks, dtype=jnp.int32), groups)
         source_group = jnp.repeat(jnp.arange(groups, dtype=jnp.int32), ranks)
@@ -733,7 +899,6 @@
         rows_in, _ = lax.optimization_barrier((rows_in, last))
     both = lax.all_gather(rows_in, "tensor", axis=2, tiled=True)
     hidden = both[0].reshape(tokens, width).astype(f32)
-    top_grad = both[1].reshape(tokens, width).astype(f32)
 
     head_bias = spread_heads(vectors[11:15], ranks)
     none = jnp.zeros_like(head_bias[0])
@@ -760,25 +925,18 @@
     cross_queries = split((product(n2, c_q) + head_bias[2]).astype(bf16))
     mixed, cross_logs = cross_forward(cross_queries, keys_values, ranks, heads)
     mixed = flat(mixed)
-    second_sum = first_sum + product(mixed, c_o) + vectors[9]
-    n3 = normalize(second_sum, vectors[4], vectors[5]).astype(bf16)
-    active, slope = gelu_pair(product(n3, w_in) + inner_bias)
-    active, slope = active.astype(bf16), slope.astype(bf16)
-    third_sum = second_sum + product(active, w_out) + vectors[10]
-    block_out = own_rows(normalize(third_sum, vectors[6], vectors[7]))
-
-    grad_third, gain_final, shift_final = normalize_back(third_sum, vectors[6], top_grad)
-    b3 = grad_third.astype(bf16)
-    grad_up = (times_transpose(b3, w_out) * slope.astype(f32)).astype(bf16)
-    back, gain_three, shift_three = normalize_back(second_sum, vectors[4], times_transpose(grad_up, w_in))
-    grad_second = grad_third + back
-    b2 = grad_second.astype(bf16)
-    grad_mixed = split(times_transpose(b2, c_o).astype(bf16))
+    top_grad = both[1].reshape(tokens, width)
+    out_rows, grad_second, grad_mixed, n3, b2, b3, active, grad_up, sums, up_sum = middle(
+        rank_ref, mixed, first_sum, top_grad, c_o, w_in, w_out, vectors, inner_bias[None]
+    )
+    block_out = own_rows(out_rows)
+    grad_mixed = split(grad_mixed)
     dcq, dk, dv = cross_backward(
         rank_ref, cross_queries, keys_values, grad_mixed, split(mixed), cross_logs, ranks, heads
     )
     dcq = flat(dcq)
     frames_part = frames_back(rank_ref, dk, dv, c_kv, ranks)
+    dcq, frames_part = lax.optimization_barrier((dcq, frames_part))
     frames_sum = lax.psum_scatter(
         frames_part.reshape(ranks * seqs, frames_part.shape[2], width), "tensor", scatter_dimension=0, tiled=True
     )
@@ -793,41 +951,49 @@
         )
     )
 
-    own_weight = lax.dynamic_slice_in_dim(w_qkv.reshape(width, 3, ranks * SLOT), rank * SLOT, SLOT, axis=2)
-    part_one = times_transpose(dqkv, own_weight.reshape(width, 3 * SLOT))
-    unit_one, _ = unit_rows(hidden)
-    gain_one, shift_one = jnp.sum(part_one * unit_one, axis=0), jnp.sum(part_one, axis=0)
-    grad_one = lax.psum_scatter(split(part_one.astype(bf16)), "tensor", scatter_dimension=1, tiled=True).astype(f32)
+    part_one, first_sums = first_back(rank_ref, dqkv, w_qkv, hidden, ranks)
+    grad_one = lax.psum_scatter(split(part_one), "tensor", scatter_dimension=1, tiled=True).astype(f32)
     back, _, _ = normalize_back(
         hidden_in.astype(f32).reshape(-1, width), vectors[0], grad_one.reshape(-1, width)
     )
     input_grad = own_rows(grad_first) + back.reshape(hidden_in.shape)
 
-    tile_terms = weight_grads(
-        rank_ref, place, side, n1, dqkv, n2, dcq, frames, dk, dv, attended, b1, mixed, b2, n3, grad_up, active, b3
-    )
-    owned_grads = lax.psum_scatter(tile_terms, "dp", scatter_dimension=0, tiled=True)
-
     def total(values):
         return jnp.sum(values.astype(f32), axis=tuple(range(values.ndim - 1)))
 
     same = jnp.stack(
-        [gain_two, shift_two, gain_three, shift_three, gain_final, shift_final, total(b1), total(b2), total(b3)]
+        [gain_two, shift_two, sums[0], sums[1], sums[2], sums[3], total(b1), sums[4], sums[5]]
     )
     query_sum = total(dcq).reshape(ranks, SLOT)[:, :side].reshape(1, width)
-    up_sum = total(grad_up).reshape(4, width)
     even = 1.0 / ranks
     dqkv_sum = total(dqkv)
     own_sums = jnp.stack([dqkv_sum[:side], dqkv_sum[2 * SLOT : 2 * SLOT + side], total(dv)[:side]])
     own_sums = lax.dynamic_update_slice(jnp.zeros((3, width), f32), own_sums, (0, rank * side))
     vector_terms = jnp.concatenate(
-        [gain_one[None], shift_one[None], same * even, own_sums[:2], query_sum * even, own_sums[2:], up_sum * even]
-    )
-    vector_sums = lax.psum(vector_terms.reshape(-1), ("dp", "tensor"))
-    vector_grad = lax.dynamic_slice_in_dim(vector_sums, group * length, length)
+        [first_sums, same * even, own_sums[:2], query_sum * even, own_sums[2:], up_sum * even]
+    )
+    lines = vector_terms.reshape(groups, length)
+    owner = place // own_tiles
+    if groups == 8:
+        bits = owner ^ group
+        slot = (bits & 1) * (groups // 2) + (bits >> 1)
+        at = jnp.arange(groups, dtype=jnp.int32)
+        wanted = group ^ (2 * (at % (groups // 2)) + at // (groups // 2))
+        lines = jnp.sum(jnp.where((wanted[:, None] == at[None])[:, :, None], lines[None], 0.0), axis=1)
+    else:
+        slot = owner
+    lines = jnp.pad(lines, ((0, 0), (0, line_rows * LANES - length))).reshape(groups, line_rows, LANES)
+    blocks = weight_grads(
+        rank_ref, slot, place % own_tiles, side, groups, own_tiles, lines,
+        n1, dqkv, n2, dcq, frames, dk, dv, attended, b1, mixed, b2, n3, grad_up, active, b3,
+    )
+    owned = scatter_blocks(blocks, ranks, groups)
+    line = owned[-line_rows:]
+    turns = [[(i, (i + step) % ranks) for i in range(ranks)] for step in range(1, ranks)]
+    vector_grad = (line + sum(lax.ppermute(line, "tensor", turn) for turn in turns)).reshape(-1)[:length]
 
     new_first, new_second, new_master, new_stats, new_bases = soap(
-        owned_grads, master_tiles[0], tile_first[0], tile_second[0], tile_stats[0], tile_bases[0]
+        owned, master_tiles[0], tile_first[0], tile_second[0], tile_stats[0], tile_bases[0], *ready
     )
     new_vector_first = beta_one * vector_first + (1.0 - beta_one) * vector_grad
     new_vector_second = beta_two * vector_second + (1.0 - beta_two) * vector_grad * vector_grad

time: 588 us -> 469 us (0.80); the launches traced: 577 us -> 465 us
  waiting for transfers between devices: 109 us -> 42.3 us
  matrix products: 78.2 us -> 18.9 us
  Pallas kernels: 209 us -> 260 us
  blocking collectives: 42.9 us -> 0 us
  starting transfers between devices: 28.4 us -> 51.6 us
  local copies, waits for them, and re-layouts: 47 us -> 33.7 us
    pallas_call x2 -> x4, Pallas kernels: 36.6 us -> 88.2 us  [the longest x1 46.7 us: middle(): pl.pallas_call(middle_kernel, grid_spec=pltpu.PrefetchScalarGridSpec(num_...]
    psum x1 -> x0, blocking collectives: 42.9 us -> none  [shards(): vector_sums = lax.psum(vector_terms.reshape(-1), ('dp', 'tensor'))]
    ppermute x23 -> x31, waiting for transfers between devices: 77.7 us -> 42.2 us  [the longest x5 20.3 us: sent(): lax.ppermute(values.astype(bf16), 'dp', [(i, i ^ bits) for i in range(gro...]
    dot_general x6 -> x2, matrix products: 38 us -> 6.58 us  [times_transpose(): lax.dot_general(left_part, right_part, (NT, ((), ())), preferred_element_...]
    reduce_scatter x1, waiting for transfers between devices: 29.1 us -> 0.01 us  [shards(): lax.psum_scatter(frames_part.reshape(ranks * seqs, frames_part.shape[2],...]
    dot_general x6 -> x3, matrix products: 40.3 us -> 12.3 us  [product(): return jnp.dot(left_part, right_part, preferred_element_type=jnp.float32)]
    ppermute x23 -> x31, starting transfers between devices: 28 us -> 51.3 us  [the longest x3 22.8 us: turn(): lax.ppermute(values, 'tensor', [(i, (i + step) % ranks) for i in range(ra...]
    pallas_call x1 -> x0, local copies, waits for them, and re-layouts: 6.62 us -> none  [assemble(): pl.pallas_call(functools.partial(assemble_kernel, sources=len(arrays), ow...]
  transfers between devices with their start and end apart: 27 -> 34, of which waited for: 8 -> 9; matrix products, arithmetic and copies ran while one was open for 10% -> 12% of each run, Pallas kernels for 22% -> 25%
where the time goes in v4:
time: 469 us; the launch traced here: 465 us
  Pallas kernels  260 us (55%)
  starting transfers between devices  51.6 us (11%)
  other arithmetic  43.6 us (9%)
  waiting for transfers between devices  42.3 us (9%)
  local copies, waits for them, and re-layouts  33.7 us (7%)
  matrix products  18.9 us (4%)
  between operations  14.8 us (3%)
    pallas_call x1, Pallas kernels, middle(): pl.pallas_call(middle_kernel, grid_spec=pltpu.PrefetchScalarGridSpec(num_...  46.7 us
    pallas_call x1, Pallas kernels, chol_bases(): pl.pallas_call(functools.partial(chol_kernel, block=block, unroll=unroll,...  38.3 us
    pallas_call x1, Pallas kernels, cross_backward(): pl.pallas_call(functools.partial(cross_backward_kernel, heads=heads, chun...  37.5 us
    pallas_call x1, Pallas kernels, cross_forward(): pl.pallas_call(functools.partial(cross_forward_kernel, heads=heads, chunk...  25.2 us
    ppermute x3, starting transfers between devices, turn(): lax.ppermute(values, 'tensor', [(i, (i + step) % ranks) for i in range(ra...  22.8 us
    ppermute x5, waiting for transfers between devices, sent(): lax.ppermute(values.astype(bf16), 'dp', [(i, i ^ bits) for i in range(gro...  20.3 us
    pallas_call x1, Pallas kernels, weight_grads(): pl.pallas_call(functools.partial(weight_grads_kernel, side=side), grid_sp...  18.3 us
    pallas_call x1, Pallas kernels, soap_main(): pl.pallas_call(soap_main_kernel, grid=(n,), in_specs=[pl.BlockSpec((side...  18 us
  transfers between devices with their start and end apart: 34, of which 9 were waited for; matrix products, arithmetic and copies ran while one was open for 12% of the time, Pallas kernels for 25%

profile of v4, /device:TPU:0, one launch (start us, length us, event | category | flops | bytes accessed | tf_op | source)
XLA Modules:
  0.0 465.4 jit_solution(10930875012080613462)
XLA Ops:
  7.2 1.3 pad_bitcast_fusion.1.line
  8.5 2.3 pack.1
  10.9 3.0 collective-permute-start.6
  13.9 1.5 collective-permute-start
  15.4 1.5 collective-permute-start.1
  16.9 2.2 collective-permute-start.12
  19.2 5.0 %copy.39.frames = bf16[2,1500,768]{2,1,0:T(8,128)(2,1)} copy(bf16[2,1500,768]{2,0,1:T(2,128)(2,1)} %param.17) | data formatting | bytes 9216000 | tf_op args[1]
  24.1 10.0 %soap_pre.1 = (f32[8,192,192]{2,1,0:T(8,128)}, f32[8,2,192,192]{3,2,1,0:T(8,128)}) custom-call(f32[8,192,192]{2,1,0:T(8,128)} %bitcast.124, f32[8,2,192,192]{3,2,1,0:T(8,128)} %bitcast.110, f32[8,2,192,192]{3,2,1,0:T(8,128)} %bitcast.112), custom_call_target="tpu_custom_call" | custom-call | tf_op jit(solution)/shard_map/soap_pre/pallas_call | solution.py:127
  35.8 17.5 %collective-permute-start.2 = (bf16[2320,128]{1,0:T(8,128)(2,1)S(1)}, bf16[2320,128]{1,0:T(8,128)(2,1)}, u32[]{:S(2)}, u32[]{:S(2)}) collective-permute-start(bf16[2320,128]{1,0:T(8,128)(2,1)S(1)} %copy-done.16), channel_id=1, source_target_pairs={{0,2},{1,3},{2,0},{3,1},{4,6},{5,7},{6,4},{7,5},{8,10},{9,11},{10,... | collective-permute-start | bytes 1781768 | tf_op jit(solution)/shard_map/ppermute | solution.py:423
  55.9 1.5 collective-permute-start.4
  57.4 1.7 slice.215
  59.1 1.5 collective-permute-start.3
  61.5 6.3 %collective-permute-done.2 = bf16[2320,128]{1,0:T(8,128)(2,1)} collective-permute-done((bf16[2320,128]{1,0:T(8,128)(2,1)S(1)}, bf16[2320,128]{1,0:T(8,128)(2,1)}, u32[]{:S(2)}, u32[]{:S(2)}) %collective-permute-start.2) | collective-permute-done | bytes 593952 | tf_op jit(solution)/shard_map/ppermute | solution.py:423
  68.2 1.6 collective-permute-start.10
  70.7 1.6 collective-permute-start.9
  73.4 2.5 maximum_maximum_fusion.refs_0_
  76.0 1.2 slice.224
  77.3 3.5 collective-permute-done.9
  81.3 1.5 collective-permute-start.15
  82.8 4.4 maximum_maximum_fusion.1.refs_2_
  87.2 6.2 %collective-permute-done.19 = bf16[1,2320,128]{2,1,0:T(8,128)(2,1)S(1)} collective-permute-done((bf16[1,2320,128]{2,1,0:T(8,128)(2,1)}, bf16[1,2320,128]{2,1,0:T(8,128)(2,1)S(1)}, u32[]{:S(2)}, u32[]{:S(2)}) %collective-permute-start.19) | collective-permute-done | bytes 593952 | tf_op jit(solution)/shard_map/ppermute | solution.py:420
  94.1 4.3 collective-permute-done.15
  98.4 1.5 collective-permute-start.20
  99.9 4.5 maximum_maximum_fusion.2.refs_4_
  104.6 1.6 collective-permute-done.20
  106.1 4.4 maximum_maximum_fusion.3.refs_6_
  117.4 17.0 %assemble.1 = (bf16[768,3072]{1,0:T(8,128)(2,1)}, bf16[768,2048]{1,0:T(8,128)(2,1)}, bf16[768,1024]{1,0:T(8,128)(2,1)}, bf16[1024,768]{1,0:T(8,128)(2,1)}, bf16[...) custom-call(s32[256]{0:T(256)} %add.211.target, bf16[4,2320,128]{2,1,0:T(8,128)(2,1)} %copy-done.8, ...), custom_call_target="tpu_custom_call" | custom-call | tf_op jit(solution)/shard_map/assemble/pallas_call | solution.py:533
  134.4 16.3 %frame_projection.1.key.value = bf16[2,1500,2048]{2,1,0:T(8,128)(2,1)} custom-call(bf16[2,1500,768]{2,1,0:T(8,128)(2,1)} %copy.39.frames, bf16[768,2048]{1,0:T(8,128)(2,1)} %get-tuple-element.69.weight.key_weight.value_weight, f32[1,2048]{1,0:T(1,128)} %bitcast.142), custom_call_target="tpu_custom_call" | custom-call | tf_op jit(solution)/shard_map/frame_projection/pallas_call | solution.py:667
  150.7 1.7 fusion
  152.5 1.9 multiply_reduce_fusion.3
  154.5 1.4 fusion.26
  156.4 2.0 slice-done.1
  158.4 6.3 %add_convert_fusion = bf16[896,3072]{1,0:T(8,128)(2,1)} fusion(f32[3072]{0:T(1024)S(1)} %pad_maximum_fusion.3, bf16[896,768]{1,0:T(8,128)(2,1)S(1)} %add_convert_fusion.4.n1, bf16[768,3072]{1,0:T(8,128)(2,1)S(1)} %bitcast.102), kind=kOutput, calls=%fused_computation | convolution fusion | flops 4233363456 | bytes 11612160 | tf_op jit(solution)/shard_map/dot_general | solution.py:714
  164.7 12.6 %self_forward.1 = (bf16[2,448,1024]{2,1,0:T(8,128)(2,1)}, f32[2,4,8,448]{3,2,1,0:T(8,128)}) custom-call(bf16[2,448,3072]{2,1,0:T(8,128)(2,1)} %bitcast.95, bf16[2,448,3072]{2,1,0:T(8,128)(2,1)} %bitcast.96, bf16[2,448,3072]{2,1,0:T(8,128)(2,1)} %bitcast.97, s32[2,448,1]{2,1,0:T(8,128)} %copy.40.seg_col, s32[2,1,448]{2,1,0:T(1,128)} %broadcast_in_dim.148.seg_row, ...), custom_call_target="tpu_custom_call" | custom-call | tf_op jit(solution)/shard_map/self_forward/pallas_call | solution.py:310
  177.4 3.2 fusion.29
  182.9 2.8 add_convert_fusion.2
  185.7 25.2 %cross_forward.1 = (bf16[2,448,1024]{2,1,0:T(8,128)(2,1)}, f32[2,4,8,448]{3,2,1,0:T(8,128)}) custom-call(bf16[2,448,1024]{2,1,0:T(8,128)(2,1)} %bitcast.115, bf16[2,1500,2048]{2,1,0:T(8,128)(2,1)} %frame_projection.1.key.value, bf16[2,1500,2048]{2,1,0:T(8,128)(2,1)} %frame_projection.1.key.value), custom_call_target="tpu_custom_call" | custom-call | tf_op jit(solution)/shard_map/cross_forward/pallas_call | solution.py:327
  211.0 46.7 %middle.1 = (f32[896,768]{1,0:T(8,128)}, f32[896,768]{1,0:T(8,128)}, bf16[896,1024]{1,0:T(8,128)(2,1)}, bf16[896,768]{1,0:T(8,128)(2,1)}, bf16[896,768]{1,0:T(8,...) custom-call(s32[1]{0:T(128)} %bitcast.rank, ...), custom_call_target="tpu_custom_call" | custom-call | tf_op jit(solution)/shard_map/middle/pallas_call | solution.py:828
  257.7 37.5 %cross_backward.1 = (bf16[2,448,1024]{2,1,0:T(8,128)(2,1)}, bf16[2,1500,256]{2,1,0:T(8,128)(2,1)}, bf16[2,1500,256]{2,1,0:T(8,128)(2,1)}) custom-call(s32[1]{0:T(128)} %bitcast.rank, bf16[2,448,1024]{2,1,0:T(8,128)(2,1)} %bitcast.116, bf16[2,1500,2048]{2,1,0:T(8,128)(2,1)} %frame_projection.1.key.value, bf16[2,1500,2048]{2,1,0:T(8,128)(2,1)} %frame_projection.1.key.value, ...), custom_call_target="tpu_custom_call" | custom-call | tf_op jit(solution)/shard_map/cross_backward/pallas_call | solution.py:350
  295.2 6.0 %frames_back.1 = bf16[4,2,384,768]{3,2,1,0:T(8,128)(2,1)} custom-call(s32[1]{0:T(128)} %bitcast.rank, bf16[2,1500,256]{2,1,0:T(8,128)(2,1)} %get-tuple-element.79.dk, bf16[2,1500,256]{2,1,0:T(8,128)(2,1)} %get-tuple-element.80.dv, bf16[768,2048]{1,0:T(8,128)(2,1)} %get-tuple-element.69.weight.key_weight.value_weight, ...), custom_call_target="tpu_custom_call" | custom-call | tf_op jit(solution)/shard_map/frames_back/pallas_call | solution.py:695
  301.2 3.7 multiply_reduce_fusion
  304.9 2.3 convert_reduce_fusion.3
  307.2 2.8 convolution_convert_fusion
  310.1 7.1 %self_backward.1 = bf16[2,448,768]{2,1,0:T(8,128)(2,1)} custom-call(s32[1]{0:T(128)} %bitcast.rank, bf16[2,448,3072]{2,1,0:T(8,128)(2,1)} %bitcast.98, bf16[2,448,3072]{2,1,0:T(8,128)(2,1)} %bitcast.99, bf16[2,448,3072]{2,1,0:T(8,128)(2,1)} %bitcast.100, bf16[2,448,1024]{2,1,0:T(8,128)(2,1)} %bitcast.134, bf16[2,448,1024]{2,1,0:T(8,128)(2,1)} %get-tuple-element.65.mixed, ...), custom_call_target="tpu_custom_call" | custom-call | tf_op jit(solution)/shard_map/self_backward/pallas_call | solution.py:378
  317.1 5.2 %first_back.1 = (bf16[896,768]{1,0:T(8,128)(2,1)}, f32[2,768]{1,0:T(2,128)}) custom-call(s32[1]{0:T(128)} %bitcast.rank, bf16[896,768]{1,0:T(8,128)(2,1)} %bitcast.105, bf16[768,3072]{1,0:T(8,128)(2,1)} %get-tuple-element.64.query_weight.key_weight.value_weight, bf16[768,3072]{1,0:T(8,128)(2,1)} %get-tuple-element.64.query_weight.key_weight.value_weight, ...), custom_call_target="tpu_custom_call" | custom-call | tf_op jit(solution)/shard_map/first_back/pallas_call | solution.py:646
  324.8 1.8 convert_reduce_fusion
  328.6 18.3 %weight_grads.1 = bf16[8,2320,128]{2,1,0:T(8,128)(2,1)} custom-call(s32[1]{0:T(128)} %bitcast.rank, s32[64]{0:T(128)} %get-tuple-element.155.slot, s32[64]{0:T(128)} %get-tuple-element.154.sub, bf16[896,768]{1,0:T(8,128)(2,1)} %copy-done.12, bf16[896,768]{1,0:T(8,128)(2,1)} %bitcast.106, bf16[896,768]{1,0:T(8,128)(2,1)} %copy-done.13, ...), custom_call_target="tpu_custom_call" | custom-call | tf_op jit(solution)/shard_map/weight_grads/pallas_call | solution.py:596
  346.9 1.9 slice.239
  349.6 2.0 constant_dynamic-slice_fusion
  351.7 1.9 collective-permute-done.23
  353.6 3.0 add_convert_fusion.1
  357.5 1.6 collective-permute-start.26
  360.7 1.3 fusion.10
  362.0 2.4 fusion.8
  364.4 11.2 %collective-permute-done.24 = bf16[2,1152,128]{2,1,0:T(8,128)(2,1)} collective-permute-done((bf16[2,1152,128]{2,1,0:T(8,128)(2,1)}, bf16[2,1152,128]{2,1,0:T(8,128)(2,1)}, u32[]{:S(2)}, u32[]{:S(2)}) %collective-permute-start.24) | collective-permute-done | bytes 589856 | tf_op jit(solution)/shard_map/ppermute | solution.py:620
  379.4 5.7 %collective-permute-done.25 = bf16[1152,128]{1,0:T(8,128)(2,1)S(1)} collective-permute-done((bf16[1152,128]{1,0:T(8,128)(2,1)S(1)}, bf16[1152,128]{1,0:T(8,128)(2,1)S(1)}, u32[]{:S(2)}, u32[]{:S(2)}) %collective-permute-start.25) | collective-permute-done | bytes 294944 | tf_op jit(solution)/shard_map/ppermute | solution.py:620
  385.1 1.5 collective-permute-done.27
  386.8 5.0 %collective-permute-start.29 = (f32[16,128]{1,0:T(8,128)S(1)}, f32[16,128]{1,0:T(8,128)S(1)}, u32[]{:S(2)}, u32[]{:S(2)}) collective-permute-start(f32[16,128]{1,0:T(8,128)S(1)} %slice.250), channel_id=1, source_target_pairs={{0,2},{1,3},{2,0},{3,1},{4,6},{5,7},{6,4},{7,5},{8,10},{9,11},{10,... | collective-permute-start | bytes 24584 | tf_op jit(solution)/shard_map/ppermute | solution.py:993
  391.8 2.8 collective-permute-start.30
  395.8 18.0 %soap_main.1 = (f32[8,192,192]{2,1,0:T(8,128)}, f32[8,192,192]{2,1,0:T(8,128)}, f32[8,192,192]{2,1,0:T(8,128)}, f32[8,2,192,192]{3,2,1,0:T(8,128)}, f32[8,2,192,...) custom-call(f32[2320,128]{1,0:T(8,128)} %pad_maximum_fusion.grad, f32[8,192,192]{2,1,0:T(8,128)} %bitcast.123, ...), custom_call_target="tpu_custom_call" | custom-call | tf_op jit(solution)/shard_map/soap_main/pallas_call | solution.py:136
  413.7 1.9 copy-done
  415.6 38.3 %chol_bases.1 = f32[16,192,192]{2,1,0:T(8,128)} custom-call(f32[16,192,192]{2,1,0:T(8,128)S(1)} %bitcast.94, f32[16,192,192]{2,1,0:T(8,128)} %bitcast.129), custom_call_target="tpu_custom_call" | custom-call | tf_op jit(solution)/shard_map/chol_bases/pallas_call | solution.py:144
  454.6 1.4 slice_convert_fusion.1
  456.0 2.6 copy.43
  (227 shorter events, 32.0 us)
Async XLA Ops:
  7.2 143.5 %all-gather.2.cloned.1.call-start = ((), (), s32[]{:S(2)}) async-start(), calls=%async_computation.2 | async-start | bytes 3440640 | tf_op jit(solution)/shard_map/all_gather | solution.py:900
  10.9 23.2 %collective-permute-start.6 = (bf16[2320,128]{1,0:T(8,128)(2,1)}, bf16[2320,128]{1,0:T(8,128)(2,1)}, u32[]{:S(2)}, u32[]{:S(2)}) collective-permute-start(bf16[2320,128]{1,0:T(8,128)(2,1)} %pack.1), channel_id=1, source_target_pairs={{0,1},{1,2},{2,3},{3,0},{4,5},{5,6},{6,7},{7,4},{8,9},{9,10},{10,1... | collective-permute-start | bytes 1781768 | tf_op jit(solution)/shard_map/ppermute | solution.py:423
  13.9 20.2 %collective-permute-start = (bf16[1,2320,128]{2,1,0:T(8,128)(2,1)}, bf16[1,2320,128]{2,1,0:T(8,128)(2,1)S(1)}, u32[]{:S(2)}, u32[]{:S(2)}) collective-permute-start(bf16[1,2320,128]{2,1,0:T(8,128)(2,1)} %bitcast.130), channel_id=1, source_target_pairs={{0,8},{4,12},{8,0},{12,4},{16,24},{20,28},{24,16},{28,20},{1,9},{5... | collective-permute-start | bytes 1781768 | tf_op jit(solution)/shard_map/ppermute | solution.py:420
  15.4 18.7 %collective-permute-start.1 = (bf16[1,2320,128]{2,1,0:T(8,128)(2,1)}, bf16[1,2320,128]{2,1,0:T(8,128)(2,1)S(1)}, u32[]{:S(2)}, u32[]{:S(2)}) collective-permute-start(bf16[1,2320,128]{2,1,0:T(8,128)(2,1)} %bitcast.131), channel_id=1, source_target_pairs={{0,16},{4,20},{8,24},{12,28},{16,0},{20,4},{24,8},{28,12},{1,17},{... | collective-permute-start | bytes 1781768 | tf_op jit(solution)/shard_map/ppermute | solution.py:420
  16.9 36.4 %collective-permute-start.12 = (bf16[2320,128]{1,0:T(8,128)(2,1)}, bf16[2320,128]{1,0:T(8,128)(2,1)}, u32[]{:S(2)}, u32[]{:S(2)}) collective-permute-start(bf16[2320,128]{1,0:T(8,128)(2,1)} %pack.1), channel_id=1, source_target_pairs={{0,3},{1,0},{2,1},{3,2},{4,7},{5,4},{6,5},{7,6},{8,11},{9,8},{10,9... | collective-permute-start | bytes 1781768 | tf_op jit(solution)/shard_map/ppermute | solution.py:423
  24.1 11.6 %copy-start.16 = (bf16[2320,128]{1,0:T(8,128)(2,1)S(1)}, bf16[2320,128]{1,0:T(8,128)(2,1)}, u32[]{:S(2)}) copy-start(bf16[2320,128]{1,0:T(8,128)(2,1)} %pack.1) | copy-start | bytes 1781764
  24.1 36.5 %copy-start.9 = (bf16[2,112,768]{2,1,0:T(8,128)(2,1)S(1)}, bf16[2,112,768]{2,1,0:T(8,128)(2,1)}, u32[]{:S(2)}) copy-start(bf16[2,112,768]{2,1,0:T(8,128)(2,1)} %param.16) | copy-start | bytes 1032196
  24.1 36.5 %copy-start.26 = (bf16[2,112,768]{2,1,0:T(8,128)(2,1)S(1)}, bf16[2,112,768]{2,1,0:T(8,128)(2,1)}, u32[]{:S(2)}) copy-start(bf16[2,112,768]{2,1,0:T(8,128)(2,1)} %param.18) | copy-start | bytes 1032196
  34.9 38.4 %copy-start.21 = (bf16[1,2320,128]{2,1,0:T(8,128)(2,1)}, bf16[1,2320,128]{2,1,0:T(8,128)(2,1)S(1)}, u32[]{:S(2)}) copy-start(bf16[1,2320,128]{2,1,0:T(8,128)(2,1)S(1)} %collective-permute-done.1) | copy-start | bytes 1781764
  34.9 18.4 %collective-permute-start.7 = (bf16[1,2320,128]{2,1,0:T(8,128)(2,1)}, bf16[1,2320,128]{2,1,0:T(8,128)(2,1)S(1)}, u32[]{:S(2)}, u32[]{:S(2)}) collective-permute-start(bf16[1,2320,128]{2,1,0:T(8,128)(2,1)} %bitcast.10), channel_id=1, source_target_pairs={{0,8},{4,12},{8,0},{12,4},{16,24},{20,28},{24,16},{28,20},{1,9},{5... | collective-permute-start | bytes 1781768 | tf_op jit(solution)/shard_map/ppermute | solution.py:420
  35.5 17.8 %collective-permute-start.8 = (bf16[1,2320,128]{2,1,0:T(8,128)(2,1)}, bf16[1,2320,128]{2,1,0:T(8,128)(2,1)S(1)}, u32[]{:S(2)}, u32[]{:S(2)}) collective-permute-start(bf16[1,2320,128]{2,1,0:T(8,128)(2,1)} %bitcast.10), channel_id=1, source_target_pairs={{0,16},{4,20},{8,24},{12,28},{16,0},{20,4},{24,8},{28,12},{1,17},{... | collective-permute-start | bytes 1781768 | tf_op jit(solution)/shard_map/ppermute | solution.py:420
  35.8 32.1 %collective-permute-start.2 = (bf16[2320,128]{1,0:T(8,128)(2,1)S(1)}, bf16[2320,128]{1,0:T(8,128)(2,1)}, u32[]{:S(2)}, u32[]{:S(2)}) collective-permute-start(bf16[2320,128]{1,0:T(8,128)(2,1)S(1)} %copy-done.16), channel_id=1, source_target_pairs={{0,2},{1,3},{2,0},{3,1},{4,6},{5,7},{6,4},{7,5},{8,10},{9,11},{10,... | collective-permute-start | bytes 1781768 | tf_op jit(solution)/shard_map/ppermute | solution.py:423
  53.3 20.1 %copy-start.19 = (bf16[1,2320,128]{2,1,0:T(8,128)(2,1)}, bf16[1,2320,128]{2,1,0:T(8,128)(2,1)S(1)}, u32[]{:S(2)}) copy-start(bf16[1,2320,128]{2,1,0:T(8,128)(2,1)S(1)} %collective-permute-done.8) | copy-start | bytes 1781764
  54.1 16.6 %collective-permute-start.13 = (bf16[1,2320,128]{2,1,0:T(8,128)(2,1)}, bf16[1,2320,128]{2,1,0:T(8,128)(2,1)}, u32[]{:S(2)}, u32[]{:S(2)}) collective-permute-start(bf16[1,2320,128]{2,1,0:T(8,128)(2,1)} %bitcast.11), channel_id=1, source_target_pairs={{0,8},{4,12},{8,0},{12,4},{16,24},{20,28},{24,16},{28,20},{1,9},{5... | collective-permute-start | bytes 1781768 | tf_op jit(solution)/shard_map/ppermute | solution.py:420
  54.7 17.7 %collective-permute-start.14 = (bf16[1,2320,128]{2,1,0:T(8,128)(2,1)}, bf16[1,2320,128]{2,1,0:T(8,128)(2,1)S(1)}, u32[]{:S(2)}, u32[]{:S(2)}) collective-permute-start(bf16[1,2320,128]{2,1,0:T(8,128)(2,1)} %bitcast.11), channel_id=1, source_target_pairs={{0,16},{4,20},{8,24},{12,28},{16,0},{20,4},{24,8},{28,12},{1,17},{... | collective-permute-start | bytes 1781768 | tf_op jit(solution)/shard_map/ppermute | solution.py:420
  55.9 17.5 %collective-permute-start.4 = (bf16[1,1168,128]{2,1,0:T(8,128)(2,1)}, bf16[1,1168,128]{2,1,0:T(8,128)(2,1)}, u32[]{:S(2)}, u32[]{:S(2)}) collective-permute-start(bf16[1,1168,128]{2,1,0:T(8,128)(2,1)} %slice.216), channel_id=1, source_target_pairs={{0,8},{4,12},{8,0},{12,4},{16,24},{20,28},{24,16},{28,20},{1,9},{5... | collective-permute-start | bytes 897032 | tf_op jit(solution)/shard_map/ppermute | solution.py:420
  59.1 13.7 %collective-permute-start.3 = (bf16[1,1152,128]{2,1,0:T(8,128)(2,1)}, bf16[1,1152,128]{2,1,0:T(8,128)(2,1)}, u32[]{:S(2)}, u32[]{:S(2)}) collective-permute-start(bf16[1,1152,128]{2,1,0:T(8,128)(2,1)} %slice.215), channel_id=1, source_target_pairs={{0,16},{4,20},{8,24},{12,28},{16,0},{20,4},{24,8},{28,12},{1,17},{... | collective-permute-start | bytes 884744 | tf_op jit(solution)/shard_map/ppermute | solution.py:420
  67.9 292.9 %reduce-scatter.3.cloned.1.call-start = ((), (), s32[]{:S(2)}) async-start(), calls=%async_computation.3 | async-start | bytes 1720320 | tf_op jit(solution)/shard_map/reduce_scatter | solution.py:955
  68.2 13.1 %collective-permute-start.10 = (bf16[1,1168,128]{2,1,0:T(8,128)(2,1)S(1)}, bf16[1,1168,128]{2,1,0:T(8,128)(2,1)S(1)}, u32[]{:S(2)}, u32[]{:S(2)}) collective-permute-start(bf16[1,1168,128]{2,1,0:T(8,128)(2,1)S(1)} %slice.223), channel_id=1, source_target_pairs={{0,8},{4,12},{8,0},{12,4},{16,24},{20,28},{24,16},{28,20},{1,9},{5... | collective-permute-start | bytes 897032 | tf_op jit(solution)/shard_map/ppermute | solution.py:420
  70.7 10.0 %collective-permute-start.9 = (bf16[1,1152,128]{2,1,0:T(8,128)(2,1)S(1)}, bf16[1,1152,128]{2,1,0:T(8,128)(2,1)S(1)}, u32[]{:S(2)}, u32[]{:S(2)}) collective-permute-start(bf16[1,1152,128]{2,1,0:T(8,128)(2,1)S(1)} %slice.222), channel_id=1, source_target_pairs={{0,16},{4,20},{8,24},{12,28},{16,0},{20,4},{24,8},{28,12},{1,17},{... | collective-permute-start | bytes 884744 | tf_op jit(solution)/shard_map/ppermute | solution.py:420
  72.3 10.5 %copy-start.23 = (bf16[1,2320,128]{2,1,0:T(8,128)(2,1)S(1)}, bf16[1,2320,128]{2,1,0:T(8,128)(2,1)}, u32[]{:S(2)}) copy-start(bf16[1,2320,128]{2,1,0:T(8,128)(2,1)} %copy-done.22) | copy-start | bytes 1781764
  72.3 21.1 %collective-permute-start.19 = (bf16[1,2320,128]{2,1,0:T(8,128)(2,1)}, bf16[1,2320,128]{2,1,0:T(8,128)(2,1)S(1)}, u32[]{:S(2)}, u32[]{:S(2)}) collective-permute-start(bf16[1,2320,128]{2,1,0:T(8,128)(2,1)} %bitcast.12), channel_id=1, source_target_pairs={{0,16},{4,20},{8,24},{12,28},{16,0},{20,4},{24,8},{28,12},{1,17},{... | collective-permute-start | bytes 1781768 | tf_op jit(solution)/shard_map/ppermute | solution.py:420
  72.8 20.6 %collective-permute-start.18 = (bf16[1,2320,128]{2,1,0:T(8,128)(2,1)}, bf16[1,2320,128]{2,1,0:T(8,128)(2,1)S(1)}, u32[]{:S(2)}, u32[]{:S(2)}) collective-permute-start(bf16[1,2320,128]{2,1,0:T(8,128)(2,1)} %bitcast.12), channel_id=1, source_target_pairs={{0,8},{4,12},{8,0},{12,4},{16,24},{20,28},{24,16},{28,20},{1,9},{5... | collective-permute-start | bytes 1781768 | tf_op jit(solution)/shard_map/ppermute | solution.py:420
  73.4 2.6 copy-start.18
  73.4 9.4 %copy-start.20 = (bf16[1,2320,128]{2,1,0:T(8,128)(2,1)S(1)}, bf16[1,2320,128]{2,1,0:T(8,128)(2,1)}, u32[]{:S(2)}) copy-start(bf16[1,2320,128]{2,1,0:T(8,128)(2,1)} %copy-done.19) | copy-start | bytes 1781764
  75.9 38.9 %copy-start.8 = (bf16[4,2320,128]{2,1,0:T(8,128)(2,1)}, bf16[4,2320,128]{2,1,0:T(8,128)(2,1)S(1)}, u32[]{:S(2)}) copy-start(bf16[4,2320,128]{2,1,0:T(8,128)(2,1)S(1)} %maximum_maximum_fusion.refs_0_) | copy-start | bytes 7127044
  75.9 38.9 %collective-permute-start.5 = (bf16[4,2320,128]{2,1,0:T(8,128)(2,1)S(1)}, bf16[4,2320,128]{2,1,0:T(8,128)(2,1)}, u32[]{:S(2)}, u32[]{:S(2)}) collective-permute-start(bf16[4,2320,128]{2,1,0:T(8,128)(2,1)S(1)} %maximum_maximum_fusion.refs_0_), channel_id=1, source_target_pairs={{0,4},{4,0},{8,12},{12,8},{16,20},{20,16},{24,28},{28,24},{1,5},{5... | collective-permute-start | bytes 7127048 | tf_op jit(solution)/shard_map/ppermute | solution.py:420
  80.7 19.2 %collective-permute-start.16 = (bf16[1,1168,128]{2,1,0:T(8,128)(2,1)S(1)}, bf16[1,1168,128]{2,1,0:T(8,128)(2,1)S(1)}, u32[]{:S(2)}, u32[]{:S(2)}) collective-permute-start(bf16[1,1168,128]{2,1,0:T(8,128)(2,1)S(1)} %slice.225), channel_id=1, source_target_pairs={{0,8},{4,12},{8,0},{12,4},{16,24},{20,28},{24,16},{28,20},{1,9},{5... | collective-permute-start | bytes 897032 | tf_op jit(solution)/shard_map/ppermute | solution.py:420
  81.3 17.1 %collective-permute-start.15 = (bf16[1,1152,128]{2,1,0:T(8,128)(2,1)S(1)}, bf16[1,1152,128]{2,1,0:T(8,128)(2,1)S(1)}, u32[]{:S(2)}, u32[]{:S(2)}) collective-permute-start(bf16[1,1152,128]{2,1,0:T(8,128)(2,1)S(1)} %slice.224), channel_id=1, source_target_pairs={{0,16},{4,20},{8,24},{12,28},{16,0},{20,4},{24,8},{28,12},{1,17},{... | collective-permute-start | bytes 884744 | tf_op jit(solution)/shard_map/ppermute | solution.py:420
  93.5 23.9 %collective-permute-start.11 = (bf16[4,2320,128]{2,1,0:T(8,128)(2,1)}, bf16[4,2320,128]{2,1,0:T(8,128)(2,1)}, u32[]{:S(2)}, u32[]{:S(2)}) collective-permute-start(bf16[4,2320,128]{2,1,0:T(8,128)(2,1)} %maximum_maximum_fusion.1.refs_2_), channel_id=1, source_target_pairs={{0,4},{4,0},{8,12},{12,8},{16,20},{20,16},{24,28},{28,24},{1,5},{5... | collective-permute-start | bytes 7127048 | tf_op jit(solution)/shard_map/ppermute | solution.py:420
  93.5 12.6 %collective-permute-start.21 = (bf16[1,1168,128]{2,1,0:T(8,128)(2,1)S(1)}, bf16[1,1168,128]{2,1,0:T(8,128)(2,1)S(1)}, u32[]{:S(2)}, u32[]{:S(2)}) collective-permute-start(bf16[1,1168,128]{2,1,0:T(8,128)(2,1)S(1)} %slice.227), channel_id=1, source_target_pairs={{0,8},{4,12},{8,0},{12,4},{16,24},{20,28},{24,16},{28,20},{1,9},{5... | collective-permute-start | bytes 897032 | tf_op jit(solution)/shard_map/ppermute | solution.py:420
  98.4 7.7 %collective-permute-start.20 = (bf16[1,1152,128]{2,1,0:T(8,128)(2,1)S(1)}, bf16[1,1152,128]{2,1,0:T(8,128)(2,1)S(1)}, u32[]{:S(2)}, u32[]{:S(2)}) collective-permute-start(bf16[1,1152,128]{2,1,0:T(8,128)(2,1)S(1)} %slice.226), channel_id=1, source_target_pairs={{0,16},{4,20},{8,24},{12,28},{16,0},{20,4},{24,8},{28,12},{1,17},{... | collective-permute-start | bytes 884744 | tf_op jit(solution)/shard_map/ppermute | solution.py:420
  104.5 6.1 %copy-start.36 = (s32[32]{0:T(128)S(1)}, s32[32]{0:T(128)}, u32[]{:S(2)}) copy-start(s32[32]{0:T(128)} %constant.135.clone) | copy-start | bytes 388
  104.5 6.3 %copy-start.39 = (s32[32]{0:T(128)S(1)}, s32[32]{0:T(128)}, u32[]{:S(2)}) copy-start(s32[32]{0:T(128)} %constant.154) | copy-start | bytes 388
  104.5 6.5 %copy-start.28 = (s32[2,448]{1,0:T(2,128)S(1)}, s32[2,448]{1,0:T(2,128)}, u32[]{:S(2)}) copy-start(s32[2,448]{1,0:T(2,128)} %param.19) | copy-start | bytes 10756
  104.5 8.1 %copy-start.29 = (s32[2,448]{1,0:T(2,128)S(1)}, s32[2,448]{1,0:T(2,128)}, u32[]{:S(2)}) copy-start(s32[2,448]{1,0:T(2,128)} %param.20) | copy-start | bytes 10756
  104.5 9.7 %copy-start.35 = (s32[64]{0:T(128)S(1)}, s32[64]{0:T(128)}, u32[]{:S(2)}) copy-start(s32[64]{0:T(128)} %param.21) | copy-start | bytes 772
  104.5 12.9 %collective-permute-start.17 = (bf16[4,2320,128]{2,1,0:T(8,128)(2,1)}, bf16[4,2320,128]{2,1,0:T(8,128)(2,1)}, u32[]{:S(2)}, u32[]{:S(2)}) collective-permute-start(bf16[4,2320,128]{2,1,0:T(8,128)(2,1)} %maximum_maximum_fusion.2.refs_4_), channel_id=1, source_target_pairs={{0,4},{4,0},{8,12},{12,8},{16,20},{20,16},{24,28},{28,24},{1,5},{5... | collective-permute-start | bytes 7127048 | tf_op jit(solution)/shard_map/ppermute | solution.py:420
  110.6 6.8 %collective-permute-start.22 = (bf16[4,2320,128]{2,1,0:T(8,128)(2,1)}, bf16[4,2320,128]{2,1,0:T(8,128)(2,1)}, u32[]{:S(2)}, u32[]{:S(2)}) collective-permute-start(bf16[4,2320,128]{2,1,0:T(8,128)(2,1)} %maximum_maximum_fusion.3.refs_6_), channel_id=1, source_target_pairs={{0,4},{4,0},{8,12},{12,8},{16,20},{20,16},{24,28},{28,24},{1,5},{5... | collective-permute-start | bytes 7127048 | tf_op jit(solution)/shard_map/ppermute | solution.py:420
  115.9 18.5 %copy-start.25 = (f32[19,768]{1,0:T(8,128)}, f32[19,768]{1,0:T(8,128)S(1)}, u32[]{:S(2)}) copy-start(f32[19,768]{1,0:T(8,128)S(1)} %reshape.344.vectors) | copy-start | bytes 175108
  150.7 3.8 copy-start.7
  154.5 3.9 slice-start.1
  155.9 8.8 %copy-start.3 = (f32[1,2,448,768]{3,2,1,0:T(8,128)}, f32[1,2,448,768]{3,2,1,0:T(8,128)S(1)}, u32[]{:S(2)}) copy-start(f32[1,2,448,768]{3,2,1,0:T(8,128)S(1)} %get-tuple-element.141) | copy-start | bytes 8257540
  156.4 8.3 %copy-start.12 = (bf16[896,768]{1,0:T(8,128)(2,1)}, bf16[896,768]{1,0:T(8,128)(2,1)S(1)}, u32[]{:S(2)}) copy-start(bf16[896,768]{1,0:T(8,128)(2,1)S(1)} %add_convert_fusion.4.n1) | copy-start | bytes 4128772
  164.7 12.6 %copy-start.4 = (f32[1,2,448,768]{3,2,1,0:T(8,128)S(1)}, f32[1,2,448,768]{3,2,1,0:T(8,128)}, u32[]{:S(2)}) copy-start(f32[1,2,448,768]{3,2,1,0:T(8,128)} %copy-done.3) | copy-start | bytes 8257540
  164.7 12.7 %copy-start.37 = (bf16[1024,768]{1,0:T(8,128)(2,1)S(1)}, bf16[1024,768]{1,0:T(8,128)(2,1)}, u32[]{:S(2)}) copy-start(bf16[1024,768]{1,0:T(8,128)(2,1)} %get-tuple-element.66) | copy-start | bytes 4718596
  182.0 3.7 copy-start.13
  295.2 6.0 %copy-start.2 = (f32[896,768]{1,0:T(8,128)S(1)}, f32[896,768]{1,0:T(8,128)}, u32[]{:S(2)}) copy-start(f32[896,768]{1,0:T(8,128)} %copy-done.1) | copy-start | bytes 8257540
  295.2 6.0 %copy-start.11 = (bf16[2,448,1024]{2,1,0:T(8,128)(2,1)S(1)}, bf16[2,448,1024]{2,1,0:T(8,128)(2,1)}, u32[]{:S(2)}) copy-start(bf16[2,448,1024]{2,1,0:T(8,128)(2,1)} %get-tuple-element.78) | copy-start | bytes 5505028
  301.2 3.8 copy-start.15
  307.2 2.8 copy-start.14
  317.1 6.0 %copy-start.5 = (bf16[2,448,768]{2,1,0:T(8,128)(2,1)S(1)}, bf16[2,448,768]{2,1,0:T(8,128)(2,1)}, u32[]{:S(2)}) copy-start(bf16[2,448,768]{2,1,0:T(8,128)(2,1)} %self_backward.1) | copy-start | bytes 4128772
  322.4 132.2 %reduce-scatter.5.cloned.1.call-start = ((), (), s32[]{:S(2)}) async-start(), calls=%async_computation.4 | async-start | bytes 5898240 | tf_op jit(solution)/shard_map/reduce_scatter | solution.py:940
  348.8 4.8 %collective-permute-start.23 = (bf16[4,2320,128]{2,1,0:T(8,128)(2,1)S(1)}, bf16[4,2320,128]{2,1,0:T(8,128)(2,1)}, u32[]{:S(2)}, u32[]{:S(2)}) collective-permute-start(bf16[4,2320,128]{2,1,0:T(8,128)(2,1)S(1)} %slice.239), channel_id=1, source_target_pairs={{0,4},{4,0},{8,12},{12,8},{16,20},{20,16},{24,28},{28,24},{1,5},{5... | collective-permute-start | bytes 7127048 | tf_op jit(solution)/shard_map/ppermute | solution.py:620
  357.5 19.9 %collective-permute-start.26 = (bf16[2,1168,128]{2,1,0:T(8,128)(2,1)}, bf16[2,1168,128]{2,1,0:T(8,128)(2,1)}, u32[]{:S(2)}, u32[]{:S(2)}) collective-permute-start(bf16[2,1168,128]{2,1,0:T(8,128)(2,1)} %slice.247), channel_id=1, source_target_pairs={{0,16},{4,20},{8,24},{12,28},{16,0},{20,4},{24,8},{28,12},{1,17},{... | collective-permute-start | bytes 1794056 | tf_op jit(solution)/shard_map/ppermute | solution.py:620
  360.0 15.6 %collective-permute-start.24 = (bf16[2,1152,128]{2,1,0:T(8,128)(2,1)}, bf16[2,1152,128]{2,1,0:T(8,128)(2,1)}, u32[]{:S(2)}, u32[]{:S(2)}) collective-permute-start(bf16[2,1152,128]{2,1,0:T(8,128)(2,1)} %pad_maximum_fusion.2), channel_id=1, source_target_pairs={{0,8},{4,12},{8,0},{12,4},{16,24},{20,28},{24,16},{28,20},{1,9},{5... | collective-permute-start | bytes 1769480 | tf_op jit(solution)/shard_map/ppermute | solution.py:620
  376.9 8.2 %collective-permute-start.25 = (bf16[1152,128]{1,0:T(8,128)(2,1)S(1)}, bf16[1152,128]{1,0:T(8,128)(2,1)S(1)}, u32[]{:S(2)}, u32[]{:S(2)}) collective-permute-start(bf16[1152,128]{1,0:T(8,128)(2,1)S(1)} %fusion.14), channel_id=1, source_target_pairs={{0,16},{4,20},{8,24},{12,28},{16,0},{20,4},{24,8},{28,12},{1,17},{... | collective-permute-start | bytes 884744 | tf_op jit(solution)/shard_map/ppermute | solution.py:620
  378.6 8.0 %collective-permute-start.27 = (bf16[1168,128]{1,0:T(8,128)(2,1)S(1)}, bf16[1168,128]{1,0:T(8,128)(2,1)S(1)}, u32[]{:S(2)}, u32[]{:S(2)}) collective-permute-start(bf16[1168,128]{1,0:T(8,128)(2,1)S(1)} %fusion.13), channel_id=1, source_target_pairs={{0,8},{4,12},{8,0},{12,4},{16,24},{20,28},{24,16},{28,20},{1,9},{5... | collective-permute-start | bytes 897032 | tf_op jit(solution)/shard_map/ppermute | solution.py:620
  386.7 67.2 %collective-permute-start.28 = (f32[16,128]{1,0:T(8,128)S(1)}, f32[16,128]{1,0:T(8,128)S(1)}, u32[]{:S(2)}, u32[]{:S(2)}) collective-permute-start(f32[16,128]{1,0:T(8,128)S(1)} %slice.250), channel_id=1, source_target_pairs={{0,1},{1,2},{2,3},{3,0},{4,5},{5,6},{6,7},{7,4},{8,9},{9,10},{10,1... | collective-permute-start | bytes 24584 | tf_op jit(solution)/shard_map/ppermute | solution.py:993
  386.8 67.2 %collective-permute-start.29 = (f32[16,128]{1,0:T(8,128)S(1)}, f32[16,128]{1,0:T(8,128)S(1)}, u32[]{:S(2)}, u32[]{:S(2)}) collective-permute-start(f32[16,128]{1,0:T(8,128)S(1)} %slice.250), channel_id=1, source_target_pairs={{0,2},{1,3},{2,0},{3,1},{4,6},{5,7},{6,4},{7,5},{8,10},{9,11},{10,... | collective-permute-start | bytes 24584 | tf_op jit(solution)/shard_map/ppermute | solution.py:993
  391.8 62.1 %collective-permute-start.30 = (f32[16,128]{1,0:T(8,128)S(1)}, f32[16,128]{1,0:T(8,128)S(1)}, u32[]{:S(2)}, u32[]{:S(2)}) collective-permute-start(f32[16,128]{1,0:T(8,128)S(1)} %slice.250), channel_id=1, source_target_pairs={{0,3},{1,0},{2,1},{3,2},{4,7},{5,4},{6,5},{7,6},{8,11},{9,8},{10,9... | collective-permute-start | bytes 24584 | tf_op jit(solution)/shard_map/ppermute | solution.py:993
  415.6 38.3 %copy-start.27 = (f32[1824]{0:T(1024)S(1)}, f32[1824]{0:T(1024)}, u32[]{:S(2)}) copy-start(f32[1824]{0:T(1024)} %param.27) | copy-start | bytes 21892
  415.6 38.3 %copy-start.32 = (f32[1824]{0:T(1024)S(1)}, f32[1824]{0:T(1024)}, u32[]{:S(2)}) copy-start(f32[1824]{0:T(1024)} %param.28) | copy-start | bytes 21892
  415.6 38.4 %copy-start.33 = (f32[1824]{0:T(1024)S(1)}, f32[1824]{0:T(1024)}, u32[]{:S(2)}) copy-start(f32[1824]{0:T(1024)} %param.29) | copy-start | bytes 21892
  (12 other events, 17.5 us)
Sparse Core Ops, SparseCore 0:
  68.0 56.9 all-gather.1
  322.5 33.5 reduce-scatter.2
  358.5 84.6 reduce-scatter.4

commit v5 on v4

--- a/solution.py
+++ b/solution.py
@@ -205,7 +205,7 @@
 
 
 def cross_forward_kernel(query, key, value, out, logs, *, heads, chunk):
-    out[0], logs[0, 0] = forward_heads(query[0], key[0], value[0], None, heads, chunk)
+    out[0], logs[0, 0] = forward_heads(query[0], key[0, 0], value[0, 0], None, heads, chunk)
 
 
 def self_forward_kernel(query, key, value, seg_col, seg_row, stamp_row, out, logs, *, heads, chunk):
@@ -276,7 +276,7 @@
     rank, query, key, value, grad, mixed, logs, grad_query, grad_key, grad_value, probs_ref, scores_ref, *, heads, chunk
 ):
     grad_query[0] = backward_heads(
-        query[0], key[0], value[0], grad[0], mixed[0], logs[0, 0], None, heads, chunk, probs_ref, scores_ref
+        query[0], key[0, 0], value[0, 0], grad[0], mixed[0], logs[0, 0], None, heads, chunk, probs_ref, scores_ref
     )
 
     @pl.when(pl.program_id(1) == rank[0])
@@ -301,6 +301,10 @@
 
 def slot_spec(rows, offset):
     return pl.BlockSpec((1, rows, SLOT), lambda b, r: (b, 0, offset + r))
+
+
+def major_spec(rows, offset):
+    return pl.BlockSpec((1, 1, rows, SLOT), lambda b, r: (offset + r, b, 0, 0))
 
 
 def self_forward(qkv, seg_col, seg_row, stamp_row, ranks, heads, chunk=448):
@@ -323,11 +327,11 @@
 
 def cross_forward(queries, keys_values, ranks, heads, chunk=448):
     seqs, rows, _ = queries.shape
-    frames = keys_values.shape[1]
+    frames = keys_values.shape[2]
     return pl.pallas_call(
         functools.partial(cross_forward_kernel, heads=heads, chunk=chunk),
         grid=(seqs, ranks),
-        in_specs=[slot_spec(rows, 0), slot_spec(frames, 0), slot_spec(frames, ranks)],
+        in_specs=[slot_spec(rows, 0), major_spec(frames, 0), major_spec(frames, ranks)],
         out_specs=[slot_spec(rows, 0), pl.BlockSpec((1, 1, 8, rows), lambda b, r: (b, r, 0, 0))],
         out_shape=[
             jax.ShapeDtypeStruct((seqs, rows, ranks * SLOT), jnp.bfloat16),
@@ -344,7 +348,7 @@
 
 def cross_backward(rank, queries, keys_values, grads, mixed, logs, ranks, heads, chunk=512):
     seqs, rows, _ = queries.shape
-    frames = keys_values.shape[1]
+    frames = keys_values.shape[2]
     kept = pl.BlockSpec((1, frames, SLOT), lambda b, r, rank: (b, 0, 0))
     bf = jnp.bfloat16
     return pl.pallas_call(
@@ -353,7 +357,8 @@
             num_scalar_prefetch=1,
             grid=(seqs, ranks),
             in_specs=[
-                ranked_spec(rows, 0), ranked_spec(frames, 0), ranked_spec(frames, ranks), ranked_spec(rows, 0), ranked_spec(rows, 0),
+                ranked_spec(rows, 0), pl.BlockSpec((1, 1, frames, SLOT), lambda b, r, rank: (r, b, 0, 0)),
+                pl.BlockSpec((1, 1, frames, SLOT), lambda b, r, rank: (ranks + r, b, 0, 0)), ranked_spec(rows, 0), ranked_spec(rows, 0),
                 pl.BlockSpec((1, 1, 8, rows), lambda b, r, rank: (b, r, 0, 0)),
             ],
             out_specs=[ranked_spec(rows, 0), kept, kept],
@@ -446,8 +451,8 @@
 
 
 def assemble_kernel(target, *refs, sources, own_tiles, tile_rows):
-    ins, outs = refs[:sources], refs[sources : sources + 7]
-    staging, (f_qkv, f_ckv, f_cq, f_wo, f_co, f_in, f_out), arrived, sent = refs[sources + 7], refs[sources + 8 : -2], refs[-2], refs[-1]
+    ins, outs = refs[:sources], refs[sources : sources + 13]
+    staging, (f_qkv, f_ckv, f_cq, f_wo, f_co, *f_wide), arrived, sent = refs[sources + 13], refs[sources + 14 : -2], refs[-2], refs[-1]
     side = tile_rows * 2 // 3
     half = side // 2
     at = 0
@@ -509,14 +514,12 @@
     send(3, f_wo)
     padded_rows(f_co, 28)
     send(4, f_co)
-    for rank in range(4):
-        for i in range(4):
-            f_in[i * side : (i + 1) * side, rank * 4 * side : (rank + 1) * 4 * side] = joined(rank, 32 + 4 * i)
-    send(5, f_in)
-    for rank in range(4):
-        for i in range(4):
-            f_out[(rank * 4 + i) * side : (rank * 4 + i + 1) * side, :] = joined(rank, 48 + 4 * i)
-    send(6, f_out)
+    for m, base in enumerate((32, 48)):
+        for rank in range(4):
+            held = f_wide[m * 4 + rank]
+            for i in range(4):
+                held[i * side : (i + 1) * side] = joined(rank, base + 4 * i)
+            send(5 + m * 4 + rank, held)
     for copy in copies:
         copy.wait()
 
@@ -527,8 +530,7 @@
     bf = jnp.bfloat16
     shapes = [
         (width, 12 * SLOT), (width, 8 * SLOT), (width, 4 * SLOT), (4 * SLOT, width), (4 * SLOT, width),
-        (width, 4 * width), (4 * width, width),
-    ]
+    ] + [(width, width)] * 8
     anywhere = pl.BlockSpec(memory_space=pl.ANY)
     return pl.pallas_call(
         functools.partial(assemble_kernel, sources=len(arrays), own_tiles=own_tiles, tile_rows=tile_rows),
@@ -536,10 +538,10 @@
             num_scalar_prefetch=1,
             grid=(1,),
             in_specs=[anywhere] * len(arrays),
-            out_specs=[anywhere] * 7,
+            out_specs=[anywhere] * 13,
             scratch_shapes=[pltpu.VMEM((256, tile_rows, LANES), bf)]
             + [pltpu.VMEM(shape, bf) for shape in shapes]
-            + [pltpu.SemaphoreType.DMA, pltpu.SemaphoreType.DMA((7,))],
+            + [pltpu.SemaphoreType.DMA, pltpu.SemaphoreType.DMA((13,))],
         ),
         out_shape=[jax.ShapeDtypeStruct(shape, bf) for shape in shapes],
         compiler_params=pltpu.CompilerParams(vmem_limit_bytes=56 * 2**20),
@@ -548,8 +550,22 @@
 
 
 def weight_grads_kernel(
-    rank, slot, sub, n1, dqkv, n2, dcq, frames, dk, dv, attended, b1, mixed, b2, n3, grad_up, active, b3, lines, out, *, side
+    rank, slot, sub, *refs, side, owned
 ):
+    sources, lines, out, held, arrived = refs[: len(owned)], refs[len(owned)], refs[len(owned) + 1], refs[len(owned) + 2 : -1], refs[-1]
+    copies = []
+    for i, (source, to, own) in enumerate(zip(sources, held, owned)):
+        if own:
+            wide = to.shape[-1]
+            source = source.at[:, pl.ds(pl.multiple_of(rank[0] * wide, LANES), wide)]
+        copies.append(pltpu.make_async_copy(source, to, arrived.at[i]))
+        copies[-1].start()
+
+    def take(*which):
+        for i in which:
+            copies[i].wait()
+        return [held[i] for i in which]
+
     half = side // 2
     tile_rows = side + half
 
@@ -570,45 +586,46 @@
             for j in range(4):
                 keep(made[i * side : (i + 1) * side, j * side : (j + 1) * side], base + i * 4 + j)
 
-    slots(bdot(n1[...], dqkv[...], TN), (0, 4, 8))
-    slots(bdot(n2[...], dcq[...], TN), (12,))
+    n3, grad_up = take(0, 1)
+    grid_of(bdot(n3[...], grad_up[...], TN), 32, 4)
+    active, b3 = take(2, 3)
+    grid_of(bdot(active[...], b3[...], TN), 48, 4)
+    mixed, b2 = take(4, 5)
+    grid_of(bdot(mixed[...], b2[...], TN), 28, 1)
+    frames, dk, dv = take(6, 7, 8)
     slots(bdot(frames[0], dk[0], TN) + bdot(frames[1], dk[1], TN), (16,))
     slots(bdot(frames[0], dv[0], TN) + bdot(frames[1], dv[1], TN), (20,))
+    n2, dcq = take(9, 10)
+    slots(bdot(n2[...], dcq[...], TN), (12,))
+    attended, b1 = take(11, 12)
     grid_of(bdot(attended[...], b1[...], TN), 24, 1)
-    grid_of(bdot(mixed[...], b2[...], TN), 28, 1)
-    grid_of(bdot(n3[...], grad_up[...], TN), 32, 4)
-    grid_of(bdot(active[...], b3[...], TN), 48, 4)
+    n1, dqkv = take(13, 14)
+    slots(bdot(n1[...], dqkv[...], TN), (0, 4, 8))
     for i in range(out.shape[0]):
         out[i, out.shape[1] - lines.shape[1] :] = lines[i].astype(jnp.bfloat16)
 
 
 def weight_grads(rank, slot, sub, side, groups, own_tiles, lines, n1, dqkv, n2, dcq, frames, dk, dv, attended, b1, mixed, b2, n3, grad_up, active, b3):
-    def whole(x):
-        return pl.BlockSpec(x.shape, lambda i, rank, slot, sub: (0,) * x.ndim)
-
-    def own(x, width):
-        return pl.BlockSpec((x.shape[0], width), lambda i, rank, slot, sub: (0, rank[0]))
-
-    def fitted(x):
-        return own(x, 4 * side) if x.shape[1] > 4 * side else whole(x)
-
+    wide = 4 * side
+    inputs = [n3, grad_up, active, b3, mixed, b2, frames, dk, dv, n2, dcq, attended, b1, n1, dqkv]
+    widths = [0, wide, wide, 0, SLOT, 0, 0, 0, 0, 0, SLOT, SLOT, 0, 0, 0]
+    owned = [0 < size < x.shape[-1] for x, size in zip(inputs, widths)]
+    shapes = [(x.shape[0], size) if own else x.shape for x, size, own in zip(inputs, widths, owned)]
     shape = (groups, own_tiles * (side + side // 2) + lines.shape[1], LANES)
     return pl.pallas_call(
-        functools.partial(weight_grads_kernel, side=side),
+        functools.partial(weight_grads_kernel, side=side, owned=owned),
         grid_spec=pltpu.PrefetchScalarGridSpec(
             num_scalar_prefetch=3,
             grid=(1,),
-            in_specs=[
-                whole(n1), whole(dqkv), whole(n2), own(dcq, SLOT), whole(frames), whole(dk), whole(dv),
-                own(attended, SLOT), whole(b1), own(mixed, SLOT), whole(b2), whole(n3),
-                fitted(grad_up), fitted(active), whole(b3), whole(lines),
-            ],
+            in_specs=[pl.BlockSpec(memory_space=pl.ANY)] * len(inputs)
+            + [pl.BlockSpec(lines.shape, lambda i, rank, slot, sub: (0, 0, 0))],
             out_specs=pl.BlockSpec(shape, lambda i, rank, slot, sub: (0, 0, 0)),
+            scratch_shapes=[pltpu.VMEM(size, jnp.bfloat16) for size in shapes] + [pltpu.SemaphoreType.DMA((len(inputs),))],
         ),
         out_shape=jax.ShapeDtypeStruct(shape, jnp.bfloat16),
         compiler_params=pltpu.CompilerParams(vmem_limit_bytes=60 * 2**20),
         name="weight_grads",
-    )(rank, slot, sub, n1, dqkv, n2, dcq, frames, dk, dv, attended, b1, mixed, b2, n3, grad_up, active, b3, lines)
+    )(rank, slot, sub, *inputs, lines)
 
 
 def scatter_blocks(blocks, ranks, groups):
@@ -633,14 +650,14 @@
 def first_back_kernel(rank, dqkv, query_weight, key_weight, value_weight, hidden, out, sums):
     weights = jnp.concatenate([query_weight[...], key_weight[...], value_weight[...]], axis=1)
     made = bdot(dqkv[...], weights, NT)
-    unit, _ = unit_rows(hidden[...])
+    unit, _ = unit_rows(hidden[0].astype(jnp.float32))
     sums[0:1] = jnp.sum(made * unit, axis=0, keepdims=True)
     sums[1:2] = jnp.sum(made, axis=0, keepdims=True)
     out[...] = made.astype(jnp.bfloat16)
 
 
 def first_back(rank, dqkv, weight, hidden, ranks):
-    tokens, width = hidden.shape
+    _, tokens, width = hidden.shape
     own = lambda offset: pl.BlockSpec((width, SLOT), lambda i, rank: (0, offset + rank[0]))
     whole = lambda shape: pl.BlockSpec(shape, lambda i, rank: (0, 0))
     return pl.pallas_call(
@@ -648,7 +665,7 @@
         grid_spec=pltpu.PrefetchScalarGridSpec(
             num_scalar_prefetch=1,
             grid=(1,),
-            in_specs=[whole(dqkv.shape), own(0), own(ranks), own(2 * ranks), whole(hidden.shape)],
+            in_specs=[whole(dqkv.shape), own(0), own(ranks), own(2 * ranks), pl.BlockSpec((1, tokens, width), lambda i, rank: (0, 0, 0))],
             out_specs=[whole((tokens, width)), whole((2, width))],
         ),
         out_shape=[jax.ShapeDtypeStruct((tokens, width), jnp.bfloat16), jax.ShapeDtypeStruct((2, width), jnp.float32)],
@@ -658,25 +675,27 @@
 
 
 def frames_kernel(frames, weight, bias, out):
-    out[0] = (bdot(frames[0], weight[...], NN) + bias[...]).astype(jnp.bfloat16)
+    for i in range(out.shape[0]):
+        span = slice(i * SLOT, (i + 1) * SLOT)
+        out[i, 0] = (bdot(frames[0], weight[:, span], NN) + bias[i]).astype(jnp.bfloat16)
 
 
 def frame_projection(frames, weight, bias):
     seqs, count, width = frames.shape
-    total = weight.shape[1]
+    slots = weight.shape[1] // SLOT
     return pl.pallas_call(
         frames_kernel,
-        grid=(seqs, total // 512),
+        grid=(seqs, slots // 4),
         in_specs=[
             pl.BlockSpec((1, count, width), lambda b, c: (b, 0, 0)),
-            pl.BlockSpec((width, 512), lambda b, c: (0, c)),
-            pl.BlockSpec((1, 512), lambda b, c: (0, c)),
+            pl.BlockSpec((width, 4 * SLOT), lambda b, c: (0, c)),
+            pl.BlockSpec((4, 1, SLOT), lambda b, c: (c, 0, 0)),
         ],
-        out_specs=pl.BlockSpec((1, count, 512), lambda b, c: (b, 0, c)),
-        out_shape=jax.ShapeDtypeStruct((seqs, count, total), jnp.bfloat16),
+        out_specs=pl.BlockSpec((4, 1, count, SLOT), lambda b, c: (c, b, 0, 0)),
+        out_shape=jax.ShapeDtypeStruct((slots, seqs, count, SLOT), jnp.bfloat16),
         compiler_params=pltpu.CompilerParams(vmem_limit_bytes=VM),
         name="frame_projection",
-    )(frames, weight, bias[None])
+    )(frames, weight, bias.reshape(slots, 1, SLOT))
 
 
 def frames_back_kernel(rank, dk, dv, key_weight, value_weight, out, *, parts):
@@ -750,13 +769,14 @@
     return value * level, level + value * bell * 0.3989422804014327
 
 
-def middle_kernel(
-    rank, mixed, first_sum, top_grad, c_o, w_in, w_out, vectors, inner_bias,
-    block_out, grad_out, grad_mixed, n3_out, b2_out, b3_out, active_out, up_out, sums, up_sums, acts, slopes, ups,
-):
+def middle_kernel(rank, *refs, parts):
+    mixed, first_sum, top_grad, vectors, inner_bias, c_o = refs[:6]
+    w_in, w_out = refs[6 : 6 + parts], refs[6 + parts : 6 + 2 * parts]
+    (
+        block_out, grad_out, grad_mixed, n3_out, b2_out, b3_out, active_out, up_out, sums, up_sums, acts, slopes, ups,
+    ) = refs[6 + 2 * parts :]
     f32, bf16 = jnp.float32, jnp.bfloat16
     width = first_sum.shape[1]
-    parts = acts.shape[0]
     row = lambda i: vectors[i : i + 1]
     cut = lambda i: slice(i * width, (i + 1) * width)
     fold = lambda values: jnp.sum(values, axis=0, keepdims=True)
@@ -771,23 +791,23 @@
     n3_out[...] = n3
     third_sum = second_sum + row(10)
     for i in range(parts):
-        value, slope = gelu_pair(bdot(n3, w_in[:, cut(i)], NN) + inner_bias[:, cut(i)])
+        value, slope = gelu_pair(bdot(n3, w_in[i][...], NN) + inner_bias[:, cut(i)])
         acts[i] = value.astype(bf16)
         slopes[i] = slope.astype(bf16)
-        third_sum = third_sum + bdot(acts[i], w_out[cut(i)], NN)
+        third_sum = third_sum + bdot(acts[i], w_out[i][...], NN)
     active_out[...] = acts[rank[0]]
     last, last_inverse = unit_rows(third_sum)
     block_out[...] = last * row(6) + row(7)
-    grads = top_grad[...].astype(f32)
+    grads = top_grad[0].astype(f32)
     grad_third = back(last, last_inverse, grads * row(6))
     b3 = grad_third.astype(bf16)
     b3_out[...] = b3
     grad_normed, ups_now = None, []
     for i in range(parts):
-        grad_up = (bdot(b3, w_out[cut(i)], NT) * slopes[i].astype(f32)).astype(bf16)
+        grad_up = (bdot(b3, w_out[i][...], NT) * slopes[i].astype(f32)).astype(bf16)
         ups[i] = grad_up
         ups_now.append(fold(grad_up.astype(f32)))
-        term = bdot(grad_up, w_in[:, cut(i)], NT)
+        term = bdot(grad_up, w_in[i][...], NT)
         grad_normed = term if grad_normed is None else grad_normed + term
     up_out[...] = ups[rank[0]]
     grad_second = grad_third + back(unit, inverse, grad_normed * row(4))
@@ -816,23 +836,22 @@
         up_sums[...] += ups_all
 
 
-def middle(rank, mixed, first_sum, top_grad, c_o, w_in, w_out, vectors, inner_bias, block=224):
+def middle(rank, mixed, first_sum, top_grad, c_o, w_in, w_out, vectors, inner_bias, block=448):
     f32, bf16 = jnp.float32, jnp.bfloat16
     tokens, width = first_sum.shape
-    slots, hidden = mixed.shape[1], w_in.shape[1]
-    parts = hidden // width
+    slots, parts = mixed.shape[1], len(w_in)
     rows = lambda size: pl.BlockSpec((block, size), lambda i, rank: (i, 0))
     once = lambda x: pl.BlockSpec(x.shape, lambda i, rank: (0, 0), pipeline_mode=pl.Buffered(1))
     total = lambda count: pl.BlockSpec((count, width), lambda i, rank: (0, 0))
     out = lambda size, kind: jax.ShapeDtypeStruct((tokens, size), kind)
-    return pl.pallas_call(
-        middle_kernel,
+    fixed = [vectors, inner_bias, c_o, *w_in, *w_out]
+    return pl.pallas_call(
+        functools.partial(middle_kernel, parts=parts),
         grid_spec=pltpu.PrefetchScalarGridSpec(
             num_scalar_prefetch=1,
             grid=(tokens // block,),
-            in_specs=[
-                rows(slots), rows(width), rows(width), once(c_o), once(w_in), once(w_out), once(vectors), once(inner_bias),
-            ],
+            in_specs=[rows(slots), rows(width), pl.BlockSpec((1, block, width), lambda i, rank: (1, i, 0))]
+            + [once(x) for x in fixed],
             out_specs=[rows(width), rows(width), rows(slots)] + [rows(width)] * 5 + [total(8), total(parts)],
             scratch_shapes=[pltpu.VMEM((parts, block, width), bf16)] * 3,
         ),
@@ -841,7 +860,30 @@
         + [jax.ShapeDtypeStruct((8, width), f32), jax.ShapeDtypeStruct((parts, width), f32)],
         compiler_params=pltpu.CompilerParams(vmem_limit_bytes=VM),
         name="middle",
-    )(rank, mixed, first_sum, top_grad, c_o, w_in, w_out, vectors, inner_bias)
+    )(rank, mixed, first_sum, top_grad, *fixed)
+
+
+def first_kernel(hidden, vectors, bias, weight, n1, out):
+    made = (unit_rows(hidden[0].astype(jnp.float32))[0] * vectors[0:1] + vectors[1:2]).astype(jnp.bfloat16)
+    n1[...] = made
+    for low in range(0, weight.shape[1], 4 * SLOT):
+        span = slice(low, low + 4 * SLOT)
+        out[:, span] = (bdot(made, weight[:, span], NN) + bias[:, span]).astype(jnp.bfloat16)
+
+
+def first_projections(both, vectors, bias, weight, block=448):
+    _, tokens, width = both.shape
+    wide = weight.shape[1]
+    once = lambda x: pl.BlockSpec(x.shape, lambda i: (0, 0), pipeline_mode=pl.Buffered(1))
+    return pl.pallas_call(
+        first_kernel,
+        grid=(tokens // block,),
+        in_specs=[pl.BlockSpec((1, block, width), lambda i: (0, i, 0)), once(vectors), once(bias), once(weight)],
+        out_specs=[pl.BlockSpec((block, width), lambda i: (i, 0)), pl.BlockSpec((block, wide), lambda i: (i, 0))],
+        out_shape=[jax.ShapeDtypeStruct((tokens, width), jnp.bfloat16), jax.ShapeDtypeStruct((tokens, wide), jnp.bfloat16)],
+        compiler_params=pltpu.CompilerParams(vmem_limit_bytes=VM),
+        name="first_projections",
+    )(both, vectors, bias, weight)
 
 
 def spread_heads(rows, ranks):
@@ -892,13 +934,15 @@
     spot = (source_group[:, None] * own_tiles + jnp.arange(own_tiles, dtype=jnp.int32)[None]).reshape(-1)
     ident = jnp.sum(jnp.where(spot[:, None] == position[None, :], owner_list[None, :], 0), axis=1)
     target = jnp.repeat(source_rank, own_tiles) * count + ident
-    w_qkv, c_kv, c_q, w_o, c_o, w_in, w_out = assemble(target, arrays, own_tiles, side)
+    w_qkv, c_kv, c_q, w_o, c_o, *wide = assemble(target, arrays, own_tiles, side)
+    w_in, w_out = wide[:4], wide[4:]
 
     rows_in = jnp.stack([hidden_in, cotangent])
     if where is not None:
         rows_in, _ = lax.optimization_barrier((rows_in, last))
     both = lax.all_gather(rows_in, "tensor", axis=2, tiled=True)
-    hidden = both[0].reshape(tokens, width).astype(f32)
+    both = both.reshape(2, tokens, width)
+    hidden = both[0].astype(f32)
 
     head_bias = spread_heads(vectors[11:15], ranks)
     none = jnp.zeros_like(head_bias[0])
@@ -916,8 +960,8 @@
         return lax.dynamic_slice_in_dim(split(values), rank * local_rows, local_rows, axis=1)
 
     keys_values = frame_projection(frames, c_kv, jnp.concatenate([none, head_bias[3]]))
-    n1 = normalize(hidden, vectors[0], vectors[1]).astype(bf16)
-    qkv = split((product(n1, w_qkv) + jnp.concatenate([head_bias[0], none, head_bias[1]])).astype(bf16))
+    n1, qkv = first_projections(both, vectors, jnp.concatenate([head_bias[0], none, head_bias[1]])[None], w_qkv)
+    qkv = split(qkv)
     attended, self_logs = self_forward(qkv, seg_col, seg_row, stamp_row, ranks, heads)
     attended = flat(attended)
     first_sum = hidden + product(attended, w_o) + vectors[8]
@@ -925,9 +969,8 @@
     cross_queries = split((product(n2, c_q) + head_bias[2]).astype(bf16))
     mixed, cross_logs = cross_forward(cross_queries, keys_values, ranks, heads)
     mixed = flat(mixed)
-    top_grad = both[1].reshape(tokens, width)
     out_rows, grad_second, grad_mixed, n3, b2, b3, active, grad_up, sums, up_sum = middle(
-        rank_ref, mixed, first_sum, top_grad, c_o, w_in, w_out, vectors, inner_bias[None]
+        rank_ref, mixed, first_sum, both, c_o, w_in, w_out, vectors, inner_bias[None]
     )
     block_out = own_rows(out_rows)
     grad_mixed = split(grad_mixed)
@@ -951,7 +994,7 @@
         )
     )
 
-    part_one, first_sums = first_back(rank_ref, dqkv, w_qkv, hidden, ranks)
+    part_one, first_sums = first_back(rank_ref, dqkv, w_qkv, both, ranks)
     grad_one = lax.psum_scatter(split(part_one), "tensor", scatter_dimension=1, tiled=True).astype(f32)
     back, _, _ = normalize_back(
         hidden_in.astype(f32).reshape(-1, width), vectors[0], grad_one.reshape(-1, width)
@@ -989,12 +1032,16 @@
     )
     owned = scatter_blocks(blocks, ranks, groups)
     line = owned[-line_rows:]
-    turns = [[(i, (i + step) % ranks) for i in range(ranks)] for step in range(1, ranks)]
-    vector_grad = (line + sum(lax.ppermute(line, "tensor", turn) for turn in turns)).reshape(-1)[:length]
-
     new_first, new_second, new_master, new_stats, new_bases = soap(
         owned, master_tiles[0], tile_first[0], tile_second[0], tile_stats[0], tile_bases[0], *ready
     )
+    reach = 1
+    while reach < ranks:
+        other = lax.ppermute(line, "tensor", [(i, i ^ reach) for i in range(ranks)])
+        other, _ = lax.optimization_barrier((other, new_second if reach == 1 else new_bases))
+        line = line + other
+        reach *= 2
+    vector_grad = line.reshape(-1)[:length]
     new_vector_first = beta_one * vector_first + (1.0 - beta_one) * vector_grad
     new_vector_second = beta_two * vector_second + (1.0 - beta_two) * vector_grad * vector_grad
     new_vectors = master_vectors - rate_vectors * (new_vector_first / (1.0 - beta_one**STEP)) / (

time: 469 us -> 457 us (0.974)
  matrix products: 18.9 us -> 11.2 us
    dot_general x3 -> x2, matrix products: 12.3 us -> 4.59 us  [product(): return jnp.dot(left_part, right_part, preferred_element_type=jnp.float32)]
    pallas_call x3 -> x4, Pallas kernels: 81.3 us -> 84.6 us  [the longest x1 42.6 us: middle(): pl.pallas_call(functools.partial(middle_kernel, parts=parts), grid_spec=p...]
    unnamed x96 -> x90, local copies, waits for them, and re-layouts: 16.5 us -> 15.5 us
  transfers between devices with their start and end apart: 34 -> 33, of which waited for: 9 -> 9; matrix products, arithmetic and copies ran while one was open for 12% -> 12% of each run, Pallas kernels for 25% -> 26%
where the time goes in v5:
time: 457 us; the launch traced here: 453 us
  Pallas kernels  263 us (58%)
  starting transfers between devices  48.6 us (11%)
  waiting for transfers between devices  44.9 us (10%)
  other arithmetic  39.4 us (9%)
  local copies, waits for them, and re-layouts  31.4 us (7%)
  between operations  14.7 us (3%)
  matrix products  11.2 us (2%)
    pallas_call x1, Pallas kernels, middle(): pl.pallas_call(functools.partial(middle_kernel, parts=parts), grid_spec=p...  42.6 us
    pallas_call x1, Pallas kernels, chol_bases(): pl.pallas_call(functools.partial(chol_kernel, block=block, unroll=unroll,...  38.6 us
    pallas_call x1, Pallas kernels, cross_backward(): pl.pallas_call(functools.partial(cross_backward_kernel, heads=heads, chun...  37.2 us
    pallas_call x1, Pallas kernels, cross_forward(): pl.pallas_call(functools.partial(cross_forward_kernel, heads=heads, chunk...  25.2 us
    ppermute x3, starting transfers between devices, turn(): lax.ppermute(values, 'tensor', [(i, (i + step) % ranks) for i in range(ra...  22.7 us
    ppermute x5, waiting for transfers between devices, sent(): lax.ppermute(values.astype(bf16), 'dp', [(i, i ^ bits) for i in range(gro...  21.9 us
    pallas_call x1, Pallas kernels, soap_main(): pl.pallas_call(soap_main_kernel, grid=(n,), in_specs=[pl.BlockSpec((side...  17.7 us
    pallas_call x1, Pallas kernels, weight_grads(): pl.pallas_call(functools.partial(weight_grads_kernel, side=side, owned=ow...  17.3 us
  transfers between devices with their start and end apart: 33, of which 9 were waited for; matrix products, arithmetic and copies ran while one was open for 12% of the time, Pallas kernels for 26%

profile of v5, /device:TPU:0, one launch (start us, length us, event | category | flops | bytes accessed | tf_op | source)
XLA Modules:
  0.0 453.2 jit_solution(7910020861132988795)
XLA Ops:
  7.2 1.3 pad_bitcast_fusion.1.line
  8.5 2.3 pack.1
  10.9 3.0 collective-permute-start.6
  13.9 1.5 collective-permute-start
  15.4 1.5 collective-permute-start.1
  16.9 2.2 collective-permute-start.12
  19.2 5.1 %copy.39.frames.refs_6_ = bf16[2,1500,768]{2,1,0:T(8,128)(2,1)} copy(bf16[2,1500,768]{2,0,1:T(2,128)(2,1)} %param.17) | data formatting | bytes 9216000 | tf_op args[1]
  24.2 9.9 %soap_pre.1 = (f32[8,192,192]{2,1,0:T(8,128)}, f32[8,2,192,192]{3,2,1,0:T(8,128)}) custom-call(f32[8,192,192]{2,1,0:T(8,128)} %bitcast.122, f32[8,2,192,192]{3,2,1,0:T(8,128)} %bitcast.108, f32[8,2,192,192]{3,2,1,0:T(8,128)} %bitcast.110), custom_call_target="tpu_custom_call" | custom-call | tf_op jit(solution)/shard_map/soap_pre/pallas_call | solution.py:127
  35.1 17.5 %collective-permute-start.2 = (bf16[2320,128]{1,0:T(8,128)(2,1)S(1)}, bf16[2320,128]{1,0:T(8,128)(2,1)}, u32[]{:S(2)}, u32[]{:S(2)}) collective-permute-start(bf16[2320,128]{1,0:T(8,128)(2,1)S(1)} %copy-done.13), channel_id=1, source_target_pairs={{0,2},{1,3},{2,0},{3,1},{4,6},{5,7},{6,4},{7,5},{8,10},{9,11},{10,... | collective-permute-start | bytes 1781768 | tf_op jit(solution)/shard_map/ppermute | solution.py:428
  55.2 1.5 collective-permute-start.4
  56.7 1.7 slice.207
  58.4 1.5 collective-permute-start.3
  59.9 1.9 pad_maximum_fusion.1
  61.8 6.0 %collective-permute-done.2 = bf16[2320,128]{1,0:T(8,128)(2,1)} collective-permute-done((bf16[2320,128]{1,0:T(8,128)(2,1)S(1)}, bf16[2320,128]{1,0:T(8,128)(2,1)}, u32[]{:S(2)}, u32[]{:S(2)}) %collective-permute-start.2) | collective-permute-done | bytes 593952 | tf_op jit(solution)/shard_map/ppermute | solution.py:428
  68.2 1.6 collective-permute-start.10
  70.8 1.6 collective-permute-start.9
  73.5 2.5 maximum_maximum_fusion.refs_0_
  76.1 4.6 %collective-permute-done.9 = bf16[1,1152,128]{2,1,0:T(8,128)(2,1)S(1)} collective-permute-done((bf16[1,1152,128]{2,1,0:T(8,128)(2,1)S(1)}, bf16[1,1152,128]{2,1,0:T(8,128)(2,1)S(1)}, u32[]{:S(2)}, u32[]{:S(2)}) %collective-permute-start.9) | collective-permute-done | bytes 294944 | tf_op jit(solution)/shard_map/ppermute | solution.py:425
  81.3 1.5 collective-permute-start.15
  82.8 4.4 maximum_maximum_fusion.1.refs_2_
  87.2 6.2 %collective-permute-done.19 = bf16[1,2320,128]{2,1,0:T(8,128)(2,1)S(1)} collective-permute-done((bf16[1,2320,128]{2,1,0:T(8,128)(2,1)}, bf16[1,2320,128]{2,1,0:T(8,128)(2,1)S(1)}, u32[]{:S(2)}, u32[]{:S(2)}) %collective-permute-start.19) | collective-permute-done | bytes 593952 | tf_op jit(solution)/shard_map/ppermute | solution.py:425
  94.1 4.3 collective-permute-done.15
  98.4 1.5 collective-permute-start.20
  99.9 4.4 maximum_maximum_fusion.2.refs_4_
  104.5 1.7 collective-permute-done.20
  106.2 4.4 maximum_maximum_fusion.3.refs_6_
  118.0 16.7 %assemble.1 = (bf16[768,3072]{1,0:T(8,128)(2,1)}, bf16[768,2048]{1,0:T(8,128)(2,1)}, bf16[768,1024]{1,0:T(8,128)(2,1)}, bf16[1024,768]{1,0:T(8,128)(2,1)}, bf16[...) custom-call(s32[256]{0:T(256)} %add.177.target, ...), custom_call_target="tpu_custom_call" | custom-call | tf_op jit(solution)/shard_map/assemble/pallas_call | solution.py:535
  134.7 15.3 %frame_projection.1.key.value = bf16[8,2,1500,256]{3,2,1,0:T(8,128)(2,1)} custom-call(bf16[2,1500,768]{2,1,0:T(8,128)(2,1)} %copy.39.frames.refs_6_, bf16[768,2048]{1,0:T(8,128)(2,1)} %get-tuple-element.79.weight.key_weight.value_weight, f32[8,1,256]{2,1,0:T(1,128)} %bitcast.141), custom_call_target="tpu_custom_call" | custom-call | tf_op jit(solution)/shard_map/frame_projection/pallas_call | solution.py:686
  150.0 9.4 %first_projections.1 = (bf16[896,768]{1,0:T(8,128)(2,1)}, bf16[896,3072]{1,0:T(8,128)(2,1)}) custom-call(bf16[2,896,768]{2,1,0:T(8,128)(2,1)} %bitcast.100, f32[19,768]{1,0:T(8,128)} %copy-done.25, f32[1,3072]{1,0:T(1,128)} %bitcast.140, bf16[768,3072]{1,0:T(8,128)(2,1)} %get-tuple-element.73.weight.query_weight.key_weight.value_weight), custom_call_target="tpu_custom_call" | custom-call | tf_op jit(solution)/shard_map/first_projections/pallas_call | solution.py:878
  159.5 12.6 %self_forward.1 = (bf16[2,448,1024]{2,1,0:T(8,128)(2,1)}, f32[2,4,8,448]{3,2,1,0:T(8,128)}) custom-call(bf16[2,448,3072]{2,1,0:T(8,128)(2,1)} %bitcast.94, bf16[2,448,3072]{2,1,0:T(8,128)(2,1)} %bitcast.95, bf16[2,448,3072]{2,1,0:T(8,128)(2,1)} %bitcast.96, s32[2,448,1]{2,1,0:T(8,128)} %copy.40.seg_col, s32[2,1,448]{2,1,0:T(1,128)} %broadcast_in_dim.146.seg_row, ...), custom_call_target="tpu_custom_call" | custom-call | tf_op jit(solution)/shard_map/self_forward/pallas_call | solution.py:314
  172.2 1.4 copy-done.9
  173.6 1.7 fusion.28
  177.7 2.9 add_convert_fusion.1
  180.6 25.2 %cross_forward.1 = (bf16[2,448,1024]{2,1,0:T(8,128)(2,1)}, f32[2,4,8,448]{3,2,1,0:T(8,128)}) custom-call(bf16[2,448,1024]{2,1,0:T(8,128)(2,1)} %bitcast.113, bf16[8,2,1500,256]{3,2,1,0:T(8,128)(2,1)} %frame_projection.1.key.value, bf16[8,2,1500,256]{3,2,1,0:T(8,128)(2,1)} %frame_projection.1.key.value), custom_call_target="tpu_custom_call" | custom-call | tf_op jit(solution)/shard_map/cross_forward/pallas_call | solution.py:331
  205.8 42.6 %middle.1 = (f32[896,768]{1,0:T(8,128)}, f32[896,768]{1,0:T(8,128)}, bf16[896,1024]{1,0:T(8,128)(2,1)}, bf16[896,768]{1,0:T(8,128)(2,1)}, bf16[896,768]{1,0:T(8,...) custom-call(s32[1]{0:T(128)} %bitcast.rank, ...), custom_call_target="tpu_custom_call" | custom-call | tf_op jit(solution)/shard_map/middle/pallas_call | solution.py:848
  248.4 37.2 %cross_backward.1 = (bf16[2,448,1024]{2,1,0:T(8,128)(2,1)}, bf16[2,1500,256]{2,1,0:T(8,128)(2,1)}, bf16[2,1500,256]{2,1,0:T(8,128)(2,1)}) custom-call(s32[1]{0:T(128)} %bitcast.rank, bf16[2,448,1024]{2,1,0:T(8,128)(2,1)} %bitcast.114, bf16[8,2,1500,256]{3,2,1,0:T(8,128)(2,1)} %frame_projection.1.key.value, ...), custom_call_target="tpu_custom_call" | custom-call | tf_op jit(solution)/shard_map/cross_backward/pallas_call | solution.py:354
  285.6 6.0 %frames_back.1 = bf16[4,2,384,768]{3,2,1,0:T(8,128)(2,1)} custom-call(s32[1]{0:T(128)} %bitcast.rank, bf16[2,1500,256]{2,1,0:T(8,128)(2,1)} %get-tuple-element.95.dk.refs_7_, bf16[2,1500,256]{2,1,0:T(8,128)(2,1)} %get-tuple-element.96.dv.refs_8_, bf16[768,2048]{1,0:T(8,128)(2,1)} %get-tuple-element.79.weight.key_weight.value_weight, ...), custom_call_target="tpu_custom_call" | custom-call | tf_op jit(solution)/shard_map/frames_back/pallas_call | solution.py:714
  291.7 3.7 multiply_reduce_fusion
  295.5 2.3 convert_reduce_fusion.3
  297.8 2.9 convolution_convert_fusion
  300.6 7.1 %self_backward.1 = bf16[2,448,768]{2,1,0:T(8,128)(2,1)} custom-call(s32[1]{0:T(128)} %bitcast.rank, bf16[2,448,3072]{2,1,0:T(8,128)(2,1)} %bitcast.97, bf16[2,448,3072]{2,1,0:T(8,128)(2,1)} %bitcast.98, bf16[2,448,3072]{2,1,0:T(8,128)(2,1)} %bitcast.99, bf16[2,448,1024]{2,1,0:T(8,128)(2,1)} %bitcast.131, bf16[2,448,1024]{2,1,0:T(8,128)(2,1)} %get-tuple-element.75.mixed, ...), custom_call_target="tpu_custom_call" | custom-call | tf_op jit(solution)/shard_map/self_backward/pallas_call | solution.py:383
  307.7 4.9 %first_back.1 = (bf16[896,768]{1,0:T(8,128)(2,1)}, f32[2,768]{1,0:T(2,128)}) custom-call(s32[1]{0:T(128)} %bitcast.rank, bf16[896,768]{1,0:T(8,128)(2,1)} %bitcast.103, bf16[768,3072]{1,0:T(8,128)(2,1)} %get-tuple-element.73.weight.query_weight.key_weight.value_weight, bf16[768,3072]{1,0:T(8,128)(2,1)} %get-tuple-element.73.weight.query_weight.key_weight.value_weight, ...), custom_call_target="tpu_custom_call" | custom-call | tf_op jit(solution)/shard_map/first_back/pallas_call | solution.py:663
  314.8 1.8 convert_reduce_fusion
  319.0 17.3 %weight_grads.1 = bf16[8,2320,128]{2,1,0:T(8,128)(2,1)} custom-call(s32[1]{0:T(128)} %bitcast.rank, s32[64]{0:T(128)} %get-tuple-element.170.slot, s32[64]{0:T(128)} %get-tuple-element.169.sub, bf16[896,768]{1,0:T(8,128)(2,1)} %get-tuple-element.101.refs_0_, bf16[896,768]{1,0:T(8,128)(2,1)} %get-tuple-element.102.refs_1_, ...), custom_call_target="tpu_custom_call" | custom-call | tf_op jit(solution)/shard_map/weight_grads/pallas_call | solution.py:615
  336.3 1.9 slice.229
  339.1 2.0 constant_dynamic-slice_fusion
  341.1 1.9 collective-permute-done.23
  343.0 3.0 add_convert_fusion
  348.5 1.5 collective-permute-start.26
  350.0 1.3 fusion.10
  351.3 12.5 %collective-permute-done.24 = bf16[2,1152,128]{2,1,0:T(8,128)(2,1)} collective-permute-done((bf16[2,1152,128]{2,1,0:T(8,128)(2,1)}, bf16[2,1152,128]{2,1,0:T(8,128)(2,1)}, u32[]{:S(2)}, u32[]{:S(2)}) %collective-permute-start.24) | collective-permute-done | bytes 589856 | tf_op jit(solution)/shard_map/ppermute | solution.py:637
  363.8 1.2 convert_add_fusion.2
  365.0 1.6 collective-permute-start.25
  366.6 1.2 convert_add_fusion.1
  368.5 5.0 %collective-permute-done.25 = bf16[1152,128]{1,0:T(8,128)(2,1)S(1)} collective-permute-done((bf16[1152,128]{1,0:T(8,128)(2,1)S(1)}, bf16[1152,128]{1,0:T(8,128)(2,1)S(1)}, u32[]{:S(2)}, u32[]{:S(2)}) %collective-permute-start.25) | collective-permute-done | bytes 294944 | tf_op jit(solution)/shard_map/ppermute | solution.py:637
  373.6 2.6 collective-permute-done.27
  376.3 1.1 pad_maximum_fusion.grad
  377.4 17.7 %soap_main.1 = (f32[8,192,192]{2,1,0:T(8,128)}, f32[8,192,192]{2,1,0:T(8,128)}, f32[8,192,192]{2,1,0:T(8,128)}, f32[8,2,192,192]{3,2,1,0:T(8,128)}, f32[8,2,192,...) custom-call(f32[2320,128]{1,0:T(8,128)} %pad_maximum_fusion.grad, f32[8,192,192]{2,1,0:T(8,128)} %bitcast.121, ...), custom_call_target="tpu_custom_call" | custom-call | tf_op jit(solution)/shard_map/soap_main/pallas_call | solution.py:136
  395.2 3.9 collective-permute-start.29
  399.1 2.2 fusion.8
  401.3 1.9 copy-done
  403.2 38.6 %chol_bases.1 = f32[16,192,192]{2,1,0:T(8,128)} custom-call(f32[16,192,192]{2,1,0:T(8,128)S(1)} %bitcast.93, f32[16,192,192]{2,1,0:T(8,128)} %bitcast.126), custom_call_target="tpu_custom_call" | custom-call | tf_op jit(solution)/shard_map/chol_bases/pallas_call | solution.py:144
  442.5 1.4 slice_convert_fusion
  443.9 2.6 copy.43
  (212 shorter events, 26.5 us)
Async XLA Ops:
  7.2 142.9 %all-gather.2.cloned.1.call-start = ((), (), s32[]{:S(2)}) async-start(), calls=%async_computation.2 | async-start | bytes 3440640 | tf_op jit(solution)/shard_map/all_gather | solution.py:943
  10.9 23.3 %collective-permute-start.6 = (bf16[2320,128]{1,0:T(8,128)(2,1)}, bf16[2320,128]{1,0:T(8,128)(2,1)}, u32[]{:S(2)}, u32[]{:S(2)}) collective-permute-start(bf16[2320,128]{1,0:T(8,128)(2,1)} %pack.1), channel_id=1, source_target_pairs={{0,1},{1,2},{2,3},{3,0},{4,5},{5,6},{6,7},{7,4},{8,9},{9,10},{10,1... | collective-permute-start | bytes 1781768 | tf_op jit(solution)/shard_map/ppermute | solution.py:428
  13.9 20.3 %collective-permute-start = (bf16[1,2320,128]{2,1,0:T(8,128)(2,1)}, bf16[1,2320,128]{2,1,0:T(8,128)(2,1)S(1)}, u32[]{:S(2)}, u32[]{:S(2)}) collective-permute-start(bf16[1,2320,128]{2,1,0:T(8,128)(2,1)} %bitcast.127), channel_id=1, source_target_pairs={{0,8},{4,12},{8,0},{12,4},{16,24},{20,28},{24,16},{28,20},{1,9},{5... | collective-permute-start | bytes 1781768 | tf_op jit(solution)/shard_map/ppermute | solution.py:425
  15.4 18.8 %collective-permute-start.1 = (bf16[1,2320,128]{2,1,0:T(8,128)(2,1)}, bf16[1,2320,128]{2,1,0:T(8,128)(2,1)S(1)}, u32[]{:S(2)}, u32[]{:S(2)}) collective-permute-start(bf16[1,2320,128]{2,1,0:T(8,128)(2,1)} %bitcast.128), channel_id=1, source_target_pairs={{0,16},{4,20},{8,24},{12,28},{16,0},{20,4},{24,8},{28,12},{1,17},{... | collective-permute-start | bytes 1781768 | tf_op jit(solution)/shard_map/ppermute | solution.py:425
  16.9 35.7 %collective-permute-start.12 = (bf16[2320,128]{1,0:T(8,128)(2,1)}, bf16[2320,128]{1,0:T(8,128)(2,1)}, u32[]{:S(2)}, u32[]{:S(2)}) collective-permute-start(bf16[2320,128]{1,0:T(8,128)(2,1)} %pack.1), channel_id=1, source_target_pairs={{0,3},{1,0},{2,1},{3,2},{4,7},{5,4},{6,5},{7,6},{8,11},{9,8},{10,9... | collective-permute-start | bytes 1781768 | tf_op jit(solution)/shard_map/ppermute | solution.py:428
  24.2 10.9 %copy-start.13 = (bf16[2320,128]{1,0:T(8,128)(2,1)S(1)}, bf16[2320,128]{1,0:T(8,128)(2,1)}, u32[]{:S(2)}) copy-start(bf16[2320,128]{1,0:T(8,128)(2,1)} %pack.1) | copy-start | bytes 1781764
  24.2 35.7 %copy-start.7 = (bf16[2,112,768]{2,1,0:T(8,128)(2,1)S(1)}, bf16[2,112,768]{2,1,0:T(8,128)(2,1)}, u32[]{:S(2)}) copy-start(bf16[2,112,768]{2,1,0:T(8,128)(2,1)} %param.16) | copy-start | bytes 1032196
  34.2 18.4 %copy-start.24 = (bf16[1,2320,128]{2,1,0:T(8,128)(2,1)}, bf16[1,2320,128]{2,1,0:T(8,128)(2,1)S(1)}, u32[]{:S(2)}) copy-start(bf16[1,2320,128]{2,1,0:T(8,128)(2,1)S(1)} %collective-permute-done) | copy-start | bytes 1781764
  34.2 39.2 %copy-start.19 = (bf16[1,2320,128]{2,1,0:T(8,128)(2,1)}, bf16[1,2320,128]{2,1,0:T(8,128)(2,1)S(1)}, u32[]{:S(2)}) copy-start(bf16[1,2320,128]{2,1,0:T(8,128)(2,1)S(1)} %collective-permute-done.1) | copy-start | bytes 1781764
  34.2 18.4 %collective-permute-start.7 = (bf16[1,2320,128]{2,1,0:T(8,128)(2,1)}, bf16[1,2320,128]{2,1,0:T(8,128)(2,1)S(1)}, u32[]{:S(2)}, u32[]{:S(2)}) collective-permute-start(bf16[1,2320,128]{2,1,0:T(8,128)(2,1)} %bitcast.12), channel_id=1, source_target_pairs={{0,8},{4,12},{8,0},{12,4},{16,24},{20,28},{24,16},{28,20},{1,9},{5... | collective-permute-start | bytes 1781768 | tf_op jit(solution)/shard_map/ppermute | solution.py:425
  34.8 17.8 %collective-permute-start.8 = (bf16[1,2320,128]{2,1,0:T(8,128)(2,1)}, bf16[1,2320,128]{2,1,0:T(8,128)(2,1)S(1)}, u32[]{:S(2)}, u32[]{:S(2)}) collective-permute-start(bf16[1,2320,128]{2,1,0:T(8,128)(2,1)} %bitcast.12), channel_id=1, source_target_pairs={{0,16},{4,20},{8,24},{12,28},{16,0},{20,4},{24,8},{28,12},{1,17},{... | collective-permute-start | bytes 1781768 | tf_op jit(solution)/shard_map/ppermute | solution.py:425
  35.1 32.7 %collective-permute-start.2 = (bf16[2320,128]{1,0:T(8,128)(2,1)S(1)}, bf16[2320,128]{1,0:T(8,128)(2,1)}, u32[]{:S(2)}, u32[]{:S(2)}) collective-permute-start(bf16[2320,128]{1,0:T(8,128)(2,1)S(1)} %copy-done.13), channel_id=1, source_target_pairs={{0,2},{1,3},{2,0},{3,1},{4,6},{5,7},{6,4},{7,5},{8,10},{9,11},{10,... | collective-permute-start | bytes 1781768 | tf_op jit(solution)/shard_map/ppermute | solution.py:428
  52.6 20.8 %copy-start.17 = (bf16[1,2320,128]{2,1,0:T(8,128)(2,1)}, bf16[1,2320,128]{2,1,0:T(8,128)(2,1)S(1)}, u32[]{:S(2)}) copy-start(bf16[1,2320,128]{2,1,0:T(8,128)(2,1)S(1)} %collective-permute-done.8) | copy-start | bytes 1781764
  53.4 17.3 %collective-permute-start.13 = (bf16[1,2320,128]{2,1,0:T(8,128)(2,1)}, bf16[1,2320,128]{2,1,0:T(8,128)(2,1)S(1)}, u32[]{:S(2)}, u32[]{:S(2)}) collective-permute-start(bf16[1,2320,128]{2,1,0:T(8,128)(2,1)} %bitcast.13), channel_id=1, source_target_pairs={{0,8},{4,12},{8,0},{12,4},{16,24},{20,28},{24,16},{28,20},{1,9},{5... | collective-permute-start | bytes 1781768 | tf_op jit(solution)/shard_map/ppermute | solution.py:425
  53.9 18.4 %collective-permute-start.14 = (bf16[1,2320,128]{2,1,0:T(8,128)(2,1)}, bf16[1,2320,128]{2,1,0:T(8,128)(2,1)S(1)}, u32[]{:S(2)}, u32[]{:S(2)}) collective-permute-start(bf16[1,2320,128]{2,1,0:T(8,128)(2,1)} %bitcast.13), channel_id=1, source_target_pairs={{0,16},{4,20},{8,24},{12,28},{16,0},{20,4},{24,8},{28,12},{1,17},{... | collective-permute-start | bytes 1781768 | tf_op jit(solution)/shard_map/ppermute | solution.py:425
  55.2 18.2 %collective-permute-start.4 = (bf16[1,1168,128]{2,1,0:T(8,128)(2,1)}, bf16[1,1168,128]{2,1,0:T(8,128)(2,1)}, u32[]{:S(2)}, u32[]{:S(2)}) collective-permute-start(bf16[1,1168,128]{2,1,0:T(8,128)(2,1)} %slice.208), channel_id=1, source_target_pairs={{0,8},{4,12},{8,0},{12,4},{16,24},{20,28},{24,16},{28,20},{1,9},{5... | collective-permute-start | bytes 897032 | tf_op jit(solution)/shard_map/ppermute | solution.py:425
  58.4 14.5 %collective-permute-start.3 = (bf16[1,1152,128]{2,1,0:T(8,128)(2,1)}, bf16[1,1152,128]{2,1,0:T(8,128)(2,1)}, u32[]{:S(2)}, u32[]{:S(2)}) collective-permute-start(bf16[1,1152,128]{2,1,0:T(8,128)(2,1)} %slice.207), channel_id=1, source_target_pairs={{0,16},{4,20},{8,24},{12,28},{16,0},{20,4},{24,8},{28,12},{1,17},{... | collective-permute-start | bytes 884744 | tf_op jit(solution)/shard_map/ppermute | solution.py:425
  67.9 282.2 %reduce-scatter.3.cloned.1.call-start = ((), (), s32[]{:S(2)}) async-start(), calls=%async_computation.3 | async-start | bytes 1720320 | tf_op jit(solution)/shard_map/reduce_scatter | solution.py:998
  68.2 13.1 %collective-permute-start.10 = (bf16[1,1168,128]{2,1,0:T(8,128)(2,1)S(1)}, bf16[1,1168,128]{2,1,0:T(8,128)(2,1)S(1)}, u32[]{:S(2)}, u32[]{:S(2)}) collective-permute-start(bf16[1,1168,128]{2,1,0:T(8,128)(2,1)S(1)} %slice.214), channel_id=1, source_target_pairs={{0,8},{4,12},{8,0},{12,4},{16,24},{20,28},{24,16},{28,20},{1,9},{5... | collective-permute-start | bytes 897032 | tf_op jit(solution)/shard_map/ppermute | solution.py:425
  70.7 2.7 copy-start.20
  70.8 10.0 %collective-permute-start.9 = (bf16[1,1152,128]{2,1,0:T(8,128)(2,1)S(1)}, bf16[1,1152,128]{2,1,0:T(8,128)(2,1)S(1)}, u32[]{:S(2)}, u32[]{:S(2)}) collective-permute-start(bf16[1,1152,128]{2,1,0:T(8,128)(2,1)S(1)} %slice.213), channel_id=1, source_target_pairs={{0,16},{4,20},{8,24},{12,28},{16,0},{20,4},{24,8},{28,12},{1,17},{... | collective-permute-start | bytes 884744 | tf_op jit(solution)/shard_map/ppermute | solution.py:425
  72.3 10.5 %copy-start.23 = (bf16[1,2320,128]{2,1,0:T(8,128)(2,1)S(1)}, bf16[1,2320,128]{2,1,0:T(8,128)(2,1)}, u32[]{:S(2)}) copy-start(bf16[1,2320,128]{2,1,0:T(8,128)(2,1)} %copy-done.22) | copy-start | bytes 1781764
  72.3 21.1 %collective-permute-start.19 = (bf16[1,2320,128]{2,1,0:T(8,128)(2,1)}, bf16[1,2320,128]{2,1,0:T(8,128)(2,1)S(1)}, u32[]{:S(2)}, u32[]{:S(2)}) collective-permute-start(bf16[1,2320,128]{2,1,0:T(8,128)(2,1)} %bitcast.14), channel_id=1, source_target_pairs={{0,16},{4,20},{8,24},{12,28},{16,0},{20,4},{24,8},{28,12},{1,17},{... | collective-permute-start | bytes 1781768 | tf_op jit(solution)/shard_map/ppermute | solution.py:425
  72.9 20.6 %collective-permute-start.18 = (bf16[1,2320,128]{2,1,0:T(8,128)(2,1)}, bf16[1,2320,128]{2,1,0:T(8,128)(2,1)S(1)}, u32[]{:S(2)}, u32[]{:S(2)}) collective-permute-start(bf16[1,2320,128]{2,1,0:T(8,128)(2,1)} %bitcast.14), channel_id=1, source_target_pairs={{0,8},{4,12},{8,0},{12,4},{16,24},{20,28},{24,16},{28,20},{1,9},{5... | collective-permute-start | bytes 1781768 | tf_op jit(solution)/shard_map/ppermute | solution.py:425
  73.4 2.6 copy-start.16
  73.4 2.6 copy-start.21
  73.4 9.4 %copy-start.18 = (bf16[1,2320,128]{2,1,0:T(8,128)(2,1)S(1)}, bf16[1,2320,128]{2,1,0:T(8,128)(2,1)}, u32[]{:S(2)}) copy-start(bf16[1,2320,128]{2,1,0:T(8,128)(2,1)} %copy-done.17) | copy-start | bytes 1781764
  75.9 38.9 %copy-start.6 = (bf16[4,2320,128]{2,1,0:T(8,128)(2,1)}, bf16[4,2320,128]{2,1,0:T(8,128)(2,1)S(1)}, u32[]{:S(2)}) copy-start(bf16[4,2320,128]{2,1,0:T(8,128)(2,1)S(1)} %maximum_maximum_fusion.refs_0_) | copy-start | bytes 7127044
  75.9 38.9 %collective-permute-start.5 = (bf16[4,2320,128]{2,1,0:T(8,128)(2,1)S(1)}, bf16[4,2320,128]{2,1,0:T(8,128)(2,1)}, u32[]{:S(2)}, u32[]{:S(2)}) collective-permute-start(bf16[4,2320,128]{2,1,0:T(8,128)(2,1)S(1)} %maximum_maximum_fusion.refs_0_), channel_id=1, source_target_pairs={{0,4},{4,0},{8,12},{12,8},{16,20},{20,16},{24,28},{28,24},{1,5},{5... | collective-permute-start | bytes 7127048 | tf_op jit(solution)/shard_map/ppermute | solution.py:425
  80.7 19.2 %collective-permute-start.16 = (bf16[1,1168,128]{2,1,0:T(8,128)(2,1)S(1)}, bf16[1,1168,128]{2,1,0:T(8,128)(2,1)S(1)}, u32[]{:S(2)}, u32[]{:S(2)}) collective-permute-start(bf16[1,1168,128]{2,1,0:T(8,128)(2,1)S(1)} %slice.216), channel_id=1, source_target_pairs={{0,8},{4,12},{8,0},{12,4},{16,24},{20,28},{24,16},{28,20},{1,9},{5... | collective-permute-start | bytes 897032 | tf_op jit(solution)/shard_map/ppermute | solution.py:425
  81.3 17.1 %collective-permute-start.15 = (bf16[1,1152,128]{2,1,0:T(8,128)(2,1)S(1)}, bf16[1,1152,128]{2,1,0:T(8,128)(2,1)S(1)}, u32[]{:S(2)}, u32[]{:S(2)}) collective-permute-start(bf16[1,1152,128]{2,1,0:T(8,128)(2,1)S(1)} %slice.215), channel_id=1, source_target_pairs={{0,16},{4,20},{8,24},{12,28},{16,0},{20,4},{24,8},{28,12},{1,17},{... | collective-permute-start | bytes 884744 | tf_op jit(solution)/shard_map/ppermute | solution.py:425
  93.5 24.5 %collective-permute-start.11 = (bf16[4,2320,128]{2,1,0:T(8,128)(2,1)}, bf16[4,2320,128]{2,1,0:T(8,128)(2,1)}, u32[]{:S(2)}, u32[]{:S(2)}) collective-permute-start(bf16[4,2320,128]{2,1,0:T(8,128)(2,1)} %maximum_maximum_fusion.1.refs_2_), channel_id=1, source_target_pairs={{0,4},{4,0},{8,12},{12,8},{16,20},{20,16},{24,28},{28,24},{1,5},{5... | collective-permute-start | bytes 7127048 | tf_op jit(solution)/shard_map/ppermute | solution.py:425
  93.5 12.6 %collective-permute-start.21 = (bf16[1,1168,128]{2,1,0:T(8,128)(2,1)S(1)}, bf16[1,1168,128]{2,1,0:T(8,128)(2,1)S(1)}, u32[]{:S(2)}, u32[]{:S(2)}) collective-permute-start(bf16[1,1168,128]{2,1,0:T(8,128)(2,1)S(1)} %slice.218), channel_id=1, source_target_pairs={{0,8},{4,12},{8,0},{12,4},{16,24},{20,28},{24,16},{28,20},{1,9},{5... | collective-permute-start | bytes 897032 | tf_op jit(solution)/shard_map/ppermute | solution.py:425
  98.4 7.7 %collective-permute-start.20 = (bf16[1,1152,128]{2,1,0:T(8,128)(2,1)S(1)}, bf16[1,1152,128]{2,1,0:T(8,128)(2,1)S(1)}, u32[]{:S(2)}, u32[]{:S(2)}) collective-permute-start(bf16[1,1152,128]{2,1,0:T(8,128)(2,1)S(1)} %slice.217), channel_id=1, source_target_pairs={{0,16},{4,20},{8,24},{12,28},{16,0},{20,4},{24,8},{28,12},{1,17},{... | collective-permute-start | bytes 884744 | tf_op jit(solution)/shard_map/ppermute | solution.py:425
  104.4 6.2 %copy-start.35 = (s32[32]{0:T(128)S(1)}, s32[32]{0:T(128)}, u32[]{:S(2)}) copy-start(s32[32]{0:T(128)} %constant.133.clone) | copy-start | bytes 388
  104.4 6.4 %copy-start.38 = (s32[32]{0:T(128)S(1)}, s32[32]{0:T(128)}, u32[]{:S(2)}) copy-start(s32[32]{0:T(128)} %constant.152) | copy-start | bytes 388
  104.4 6.6 %copy-start.27 = (s32[2,448]{1,0:T(2,128)S(1)}, s32[2,448]{1,0:T(2,128)}, u32[]{:S(2)}) copy-start(s32[2,448]{1,0:T(2,128)} %param.19) | copy-start | bytes 10756
  104.4 8.2 %copy-start.28 = (s32[2,448]{1,0:T(2,128)S(1)}, s32[2,448]{1,0:T(2,128)}, u32[]{:S(2)}) copy-start(s32[2,448]{1,0:T(2,128)} %param.20) | copy-start | bytes 10756
  104.4 9.8 %copy-start.34 = (s32[64]{0:T(128)S(1)}, s32[64]{0:T(128)}, u32[]{:S(2)}) copy-start(s32[64]{0:T(128)} %param.21) | copy-start | bytes 772
  104.4 13.6 %collective-permute-start.17 = (bf16[4,2320,128]{2,1,0:T(8,128)(2,1)}, bf16[4,2320,128]{2,1,0:T(8,128)(2,1)}, u32[]{:S(2)}, u32[]{:S(2)}) collective-permute-start(bf16[4,2320,128]{2,1,0:T(8,128)(2,1)} %maximum_maximum_fusion.2.refs_4_), channel_id=1, source_target_pairs={{0,4},{4,0},{8,12},{12,8},{16,20},{20,16},{24,28},{28,24},{1,5},{5... | collective-permute-start | bytes 7127048 | tf_op jit(solution)/shard_map/ppermute | solution.py:425
  110.6 7.4 %collective-permute-start.22 = (bf16[4,2320,128]{2,1,0:T(8,128)(2,1)}, bf16[4,2320,128]{2,1,0:T(8,128)(2,1)}, u32[]{:S(2)}, u32[]{:S(2)}) collective-permute-start(bf16[4,2320,128]{2,1,0:T(8,128)(2,1)} %maximum_maximum_fusion.3.refs_6_), channel_id=1, source_target_pairs={{0,4},{4,0},{8,12},{12,8},{16,20},{20,16},{24,28},{28,24},{1,5},{5... | collective-permute-start | bytes 7127048 | tf_op jit(solution)/shard_map/ppermute | solution.py:425
  115.9 18.8 %copy-start.25 = (f32[19,768]{1,0:T(8,128)}, f32[19,768]{1,0:T(8,128)S(1)}, u32[]{:S(2)}) copy-start(f32[19,768]{1,0:T(8,128)S(1)} %reshape.319.vectors.refs_3_) | copy-start | bytes 175108
  159.5 12.6 %copy-start.3 = (bf16[2,2,448,768]{3,2,1,0:T(8,128)(2,1)S(1)}, bf16[2,2,448,768]{3,2,1,0:T(8,128)(2,1)}, u32[]{:S(2)}) copy-start(bf16[2,2,448,768]{3,2,1,0:T(8,128)(2,1)} %all-gather.2.cloned.1.call-done) | copy-start | bytes 8257540
  159.5 12.8 %copy-start.36 = (bf16[1024,768]{1,0:T(8,128)(2,1)S(1)}, bf16[1024,768]{1,0:T(8,128)(2,1)}, u32[]{:S(2)}) copy-start(bf16[1024,768]{1,0:T(8,128)(2,1)} %get-tuple-element.76) | copy-start | bytes 4718596
  175.8 1.9 copy-start.37
  176.9 3.7 copy-start.10
  285.6 6.0 %copy-start.2 = (f32[896,768]{1,0:T(8,128)S(1)}, f32[896,768]{1,0:T(8,128)}, u32[]{:S(2)}) copy-start(f32[896,768]{1,0:T(8,128)} %copy-done.1) | copy-start | bytes 8257540
  285.6 6.0 %copy-start.8 = (bf16[2,448,1024]{2,1,0:T(8,128)(2,1)S(1)}, bf16[2,448,1024]{2,1,0:T(8,128)(2,1)}, u32[]{:S(2)}) copy-start(bf16[2,448,1024]{2,1,0:T(8,128)(2,1)} %get-tuple-element.94) | copy-start | bytes 5505028
  291.7 3.8 copy-start.12
  297.7 2.9 copy-start.11
  307.7 5.7 %copy-start.4 = (bf16[2,448,768]{2,1,0:T(8,128)(2,1)S(1)}, bf16[2,448,768]{2,1,0:T(8,128)(2,1)}, u32[]{:S(2)}) copy-start(bf16[2,448,768]{2,1,0:T(8,128)(2,1)} %self_backward.1) | copy-start | bytes 4128772
  312.6 2.1 copy-start.29
  312.6 129.9 %reduce-scatter.5.cloned.1.call-start = ((), (), s32[]{:S(2)}) async-start(), calls=%async_computation.4 | async-start | bytes 5898240 | tf_op jit(solution)/shard_map/reduce_scatter | solution.py:983
  338.2 4.9 %collective-permute-start.23 = (bf16[4,2320,128]{2,1,0:T(8,128)(2,1)S(1)}, bf16[4,2320,128]{2,1,0:T(8,128)(2,1)}, u32[]{:S(2)}, u32[]{:S(2)}) collective-permute-start(bf16[4,2320,128]{2,1,0:T(8,128)(2,1)S(1)} %slice.229), channel_id=1, source_target_pairs={{0,4},{4,0},{8,12},{12,8},{16,20},{20,16},{24,28},{28,24},{1,5},{5... | collective-permute-start | bytes 7127048 | tf_op jit(solution)/shard_map/ppermute | solution.py:637
  347.8 15.9 %collective-permute-start.24 = (bf16[2,1152,128]{2,1,0:T(8,128)(2,1)}, bf16[2,1152,128]{2,1,0:T(8,128)(2,1)}, u32[]{:S(2)}, u32[]{:S(2)}) collective-permute-start(bf16[2,1152,128]{2,1,0:T(8,128)(2,1)} %pad_maximum_fusion.2), channel_id=1, source_target_pairs={{0,8},{4,12},{8,0},{12,4},{16,24},{20,28},{24,16},{28,20},{1,9},{5... | collective-permute-start | bytes 1769480 | tf_op jit(solution)/shard_map/ppermute | solution.py:637
  348.5 18.1 %collective-permute-start.26 = (bf16[2,1168,128]{2,1,0:T(8,128)(2,1)}, bf16[2,1168,128]{2,1,0:T(8,128)(2,1)}, u32[]{:S(2)}, u32[]{:S(2)}) collective-permute-start(bf16[2,1168,128]{2,1,0:T(8,128)(2,1)} %slice.237), channel_id=1, source_target_pairs={{0,16},{4,20},{8,24},{12,28},{16,0},{20,4},{24,8},{28,12},{1,17},{... | collective-permute-start | bytes 1794056 | tf_op jit(solution)/shard_map/ppermute | solution.py:637
  365.0 8.5 %collective-permute-start.25 = (bf16[1152,128]{1,0:T(8,128)(2,1)S(1)}, bf16[1152,128]{1,0:T(8,128)(2,1)S(1)}, u32[]{:S(2)}, u32[]{:S(2)}) collective-permute-start(bf16[1152,128]{1,0:T(8,128)(2,1)S(1)} %fusion.14), channel_id=1, source_target_pairs={{0,16},{4,20},{8,24},{12,28},{16,0},{20,4},{24,8},{28,12},{1,17},{... | collective-permute-start | bytes 884744 | tf_op jit(solution)/shard_map/ppermute | solution.py:637
  367.8 8.3 %collective-permute-start.27 = (bf16[1168,128]{1,0:T(8,128)(2,1)S(1)}, bf16[1168,128]{1,0:T(8,128)(2,1)S(1)}, u32[]{:S(2)}, u32[]{:S(2)}) collective-permute-start(bf16[1168,128]{1,0:T(8,128)(2,1)S(1)} %fusion.13), channel_id=1, source_target_pairs={{0,8},{4,12},{8,0},{12,4},{16,24},{20,28},{24,16},{28,20},{1,9},{5... | collective-permute-start | bytes 897032 | tf_op jit(solution)/shard_map/ppermute | solution.py:637
  376.2 18.9 %collective-permute-start.28 = (f32[16,128]{1,0:T(8,128)S(1)}, f32[16,128]{1,0:T(8,128)S(1)}, u32[]{:S(2)}, u32[]{:S(2)}) collective-permute-start(f32[16,128]{1,0:T(8,128)S(1)} %slice.240), channel_id=1, source_target_pairs={{0,1},{1,0},{2,3},{3,2},{4,5},{5,4},{6,7},{7,6},{8,9},{9,8},{10,11... | collective-permute-start | bytes 24584 | tf_op jit(solution)/shard_map/ppermute | solution.py:1040
  377.4 21.7 %copy-start.14 = (bf16[2,112,768]{2,1,0:T(8,128)(2,1)S(1)}, bf16[2,112,768]{2,1,0:T(8,128)(2,1)}, u32[]{:S(2)}) copy-start(bf16[2,112,768]{2,1,0:T(8,128)(2,1)} %reduce-scatter.3.cloned.1.call-done) | copy-start | bytes 1032196
  395.2 46.7 %collective-permute-start.29 = (f32[16,128]{1,0:T(8,128)S(1)}, f32[16,128]{1,0:T(8,128)S(1)}, u32[]{:S(2)}, u32[]{:S(2)}) collective-permute-start(f32[16,128]{1,0:T(8,128)S(1)} %slice_add_fusion), channel_id=1, source_target_pairs={{0,2},{1,3},{2,0},{3,1},{4,6},{5,7},{6,4},{7,5},{8,10},{9,11},{10,... | collective-permute-start | bytes 24584 | tf_op jit(solution)/shard_map/ppermute | solution.py:1040
  403.2 38.7 %copy-start.26 = (f32[1824]{0:T(1024)S(1)}, f32[1824]{0:T(1024)}, u32[]{:S(2)}) copy-start(f32[1824]{0:T(1024)} %param.27) | copy-start | bytes 21892
  403.2 38.7 %copy-start.31 = (f32[1824]{0:T(1024)S(1)}, f32[1824]{0:T(1024)}, u32[]{:S(2)}) copy-start(f32[1824]{0:T(1024)} %param.28) | copy-start | bytes 21892
  403.2 38.7 %copy-start.32 = (f32[1824]{0:T(1024)S(1)}, f32[1824]{0:T(1024)}, u32[]{:S(2)}) copy-start(f32[1824]{0:T(1024)} %param.29) | copy-start | bytes 21892
  (8 other events, 9.6 us)
Sparse Core Ops, SparseCore 0:
  68.0 57.9 all-gather.1
  312.7 33.5 reduce-scatter.2
  348.7 84.4 reduce-scatter.4

commit v6 on v5

--- a/solution.py
+++ b/solution.py
@@ -647,12 +647,13 @@
     return jnp.concatenate([low[0] + low_y, high[0] + high_x], axis=0)
 
 
-def first_back_kernel(rank, dqkv, query_weight, key_weight, value_weight, hidden, out, sums):
+def first_back_kernel(rank, dqkv, query_weight, key_weight, value_weight, hidden, out, sums, own_sums):
     weights = jnp.concatenate([query_weight[...], key_weight[...], value_weight[...]], axis=1)
     made = bdot(dqkv[...], weights, NT)
     unit, _ = unit_rows(hidden[0].astype(jnp.float32))
     sums[0:1] = jnp.sum(made * unit, axis=0, keepdims=True)
     sums[1:2] = jnp.sum(made, axis=0, keepdims=True)
+    own_sums[...] = jnp.sum(dqkv[...].astype(jnp.float32), axis=0, keepdims=True)
     out[...] = made.astype(jnp.bfloat16)
 
 
@@ -666,9 +667,12 @@
             num_scalar_prefetch=1,
             grid=(1,),
             in_specs=[whole(dqkv.shape), own(0), own(ranks), own(2 * ranks), pl.BlockSpec((1, tokens, width), lambda i, rank: (0, 0, 0))],
-            out_specs=[whole((tokens, width)), whole((2, width))],
+            out_specs=[whole((tokens, width)), whole((2, width)), whole((1, dqkv.shape[1]))],
         ),
-        out_shape=[jax.ShapeDtypeStruct((tokens, width), jnp.bfloat16), jax.ShapeDtypeStruct((2, width), jnp.float32)],
+        out_shape=[
+            jax.ShapeDtypeStruct((tokens, width), jnp.bfloat16), jax.ShapeDtypeStruct((2, width), jnp.float32),
+            jax.ShapeDtypeStruct((1, dqkv.shape[1]), jnp.float32),
+        ],
         compiler_params=pltpu.CompilerParams(vmem_limit_bytes=VM),
         name="first_back",
     )(rank, dqkv, weight, weight, weight, hidden)
@@ -994,7 +998,7 @@
         )
     )
 
-    part_one, first_sums = first_back(rank_ref, dqkv, w_qkv, both, ranks)
+    part_one, first_sums, dqkv_sum = first_back(rank_ref, dqkv, w_qkv, both, ranks)
     grad_one = lax.psum_scatter(split(part_one), "tensor", scatter_dimension=1, tiled=True).astype(f32)
     back, _, _ = normalize_back(
         hidden_in.astype(f32).reshape(-1, width), vectors[0], grad_one.reshape(-1, width)
@@ -1009,7 +1013,7 @@
     )
     query_sum = total(dcq).reshape(ranks, SLOT)[:, :side].reshape(1, width)
     even = 1.0 / ranks
-    dqkv_sum = total(dqkv)
+    dqkv_sum = dqkv_sum[0]
     own_sums = jnp.stack([dqkv_sum[:side], dqkv_sum[2 * SLOT : 2 * SLOT + side], total(dv)[:side]])
     own_sums = lax.dynamic_update_slice(jnp.zeros((3, width), f32), own_sums, (0, rank * side))
     vector_terms = jnp.concatenate(

time: 457 us -> 456 us (level)
    unnamed x90 -> x92, local copies, waits for them, and re-layouts: 15.5 us -> 15.2 us
where the time goes in v6:
time: 456 us; the launch traced here: 453 us
  Pallas kernels  263 us (58%)
  starting transfers between devices  48.6 us (11%)
  waiting for transfers between devices  44.9 us (10%)
  other arithmetic  39.1 us (9%)
  local copies, waits for them, and re-layouts  31.1 us (7%)
  between operations  14.7 us (3%)
  matrix products  11.2 us (2%)
    pallas_call x1, Pallas kernels, middle(): pl.pallas_call(functools.partial(middle_kernel, parts=parts), grid_spec=p...  42.5 us
    pallas_call x1, Pallas kernels, chol_bases(): pl.pallas_call(functools.partial(chol_kernel, block=block, unroll=unroll,...  38.6 us
    pallas_call x1, Pallas kernels, cross_backward(): pl.pallas_call(functools.partial(cross_backward_kernel, heads=heads, chun...  37.2 us
    pallas_call x1, Pallas kernels, cross_forward(): pl.pallas_call(functools.partial(cross_forward_kernel, heads=heads, chunk...  25.2 us
    ppermute x3, starting transfers between devices, turn(): lax.ppermute(values, 'tensor', [(i, (i + step) % ranks) for i in range(ra...  22.7 us
    ppermute x5, waiting for transfers between devices, sent(): lax.ppermute(values.astype(bf16), 'dp', [(i, i ^ bits) for i in range(gro...  21.9 us
    pallas_call x1, Pallas kernels, soap_main(): pl.pallas_call(soap_main_kernel, grid=(n,), in_specs=[pl.BlockSpec((side...  17.7 us
    pallas_call x1, Pallas kernels, weight_grads(): pl.pallas_call(functools.partial(weight_grads_kernel, side=side, owned=ow...  17.3 us
  transfers between devices with their start and end apart: 33, of which 9 were waited for; matrix products, arithmetic and copies ran while one was open for 12% of the time, Pallas kernels for 26%

profile of v6, /device:TPU:0, one launch (start us, length us, event | category | flops | bytes accessed | tf_op | source)
XLA Modules:
  0.0 452.6 jit_solution(5672955463262605940)
XLA Ops:
  7.2 1.3 pad_bitcast_fusion.1.line
  8.5 2.3 pack.1
  10.9 3.0 collective-permute-start.6
  13.9 1.5 collective-permute-start
  15.4 1.5 collective-permute-start.1
  16.9 2.2 collective-permute-start.12
  19.2 5.1 %copy.39.frames.refs_6_ = bf16[2,1500,768]{2,1,0:T(8,128)(2,1)} copy(bf16[2,1500,768]{2,0,1:T(2,128)(2,1)} %param.17) | data formatting | bytes 9216000 | tf_op args[1]
  24.2 9.9 %soap_pre.1 = (f32[8,192,192]{2,1,0:T(8,128)}, f32[8,2,192,192]{3,2,1,0:T(8,128)}) custom-call(f32[8,192,192]{2,1,0:T(8,128)} %bitcast.120, f32[8,2,192,192]{3,2,1,0:T(8,128)} %bitcast.104, f32[8,2,192,192]{3,2,1,0:T(8,128)} %bitcast.106), custom_call_target="tpu_custom_call" | custom-call | tf_op jit(solution)/shard_map/soap_pre/pallas_call | solution.py:127
  35.1 17.5 %collective-permute-start.2 = (bf16[2320,128]{1,0:T(8,128)(2,1)S(1)}, bf16[2320,128]{1,0:T(8,128)(2,1)}, u32[]{:S(2)}, u32[]{:S(2)}) collective-permute-start(bf16[2320,128]{1,0:T(8,128)(2,1)S(1)} %copy-done.12), channel_id=1, source_target_pairs={{0,2},{1,3},{2,0},{3,1},{4,6},{5,7},{6,4},{7,5},{8,10},{9,11},{10,... | collective-permute-start | bytes 1781768 | tf_op jit(solution)/shard_map/ppermute | solution.py:428
  55.2 1.5 collective-permute-start.4
  56.7 1.7 slice.209
  58.4 1.5 collective-permute-start.3
  59.9 1.9 pad_maximum_fusion.1
  61.8 6.0 %collective-permute-done.2 = bf16[2320,128]{1,0:T(8,128)(2,1)} collective-permute-done((bf16[2320,128]{1,0:T(8,128)(2,1)S(1)}, bf16[2320,128]{1,0:T(8,128)(2,1)}, u32[]{:S(2)}, u32[]{:S(2)}) %collective-permute-start.2) | collective-permute-done | bytes 593952 | tf_op jit(solution)/shard_map/ppermute | solution.py:428
  68.2 1.6 collective-permute-start.10
  70.8 1.6 collective-permute-start.9
  73.5 2.5 maximum_maximum_fusion.refs_0_
  76.1 4.6 %collective-permute-done.9 = bf16[1,1152,128]{2,1,0:T(8,128)(2,1)S(1)} collective-permute-done((bf16[1,1152,128]{2,1,0:T(8,128)(2,1)S(1)}, bf16[1,1152,128]{2,1,0:T(8,128)(2,1)S(1)}, u32[]{:S(2)}, u32[]{:S(2)}) %collective-permute-start.9) | collective-permute-done | bytes 294944 | tf_op jit(solution)/shard_map/ppermute | solution.py:425
  81.3 1.5 collective-permute-start.15
  82.8 4.4 maximum_maximum_fusion.1.refs_2_
  87.2 6.2 %collective-permute-done.19 = bf16[1,2320,128]{2,1,0:T(8,128)(2,1)S(1)} collective-permute-done((bf16[1,2320,128]{2,1,0:T(8,128)(2,1)}, bf16[1,2320,128]{2,1,0:T(8,128)(2,1)S(1)}, u32[]{:S(2)}, u32[]{:S(2)}) %collective-permute-start.19) | collective-permute-done | bytes 593952 | tf_op jit(solution)/shard_map/ppermute | solution.py:425
  94.1 4.3 collective-permute-done.15
  98.4 1.5 collective-permute-start.20
  99.9 4.4 maximum_maximum_fusion.2.refs_4_
  104.5 1.7 collective-permute-done.20
  106.2 4.4 maximum_maximum_fusion.3.refs_6_
  118.0 16.8 %assemble.1 = (bf16[768,3072]{1,0:T(8,128)(2,1)}, bf16[768,2048]{1,0:T(8,128)(2,1)}, bf16[768,1024]{1,0:T(8,128)(2,1)}, bf16[1024,768]{1,0:T(8,128)(2,1)}, bf16[...) custom-call(s32[256]{0:T(256)} %add.177.target, ...), custom_call_target="tpu_custom_call" | custom-call | tf_op jit(solution)/shard_map/assemble/pallas_call | solution.py:535
  134.8 15.3 %frame_projection.1.key.value = bf16[8,2,1500,256]{3,2,1,0:T(8,128)(2,1)} custom-call(bf16[2,1500,768]{2,1,0:T(8,128)(2,1)} %copy.39.frames.refs_6_, bf16[768,2048]{1,0:T(8,128)(2,1)} %get-tuple-element.80.weight.key_weight.value_weight, f32[8,1,256]{2,1,0:T(1,128)} %bitcast.139), custom_call_target="tpu_custom_call" | custom-call | tf_op jit(solution)/shard_map/frame_projection/pallas_call | solution.py:690
  150.1 9.4 %first_projections.1 = (bf16[896,768]{1,0:T(8,128)(2,1)}, bf16[896,3072]{1,0:T(8,128)(2,1)}) custom-call(bf16[2,896,768]{2,1,0:T(8,128)(2,1)} %bitcast.98, f32[19,768]{1,0:T(8,128)} %copy-done.24, f32[1,3072]{1,0:T(1,128)} %bitcast.138, bf16[768,3072]{1,0:T(8,128)(2,1)} %get-tuple-element.74.weight.query_weight.key_weight.value_weight), custom_call_target="tpu_custom_call" | custom-call | tf_op jit(solution)/shard_map/first_projections/pallas_call | solution.py:882
  159.5 12.6 %self_forward.1 = (bf16[2,448,1024]{2,1,0:T(8,128)(2,1)}, f32[2,4,8,448]{3,2,1,0:T(8,128)}) custom-call(bf16[2,448,3072]{2,1,0:T(8,128)(2,1)} %bitcast.92, bf16[2,448,3072]{2,1,0:T(8,128)(2,1)} %bitcast.93, bf16[2,448,3072]{2,1,0:T(8,128)(2,1)} %bitcast.94, s32[2,448,1]{2,1,0:T(8,128)} %copy.40.seg_col, s32[2,1,448]{2,1,0:T(1,128)} %broadcast_in_dim.146.seg_row, ...), custom_call_target="tpu_custom_call" | custom-call | tf_op jit(solution)/shard_map/self_forward/pallas_call | solution.py:314
  172.3 1.4 copy-done.8
  173.7 1.7 fusion.28
  177.8 2.9 add_convert_fusion.1
  180.6 25.2 %cross_forward.1 = (bf16[2,448,1024]{2,1,0:T(8,128)(2,1)}, f32[2,4,8,448]{3,2,1,0:T(8,128)}) custom-call(bf16[2,448,1024]{2,1,0:T(8,128)(2,1)} %bitcast.111, bf16[8,2,1500,256]{3,2,1,0:T(8,128)(2,1)} %frame_projection.1.key.value, bf16[8,2,1500,256]{3,2,1,0:T(8,128)(2,1)} %frame_projection.1.key.value), custom_call_target="tpu_custom_call" | custom-call | tf_op jit(solution)/shard_map/cross_forward/pallas_call | solution.py:331
  205.9 42.5 %middle.1 = (f32[896,768]{1,0:T(8,128)}, f32[896,768]{1,0:T(8,128)}, bf16[896,1024]{1,0:T(8,128)(2,1)}, bf16[896,768]{1,0:T(8,128)(2,1)}, bf16[896,768]{1,0:T(8,...) custom-call(s32[1]{0:T(128)} %bitcast.rank, ...), custom_call_target="tpu_custom_call" | custom-call | tf_op jit(solution)/shard_map/middle/pallas_call | solution.py:852
  248.4 37.2 %cross_backward.1 = (bf16[2,448,1024]{2,1,0:T(8,128)(2,1)}, bf16[2,1500,256]{2,1,0:T(8,128)(2,1)}, bf16[2,1500,256]{2,1,0:T(8,128)(2,1)}) custom-call(s32[1]{0:T(128)} %bitcast.rank, bf16[2,448,1024]{2,1,0:T(8,128)(2,1)} %bitcast.112, bf16[8,2,1500,256]{3,2,1,0:T(8,128)(2,1)} %frame_projection.1.key.value, ...), custom_call_target="tpu_custom_call" | custom-call | tf_op jit(solution)/shard_map/cross_backward/pallas_call | solution.py:354
  285.6 6.0 %frames_back.1 = bf16[4,2,384,768]{3,2,1,0:T(8,128)(2,1)} custom-call(s32[1]{0:T(128)} %bitcast.rank, bf16[2,1500,256]{2,1,0:T(8,128)(2,1)} %get-tuple-element.96.dk.refs_7_, bf16[2,1500,256]{2,1,0:T(8,128)(2,1)} %get-tuple-element.97.dv.refs_8_, bf16[768,2048]{1,0:T(8,128)(2,1)} %get-tuple-element.80.weight.key_weight.value_weight, ...), custom_call_target="tpu_custom_call" | custom-call | tf_op jit(solution)/shard_map/frames_back/pallas_call | solution.py:718
  291.6 3.7 multiply_reduce_fusion
  295.4 2.3 convert_reduce_fusion.2
  297.7 2.9 convolution_convert_fusion
  300.5 7.1 %self_backward.1 = bf16[2,448,768]{2,1,0:T(8,128)(2,1)} custom-call(s32[1]{0:T(128)} %bitcast.rank, bf16[2,448,3072]{2,1,0:T(8,128)(2,1)} %bitcast.95, bf16[2,448,3072]{2,1,0:T(8,128)(2,1)} %bitcast.96, bf16[2,448,3072]{2,1,0:T(8,128)(2,1)} %bitcast.97, bf16[2,448,1024]{2,1,0:T(8,128)(2,1)} %bitcast.129, bf16[2,448,1024]{2,1,0:T(8,128)(2,1)} %get-tuple-element.76.mixed, ...), custom_call_target="tpu_custom_call" | custom-call | tf_op jit(solution)/shard_map/self_backward/pallas_call | solution.py:383
  307.6 4.9 %first_back.1 = (bf16[896,768]{1,0:T(8,128)(2,1)}, f32[2,768]{1,0:T(2,128)}, f32[1,768]{1,0:T(1,128)}) custom-call(s32[1]{0:T(128)} %bitcast.rank, bf16[896,768]{1,0:T(8,128)(2,1)} %bitcast.108, bf16[768,3072]{1,0:T(8,128)(2,1)} %get-tuple-element.74.weight.query_weight.key_weight.value_weight, ...), custom_call_target="tpu_custom_call" | custom-call | tf_op jit(solution)/shard_map/first_back/pallas_call | solution.py:664
  314.2 1.8 convert_reduce_fusion
  318.4 17.3 %weight_grads.1 = bf16[8,2320,128]{2,1,0:T(8,128)(2,1)} custom-call(s32[1]{0:T(128)} %bitcast.rank, s32[64]{0:T(128)} %get-tuple-element.172.slot, s32[64]{0:T(128)} %get-tuple-element.171.sub, bf16[896,768]{1,0:T(8,128)(2,1)} %get-tuple-element.102.refs_0_, bf16[896,768]{1,0:T(8,128)(2,1)} %get-tuple-element.103.refs_1_, ...), custom_call_target="tpu_custom_call" | custom-call | tf_op jit(solution)/shard_map/weight_grads/pallas_call | solution.py:615
  335.7 1.8 slice.231
  338.5 2.0 constant_dynamic-slice_fusion
  340.5 1.9 collective-permute-done.23
  342.4 3.0 add_convert_fusion
  348.0 1.5 collective-permute-start.26
  349.5 1.3 fusion.10
  350.8 12.4 %collective-permute-done.24 = bf16[2,1152,128]{2,1,0:T(8,128)(2,1)} collective-permute-done((bf16[2,1152,128]{2,1,0:T(8,128)(2,1)}, bf16[2,1152,128]{2,1,0:T(8,128)(2,1)}, u32[]{:S(2)}, u32[]{:S(2)}) %collective-permute-start.24) | collective-permute-done | bytes 589856 | tf_op jit(solution)/shard_map/ppermute | solution.py:637
  363.2 1.2 convert_add_fusion.2
  364.4 1.6 collective-permute-start.25
  366.0 1.2 convert_add_fusion.1
  368.0 5.0 %collective-permute-done.25 = bf16[1152,128]{1,0:T(8,128)(2,1)S(1)} collective-permute-done((bf16[1152,128]{1,0:T(8,128)(2,1)S(1)}, bf16[1152,128]{1,0:T(8,128)(2,1)S(1)}, u32[]{:S(2)}, u32[]{:S(2)}) %collective-permute-start.25) | collective-permute-done | bytes 294944 | tf_op jit(solution)/shard_map/ppermute | solution.py:637
  373.0 2.6 collective-permute-done.27
  375.8 1.1 pad_maximum_fusion.grad
  376.9 17.7 %soap_main.1 = (f32[8,192,192]{2,1,0:T(8,128)}, f32[8,192,192]{2,1,0:T(8,128)}, f32[8,192,192]{2,1,0:T(8,128)}, f32[8,2,192,192]{3,2,1,0:T(8,128)}, f32[8,2,192,...) custom-call(f32[2320,128]{1,0:T(8,128)} %pad_maximum_fusion.grad, f32[8,192,192]{2,1,0:T(8,128)} %bitcast.119, ...), custom_call_target="tpu_custom_call" | custom-call | tf_op jit(solution)/shard_map/soap_main/pallas_call | solution.py:136
  394.6 3.8 collective-permute-start.29
  398.4 2.3 fusion.8
  400.7 1.9 copy-done
  402.6 38.6 %chol_bases.1 = f32[16,192,192]{2,1,0:T(8,128)} custom-call(f32[16,192,192]{2,1,0:T(8,128)S(1)} %bitcast.91, f32[16,192,192]{2,1,0:T(8,128)} %bitcast.124), custom_call_target="tpu_custom_call" | custom-call | tf_op jit(solution)/shard_map/chol_bases/pallas_call | solution.py:144
  441.9 1.4 slice_convert_fusion
  443.3 2.6 copy.43
  (213 shorter events, 26.1 us)
Async XLA Ops:
  7.2 142.9 %all-gather.2.cloned.1.call-start = ((), (), s32[]{:S(2)}) async-start(), calls=%async_computation.2 | async-start | bytes 3440640 | tf_op jit(solution)/shard_map/all_gather | solution.py:947
  10.9 23.3 %collective-permute-start.6 = (bf16[2320,128]{1,0:T(8,128)(2,1)}, bf16[2320,128]{1,0:T(8,128)(2,1)}, u32[]{:S(2)}, u32[]{:S(2)}) collective-permute-start(bf16[2320,128]{1,0:T(8,128)(2,1)} %pack.1), channel_id=1, source_target_pairs={{0,1},{1,2},{2,3},{3,0},{4,5},{5,6},{6,7},{7,4},{8,9},{9,10},{10,1... | collective-permute-start | bytes 1781768 | tf_op jit(solution)/shard_map/ppermute | solution.py:428
  13.9 20.3 %collective-permute-start = (bf16[1,2320,128]{2,1,0:T(8,128)(2,1)}, bf16[1,2320,128]{2,1,0:T(8,128)(2,1)S(1)}, u32[]{:S(2)}, u32[]{:S(2)}) collective-permute-start(bf16[1,2320,128]{2,1,0:T(8,128)(2,1)} %bitcast.125), channel_id=1, source_target_pairs={{0,8},{4,12},{8,0},{12,4},{16,24},{20,28},{24,16},{28,20},{1,9},{5... | collective-permute-start | bytes 1781768 | tf_op jit(solution)/shard_map/ppermute | solution.py:425
  15.4 18.8 %collective-permute-start.1 = (bf16[1,2320,128]{2,1,0:T(8,128)(2,1)}, bf16[1,2320,128]{2,1,0:T(8,128)(2,1)S(1)}, u32[]{:S(2)}, u32[]{:S(2)}) collective-permute-start(bf16[1,2320,128]{2,1,0:T(8,128)(2,1)} %bitcast.126), channel_id=1, source_target_pairs={{0,16},{4,20},{8,24},{12,28},{16,0},{20,4},{24,8},{28,12},{1,17},{... | collective-permute-start | bytes 1781768 | tf_op jit(solution)/shard_map/ppermute | solution.py:425
  16.9 35.7 %collective-permute-start.12 = (bf16[2320,128]{1,0:T(8,128)(2,1)}, bf16[2320,128]{1,0:T(8,128)(2,1)}, u32[]{:S(2)}, u32[]{:S(2)}) collective-permute-start(bf16[2320,128]{1,0:T(8,128)(2,1)} %pack.1), channel_id=1, source_target_pairs={{0,3},{1,0},{2,1},{3,2},{4,7},{5,4},{6,5},{7,6},{8,11},{9,8},{10,9... | collective-permute-start | bytes 1781768 | tf_op jit(solution)/shard_map/ppermute | solution.py:428
  24.2 10.9 %copy-start.12 = (bf16[2320,128]{1,0:T(8,128)(2,1)S(1)}, bf16[2320,128]{1,0:T(8,128)(2,1)}, u32[]{:S(2)}) copy-start(bf16[2320,128]{1,0:T(8,128)(2,1)} %pack.1) | copy-start | bytes 1781764
  24.2 35.7 %copy-start.6 = (bf16[2,112,768]{2,1,0:T(8,128)(2,1)S(1)}, bf16[2,112,768]{2,1,0:T(8,128)(2,1)}, u32[]{:S(2)}) copy-start(bf16[2,112,768]{2,1,0:T(8,128)(2,1)} %param.16) | copy-start | bytes 1032196
  34.2 18.4 %copy-start.23 = (bf16[1,2320,128]{2,1,0:T(8,128)(2,1)}, bf16[1,2320,128]{2,1,0:T(8,128)(2,1)S(1)}, u32[]{:S(2)}) copy-start(bf16[1,2320,128]{2,1,0:T(8,128)(2,1)S(1)} %collective-permute-done) | copy-start | bytes 1781764
  34.2 39.2 %copy-start.18 = (bf16[1,2320,128]{2,1,0:T(8,128)(2,1)}, bf16[1,2320,128]{2,1,0:T(8,128)(2,1)S(1)}, u32[]{:S(2)}) copy-start(bf16[1,2320,128]{2,1,0:T(8,128)(2,1)S(1)} %collective-permute-done.1) | copy-start | bytes 1781764
  34.2 18.4 %collective-permute-start.7 = (bf16[1,2320,128]{2,1,0:T(8,128)(2,1)}, bf16[1,2320,128]{2,1,0:T(8,128)(2,1)S(1)}, u32[]{:S(2)}, u32[]{:S(2)}) collective-permute-start(bf16[1,2320,128]{2,1,0:T(8,128)(2,1)} %bitcast.12), channel_id=1, source_target_pairs={{0,8},{4,12},{8,0},{12,4},{16,24},{20,28},{24,16},{28,20},{1,9},{5... | collective-permute-start | bytes 1781768 | tf_op jit(solution)/shard_map/ppermute | solution.py:425
  34.8 17.8 %collective-permute-start.8 = (bf16[1,2320,128]{2,1,0:T(8,128)(2,1)}, bf16[1,2320,128]{2,1,0:T(8,128)(2,1)S(1)}, u32[]{:S(2)}, u32[]{:S(2)}) collective-permute-start(bf16[1,2320,128]{2,1,0:T(8,128)(2,1)} %bitcast.12), channel_id=1, source_target_pairs={{0,16},{4,20},{8,24},{12,28},{16,0},{20,4},{24,8},{28,12},{1,17},{... | collective-permute-start | bytes 1781768 | tf_op jit(solution)/shard_map/ppermute | solution.py:425
  35.1 32.7 %collective-permute-start.2 = (bf16[2320,128]{1,0:T(8,128)(2,1)S(1)}, bf16[2320,128]{1,0:T(8,128)(2,1)}, u32[]{:S(2)}, u32[]{:S(2)}) collective-permute-start(bf16[2320,128]{1,0:T(8,128)(2,1)S(1)} %copy-done.12), channel_id=1, source_target_pairs={{0,2},{1,3},{2,0},{3,1},{4,6},{5,7},{6,4},{7,5},{8,10},{9,11},{10,... | collective-permute-start | bytes 1781768 | tf_op jit(solution)/shard_map/ppermute | solution.py:428
  52.6 20.8 %copy-start.16 = (bf16[1,2320,128]{2,1,0:T(8,128)(2,1)}, bf16[1,2320,128]{2,1,0:T(8,128)(2,1)S(1)}, u32[]{:S(2)}) copy-start(bf16[1,2320,128]{2,1,0:T(8,128)(2,1)S(1)} %collective-permute-done.8) | copy-start | bytes 1781764
  53.4 17.3 %collective-permute-start.13 = (bf16[1,2320,128]{2,1,0:T(8,128)(2,1)}, bf16[1,2320,128]{2,1,0:T(8,128)(2,1)S(1)}, u32[]{:S(2)}, u32[]{:S(2)}) collective-permute-start(bf16[1,2320,128]{2,1,0:T(8,128)(2,1)} %bitcast.13), channel_id=1, source_target_pairs={{0,8},{4,12},{8,0},{12,4},{16,24},{20,28},{24,16},{28,20},{1,9},{5... | collective-permute-start | bytes 1781768 | tf_op jit(solution)/shard_map/ppermute | solution.py:425
  53.9 18.4 %collective-permute-start.14 = (bf16[1,2320,128]{2,1,0:T(8,128)(2,1)}, bf16[1,2320,128]{2,1,0:T(8,128)(2,1)S(1)}, u32[]{:S(2)}, u32[]{:S(2)}) collective-permute-start(bf16[1,2320,128]{2,1,0:T(8,128)(2,1)} %bitcast.13), channel_id=1, source_target_pairs={{0,16},{4,20},{8,24},{12,28},{16,0},{20,4},{24,8},{28,12},{1,17},{... | collective-permute-start | bytes 1781768 | tf_op jit(solution)/shard_map/ppermute | solution.py:425
  55.2 18.2 %collective-permute-start.4 = (bf16[1,1168,128]{2,1,0:T(8,128)(2,1)}, bf16[1,1168,128]{2,1,0:T(8,128)(2,1)}, u32[]{:S(2)}, u32[]{:S(2)}) collective-permute-start(bf16[1,1168,128]{2,1,0:T(8,128)(2,1)} %slice.210), channel_id=1, source_target_pairs={{0,8},{4,12},{8,0},{12,4},{16,24},{20,28},{24,16},{28,20},{1,9},{5... | collective-permute-start | bytes 897032 | tf_op jit(solution)/shard_map/ppermute | solution.py:425
  58.4 14.5 %collective-permute-start.3 = (bf16[1,1152,128]{2,1,0:T(8,128)(2,1)}, bf16[1,1152,128]{2,1,0:T(8,128)(2,1)}, u32[]{:S(2)}, u32[]{:S(2)}) collective-permute-start(bf16[1,1152,128]{2,1,0:T(8,128)(2,1)} %slice.209), channel_id=1, source_target_pairs={{0,16},{4,20},{8,24},{12,28},{16,0},{20,4},{24,8},{28,12},{1,17},{... | collective-permute-start | bytes 884744 | tf_op jit(solution)/shard_map/ppermute | solution.py:425
  67.9 281.6 %reduce-scatter.3.cloned.1.call-start = ((), (), s32[]{:S(2)}) async-start(), calls=%async_computation.3 | async-start | bytes 1720320 | tf_op jit(solution)/shard_map/reduce_scatter | solution.py:1002
  68.2 13.1 %collective-permute-start.10 = (bf16[1,1168,128]{2,1,0:T(8,128)(2,1)S(1)}, bf16[1,1168,128]{2,1,0:T(8,128)(2,1)S(1)}, u32[]{:S(2)}, u32[]{:S(2)}) collective-permute-start(bf16[1,1168,128]{2,1,0:T(8,128)(2,1)S(1)} %slice.216), channel_id=1, source_target_pairs={{0,8},{4,12},{8,0},{12,4},{16,24},{20,28},{24,16},{28,20},{1,9},{5... | collective-permute-start | bytes 897032 | tf_op jit(solution)/shard_map/ppermute | solution.py:425
  70.7 2.7 copy-start.19
  70.8 10.0 %collective-permute-start.9 = (bf16[1,1152,128]{2,1,0:T(8,128)(2,1)S(1)}, bf16[1,1152,128]{2,1,0:T(8,128)(2,1)S(1)}, u32[]{:S(2)}, u32[]{:S(2)}) collective-permute-start(bf16[1,1152,128]{2,1,0:T(8,128)(2,1)S(1)} %slice.215), channel_id=1, source_target_pairs={{0,16},{4,20},{8,24},{12,28},{16,0},{20,4},{24,8},{28,12},{1,17},{... | collective-permute-start | bytes 884744 | tf_op jit(solution)/shard_map/ppermute | solution.py:425
  72.3 10.5 %copy-start.22 = (bf16[1,2320,128]{2,1,0:T(8,128)(2,1)S(1)}, bf16[1,2320,128]{2,1,0:T(8,128)(2,1)}, u32[]{:S(2)}) copy-start(bf16[1,2320,128]{2,1,0:T(8,128)(2,1)} %copy-done.21) | copy-start | bytes 1781764
  72.3 21.1 %collective-permute-start.19 = (bf16[1,2320,128]{2,1,0:T(8,128)(2,1)}, bf16[1,2320,128]{2,1,0:T(8,128)(2,1)S(1)}, u32[]{:S(2)}, u32[]{:S(2)}) collective-permute-start(bf16[1,2320,128]{2,1,0:T(8,128)(2,1)} %bitcast.14), channel_id=1, source_target_pairs={{0,16},{4,20},{8,24},{12,28},{16,0},{20,4},{24,8},{28,12},{1,17},{... | collective-permute-start | bytes 1781768 | tf_op jit(solution)/shard_map/ppermute | solution.py:425
  72.9 20.6 %collective-permute-start.18 = (bf16[1,2320,128]{2,1,0:T(8,128)(2,1)}, bf16[1,2320,128]{2,1,0:T(8,128)(2,1)S(1)}, u32[]{:S(2)}, u32[]{:S(2)}) collective-permute-start(bf16[1,2320,128]{2,1,0:T(8,128)(2,1)} %bitcast.14), channel_id=1, source_target_pairs={{0,8},{4,12},{8,0},{12,4},{16,24},{20,28},{24,16},{28,20},{1,9},{5... | collective-permute-start | bytes 1781768 | tf_op jit(solution)/shard_map/ppermute | solution.py:425
  73.4 2.6 copy-start.15
  73.4 2.6 copy-start.20
  73.4 9.4 %copy-start.17 = (bf16[1,2320,128]{2,1,0:T(8,128)(2,1)S(1)}, bf16[1,2320,128]{2,1,0:T(8,128)(2,1)}, u32[]{:S(2)}) copy-start(bf16[1,2320,128]{2,1,0:T(8,128)(2,1)} %copy-done.16) | copy-start | bytes 1781764
  75.9 38.9 %copy-start.5 = (bf16[4,2320,128]{2,1,0:T(8,128)(2,1)}, bf16[4,2320,128]{2,1,0:T(8,128)(2,1)S(1)}, u32[]{:S(2)}) copy-start(bf16[4,2320,128]{2,1,0:T(8,128)(2,1)S(1)} %maximum_maximum_fusion.refs_0_) | copy-start | bytes 7127044
  75.9 38.9 %collective-permute-start.5 = (bf16[4,2320,128]{2,1,0:T(8,128)(2,1)S(1)}, bf16[4,2320,128]{2,1,0:T(8,128)(2,1)}, u32[]{:S(2)}, u32[]{:S(2)}) collective-permute-start(bf16[4,2320,128]{2,1,0:T(8,128)(2,1)S(1)} %maximum_maximum_fusion.refs_0_), channel_id=1, source_target_pairs={{0,4},{4,0},{8,12},{12,8},{16,20},{20,16},{24,28},{28,24},{1,5},{5... | collective-permute-start | bytes 7127048 | tf_op jit(solution)/shard_map/ppermute | solution.py:425
  80.7 19.2 %collective-permute-start.16 = (bf16[1,1168,128]{2,1,0:T(8,128)(2,1)S(1)}, bf16[1,1168,128]{2,1,0:T(8,128)(2,1)S(1)}, u32[]{:S(2)}, u32[]{:S(2)}) collective-permute-start(bf16[1,1168,128]{2,1,0:T(8,128)(2,1)S(1)} %slice.218), channel_id=1, source_target_pairs={{0,8},{4,12},{8,0},{12,4},{16,24},{20,28},{24,16},{28,20},{1,9},{5... | collective-permute-start | bytes 897032 | tf_op jit(solution)/shard_map/ppermute | solution.py:425
  81.3 17.1 %collective-permute-start.15 = (bf16[1,1152,128]{2,1,0:T(8,128)(2,1)S(1)}, bf16[1,1152,128]{2,1,0:T(8,128)(2,1)S(1)}, u32[]{:S(2)}, u32[]{:S(2)}) collective-permute-start(bf16[1,1152,128]{2,1,0:T(8,128)(2,1)S(1)} %slice.217), channel_id=1, source_target_pairs={{0,16},{4,20},{8,24},{12,28},{16,0},{20,4},{24,8},{28,12},{1,17},{... | collective-permute-start | bytes 884744 | tf_op jit(solution)/shard_map/ppermute | solution.py:425
  93.5 24.5 %collective-permute-start.11 = (bf16[4,2320,128]{2,1,0:T(8,128)(2,1)}, bf16[4,2320,128]{2,1,0:T(8,128)(2,1)}, u32[]{:S(2)}, u32[]{:S(2)}) collective-permute-start(bf16[4,2320,128]{2,1,0:T(8,128)(2,1)} %maximum_maximum_fusion.1.refs_2_), channel_id=1, source_target_pairs={{0,4},{4,0},{8,12},{12,8},{16,20},{20,16},{24,28},{28,24},{1,5},{5... | collective-permute-start | bytes 7127048 | tf_op jit(solution)/shard_map/ppermute | solution.py:425
  93.5 12.6 %collective-permute-start.21 = (bf16[1,1168,128]{2,1,0:T(8,128)(2,1)S(1)}, bf16[1,1168,128]{2,1,0:T(8,128)(2,1)S(1)}, u32[]{:S(2)}, u32[]{:S(2)}) collective-permute-start(bf16[1,1168,128]{2,1,0:T(8,128)(2,1)S(1)} %slice.220), channel_id=1, source_target_pairs={{0,8},{4,12},{8,0},{12,4},{16,24},{20,28},{24,16},{28,20},{1,9},{5... | collective-permute-start | bytes 897032 | tf_op jit(solution)/shard_map/ppermute | solution.py:425
  98.4 7.7 %collective-permute-start.20 = (bf16[1,1152,128]{2,1,0:T(8,128)(2,1)S(1)}, bf16[1,1152,128]{2,1,0:T(8,128)(2,1)S(1)}, u32[]{:S(2)}, u32[]{:S(2)}) collective-permute-start(bf16[1,1152,128]{2,1,0:T(8,128)(2,1)S(1)} %slice.219), channel_id=1, source_target_pairs={{0,16},{4,20},{8,24},{12,28},{16,0},{20,4},{24,8},{28,12},{1,17},{... | collective-permute-start | bytes 884744 | tf_op jit(solution)/shard_map/ppermute | solution.py:425
  104.4 6.2 %copy-start.35 = (s32[32]{0:T(128)S(1)}, s32[32]{0:T(128)}, u32[]{:S(2)}) copy-start(s32[32]{0:T(128)} %constant.133.clone) | copy-start | bytes 388
  104.4 6.4 %copy-start.39 = (s32[32]{0:T(128)S(1)}, s32[32]{0:T(128)}, u32[]{:S(2)}) copy-start(s32[32]{0:T(128)} %constant.152) | copy-start | bytes 388
  104.4 6.6 %copy-start.26 = (s32[2,448]{1,0:T(2,128)S(1)}, s32[2,448]{1,0:T(2,128)}, u32[]{:S(2)}) copy-start(s32[2,448]{1,0:T(2,128)} %param.19) | copy-start | bytes 10756
  104.4 8.2 %copy-start.27 = (s32[2,448]{1,0:T(2,128)S(1)}, s32[2,448]{1,0:T(2,128)}, u32[]{:S(2)}) copy-start(s32[2,448]{1,0:T(2,128)} %param.20) | copy-start | bytes 10756
  104.4 9.8 %copy-start.34 = (s32[64]{0:T(128)S(1)}, s32[64]{0:T(128)}, u32[]{:S(2)}) copy-start(s32[64]{0:T(128)} %param.21) | copy-start | bytes 772
  104.4 13.6 %collective-permute-start.17 = (bf16[4,2320,128]{2,1,0:T(8,128)(2,1)}, bf16[4,2320,128]{2,1,0:T(8,128)(2,1)}, u32[]{:S(2)}, u32[]{:S(2)}) collective-permute-start(bf16[4,2320,128]{2,1,0:T(8,128)(2,1)} %maximum_maximum_fusion.2.refs_4_), channel_id=1, source_target_pairs={{0,4},{4,0},{8,12},{12,8},{16,20},{20,16},{24,28},{28,24},{1,5},{5... | collective-permute-start | bytes 7127048 | tf_op jit(solution)/shard_map/ppermute | solution.py:425
  110.6 7.4 %collective-permute-start.22 = (bf16[4,2320,128]{2,1,0:T(8,128)(2,1)}, bf16[4,2320,128]{2,1,0:T(8,128)(2,1)}, u32[]{:S(2)}, u32[]{:S(2)}) collective-permute-start(bf16[4,2320,128]{2,1,0:T(8,128)(2,1)} %maximum_maximum_fusion.3.refs_6_), channel_id=1, source_target_pairs={{0,4},{4,0},{8,12},{12,8},{16,20},{20,16},{24,28},{28,24},{1,5},{5... | collective-permute-start | bytes 7127048 | tf_op jit(solution)/shard_map/ppermute | solution.py:425
  115.9 18.8 %copy-start.24 = (f32[19,768]{1,0:T(8,128)}, f32[19,768]{1,0:T(8,128)S(1)}, u32[]{:S(2)}) copy-start(f32[19,768]{1,0:T(8,128)S(1)} %reshape.323.vectors.refs_3_) | copy-start | bytes 175108
  159.5 12.6 %copy-start.3 = (bf16[2,2,448,768]{3,2,1,0:T(8,128)(2,1)S(1)}, bf16[2,2,448,768]{3,2,1,0:T(8,128)(2,1)}, u32[]{:S(2)}) copy-start(bf16[2,2,448,768]{3,2,1,0:T(8,128)(2,1)} %all-gather.2.cloned.1.call-done) | copy-start | bytes 8257540
  159.5 12.8 %copy-start.36 = (bf16[1024,768]{1,0:T(8,128)(2,1)S(1)}, bf16[1024,768]{1,0:T(8,128)(2,1)}, u32[]{:S(2)}) copy-start(bf16[1024,768]{1,0:T(8,128)(2,1)} %get-tuple-element.77) | copy-start | bytes 4718596
  175.9 1.9 copy-start.38
  176.9 3.7 copy-start.9
  285.6 6.0 %copy-start.2 = (f32[896,768]{1,0:T(8,128)S(1)}, f32[896,768]{1,0:T(8,128)}, u32[]{:S(2)}) copy-start(f32[896,768]{1,0:T(8,128)} %copy-done.1) | copy-start | bytes 8257540
  285.6 6.0 %copy-start.7 = (bf16[2,448,1024]{2,1,0:T(8,128)(2,1)S(1)}, bf16[2,448,1024]{2,1,0:T(8,128)(2,1)}, u32[]{:S(2)}) copy-start(bf16[2,448,1024]{2,1,0:T(8,128)(2,1)} %get-tuple-element.95) | copy-start | bytes 5505028
  291.6 3.8 copy-start.11
  295.4 2.3 copy-start.37
  297.7 2.9 copy-start.10
  307.6 5.7 %copy-start.4 = (bf16[2,1500,256]{2,1,0:T(8,128)(2,1)S(1)}, bf16[2,1500,256]{2,1,0:T(8,128)(2,1)}, u32[]{:S(2)}) copy-start(bf16[2,1500,256]{2,1,0:T(8,128)(2,1)} %get-tuple-element.97.dv.refs_8_) | copy-start | bytes 4608004
  312.6 129.3 %reduce-scatter.5.cloned.1.call-start = ((), (), s32[]{:S(2)}) async-start(), calls=%async_computation.4 | async-start | bytes 5898240 | tf_op jit(solution)/shard_map/reduce_scatter | solution.py:987
  337.5 4.9 %collective-permute-start.23 = (bf16[4,2320,128]{2,1,0:T(8,128)(2,1)S(1)}, bf16[4,2320,128]{2,1,0:T(8,128)(2,1)}, u32[]{:S(2)}, u32[]{:S(2)}) collective-permute-start(bf16[4,2320,128]{2,1,0:T(8,128)(2,1)S(1)} %slice.231), channel_id=1, source_target_pairs={{0,4},{4,0},{8,12},{12,8},{16,20},{20,16},{24,28},{28,24},{1,5},{5... | collective-permute-start | bytes 7127048 | tf_op jit(solution)/shard_map/ppermute | solution.py:637
  347.3 15.9 %collective-permute-start.24 = (bf16[2,1152,128]{2,1,0:T(8,128)(2,1)}, bf16[2,1152,128]{2,1,0:T(8,128)(2,1)}, u32[]{:S(2)}, u32[]{:S(2)}) collective-permute-start(bf16[2,1152,128]{2,1,0:T(8,128)(2,1)} %pad_maximum_fusion.2), channel_id=1, source_target_pairs={{0,8},{4,12},{8,0},{12,4},{16,24},{20,28},{24,16},{28,20},{1,9},{5... | collective-permute-start | bytes 1769480 | tf_op jit(solution)/shard_map/ppermute | solution.py:637
  348.0 18.0 %collective-permute-start.26 = (bf16[2,1168,128]{2,1,0:T(8,128)(2,1)}, bf16[2,1168,128]{2,1,0:T(8,128)(2,1)}, u32[]{:S(2)}, u32[]{:S(2)}) collective-permute-start(bf16[2,1168,128]{2,1,0:T(8,128)(2,1)} %slice.239), channel_id=1, source_target_pairs={{0,16},{4,20},{8,24},{12,28},{16,0},{20,4},{24,8},{28,12},{1,17},{... | collective-permute-start | bytes 1794056 | tf_op jit(solution)/shard_map/ppermute | solution.py:637
  364.4 8.5 %collective-permute-start.25 = (bf16[1152,128]{1,0:T(8,128)(2,1)S(1)}, bf16[1152,128]{1,0:T(8,128)(2,1)S(1)}, u32[]{:S(2)}, u32[]{:S(2)}) collective-permute-start(bf16[1152,128]{1,0:T(8,128)(2,1)S(1)} %fusion.14), channel_id=1, source_target_pairs={{0,16},{4,20},{8,24},{12,28},{16,0},{20,4},{24,8},{28,12},{1,17},{... | collective-permute-start | bytes 884744 | tf_op jit(solution)/shard_map/ppermute | solution.py:637
  367.2 8.3 %collective-permute-start.27 = (bf16[1168,128]{1,0:T(8,128)(2,1)S(1)}, bf16[1168,128]{1,0:T(8,128)(2,1)S(1)}, u32[]{:S(2)}, u32[]{:S(2)}) collective-permute-start(bf16[1168,128]{1,0:T(8,128)(2,1)S(1)} %fusion.13), channel_id=1, source_target_pairs={{0,8},{4,12},{8,0},{12,4},{16,24},{20,28},{24,16},{28,20},{1,9},{5... | collective-permute-start | bytes 897032 | tf_op jit(solution)/shard_map/ppermute | solution.py:637
  375.7 18.9 %collective-permute-start.28 = (f32[16,128]{1,0:T(8,128)S(1)}, f32[16,128]{1,0:T(8,128)S(1)}, u32[]{:S(2)}, u32[]{:S(2)}) collective-permute-start(f32[16,128]{1,0:T(8,128)S(1)} %slice.242), channel_id=1, source_target_pairs={{0,1},{1,0},{2,3},{3,2},{4,5},{5,4},{6,7},{7,6},{8,9},{9,8},{10,11... | collective-permute-start | bytes 24584 | tf_op jit(solution)/shard_map/ppermute | solution.py:1044
  376.9 21.6 %copy-start.13 = (bf16[2,112,768]{2,1,0:T(8,128)(2,1)S(1)}, bf16[2,112,768]{2,1,0:T(8,128)(2,1)}, u32[]{:S(2)}) copy-start(bf16[2,112,768]{2,1,0:T(8,128)(2,1)} %reduce-scatter.3.cloned.1.call-done) | copy-start | bytes 1032196
  394.6 46.6 %collective-permute-start.29 = (f32[16,128]{1,0:T(8,128)S(1)}, f32[16,128]{1,0:T(8,128)S(1)}, u32[]{:S(2)}, u32[]{:S(2)}) collective-permute-start(f32[16,128]{1,0:T(8,128)S(1)} %slice_add_fusion), channel_id=1, source_target_pairs={{0,2},{1,3},{2,0},{3,1},{4,6},{5,7},{6,4},{7,5},{8,10},{9,11},{10,... | collective-permute-start | bytes 24584 | tf_op jit(solution)/shard_map/ppermute | solution.py:1044
  402.6 38.7 %copy-start.25 = (f32[1824]{0:T(1024)S(1)}, f32[1824]{0:T(1024)}, u32[]{:S(2)}) copy-start(f32[1824]{0:T(1024)} %param.27) | copy-start | bytes 21892
  402.6 38.7 %copy-start.30 = (f32[1824]{0:T(1024)S(1)}, f32[1824]{0:T(1024)}, u32[]{:S(2)}) copy-start(f32[1824]{0:T(1024)} %param.28) | copy-start | bytes 21892
  402.6 38.7 %copy-start.31 = (f32[1824]{0:T(1024)S(1)}, f32[1824]{0:T(1024)}, u32[]{:S(2)}) copy-start(f32[1824]{0:T(1024)} %param.29) | copy-start | bytes 21892
  (9 other events, 11.0 us)
Sparse Core Ops, SparseCore 0:
  68.0 57.9 all-gather.1
  312.7 33.5 reduce-scatter.2
  348.7 84.4 reduce-scatter.4

commit v7 on v6

--- a/solution.py
+++ b/solution.py
@@ -137,7 +137,7 @@
         out_specs=[t, t, t, p, p, p], out_shape=[ts, ts, ts, ps, ps, ps], name="soap_main")(
         grad, master, first, second, stats, bases, rot_first, stats_rot)
 
-def chol_bases(turned, grams, block=64, unroll=4, passes=3):
+def chol_bases(turned, grams, block=64, unroll=8, passes=3):
     n, _, side, _ = turned.shape
     shape = (2 * n, side, side)
     unroll = min(unroll, 2 * n)

time: 456 us -> 455 us (level)
  transfers between devices with their start and end apart: 33 -> 33, of which waited for: 9 -> 9; matrix products, arithmetic and copies ran while one was open for 12% -> 12% of each run, Pallas kernels for 26% -> 25%
where the time goes in v7:
time: 455 us; the launch traced here: 452 us
  Pallas kernels  262 us (58%)
  starting transfers between devices  48.7 us (11%)
  waiting for transfers between devices  44.8 us (10%)
  other arithmetic  39.1 us (9%)
  local copies, waits for them, and re-layouts  31.1 us (7%)
  between operations  14.8 us (3%)
  matrix products  11.2 us (2%)
    pallas_call x1, Pallas kernels, middle(): pl.pallas_call(functools.partial(middle_kernel, parts=parts), grid_spec=p...  42.5 us
    pallas_call x1, Pallas kernels, chol_bases(): pl.pallas_call(functools.partial(chol_kernel, block=block, unroll=unroll,...  37.6 us
    pallas_call x1, Pallas kernels, cross_backward(): pl.pallas_call(functools.partial(cross_backward_kernel, heads=heads, chun...  37.2 us
    pallas_call x1, Pallas kernels, cross_forward(): pl.pallas_call(functools.partial(cross_forward_kernel, heads=heads, chunk...  25.2 us
    ppermute x3, starting transfers between devices, turn(): lax.ppermute(values, 'tensor', [(i, (i + step) % ranks) for i in range(ra...  22.7 us
    ppermute x5, waiting for transfers between devices, sent(): lax.ppermute(values.astype(bf16), 'dp', [(i, i ^ bits) for i in range(gro...  21.8 us
    pallas_call x1, Pallas kernels, soap_main(): pl.pallas_call(soap_main_kernel, grid=(n,), in_specs=[pl.BlockSpec((side...  17.7 us
    pallas_call x1, Pallas kernels, weight_grads(): pl.pallas_call(functools.partial(weight_grads_kernel, side=side, owned=ow...  17.3 us
  transfers between devices with their start and end apart: 33, of which 9 were waited for; matrix products, arithmetic and copies ran while one was open for 12% of the time, Pallas kernels for 25%

profile of v7, /device:TPU:0, one launch (start us, length us, event | category | flops | bytes accessed | tf_op | source)
XLA Modules:
  0.0 451.7 jit_solution(9258385302214309265)
XLA Ops:
  7.2 1.3 pad_bitcast_fusion.1.line
  8.5 2.3 pack.1
  10.9 3.0 collective-permute-start.6
  13.9 1.5 collective-permute-start
  15.4 1.5 collective-permute-start.1
  16.9 2.2 collective-permute-start.12
  19.2 5.1 %copy.39.frames.refs_6_ = bf16[2,1500,768]{2,1,0:T(8,128)(2,1)} copy(bf16[2,1500,768]{2,0,1:T(2,128)(2,1)} %param.17) | data formatting | bytes 9216000 | tf_op args[1]
  24.2 9.9 %soap_pre.1 = (f32[8,192,192]{2,1,0:T(8,128)}, f32[8,2,192,192]{3,2,1,0:T(8,128)}) custom-call(f32[8,192,192]{2,1,0:T(8,128)} %bitcast.120, f32[8,2,192,192]{3,2,1,0:T(8,128)} %bitcast.104, f32[8,2,192,192]{3,2,1,0:T(8,128)} %bitcast.106), custom_call_target="tpu_custom_call" | custom-call | tf_op jit(solution)/shard_map/soap_pre/pallas_call | solution.py:127
  35.1 17.5 %collective-permute-start.2 = (bf16[2320,128]{1,0:T(8,128)(2,1)S(1)}, bf16[2320,128]{1,0:T(8,128)(2,1)}, u32[]{:S(2)}, u32[]{:S(2)}) collective-permute-start(bf16[2320,128]{1,0:T(8,128)(2,1)S(1)} %copy-done.12), channel_id=1, source_target_pairs={{0,2},{1,3},{2,0},{3,1},{4,6},{5,7},{6,4},{7,5},{8,10},{9,11},{10,... | collective-permute-start | bytes 1781768 | tf_op jit(solution)/shard_map/ppermute | solution.py:428
  55.2 1.5 collective-permute-start.4
  56.7 1.7 slice.209
  58.4 1.5 collective-permute-start.3
  59.9 1.9 pad_maximum_fusion.1
  61.8 6.0 %collective-permute-done.2 = bf16[2320,128]{1,0:T(8,128)(2,1)} collective-permute-done((bf16[2320,128]{1,0:T(8,128)(2,1)S(1)}, bf16[2320,128]{1,0:T(8,128)(2,1)}, u32[]{:S(2)}, u32[]{:S(2)}) %collective-permute-start.2) | collective-permute-done | bytes 593952 | tf_op jit(solution)/shard_map/ppermute | solution.py:428
  68.2 1.6 collective-permute-start.10
  70.8 1.6 collective-permute-start.9
  73.5 2.5 maximum_maximum_fusion.refs_0_
  76.1 4.6 %collective-permute-done.9 = bf16[1,1152,128]{2,1,0:T(8,128)(2,1)S(1)} collective-permute-done((bf16[1,1152,128]{2,1,0:T(8,128)(2,1)S(1)}, bf16[1,1152,128]{2,1,0:T(8,128)(2,1)S(1)}, u32[]{:S(2)}, u32[]{:S(2)}) %collective-permute-start.9) | collective-permute-done | bytes 294944 | tf_op jit(solution)/shard_map/ppermute | solution.py:425
  81.3 1.5 collective-permute-start.15
  82.8 4.4 maximum_maximum_fusion.1.refs_2_
  87.3 6.2 %collective-permute-done.19 = bf16[1,2320,128]{2,1,0:T(8,128)(2,1)S(1)} collective-permute-done((bf16[1,2320,128]{2,1,0:T(8,128)(2,1)}, bf16[1,2320,128]{2,1,0:T(8,128)(2,1)S(1)}, u32[]{:S(2)}, u32[]{:S(2)}) %collective-permute-start.19) | collective-permute-done | bytes 593952 | tf_op jit(solution)/shard_map/ppermute | solution.py:425
  94.2 4.3 collective-permute-done.15
  98.4 1.5 collective-permute-start.20
  100.0 4.4 maximum_maximum_fusion.2.refs_4_
  104.5 1.7 collective-permute-done.20
  106.2 4.4 maximum_maximum_fusion.3.refs_6_
  118.0 16.8 %assemble.1 = (bf16[768,3072]{1,0:T(8,128)(2,1)}, bf16[768,2048]{1,0:T(8,128)(2,1)}, bf16[768,1024]{1,0:T(8,128)(2,1)}, bf16[1024,768]{1,0:T(8,128)(2,1)}, bf16[...) custom-call(s32[256]{0:T(256)} %add.177.target, ...), custom_call_target="tpu_custom_call" | custom-call | tf_op jit(solution)/shard_map/assemble/pallas_call | solution.py:535
  134.8 15.4 %frame_projection.1.key.value = bf16[8,2,1500,256]{3,2,1,0:T(8,128)(2,1)} custom-call(bf16[2,1500,768]{2,1,0:T(8,128)(2,1)} %copy.39.frames.refs_6_, bf16[768,2048]{1,0:T(8,128)(2,1)} %get-tuple-element.80.weight.key_weight.value_weight, f32[8,1,256]{2,1,0:T(1,128)} %bitcast.139), custom_call_target="tpu_custom_call" | custom-call | tf_op jit(solution)/shard_map/frame_projection/pallas_call | solution.py:690
  150.2 9.4 %first_projections.1 = (bf16[896,768]{1,0:T(8,128)(2,1)}, bf16[896,3072]{1,0:T(8,128)(2,1)}) custom-call(bf16[2,896,768]{2,1,0:T(8,128)(2,1)} %bitcast.98, f32[19,768]{1,0:T(8,128)} %copy-done.24, f32[1,3072]{1,0:T(1,128)} %bitcast.138, bf16[768,3072]{1,0:T(8,128)(2,1)} %get-tuple-element.74.weight.query_weight.key_weight.value_weight), custom_call_target="tpu_custom_call" | custom-call | tf_op jit(solution)/shard_map/first_projections/pallas_call | solution.py:882
  159.6 12.6 %self_forward.1 = (bf16[2,448,1024]{2,1,0:T(8,128)(2,1)}, f32[2,4,8,448]{3,2,1,0:T(8,128)}) custom-call(bf16[2,448,3072]{2,1,0:T(8,128)(2,1)} %bitcast.92, bf16[2,448,3072]{2,1,0:T(8,128)(2,1)} %bitcast.93, bf16[2,448,3072]{2,1,0:T(8,128)(2,1)} %bitcast.94, s32[2,448,1]{2,1,0:T(8,128)} %copy.40.seg_col, s32[2,1,448]{2,1,0:T(1,128)} %broadcast_in_dim.146.seg_row, ...), custom_call_target="tpu_custom_call" | custom-call | tf_op jit(solution)/shard_map/self_forward/pallas_call | solution.py:314
  172.4 1.4 copy-done.8
  173.8 1.7 fusion.28
  177.9 2.9 add_convert_fusion.1
  180.7 25.2 %cross_forward.1 = (bf16[2,448,1024]{2,1,0:T(8,128)(2,1)}, f32[2,4,8,448]{3,2,1,0:T(8,128)}) custom-call(bf16[2,448,1024]{2,1,0:T(8,128)(2,1)} %bitcast.111, bf16[8,2,1500,256]{3,2,1,0:T(8,128)(2,1)} %frame_projection.1.key.value, bf16[8,2,1500,256]{3,2,1,0:T(8,128)(2,1)} %frame_projection.1.key.value), custom_call_target="tpu_custom_call" | custom-call | tf_op jit(solution)/shard_map/cross_forward/pallas_call | solution.py:331
  206.0 42.5 %middle.1 = (f32[896,768]{1,0:T(8,128)}, f32[896,768]{1,0:T(8,128)}, bf16[896,1024]{1,0:T(8,128)(2,1)}, bf16[896,768]{1,0:T(8,128)(2,1)}, bf16[896,768]{1,0:T(8,...) custom-call(s32[1]{0:T(128)} %bitcast.rank, ...), custom_call_target="tpu_custom_call" | custom-call | tf_op jit(solution)/shard_map/middle/pallas_call | solution.py:852
  248.5 37.2 %cross_backward.1 = (bf16[2,448,1024]{2,1,0:T(8,128)(2,1)}, bf16[2,1500,256]{2,1,0:T(8,128)(2,1)}, bf16[2,1500,256]{2,1,0:T(8,128)(2,1)}) custom-call(s32[1]{0:T(128)} %bitcast.rank, bf16[2,448,1024]{2,1,0:T(8,128)(2,1)} %bitcast.112, bf16[8,2,1500,256]{3,2,1,0:T(8,128)(2,1)} %frame_projection.1.key.value, ...), custom_call_target="tpu_custom_call" | custom-call | tf_op jit(solution)/shard_map/cross_backward/pallas_call | solution.py:354
  285.7 6.0 %frames_back.1 = bf16[4,2,384,768]{3,2,1,0:T(8,128)(2,1)} custom-call(s32[1]{0:T(128)} %bitcast.rank, bf16[2,1500,256]{2,1,0:T(8,128)(2,1)} %get-tuple-element.96.dk.refs_7_, bf16[2,1500,256]{2,1,0:T(8,128)(2,1)} %get-tuple-element.97.dv.refs_8_, bf16[768,2048]{1,0:T(8,128)(2,1)} %get-tuple-element.80.weight.key_weight.value_weight, ...), custom_call_target="tpu_custom_call" | custom-call | tf_op jit(solution)/shard_map/frames_back/pallas_call | solution.py:718
  291.7 3.7 multiply_reduce_fusion
  295.5 2.3 convert_reduce_fusion.2
  297.8 2.9 convolution_convert_fusion
  300.7 7.1 %self_backward.1 = bf16[2,448,768]{2,1,0:T(8,128)(2,1)} custom-call(s32[1]{0:T(128)} %bitcast.rank, bf16[2,448,3072]{2,1,0:T(8,128)(2,1)} %bitcast.95, bf16[2,448,3072]{2,1,0:T(8,128)(2,1)} %bitcast.96, bf16[2,448,3072]{2,1,0:T(8,128)(2,1)} %bitcast.97, bf16[2,448,1024]{2,1,0:T(8,128)(2,1)} %bitcast.129, bf16[2,448,1024]{2,1,0:T(8,128)(2,1)} %get-tuple-element.76.mixed, ...), custom_call_target="tpu_custom_call" | custom-call | tf_op jit(solution)/shard_map/self_backward/pallas_call | solution.py:383
  307.7 4.9 %first_back.1 = (bf16[896,768]{1,0:T(8,128)(2,1)}, f32[2,768]{1,0:T(2,128)}, f32[1,768]{1,0:T(1,128)}) custom-call(s32[1]{0:T(128)} %bitcast.rank, bf16[896,768]{1,0:T(8,128)(2,1)} %bitcast.108, bf16[768,3072]{1,0:T(8,128)(2,1)} %get-tuple-element.74.weight.query_weight.key_weight.value_weight, ...), custom_call_target="tpu_custom_call" | custom-call | tf_op jit(solution)/shard_map/first_back/pallas_call | solution.py:664
  314.3 1.8 convert_reduce_fusion
  318.5 17.3 %weight_grads.1 = bf16[8,2320,128]{2,1,0:T(8,128)(2,1)} custom-call(s32[1]{0:T(128)} %bitcast.rank, s32[64]{0:T(128)} %get-tuple-element.172.slot, s32[64]{0:T(128)} %get-tuple-element.171.sub, bf16[896,768]{1,0:T(8,128)(2,1)} %get-tuple-element.102.refs_0_, bf16[896,768]{1,0:T(8,128)(2,1)} %get-tuple-element.103.refs_1_, ...), custom_call_target="tpu_custom_call" | custom-call | tf_op jit(solution)/shard_map/weight_grads/pallas_call | solution.py:615
  335.8 1.8 slice.231
  338.6 2.0 constant_dynamic-slice_fusion
  340.6 1.9 collective-permute-done.23
  342.5 3.0 add_convert_fusion
  348.1 1.5 collective-permute-start.26
  349.6 1.3 fusion.10
  350.9 12.4 %collective-permute-done.24 = bf16[2,1152,128]{2,1,0:T(8,128)(2,1)} collective-permute-done((bf16[2,1152,128]{2,1,0:T(8,128)(2,1)}, bf16[2,1152,128]{2,1,0:T(8,128)(2,1)}, u32[]{:S(2)}, u32[]{:S(2)}) %collective-permute-start.24) | collective-permute-done | bytes 589856 | tf_op jit(solution)/shard_map/ppermute | solution.py:637
  363.3 1.2 convert_add_fusion.2
  364.5 1.6 collective-permute-start.25
  366.1 1.2 convert_add_fusion.1
  368.1 5.0 %collective-permute-done.25 = bf16[1152,128]{1,0:T(8,128)(2,1)S(1)} collective-permute-done((bf16[1152,128]{1,0:T(8,128)(2,1)S(1)}, bf16[1152,128]{1,0:T(8,128)(2,1)S(1)}, u32[]{:S(2)}, u32[]{:S(2)}) %collective-permute-start.25) | collective-permute-done | bytes 294944 | tf_op jit(solution)/shard_map/ppermute | solution.py:637
  373.1 2.6 collective-permute-done.27
  375.9 1.1 pad_maximum_fusion.grad
  377.0 17.7 %soap_main.1 = (f32[8,192,192]{2,1,0:T(8,128)}, f32[8,192,192]{2,1,0:T(8,128)}, f32[8,192,192]{2,1,0:T(8,128)}, f32[8,2,192,192]{3,2,1,0:T(8,128)}, f32[8,2,192,...) custom-call(f32[2320,128]{1,0:T(8,128)} %pad_maximum_fusion.grad, f32[8,192,192]{2,1,0:T(8,128)} %bitcast.119, ...), custom_call_target="tpu_custom_call" | custom-call | tf_op jit(solution)/shard_map/soap_main/pallas_call | solution.py:136
  394.7 3.8 collective-permute-start.29
  398.5 2.3 fusion.8
  400.8 1.9 copy-done
  402.7 37.6 %chol_bases.1 = f32[16,192,192]{2,1,0:T(8,128)} custom-call(f32[16,192,192]{2,1,0:T(8,128)S(1)} %bitcast.91, f32[16,192,192]{2,1,0:T(8,128)} %bitcast.124), custom_call_target="tpu_custom_call" | custom-call | tf_op jit(solution)/shard_map/chol_bases/pallas_call | solution.py:144
  441.0 1.4 slice_convert_fusion
  442.4 2.6 copy.43
  (213 shorter events, 26.1 us)
Async XLA Ops:
  7.2 143.0 %all-gather.2.cloned.1.call-start = ((), (), s32[]{:S(2)}) async-start(), calls=%async_computation.2 | async-start | bytes 3440640 | tf_op jit(solution)/shard_map/all_gather | solution.py:947
  10.9 23.3 %collective-permute-start.6 = (bf16[2320,128]{1,0:T(8,128)(2,1)}, bf16[2320,128]{1,0:T(8,128)(2,1)}, u32[]{:S(2)}, u32[]{:S(2)}) collective-permute-start(bf16[2320,128]{1,0:T(8,128)(2,1)} %pack.1), channel_id=1, source_target_pairs={{0,1},{1,2},{2,3},{3,0},{4,5},{5,6},{6,7},{7,4},{8,9},{9,10},{10,1... | collective-permute-start | bytes 1781768 | tf_op jit(solution)/shard_map/ppermute | solution.py:428
  13.9 20.3 %collective-permute-start = (bf16[1,2320,128]{2,1,0:T(8,128)(2,1)}, bf16[1,2320,128]{2,1,0:T(8,128)(2,1)S(1)}, u32[]{:S(2)}, u32[]{:S(2)}) collective-permute-start(bf16[1,2320,128]{2,1,0:T(8,128)(2,1)} %bitcast.125), channel_id=1, source_target_pairs={{0,8},{4,12},{8,0},{12,4},{16,24},{20,28},{24,16},{28,20},{1,9},{5... | collective-permute-start | bytes 1781768 | tf_op jit(solution)/shard_map/ppermute | solution.py:425
  15.4 18.8 %collective-permute-start.1 = (bf16[1,2320,128]{2,1,0:T(8,128)(2,1)}, bf16[1,2320,128]{2,1,0:T(8,128)(2,1)S(1)}, u32[]{:S(2)}, u32[]{:S(2)}) collective-permute-start(bf16[1,2320,128]{2,1,0:T(8,128)(2,1)} %bitcast.126), channel_id=1, source_target_pairs={{0,16},{4,20},{8,24},{12,28},{16,0},{20,4},{24,8},{28,12},{1,17},{... | collective-permute-start | bytes 1781768 | tf_op jit(solution)/shard_map/ppermute | solution.py:425
  16.9 35.7 %collective-permute-start.12 = (bf16[2320,128]{1,0:T(8,128)(2,1)}, bf16[2320,128]{1,0:T(8,128)(2,1)}, u32[]{:S(2)}, u32[]{:S(2)}) collective-permute-start(bf16[2320,128]{1,0:T(8,128)(2,1)} %pack.1), channel_id=1, source_target_pairs={{0,3},{1,0},{2,1},{3,2},{4,7},{5,4},{6,5},{7,6},{8,11},{9,8},{10,9... | collective-permute-start | bytes 1781768 | tf_op jit(solution)/shard_map/ppermute | solution.py:428
  24.2 10.9 %copy-start.12 = (bf16[2320,128]{1,0:T(8,128)(2,1)S(1)}, bf16[2320,128]{1,0:T(8,128)(2,1)}, u32[]{:S(2)}) copy-start(bf16[2320,128]{1,0:T(8,128)(2,1)} %pack.1) | copy-start | bytes 1781764
  24.2 35.7 %copy-start.6 = (bf16[2,112,768]{2,1,0:T(8,128)(2,1)S(1)}, bf16[2,112,768]{2,1,0:T(8,128)(2,1)}, u32[]{:S(2)}) copy-start(bf16[2,112,768]{2,1,0:T(8,128)(2,1)} %param.16) | copy-start | bytes 1032196
  34.2 18.4 %copy-start.23 = (bf16[1,2320,128]{2,1,0:T(8,128)(2,1)}, bf16[1,2320,128]{2,1,0:T(8,128)(2,1)S(1)}, u32[]{:S(2)}) copy-start(bf16[1,2320,128]{2,1,0:T(8,128)(2,1)S(1)} %collective-permute-done) | copy-start | bytes 1781764
  34.2 39.2 %copy-start.18 = (bf16[1,2320,128]{2,1,0:T(8,128)(2,1)}, bf16[1,2320,128]{2,1,0:T(8,128)(2,1)S(1)}, u32[]{:S(2)}) copy-start(bf16[1,2320,128]{2,1,0:T(8,128)(2,1)S(1)} %collective-permute-done.1) | copy-start | bytes 1781764
  34.2 18.4 %collective-permute-start.7 = (bf16[1,2320,128]{2,1,0:T(8,128)(2,1)}, bf16[1,2320,128]{2,1,0:T(8,128)(2,1)S(1)}, u32[]{:S(2)}, u32[]{:S(2)}) collective-permute-start(bf16[1,2320,128]{2,1,0:T(8,128)(2,1)} %bitcast.12), channel_id=1, source_target_pairs={{0,8},{4,12},{8,0},{12,4},{16,24},{20,28},{24,16},{28,20},{1,9},{5... | collective-permute-start | bytes 1781768 | tf_op jit(solution)/shard_map/ppermute | solution.py:425
  34.8 17.8 %collective-permute-start.8 = (bf16[1,2320,128]{2,1,0:T(8,128)(2,1)}, bf16[1,2320,128]{2,1,0:T(8,128)(2,1)S(1)}, u32[]{:S(2)}, u32[]{:S(2)}) collective-permute-start(bf16[1,2320,128]{2,1,0:T(8,128)(2,1)} %bitcast.12), channel_id=1, source_target_pairs={{0,16},{4,20},{8,24},{12,28},{16,0},{20,4},{24,8},{28,12},{1,17},{... | collective-permute-start | bytes 1781768 | tf_op jit(solution)/shard_map/ppermute | solution.py:425
  35.1 32.7 %collective-permute-start.2 = (bf16[2320,128]{1,0:T(8,128)(2,1)S(1)}, bf16[2320,128]{1,0:T(8,128)(2,1)}, u32[]{:S(2)}, u32[]{:S(2)}) collective-permute-start(bf16[2320,128]{1,0:T(8,128)(2,1)S(1)} %copy-done.12), channel_id=1, source_target_pairs={{0,2},{1,3},{2,0},{3,1},{4,6},{5,7},{6,4},{7,5},{8,10},{9,11},{10,... | collective-permute-start | bytes 1781768 | tf_op jit(solution)/shard_map/ppermute | solution.py:428
  52.6 20.8 %copy-start.16 = (bf16[1,2320,128]{2,1,0:T(8,128)(2,1)}, bf16[1,2320,128]{2,1,0:T(8,128)(2,1)S(1)}, u32[]{:S(2)}) copy-start(bf16[1,2320,128]{2,1,0:T(8,128)(2,1)S(1)} %collective-permute-done.8) | copy-start | bytes 1781764
  53.4 17.4 %collective-permute-start.13 = (bf16[1,2320,128]{2,1,0:T(8,128)(2,1)}, bf16[1,2320,128]{2,1,0:T(8,128)(2,1)S(1)}, u32[]{:S(2)}, u32[]{:S(2)}) collective-permute-start(bf16[1,2320,128]{2,1,0:T(8,128)(2,1)} %bitcast.13), channel_id=1, source_target_pairs={{0,8},{4,12},{8,0},{12,4},{16,24},{20,28},{24,16},{28,20},{1,9},{5... | collective-permute-start | bytes 1781768 | tf_op jit(solution)/shard_map/ppermute | solution.py:425
  53.9 18.4 %collective-permute-start.14 = (bf16[1,2320,128]{2,1,0:T(8,128)(2,1)}, bf16[1,2320,128]{2,1,0:T(8,128)(2,1)S(1)}, u32[]{:S(2)}, u32[]{:S(2)}) collective-permute-start(bf16[1,2320,128]{2,1,0:T(8,128)(2,1)} %bitcast.13), channel_id=1, source_target_pairs={{0,16},{4,20},{8,24},{12,28},{16,0},{20,4},{24,8},{28,12},{1,17},{... | collective-permute-start | bytes 1781768 | tf_op jit(solution)/shard_map/ppermute | solution.py:425
  55.2 18.3 %collective-permute-start.4 = (bf16[1,1168,128]{2,1,0:T(8,128)(2,1)}, bf16[1,1168,128]{2,1,0:T(8,128)(2,1)}, u32[]{:S(2)}, u32[]{:S(2)}) collective-permute-start(bf16[1,1168,128]{2,1,0:T(8,128)(2,1)} %slice.210), channel_id=1, source_target_pairs={{0,8},{4,12},{8,0},{12,4},{16,24},{20,28},{24,16},{28,20},{1,9},{5... | collective-permute-start | bytes 897032 | tf_op jit(solution)/shard_map/ppermute | solution.py:425
  58.4 14.5 %collective-permute-start.3 = (bf16[1,1152,128]{2,1,0:T(8,128)(2,1)}, bf16[1,1152,128]{2,1,0:T(8,128)(2,1)}, u32[]{:S(2)}, u32[]{:S(2)}) collective-permute-start(bf16[1,1152,128]{2,1,0:T(8,128)(2,1)} %slice.209), channel_id=1, source_target_pairs={{0,16},{4,20},{8,24},{12,28},{16,0},{20,4},{24,8},{28,12},{1,17},{... | collective-permute-start | bytes 884744 | tf_op jit(solution)/shard_map/ppermute | solution.py:425
  67.9 281.8 %reduce-scatter.3.cloned.1.call-start = ((), (), s32[]{:S(2)}) async-start(), calls=%async_computation.3 | async-start | bytes 1720320 | tf_op jit(solution)/shard_map/reduce_scatter | solution.py:1002
  68.2 13.1 %collective-permute-start.10 = (bf16[1,1168,128]{2,1,0:T(8,128)(2,1)S(1)}, bf16[1,1168,128]{2,1,0:T(8,128)(2,1)S(1)}, u32[]{:S(2)}, u32[]{:S(2)}) collective-permute-start(bf16[1,1168,128]{2,1,0:T(8,128)(2,1)S(1)} %slice.216), channel_id=1, source_target_pairs={{0,8},{4,12},{8,0},{12,4},{16,24},{20,28},{24,16},{28,20},{1,9},{5... | collective-permute-start | bytes 897032 | tf_op jit(solution)/shard_map/ppermute | solution.py:425
  70.8 2.7 copy-start.19
  70.8 10.0 %collective-permute-start.9 = (bf16[1,1152,128]{2,1,0:T(8,128)(2,1)S(1)}, bf16[1,1152,128]{2,1,0:T(8,128)(2,1)S(1)}, u32[]{:S(2)}, u32[]{:S(2)}) collective-permute-start(bf16[1,1152,128]{2,1,0:T(8,128)(2,1)S(1)} %slice.215), channel_id=1, source_target_pairs={{0,16},{4,20},{8,24},{12,28},{16,0},{20,4},{24,8},{28,12},{1,17},{... | collective-permute-start | bytes 884744 | tf_op jit(solution)/shard_map/ppermute | solution.py:425
  72.4 10.5 %copy-start.22 = (bf16[1,2320,128]{2,1,0:T(8,128)(2,1)S(1)}, bf16[1,2320,128]{2,1,0:T(8,128)(2,1)}, u32[]{:S(2)}) copy-start(bf16[1,2320,128]{2,1,0:T(8,128)(2,1)} %copy-done.21) | copy-start | bytes 1781764
  72.4 21.1 %collective-permute-start.19 = (bf16[1,2320,128]{2,1,0:T(8,128)(2,1)}, bf16[1,2320,128]{2,1,0:T(8,128)(2,1)S(1)}, u32[]{:S(2)}, u32[]{:S(2)}) collective-permute-start(bf16[1,2320,128]{2,1,0:T(8,128)(2,1)} %bitcast.14), channel_id=1, source_target_pairs={{0,16},{4,20},{8,24},{12,28},{16,0},{20,4},{24,8},{28,12},{1,17},{... | collective-permute-start | bytes 1781768 | tf_op jit(solution)/shard_map/ppermute | solution.py:425
  72.9 20.6 %collective-permute-start.18 = (bf16[1,2320,128]{2,1,0:T(8,128)(2,1)}, bf16[1,2320,128]{2,1,0:T(8,128)(2,1)S(1)}, u32[]{:S(2)}, u32[]{:S(2)}) collective-permute-start(bf16[1,2320,128]{2,1,0:T(8,128)(2,1)} %bitcast.14), channel_id=1, source_target_pairs={{0,8},{4,12},{8,0},{12,4},{16,24},{20,28},{24,16},{28,20},{1,9},{5... | collective-permute-start | bytes 1781768 | tf_op jit(solution)/shard_map/ppermute | solution.py:425
  73.5 2.6 copy-start.15
  73.5 2.6 copy-start.20
  73.5 9.4 %copy-start.17 = (bf16[1,2320,128]{2,1,0:T(8,128)(2,1)S(1)}, bf16[1,2320,128]{2,1,0:T(8,128)(2,1)}, u32[]{:S(2)}) copy-start(bf16[1,2320,128]{2,1,0:T(8,128)(2,1)} %copy-done.16) | copy-start | bytes 1781764
  76.0 38.9 %copy-start.5 = (bf16[4,2320,128]{2,1,0:T(8,128)(2,1)}, bf16[4,2320,128]{2,1,0:T(8,128)(2,1)S(1)}, u32[]{:S(2)}) copy-start(bf16[4,2320,128]{2,1,0:T(8,128)(2,1)S(1)} %maximum_maximum_fusion.refs_0_) | copy-start | bytes 7127044
  76.0 38.9 %collective-permute-start.5 = (bf16[4,2320,128]{2,1,0:T(8,128)(2,1)S(1)}, bf16[4,2320,128]{2,1,0:T(8,128)(2,1)}, u32[]{:S(2)}, u32[]{:S(2)}) collective-permute-start(bf16[4,2320,128]{2,1,0:T(8,128)(2,1)S(1)} %maximum_maximum_fusion.refs_0_), channel_id=1, source_target_pairs={{0,4},{4,0},{8,12},{12,8},{16,20},{20,16},{24,28},{28,24},{1,5},{5... | collective-permute-start | bytes 7127048 | tf_op jit(solution)/shard_map/ppermute | solution.py:425
  80.8 19.2 %collective-permute-start.16 = (bf16[1,1168,128]{2,1,0:T(8,128)(2,1)S(1)}, bf16[1,1168,128]{2,1,0:T(8,128)(2,1)S(1)}, u32[]{:S(2)}, u32[]{:S(2)}) collective-permute-start(bf16[1,1168,128]{2,1,0:T(8,128)(2,1)S(1)} %slice.218), channel_id=1, source_target_pairs={{0,8},{4,12},{8,0},{12,4},{16,24},{20,28},{24,16},{28,20},{1,9},{5... | collective-permute-start | bytes 897032 | tf_op jit(solution)/shard_map/ppermute | solution.py:425
  81.3 17.1 %collective-permute-start.15 = (bf16[1,1152,128]{2,1,0:T(8,128)(2,1)S(1)}, bf16[1,1152,128]{2,1,0:T(8,128)(2,1)S(1)}, u32[]{:S(2)}, u32[]{:S(2)}) collective-permute-start(bf16[1,1152,128]{2,1,0:T(8,128)(2,1)S(1)} %slice.217), channel_id=1, source_target_pairs={{0,16},{4,20},{8,24},{12,28},{16,0},{20,4},{24,8},{28,12},{1,17},{... | collective-permute-start | bytes 884744 | tf_op jit(solution)/shard_map/ppermute | solution.py:425
  93.5 24.5 %collective-permute-start.11 = (bf16[4,2320,128]{2,1,0:T(8,128)(2,1)}, bf16[4,2320,128]{2,1,0:T(8,128)(2,1)}, u32[]{:S(2)}, u32[]{:S(2)}) collective-permute-start(bf16[4,2320,128]{2,1,0:T(8,128)(2,1)} %maximum_maximum_fusion.1.refs_2_), channel_id=1, source_target_pairs={{0,4},{4,0},{8,12},{12,8},{16,20},{20,16},{24,28},{28,24},{1,5},{5... | collective-permute-start | bytes 7127048 | tf_op jit(solution)/shard_map/ppermute | solution.py:425
  93.5 12.6 %collective-permute-start.21 = (bf16[1,1168,128]{2,1,0:T(8,128)(2,1)S(1)}, bf16[1,1168,128]{2,1,0:T(8,128)(2,1)S(1)}, u32[]{:S(2)}, u32[]{:S(2)}) collective-permute-start(bf16[1,1168,128]{2,1,0:T(8,128)(2,1)S(1)} %slice.220), channel_id=1, source_target_pairs={{0,8},{4,12},{8,0},{12,4},{16,24},{20,28},{24,16},{28,20},{1,9},{5... | collective-permute-start | bytes 897032 | tf_op jit(solution)/shard_map/ppermute | solution.py:425
  98.4 7.7 %collective-permute-start.20 = (bf16[1,1152,128]{2,1,0:T(8,128)(2,1)S(1)}, bf16[1,1152,128]{2,1,0:T(8,128)(2,1)S(1)}, u32[]{:S(2)}, u32[]{:S(2)}) collective-permute-start(bf16[1,1152,128]{2,1,0:T(8,128)(2,1)S(1)} %slice.219), channel_id=1, source_target_pairs={{0,16},{4,20},{8,24},{12,28},{16,0},{20,4},{24,8},{28,12},{1,17},{... | collective-permute-start | bytes 884744 | tf_op jit(solution)/shard_map/ppermute | solution.py:425
  104.4 6.2 %copy-start.35 = (s32[32]{0:T(128)S(1)}, s32[32]{0:T(128)}, u32[]{:S(2)}) copy-start(s32[32]{0:T(128)} %constant.133.clone) | copy-start | bytes 388
  104.4 6.4 %copy-start.39 = (s32[32]{0:T(128)S(1)}, s32[32]{0:T(128)}, u32[]{:S(2)}) copy-start(s32[32]{0:T(128)} %constant.152) | copy-start | bytes 388
  104.4 6.6 %copy-start.26 = (s32[2,448]{1,0:T(2,128)S(1)}, s32[2,448]{1,0:T(2,128)}, u32[]{:S(2)}) copy-start(s32[2,448]{1,0:T(2,128)} %param.19) | copy-start | bytes 10756
  104.4 8.2 %copy-start.27 = (s32[2,448]{1,0:T(2,128)S(1)}, s32[2,448]{1,0:T(2,128)}, u32[]{:S(2)}) copy-start(s32[2,448]{1,0:T(2,128)} %param.20) | copy-start | bytes 10756
  104.4 9.8 %copy-start.34 = (s32[64]{0:T(128)S(1)}, s32[64]{0:T(128)}, u32[]{:S(2)}) copy-start(s32[64]{0:T(128)} %param.21) | copy-start | bytes 772
  104.4 13.6 %collective-permute-start.17 = (bf16[4,2320,128]{2,1,0:T(8,128)(2,1)}, bf16[4,2320,128]{2,1,0:T(8,128)(2,1)}, u32[]{:S(2)}, u32[]{:S(2)}) collective-permute-start(bf16[4,2320,128]{2,1,0:T(8,128)(2,1)} %maximum_maximum_fusion.2.refs_4_), channel_id=1, source_target_pairs={{0,4},{4,0},{8,12},{12,8},{16,20},{20,16},{24,28},{28,24},{1,5},{5... | collective-permute-start | bytes 7127048 | tf_op jit(solution)/shard_map/ppermute | solution.py:425
  110.6 7.4 %collective-permute-start.22 = (bf16[4,2320,128]{2,1,0:T(8,128)(2,1)}, bf16[4,2320,128]{2,1,0:T(8,128)(2,1)}, u32[]{:S(2)}, u32[]{:S(2)}) collective-permute-start(bf16[4,2320,128]{2,1,0:T(8,128)(2,1)} %maximum_maximum_fusion.3.refs_6_), channel_id=1, source_target_pairs={{0,4},{4,0},{8,12},{12,8},{16,20},{20,16},{24,28},{28,24},{1,5},{5... | collective-permute-start | bytes 7127048 | tf_op jit(solution)/shard_map/ppermute | solution.py:425
  116.0 18.8 %copy-start.24 = (f32[19,768]{1,0:T(8,128)}, f32[19,768]{1,0:T(8,128)S(1)}, u32[]{:S(2)}) copy-start(f32[19,768]{1,0:T(8,128)S(1)} %reshape.323.vectors.refs_3_) | copy-start | bytes 175108
  159.6 12.6 %copy-start.3 = (bf16[2,2,448,768]{3,2,1,0:T(8,128)(2,1)S(1)}, bf16[2,2,448,768]{3,2,1,0:T(8,128)(2,1)}, u32[]{:S(2)}) copy-start(bf16[2,2,448,768]{3,2,1,0:T(8,128)(2,1)} %all-gather.2.cloned.1.call-done) | copy-start | bytes 8257540
  159.6 12.8 %copy-start.36 = (bf16[1024,768]{1,0:T(8,128)(2,1)S(1)}, bf16[1024,768]{1,0:T(8,128)(2,1)}, u32[]{:S(2)}) copy-start(bf16[1024,768]{1,0:T(8,128)(2,1)} %get-tuple-element.77) | copy-start | bytes 4718596
  176.0 1.9 copy-start.38
  177.0 3.7 copy-start.9
  285.7 6.0 %copy-start.2 = (f32[896,768]{1,0:T(8,128)S(1)}, f32[896,768]{1,0:T(8,128)}, u32[]{:S(2)}) copy-start(f32[896,768]{1,0:T(8,128)} %copy-done.1) | copy-start | bytes 8257540
  285.7 6.0 %copy-start.7 = (bf16[2,448,1024]{2,1,0:T(8,128)(2,1)S(1)}, bf16[2,448,1024]{2,1,0:T(8,128)(2,1)}, u32[]{:S(2)}) copy-start(bf16[2,448,1024]{2,1,0:T(8,128)(2,1)} %get-tuple-element.95) | copy-start | bytes 5505028
  291.7 3.8 copy-start.11
  295.5 2.3 copy-start.37
  297.8 2.9 copy-start.10
  307.7 5.7 %copy-start.4 = (bf16[2,1500,256]{2,1,0:T(8,128)(2,1)S(1)}, bf16[2,1500,256]{2,1,0:T(8,128)(2,1)}, u32[]{:S(2)}) copy-start(bf16[2,1500,256]{2,1,0:T(8,128)(2,1)} %get-tuple-element.97.dv.refs_8_) | copy-start | bytes 4608004
  312.7 128.3 %reduce-scatter.5.cloned.1.call-start = ((), (), s32[]{:S(2)}) async-start(), calls=%async_computation.4 | async-start | bytes 5898240 | tf_op jit(solution)/shard_map/reduce_scatter | solution.py:987
  337.6 4.9 %collective-permute-start.23 = (bf16[4,2320,128]{2,1,0:T(8,128)(2,1)S(1)}, bf16[4,2320,128]{2,1,0:T(8,128)(2,1)}, u32[]{:S(2)}, u32[]{:S(2)}) collective-permute-start(bf16[4,2320,128]{2,1,0:T(8,128)(2,1)S(1)} %slice.231), channel_id=1, source_target_pairs={{0,4},{4,0},{8,12},{12,8},{16,20},{20,16},{24,28},{28,24},{1,5},{5... | collective-permute-start | bytes 7127048 | tf_op jit(solution)/shard_map/ppermute | solution.py:637
  347.3 15.9 %collective-permute-start.24 = (bf16[2,1152,128]{2,1,0:T(8,128)(2,1)}, bf16[2,1152,128]{2,1,0:T(8,128)(2,1)}, u32[]{:S(2)}, u32[]{:S(2)}) collective-permute-start(bf16[2,1152,128]{2,1,0:T(8,128)(2,1)} %pad_maximum_fusion.2), channel_id=1, source_target_pairs={{0,8},{4,12},{8,0},{12,4},{16,24},{20,28},{24,16},{28,20},{1,9},{5... | collective-permute-start | bytes 1769480 | tf_op jit(solution)/shard_map/ppermute | solution.py:637
  348.1 18.0 %collective-permute-start.26 = (bf16[2,1168,128]{2,1,0:T(8,128)(2,1)}, bf16[2,1168,128]{2,1,0:T(8,128)(2,1)}, u32[]{:S(2)}, u32[]{:S(2)}) collective-permute-start(bf16[2,1168,128]{2,1,0:T(8,128)(2,1)} %slice.239), channel_id=1, source_target_pairs={{0,16},{4,20},{8,24},{12,28},{16,0},{20,4},{24,8},{28,12},{1,17},{... | collective-permute-start | bytes 1794056 | tf_op jit(solution)/shard_map/ppermute | solution.py:637
  364.5 8.5 %collective-permute-start.25 = (bf16[1152,128]{1,0:T(8,128)(2,1)S(1)}, bf16[1152,128]{1,0:T(8,128)(2,1)S(1)}, u32[]{:S(2)}, u32[]{:S(2)}) collective-permute-start(bf16[1152,128]{1,0:T(8,128)(2,1)S(1)} %fusion.14), channel_id=1, source_target_pairs={{0,16},{4,20},{8,24},{12,28},{16,0},{20,4},{24,8},{28,12},{1,17},{... | collective-permute-start | bytes 884744 | tf_op jit(solution)/shard_map/ppermute | solution.py:637
  367.4 8.3 %collective-permute-start.27 = (bf16[1168,128]{1,0:T(8,128)(2,1)S(1)}, bf16[1168,128]{1,0:T(8,128)(2,1)S(1)}, u32[]{:S(2)}, u32[]{:S(2)}) collective-permute-start(bf16[1168,128]{1,0:T(8,128)(2,1)S(1)} %fusion.13), channel_id=1, source_target_pairs={{0,8},{4,12},{8,0},{12,4},{16,24},{20,28},{24,16},{28,20},{1,9},{5... | collective-permute-start | bytes 897032 | tf_op jit(solution)/shard_map/ppermute | solution.py:637
  375.8 18.9 %collective-permute-start.28 = (f32[16,128]{1,0:T(8,128)S(1)}, f32[16,128]{1,0:T(8,128)S(1)}, u32[]{:S(2)}, u32[]{:S(2)}) collective-permute-start(f32[16,128]{1,0:T(8,128)S(1)} %slice.242), channel_id=1, source_target_pairs={{0,1},{1,0},{2,3},{3,2},{4,5},{5,4},{6,7},{7,6},{8,9},{9,8},{10,11... | collective-permute-start | bytes 24584 | tf_op jit(solution)/shard_map/ppermute | solution.py:1044
  377.0 21.5 %copy-start.13 = (bf16[2,112,768]{2,1,0:T(8,128)(2,1)S(1)}, bf16[2,112,768]{2,1,0:T(8,128)(2,1)}, u32[]{:S(2)}) copy-start(bf16[2,112,768]{2,1,0:T(8,128)(2,1)} %reduce-scatter.3.cloned.1.call-done) | copy-start | bytes 1032196
  394.7 45.6 %collective-permute-start.29 = (f32[16,128]{1,0:T(8,128)S(1)}, f32[16,128]{1,0:T(8,128)S(1)}, u32[]{:S(2)}, u32[]{:S(2)}) collective-permute-start(f32[16,128]{1,0:T(8,128)S(1)} %slice_add_fusion), channel_id=1, source_target_pairs={{0,2},{1,3},{2,0},{3,1},{4,6},{5,7},{6,4},{7,5},{8,10},{9,11},{10,... | collective-permute-start | bytes 24584 | tf_op jit(solution)/shard_map/ppermute | solution.py:1044
  402.7 37.7 %copy-start.25 = (f32[1824]{0:T(1024)S(1)}, f32[1824]{0:T(1024)}, u32[]{:S(2)}) copy-start(f32[1824]{0:T(1024)} %param.27) | copy-start | bytes 21892
  402.7 37.7 %copy-start.30 = (f32[1824]{0:T(1024)S(1)}, f32[1824]{0:T(1024)}, u32[]{:S(2)}) copy-start(f32[1824]{0:T(1024)} %param.28) | copy-start | bytes 21892
  402.7 37.7 %copy-start.31 = (f32[1824]{0:T(1024)S(1)}, f32[1824]{0:T(1024)}, u32[]{:S(2)}) copy-start(f32[1824]{0:T(1024)} %param.29) | copy-start | bytes 21892
  (9 other events, 11.0 us)
Sparse Core Ops, SparseCore 0:
  68.0 57.9 all-gather.1
  312.8 33.4 reduce-scatter.2
  348.7 84.4 reduce-scatter.4
